TPU v7x, 32 devices: a whole 2x2x4 slice. The times are simulated.
32 devices in a mesh: ctx: 8 (over z, core), dp: 2 (over x), pipe: 2 (over y).
Axes of the slice: x: 2, y: 2, z: 4, core: 2. Of those that a mesh axis runs over, the one named last changes fastest.
Arguments:
- queries: bfloat16 [2, 2048, 4096], P('pipe', ('dp', 'ctx')), parts along dimension 1, may hold values from -6 to 6
- keys: bfloat16 [2, 2048, 4096], P('pipe', ('dp', 'ctx')), parts along dimension 1, may hold values from -6 to 6
- values: bfloat16 [2, 2048, 4096], P('pipe', ('dp', 'ctx')), parts along dimension 1, may hold values from -6 to 6
- residual: bfloat16 [2048, 4096], P(('dp', 'ctx')), parts along dimension 0, may hold values from -6 to 6
- filter_bank: bfloat16 [2, 256, 128], P('pipe'), may hold values from -0.5 to 0.5
- filter_scales: float32 [2, 256], P('pipe'), may hold values from 0.25 to 4
- group_filter: int32 [2, 256], P('pipe'), may hold values from 0 to 255
- context_start: int32 [2], P('dp'), parts along dimension 0, may hold values from 0 to 255
Outputs:
- section_out: bfloat16 [2, 2048, 4096], P('pipe', ('dp', 'ctx')), parts along dimension 1
There are 2 independent parts, one for each index of `dp`. A program takes and returns all parts, laid end to end along the dimension named above; an argument that names none is the same for every part. Nothing has to cross between parts.
All inputs are finite; a program needn't handle non-finite values.
Results may differ from a plain program's by a relative error of at most 0.0058.
Values may be sent and summed in bfloat16 or wider, within the bound.
No kernel may reach another device: no remote copies, remote signals or barrier semaphores. Data moves between devices by JAX's collectives and lax.ppermute only.
A program may use at most 64 MiB of HBM per device.

v0:
```python
import jax
import jax.numpy as jnp
from jax import lax
from jax.sharding import PartitionSpec as P


def from_behind(value, axis, steps):
    count = lax.axis_size(axis)
    first, last = (max(0, -steps), min(count, count - steps))
    return lax.ppermute(value, axis, [(source, source + steps) for source in range(first, last)])


def kernel_for(bank_rows, scale_rows, assign_rows, chan_width):
    bank_size = bank_rows.shape[0]
    groups = assign_rows.shape[0]
    onehot = (assign_rows[:, None] == jnp.arange(bank_size, dtype=jnp.int32)[None, :]).astype(
        jnp.bfloat16
    )
    tap_values = (
        jnp.dot(onehot, bank_rows, preferred_element_type=jnp.float32) * scale_rows[:, None]
    ).astype(jnp.bfloat16)
    per_channel = jnp.repeat(tap_values, chan_width // groups, axis=0)
    return jnp.flip(per_channel.T, 0)[:, None, :]


def causal_filter(extended, kernel):
    result = lax.conv_general_dilated(
        extended[None],
        kernel,
        (1,),
        "VALID",
        dimension_numbers=("NWC", "WIO", "NWC"),
        feature_group_count=kernel.shape[2],
        preferred_element_type=jnp.float32,
    )
    return result[0]


def body(queries, keys, values, residual, filter_bank, filter_scales, group_filter, context_start):
    row_count = queries.shape[1]
    chan_width = queries.shape[2]
    tap_count = filter_bank.shape[2]
    edge_rows = tap_count - 1
    kernel = kernel_for(filter_bank[0], filter_scales[0], group_filter[0], chan_width)
    slab_start = lax.axis_index("ctx") * row_count
    positions = slab_start + jnp.arange(row_count, dtype=jnp.int32)
    inside = (positions >= context_start[0]).astype(jnp.float32)[:, None]
    product = (inside * keys[0].astype(jnp.float32) * values[0].astype(jnp.float32)).astype(
        jnp.bfloat16
    )
    product_edge = from_behind(product[row_count - edge_rows :], "ctx", 1)
    mixed = causal_filter(jnp.concatenate([product_edge, product], axis=0), kernel)
    gated = queries[0].astype(jnp.float32) * mixed
    own = (residual.astype(jnp.float32) + gated).astype(jnp.bfloat16)
    received = from_behind(own, "pipe", 1)
    later = (received.astype(jnp.float32) + gated).astype(jnp.bfloat16)
    is_first = lax.axis_index("pipe") == 0
    output = jnp.where(is_first, own, later)
    return output[None]


def solution(mesh):
    return jax.shard_map(
        body,
        mesh=mesh,
        in_specs=(
            P("pipe", ("dp", "ctx"), None),
            P("pipe", ("dp", "ctx"), None),
            P("pipe", ("dp", "ctx"), None),
            P(("dp", "ctx"), None),
            P("pipe", None, None),
            P("pipe", None),
            P("pipe", None),
            P("dp"),
        ),
        out_specs=P("pipe", ("dp", "ctx"), None),
        check_vma=False,
    )
```

profile of v0, /device:TPU:12, one launch (start us, length us, event | category | flops | bytes accessed | tf_op | source)
XLA Modules:
  0.0 85.3 jit_solution(9159229470053849115)
XLA Ops:
  0.0 0.0 copy-start
  0.7 0.0 copy-start.4
  0.7 0.0 copy-start.5
  0.7 2.0 %fusion.3 = bf16[128,4096]{1,0:T(8,128)(2,1)S(1)} fusion(bf16[1,128,4096]{2,1,0:T(8,128)(2,1)} %param.10, bf16[1,128,4096]{2,1,0:T(8,128)(2,1)} %param.9, f32[128]{0:T(128)S(1)} %compare_convert_fusion), kind=kLoop, calls=%fused_computation.8 | loop fusion | flops 2621440 | bytes 3146240 | tf_op jit(solution)/shard_map/convert_element_type | solution.py:48
  2.7 1.2 %slice.4 = bf16[127,4096]{1,0:T(8,128)(2,1)} slice(bf16[128,4096]{1,0:T(8,128)(2,1)S(1)} %fusion.3), slice={[1:128], [0:4096]} | slice | bytes 2080768 | tf_op jit(solution)/shard_map/slice | solution.py:51
  3.9 1.9 %collective-permute-start = (bf16[127,4096]{1,0:T(8,128)(2,1)}, bf16[127,4096]{1,0:T(8,128)(2,1)}, u32[]{:S(2)}, u32[]{:S(2)}) collective-permute-start(bf16[127,4096]{1,0:T(8,128)(2,1)} %slice.4), channel_id=1, source_target_pairs={{0,4},{4,8},{8,12},{12,16},{16,20},{20,24},{24,28},{1,5},{5,9},{9,... | collective-permute-start | bytes 3121160 | tf_op jit(solution)/shard_map/ppermute | solution.py:10
  5.8 0.0 copy-done
  5.8 0.0 copy-done.4
  5.9 0.0 copy-done.5
  5.9 0.2 fusion.4
  6.1 0.1 broadcast_in_dim.15
  6.2 2.9 %rev.4 = bf16[128,4096]{0,1:T(8,128)(2,1)S(1)} reverse(bf16[128,4096]{0,1:T(8,128)(2,1)S(1)} %bitcast.34), dimensions={0} | reverse | bytes 2097152 | tf_op jit(solution)/shard_map/jit(_flip)/rev | solution.py:23
  9.2 4.3 %copy.14 = bf16[128,1,4096]{2,1,0:T(2,128)(2,1)} copy(bf16[128,1,4096]{0,2,1:T(8,128)(2,1)S(1)} %bitcast.33) | data formatting | bytes 2097152 | tf_op jit(solution)/shard_map/broadcast_in_dim | solution.py:23
  13.4 0.0 copy-start.1
  13.4 0.0 copy-start.3
  13.4 6.9 %collective-permute-done = bf16[127,4096]{1,0:T(8,128)(2,1)} collective-permute-done((bf16[127,4096]{1,0:T(8,128)(2,1)}, bf16[127,4096]{1,0:T(8,128)(2,1)}, u32[]{:S(2)}, u32[]{:S(2)}) %collective-permute-start) | collective-permute-done | bytes 1040416 | tf_op jit(solution)/shard_map/ppermute | solution.py:10
  20.3 1.5 %maximum_bitcast_fusion = bf16[1,255,4096]{2,1,0:T(8,128)(2,1)S(1)} fusion(bf16[128,4096]{1,0:T(8,128)(2,1)S(1)} %fusion.3, bf16[127,4096]{1,0:T(8,128)(2,1)} %collective-permute-done), kind=kLoop, calls=%fused_computation.2 | loop fusion | flops 4177920 | bytes 4177920 | tf_op jit(solution)/shard_map/broadcast_in_dim | solution.py:28
  21.9 0.0 copy-done.1
  21.9 0.0 copy-done.3
  21.9 0.0 copy-start.2
  21.9 31.6 %convolution_multiply_fusion = f32[1,128,4096]{2,0,1:T(1,128)S(1)} fusion(bf16[128,1,4096]{2,1,0:T(2,128)(2,1)S(1)} %copy-done.1, bf16[1,255,4096]{2,1,0:T(8,128)(2,1)S(1)} %maximum_bitcast_fusion, bf16[1,128,4096]{2,1,0:T(8,128)(2,1)S(1)} %copy-done.3), kind=kOutput, calls=%fused_computation | convolution fusion | flops 135266304 | bytes 6283264 | tf_op jit(solution)/shard_map/conv_general_dilated | solution.py:27
  53.5 0.0 copy-done.2
  53.5 1.9 %fusion.1 = bf16[128,4096]{1,0:T(8,128)(2,1)S(1)} fusion(bf16[128,4096]{1,0:T(8,128)(2,1)S(1)} %copy-done.2, f32[1,128,4096]{2,0,1:T(1,128)S(1)} %convolution_multiply_fusion), kind=kLoop, calls=%fused_computation.5 | loop fusion | flops 1572864 | bytes 4194304 | tf_op jit(solution)/shard_map/convert_element_type | solution.py:54
  55.4 1.3 %collective-permute-start.1 = (bf16[128,4096]{1,0:T(8,128)(2,1)S(1)}, bf16[128,4096]{1,0:T(8,128)(2,1)}, u32[]{:S(2)}, u32[]{:S(2)}) collective-permute-start(bf16[128,4096]{1,0:T(8,128)(2,1)S(1)} %fusion.1), channel_id=1, source_target_pairs={{0,1},{2,3},{4,5},{6,7},{8,9},{10,11},{12,13},{14,15},{16,17},{18,... | collective-permute-start | bytes 3145736 | tf_op jit(solution)/shard_map/ppermute | solution.py:10
  56.7 25.0 %collective-permute-done.1 = bf16[128,4096]{1,0:T(8,128)(2,1)} collective-permute-done((bf16[128,4096]{1,0:T(8,128)(2,1)S(1)}, bf16[128,4096]{1,0:T(8,128)(2,1)}, u32[]{:S(2)}, u32[]{:S(2)}) %collective-permute-start.1) | collective-permute-done | bytes 1048608 | tf_op jit(solution)/shard_map/ppermute | solution.py:10
  81.7 3.6 %fusion.6 = bf16[1,128,4096]{2,1,0:T(8,128)(2,1)} fusion(bf16[128,4096]{1,0:T(8,128)(2,1)S(1)} %fusion.1, f32[1,128,4096]{2,0,1:T(1,128)S(1)} %convolution_multiply_fusion, bf16[128,4096]{1,0:T(8,128)(2,1)} %collective-permute-done.1, pred[]{:T(512)S(6)} %eq.18), kind=kLoop, calls=%fused_computation.14 | loop fusion | flops 2097152 | bytes 5242881 | tf_op jit(solution)/shard_map/broadcast_in_dim | solution.py:59
  (1 shorter events, 0.0 us)
Async XLA Ops:
  0.0 5.8 %copy-start = (bf16[1,256,128]{2,1,0:T(8,128)(2,1)S(1)}, bf16[1,256,128]{2,1,0:T(8,128)(2,1)}, u32[]{:S(2)}) copy-start(bf16[1,256,128]{2,1,0:T(8,128)(2,1)} %param.12) | copy-start | bytes 196612
  0.7 5.1 %copy-start.4 = (s32[1,256]{1,0:T(1,128)S(1)}, s32[1,256]{1,0:T(1,128)}, u32[]{:S(2)}) copy-start(s32[1,256]{1,0:T(1,128)} %param.14) | copy-start | bytes 3076
  0.7 5.1 %copy-start.5 = (f32[1,256]{1,0:T(1,128)S(1)}, f32[1,256]{1,0:T(1,128)}, u32[]{:S(2)}) copy-start(f32[1,256]{1,0:T(1,128)} %param.13) | copy-start | bytes 3076
  3.9 16.4 %collective-permute-start = (bf16[127,4096]{1,0:T(8,128)(2,1)}, bf16[127,4096]{1,0:T(8,128)(2,1)}, u32[]{:S(2)}, u32[]{:S(2)}) collective-permute-start(bf16[127,4096]{1,0:T(8,128)(2,1)} %slice.4), channel_id=1, source_target_pairs={{0,4},{4,8},{8,12},{12,16},{16,20},{20,24},{24,28},{1,5},{5,9},{9,... | collective-permute-start | bytes 3121160 | tf_op jit(solution)/shard_map/ppermute | solution.py:10
  13.4 8.5 %copy-start.1 = (bf16[128,1,4096]{2,1,0:T(2,128)(2,1)S(1)}, bf16[128,1,4096]{2,1,0:T(2,128)(2,1)}, u32[]{:S(2)}) copy-start(bf16[128,1,4096]{2,1,0:T(2,128)(2,1)} %copy.14) | copy-start | bytes 3145732
  13.4 8.5 %copy-start.3 = (bf16[1,128,4096]{2,1,0:T(8,128)(2,1)S(1)}, bf16[1,128,4096]{2,1,0:T(8,128)(2,1)}, u32[]{:S(2)}) copy-start(bf16[1,128,4096]{2,1,0:T(8,128)(2,1)} %param.8) | copy-start | bytes 3145732
  21.9 31.6 %copy-start.2 = (bf16[128,4096]{1,0:T(8,128)(2,1)S(1)}, bf16[128,4096]{1,0:T(8,128)(2,1)}, u32[]{:S(2)}) copy-start(bf16[128,4096]{1,0:T(8,128)(2,1)} %param.11) | copy-start | bytes 3145732
  55.4 26.3 %collective-permute-start.1 = (bf16[128,4096]{1,0:T(8,128)(2,1)S(1)}, bf16[128,4096]{1,0:T(8,128)(2,1)}, u32[]{:S(2)}, u32[]{:S(2)}) collective-permute-start(bf16[128,4096]{1,0:T(8,128)(2,1)S(1)} %fusion.1), channel_id=1, source_target_pairs={{0,1},{2,3},{4,5},{6,7},{8,9},{10,11},{12,13},{14,15},{16,17},{18,... | collective-permute-start | bytes 3145736 | tf_op jit(solution)/shard_map/ppermute | solution.py:10
where the time goes:
time: 85.6 us; the launch traced here: 85.3 us
  waiting for transfers between devices  31.9 us (37%)
  matrix products  31.8 us (37%)
  other arithmetic  9.02 us (11%)
  local copies, waits for them, and re-layouts  8.58 us (10%)
  starting transfers between devices  3.2 us (4%)
    ppermute x2, waiting for transfers between devices, from_behind(): lax.ppermute(value, axis, [(source, source + steps) for source in range(f...  31.9 us
    conv_general_dilated x1, matrix products, causal_filter(): lax.conv_general_dilated(extended[None], kernel, (1,), 'VALID', dimension...  31.6 us
    broadcast_in_dim x1, local copies, waits for them, and re-layouts, kernel_for(): return jnp.flip(per_channel.T, 0)[:, None, :]  4.26 us
    broadcast_in_dim x1, other arithmetic, body(): return output[None]  3.65 us
    ppermute x2, starting transfers between devices, from_behind(): lax.ppermute(value, axis, [(source, source + steps) for source in range(f...  3.2 us
    rev x1, local copies, waits for them, and re-layouts, kernel_for(): return jnp.flip(per_channel.T, 0)[:, None, :]  2.92 us
    convert_element_type x1, other arithmetic, body(): (inside * keys[0].astype(jnp.float32) * values[0].astype(jnp.float32)).as...  1.96 us
    convert_element_type x1, other arithmetic, body(): own = (residual.astype(jnp.float32) + gated).astype(jnp.bfloat16)  1.87 us
  transfers between devices with their start and end apart: 2, of which 2 were waited for; matrix products, arithmetic and copies ran while one was open for 9% of the time, Pallas kernels for 0%

commit v1 on v0

v1 whole, which is shorter than its diff:
```python
import functools

import jax
import jax.numpy as jnp
from jax import lax
from jax.experimental import pallas as pl
from jax.experimental.pallas import tpu as pltpu
from jax.sharding import PartitionSpec as P

LANES = 128
ROW_BLOCK = 32
CHUNKS = 4
F32 = jnp.float32
BF16 = jnp.bfloat16


def from_behind(value, axis, steps):
    count = lax.axis_size(axis)
    first, last = (max(0, -steps), min(count, count - steps))
    return lax.ppermute(value, axis, [(source, source + steps) for source in range(first, last)])


def smem():
    return pl.BlockSpec(memory_space=pltpu.SMEM)


def product_kernel(start_ref, keys_ref, values_ref, out_ref):
    rows, cols = out_ref.shape
    positions = lax.axis_index("ctx") * rows + lax.broadcasted_iota(jnp.int32, (rows, cols), 0)
    product = keys_ref[0].astype(F32) * values_ref[0].astype(F32)
    out_ref[...] = jnp.where(positions >= start_ref[0], product, 0.0).astype(BF16)


def product_of(context_start, keys, values, first, width, block):
    rows = keys.shape[1]
    offset = first // block
    spec = pl.BlockSpec((1, rows, block), lambda i: (0, 0, i + offset))
    return pl.pallas_call(
        product_kernel,
        grid=(width // block,),
        out_shape=jax.ShapeDtypeStruct((rows, width), BF16),
        in_specs=[smem(), spec, spec],
        out_specs=pl.BlockSpec((rows, block), lambda i: (0, i)),
        cost_estimate=pl.CostEstimate(flops=rows * width, bytes_accessed=rows * width * 6, transcendentals=0),
        name="product",
    )(context_start, keys, values)


def taps_kernel(bank_ref, scales_ref, assign_ref, out_ref):
    groups, taps = out_ref.shape
    size = bank_ref.shape[1]
    chosen = (lax.broadcasted_iota(jnp.int32, (size, groups), 0) == assign_ref[...]).astype(F32).astype(BF16)
    contract = (((0,), (0,)), ((), ()))
    picked = lax.dot_general(bank_ref[0], chosen, contract, preferred_element_type=F32)
    scaled = (picked * scales_ref[...]).astype(BF16)
    order = lax.broadcasted_iota(jnp.int32, (taps, taps), 0) + lax.broadcasted_iota(jnp.int32, (taps, taps), 1)
    flip = (order == taps - 1).astype(F32).astype(BF16)
    out_ref[...] = lax.dot_general(scaled, flip, contract, preferred_element_type=F32)


def reversed_taps(bank, scales, assign):
    groups, taps = assign.shape[1], bank.shape[2]
    return pl.pallas_call(
        taps_kernel,
        out_shape=jax.ShapeDtypeStruct((groups, taps), F32),
        cost_estimate=pl.CostEstimate(flops=groups * groups * taps * 4, bytes_accessed=300000, transcendentals=0),
        name="taps",
    )(bank, scales, assign)


def block_kernel(taps_ref, behind_ref, product_ref, queries_ref, residual_ref, out_ref):
    rows, cols = out_ref.shape
    taps = taps_ref.shape[1]
    per_lanes = taps_ref.shape[0] * LANES // cols
    chan = LANES // per_lanes
    is_first = lax.axis_index("pipe") == 0
    keep = jnp.where(is_first, 1.0, 0.0).astype(F32)
    row = lax.broadcasted_iota(jnp.int32, (ROW_BLOCK, taps), 0)
    lane = lax.broadcasted_iota(jnp.int32, (ROW_BLOCK, taps), 1)
    upper = lane > row
    member = lax.broadcasted_iota(jnp.int32, (ROW_BLOCK, LANES), 1) // chan
    for tile in range(cols // LANES):
        at = slice(tile * LANES, (tile + 1) * LANES)
        near, far = [], []
        for group in range(per_lanes):
            line = taps_ref[tile * per_lanes + group : tile * per_lanes + group + 1, :]
            turned = pltpu.roll(jnp.broadcast_to(line, (ROW_BLOCK, taps)), 1, 1, stride=1, stride_axis=0)
            far.append(jnp.where(upper, turned, 0.0).astype(BF16))
            near.append(jnp.where(upper, 0.0, turned)[:, :ROW_BLOCK].astype(BF16))
        table = jnp.concatenate([jnp.concatenate(far, axis=0), jnp.concatenate(near, axis=0)], axis=1)
        window = jnp.concatenate([behind_ref[:, at], product_ref[:, at]], axis=0)
        for first in range(0, rows, ROW_BLOCK):
            span = slice(first, first + ROW_BLOCK)
            sums = jnp.dot(table, window[first : first + taps + ROW_BLOCK], preferred_element_type=F32)
            mixed = sums[:ROW_BLOCK]
            for group in range(1, per_lanes):
                mixed = jnp.where(member == group, sums[group * ROW_BLOCK : (group + 1) * ROW_BLOCK], mixed)
            gated = queries_ref[0, span, at].astype(F32) * mixed
            out_ref[span, at] = (residual_ref[span, at].astype(F32) * keep + gated).astype(BF16)


def block_of(table, behind, product, queries, residual, first, width, local, block):
    rows, total = residual.shape
    taps = table.shape[1]
    groups = table.shape[0] * block // total
    offset, inner = first // block, local // block
    own = pl.BlockSpec((rows, block), lambda i: (0, i + inner))
    return pl.pallas_call(
        block_kernel,
        grid=(width // block,),
        out_shape=jax.ShapeDtypeStruct((rows, width), BF16),
        in_specs=[
            pl.BlockSpec((groups, taps), lambda i: (i + offset, 0)),
            own,
            own,
            pl.BlockSpec((1, rows, block), lambda i: (0, 0, i + offset)),
            pl.BlockSpec((rows, block), lambda i: (0, i + offset)),
        ],
        out_specs=pl.BlockSpec((rows, block), lambda i: (0, i)),
        cost_estimate=pl.CostEstimate(
            flops=2 * 2 * taps * rows * LANES * width // 16, bytes_accessed=rows * width * 10, transcendentals=0
        ),
        name="block",
    )(table, behind, product, queries, residual)


def finish_kernel(own_ref, received_ref, *refs):
    out_ref = refs[-1]
    out_ref[0] = (own_ref[...].astype(F32) + received_ref[...].astype(F32)).astype(BF16)


def finish(own, received, held, first, total):
    rows, width = own.shape
    offset = first // width
    spec = pl.BlockSpec((rows, width), lambda i: (0, 0))
    extra = [] if held is None else [held]
    return pl.pallas_call(
        finish_kernel,
        grid=(1,),
        out_shape=jax.ShapeDtypeStruct((1, rows, total), BF16),
        in_specs=[spec, spec] + [pl.BlockSpec(memory_space=pl.ANY)] * len(extra),
        out_specs=pl.BlockSpec((1, rows, width), lambda i: (0, 0, offset)),
        input_output_aliases={2: 0} if extra else {},
        cost_estimate=pl.CostEstimate(flops=rows * width, bytes_accessed=rows * width * 6, transcendentals=0),
        name="finish",
    )(own, received, *extra)


def body(queries, keys, values, residual, filter_bank, filter_scales, group_filter, context_start):
    total = queries.shape[2]
    width = total // CHUNKS
    block = min(width, 512)
    near = product_of(context_start, keys, values, 0, width, block)
    near_behind = from_behind(near, "ctx", 1)
    rest = product_of(context_start, keys, values, width, total - width, block)
    rest_behind = from_behind(rest, "ctx", 1)
    table = reversed_taps(filter_bank, filter_scales, group_filter)
    own, received = [], []
    for chunk in range(CHUNKS):
        first = chunk * width
        if chunk == 0:
            piece = block_of(table, near_behind, near, queries, residual, first, width, 0, block)
        else:
            piece = block_of(table, rest_behind, rest, queries, residual, first, width, first - width, block)
        own.append(piece)
        received.append(from_behind(piece, "pipe", 1))
    held = None
    for chunk in range(CHUNKS):
        held = finish(own[chunk], received[chunk], held, chunk * width, total)
    return held


def solution(mesh):
    return jax.shard_map(
        body,
        mesh=mesh,
        in_specs=(
            P("pipe", ("dp", "ctx"), None),
            P("pipe", ("dp", "ctx"), None),
            P("pipe", ("dp", "ctx"), None),
            P(("dp", "ctx"), None),
            P("pipe", None, None),
            P("pipe", None),
            P("pipe", None),
            P("dp"),
        ),
        out_specs=P("pipe", ("dp", "ctx"), None),
        check_vma=False,
    )
```

time: 85.6 us -> 55.4 us (0.65)
  matrix products: 31.8 us -> 0 us
  Pallas kernels: 0 us -> 28.8 us
  waiting for transfers between devices: 31.9 us -> 10.3 us
  other arithmetic: 9.02 us -> 0 us
  starting transfers between devices: 3.2 us -> 10.6 us
  local copies, waits for them, and re-layouts: 8.58 us -> 4.38 us
    conv_general_dilated x1 -> x0, matrix products: 31.6 us -> none  [causal_filter(): lax.conv_general_dilated(extended[None], kernel, (1,), 'VALID', dimension...]
    pallas_call x0 -> x11, Pallas kernels: none -> 28.8 us  [the longest x4 13.4 us: block_of(): pl.pallas_call(block_kernel, grid=(width // block,), out_shape=jax.ShapeD...]
    ppermute x2 -> x6, waiting for transfers between devices: 31.9 us -> 10.3 us  [from_behind(): lax.ppermute(value, axis, [(source, source + steps) for source in range(f...]
    ppermute x2 -> x6, starting transfers between devices: 3.2 us -> 10.6 us  [from_behind(): lax.ppermute(value, axis, [(source, source + steps) for source in range(f...]
    broadcast_in_dim x2 -> x0, other arithmetic: 5.18 us -> none  [the longest x1 3.65 us: body(): return output[None]]
    broadcast_in_dim x2 -> x0, local copies, waits for them, and re-layouts: 4.4 us -> none  [the longest x1 4.26 us: kernel_for(): return jnp.flip(per_channel.T, 0)[:, None, :]]
    unnamed x12, local copies, waits for them, and re-layouts: 0.03 us -> 4.38 us
    convert_element_type x3 -> x0, other arithmetic: 3.83 us -> none  [the longest x1 1.96 us: body(): (inside * keys[0].astype(jnp.float32) * values[0].astype(jnp.float32)).as...]
  transfers between devices with their start and end apart: 2 -> 6, of which waited for: 2 -> 2; matrix products, arithmetic and copies ran while one was open for 9% -> 0% of each run, Pallas kernels for 0% -> 41%
where the time goes in v1:
time: 55.4 us; the launch traced here: 54.9 us
  Pallas kernels  28.8 us (52%)
  starting transfers between devices  10.6 us (19%)
  waiting for transfers between devices  10.3 us (19%)
  local copies, waits for them, and re-layouts  4.38 us (8%)
  between operations  0.74 us (1%)
    pallas_call x4, Pallas kernels, block_of(): pl.pallas_call(block_kernel, grid=(width // block,), out_shape=jax.ShapeD...  13.4 us
    ppermute x6, starting transfers between devices, from_behind(): lax.ppermute(value, axis, [(source, source + steps) for source in range(f...  10.6 us
    ppermute x6, waiting for transfers between devices, from_behind(): lax.ppermute(value, axis, [(source, source + steps) for source in range(f...  10.3 us
    pallas_call x4, Pallas kernels, finish(): pl.pallas_call(finish_kernel, grid=(1,), out_shape=jax.ShapeDtypeStruct((...  7.17 us
    pallas_call x2, Pallas kernels, product_of(): pl.pallas_call(product_kernel, grid=(width // block,), out_shape=jax.Shap...  6.37 us
    unnamed x12, local copies, waits for them, and re-layouts  4.38 us
    pallas_call x1, Pallas kernels, reversed_taps(): pl.pallas_call(taps_kernel, out_shape=jax.ShapeDtypeStruct((groups, taps)...  1.9 us
  transfers between devices with their start and end apart: 6, of which 2 were waited for; matrix products, arithmetic and copies ran while one was open for 0% of the time, Pallas kernels for 41%

profile of v1, /device:TPU:12, one launch (start us, length us, event | category | flops | bytes accessed | tf_op | source)
XLA Modules:
  0.0 54.9 jit_solution(2866397700291446148)
XLA Ops:
  0.7 4.5 %product.2.product_ref = bf16[128,3072]{1,0:T(8,128)(2,1)} custom-call(s32[1]{0:T(128)S(6)} %copy.15.start_ref, bf16[1,128,4096]{2,1,0:T(8,128)(2,1)} %keys_ref.3, bf16[1,128,4096]{2,1,0:T(8,128)(2,1)} %values_ref.3), custom_call_target="tpu_custom_call" | custom-call | flops 393216 | bytes 2359296 | tf_op jit(solution)/shard_map/product/pallas_call | solution.py:38
  5.2 1.9 %collective-permute-start = (bf16[128,3072]{1,0:T(8,128)(2,1)}, bf16[128,3072]{1,0:T(8,128)(2,1)S(1)}, u32[]{:S(2)}, u32[]{:S(2)}) collective-permute-start(bf16[128,3072]{1,0:T(8,128)(2,1)} %product.2.product_ref), channel_id=1, source_target_pairs={{0,4},{4,8},{8,12},{12,16},{16,20},{20,24},{24,28},{1,5},{5,9},{9,... | collective-permute-start | bytes 2359304 | tf_op jit(solution)/shard_map/ppermute | solution.py:20
  7.1 1.8 %product.3.product_ref = bf16[128,1024]{1,0:T(8,128)(2,1)} custom-call(s32[1]{0:T(128)S(6)} %copy.15.start_ref, bf16[1,128,4096]{2,1,0:T(8,128)(2,1)} %keys_ref.3, bf16[1,128,4096]{2,1,0:T(8,128)(2,1)} %values_ref.3), custom_call_target="tpu_custom_call" | custom-call | flops 131072 | bytes 786432 | tf_op jit(solution)/shard_map/product/pallas_call | solution.py:38
  8.9 3.6 %collective-permute-start.4 = (bf16[128,1024]{1,0:T(8,128)(2,1)}, bf16[128,1024]{1,0:T(8,128)(2,1)S(1)}, u32[]{:S(2)}, u32[]{:S(2)}) collective-permute-start(bf16[128,1024]{1,0:T(8,128)(2,1)} %product.3.product_ref), channel_id=1, source_target_pairs={{0,4},{4,8},{8,12},{12,16},{16,20},{20,24},{24,28},{1,5},{5,9},{9,... | collective-permute-start | bytes 786440 | tf_op jit(solution)/shard_map/ppermute | solution.py:20
  12.5 1.9 %taps.1.taps_ref = f32[256,128]{1,0:T(8,128)} custom-call(bf16[1,256,128]{2,1,0:T(8,128)(2,1)} %bank_ref.1, f32[1,256]{1,0:T(1,128)} %scales_ref.1, s32[1,256]{1,0:T(1,128)} %assign_ref.1), custom_call_target="tpu_custom_call" | custom-call | flops 33554432 | bytes 300000 | tf_op jit(solution)/shard_map/taps/pallas_call | solution.py:63
  14.4 7.1 %collective-permute-done.4.behind_ref = bf16[128,1024]{1,0:T(8,128)(2,1)S(1)} collective-permute-done((bf16[128,1024]{1,0:T(8,128)(2,1)}, bf16[128,1024]{1,0:T(8,128)(2,1)S(1)}, u32[]{:S(2)}, u32[]{:S(2)}) %collective-permute-start.4) | collective-permute-done | bytes 262176 | tf_op jit(solution)/shard_map/ppermute | solution.py:20
  21.5 0.0 copy-start.4
  21.5 0.7 %copy-done.4 = bf16[128,1024]{1,0:T(8,128)(2,1)} copy-done((bf16[128,1024]{1,0:T(8,128)(2,1)}, bf16[128,1024]{1,0:T(8,128)(2,1)S(1)}, u32[]{:S(2)}) %copy-start.4) | copy-done | bytes 262168
  22.2 3.3 %block.7.own_ref = bf16[128,1024]{1,0:T(8,128)(2,1)} custom-call(f32[256,128]{1,0:T(8,128)} %taps.1.taps_ref, bf16[128,1024]{1,0:T(8,128)(2,1)} %copy-done.4, bf16[128,1024]{1,0:T(8,128)(2,1)} %product.3.product_ref, bf16[1,128,4096]{2,1,0:T(8,128)(2,1)} %queries_ref.7, bf16[128,4096]{1,0:T(8,128)(2,1)} %residual_ref.7), custom_call_target="tpu_custom_call" | custom-call | flops 536870912 | bytes 1310720 | tf_op jit(solution)/shard_map/block/pallas_call | solution.py:108
  25.5 1.3 %collective-permute-start.5 = (bf16[128,1024]{1,0:T(8,128)(2,1)}, bf16[128,1024]{1,0:T(8,128)(2,1)S(1)}, u32[]{:S(2)}, u32[]{:S(2)}) collective-permute-start(bf16[128,1024]{1,0:T(8,128)(2,1)} %block.7.own_ref), channel_id=1, source_target_pairs={{0,1},{2,3},{4,5},{6,7},{8,9},{10,11},{12,13},{14,15},{16,17},{18,... | collective-permute-start | bytes 786440 | tf_op jit(solution)/shard_map/ppermute | solution.py:20
  26.8 0.0 collective-permute-done.behind_ref
  26.8 0.0 copy-start
  26.8 0.9 %copy-done = bf16[128,3072]{1,0:T(8,128)(2,1)} copy-done((bf16[128,3072]{1,0:T(8,128)(2,1)}, bf16[128,3072]{1,0:T(8,128)(2,1)S(1)}, u32[]{:S(2)}) %copy-start) | copy-done | bytes 786456
  27.7 3.3 %block.5.own_ref = bf16[128,1024]{1,0:T(8,128)(2,1)} custom-call(f32[256,128]{1,0:T(8,128)} %taps.1.taps_ref, bf16[128,3072]{1,0:T(8,128)(2,1)} %copy-done, bf16[128,3072]{1,0:T(8,128)(2,1)} %product.2.product_ref, bf16[1,128,4096]{2,1,0:T(8,128)(2,1)} %queries_ref.7, bf16[128,4096]{1,0:T(8,128)(2,1)} %residual_ref.7), custom_call_target="tpu_custom_call" | custom-call | flops 536870912 | bytes 1310720 | tf_op jit(solution)/shard_map/block/pallas_call | solution.py:108
  31.0 1.3 %collective-permute-start.2 = (bf16[128,1024]{1,0:T(8,128)(2,1)}, bf16[128,1024]{1,0:T(8,128)(2,1)S(1)}, u32[]{:S(2)}, u32[]{:S(2)}) collective-permute-start(bf16[128,1024]{1,0:T(8,128)(2,1)} %block.5.own_ref), channel_id=1, source_target_pairs={{0,1},{2,3},{4,5},{6,7},{8,9},{10,11},{12,13},{14,15},{16,17},{18,... | collective-permute-start | bytes 786440 | tf_op jit(solution)/shard_map/ppermute | solution.py:20
  32.3 3.3 %block.6.own_ref = bf16[128,1024]{1,0:T(8,128)(2,1)} custom-call(f32[256,128]{1,0:T(8,128)} %taps.1.taps_ref, bf16[128,3072]{1,0:T(8,128)(2,1)} %copy-done, bf16[128,3072]{1,0:T(8,128)(2,1)} %product.2.product_ref, bf16[1,128,4096]{2,1,0:T(8,128)(2,1)} %queries_ref.7, bf16[128,4096]{1,0:T(8,128)(2,1)} %residual_ref.7), custom_call_target="tpu_custom_call" | custom-call | flops 536870912 | bytes 1310720 | tf_op jit(solution)/shard_map/block/pallas_call | solution.py:108
  35.7 1.3 %collective-permute-start.3 = (bf16[128,1024]{1,0:T(8,128)(2,1)}, bf16[128,1024]{1,0:T(8,128)(2,1)S(1)}, u32[]{:S(2)}, u32[]{:S(2)}) collective-permute-start(bf16[128,1024]{1,0:T(8,128)(2,1)} %block.6.own_ref), channel_id=1, source_target_pairs={{0,1},{2,3},{4,5},{6,7},{8,9},{10,11},{12,13},{14,15},{16,17},{18,... | collective-permute-start | bytes 786440 | tf_op jit(solution)/shard_map/ppermute | solution.py:20
  37.0 3.4 %block.4.own_ref = bf16[128,1024]{1,0:T(8,128)(2,1)} custom-call(f32[256,128]{1,0:T(8,128)} %taps.1.taps_ref, bf16[128,3072]{1,0:T(8,128)(2,1)} %copy-done, bf16[128,3072]{1,0:T(8,128)(2,1)} %product.2.product_ref, bf16[1,128,4096]{2,1,0:T(8,128)(2,1)} %queries_ref.7, bf16[128,4096]{1,0:T(8,128)(2,1)} %residual_ref.7), custom_call_target="tpu_custom_call" | custom-call | flops 536870912 | bytes 1310720 | tf_op jit(solution)/shard_map/block/pallas_call | solution.py:108
  40.3 1.3 %collective-permute-start.1 = (bf16[128,1024]{1,0:T(8,128)(2,1)}, bf16[128,1024]{1,0:T(8,128)(2,1)S(1)}, u32[]{:S(2)}, u32[]{:S(2)}) collective-permute-start(bf16[128,1024]{1,0:T(8,128)(2,1)} %block.4.own_ref), channel_id=1, source_target_pairs={{0,1},{2,3},{4,5},{6,7},{8,9},{10,11},{12,13},{14,15},{16,17},{18,... | collective-permute-start | bytes 786440 | tf_op jit(solution)/shard_map/ppermute | solution.py:20
  41.6 0.0 collective-permute-done.5.received_ref
  41.6 0.0 copy-start.5
  41.6 0.7 %copy-done.5 = bf16[128,1024]{1,0:T(8,128)(2,1)} copy-done((bf16[128,1024]{1,0:T(8,128)(2,1)}, bf16[128,1024]{1,0:T(8,128)(2,1)S(1)}, u32[]{:S(2)}) %copy-start.5) | copy-done | bytes 262168
  42.3 1.8 %finish.4.refs_0_ = bf16[1,128,4096]{2,1,0:T(8,128)(2,1)} custom-call(bf16[128,1024]{1,0:T(8,128)(2,1)} %block.7.own_ref, bf16[128,1024]{1,0:T(8,128)(2,1)} %copy-done.5), custom_call_target="tpu_custom_call" | custom-call | flops 131072 | bytes 786432 | tf_op jit(solution)/shard_map/finish/pallas_call | solution.py:137
  44.1 3.2 %collective-permute-done.3.received_ref = bf16[128,1024]{1,0:T(8,128)(2,1)S(1)} collective-permute-done((bf16[128,1024]{1,0:T(8,128)(2,1)}, bf16[128,1024]{1,0:T(8,128)(2,1)S(1)}, u32[]{:S(2)}, u32[]{:S(2)}) %collective-permute-start.3) | collective-permute-done | bytes 262176 | tf_op jit(solution)/shard_map/ppermute | solution.py:20
  47.4 0.0 copy-start.3
  47.4 0.7 %copy-done.3 = bf16[128,1024]{1,0:T(8,128)(2,1)} copy-done((bf16[128,1024]{1,0:T(8,128)(2,1)}, bf16[128,1024]{1,0:T(8,128)(2,1)S(1)}, u32[]{:S(2)}) %copy-start.3) | copy-done | bytes 262168
  48.1 1.8 %finish.5.refs_0_ = bf16[1,128,4096]{2,1,0:T(8,128)(2,1)} custom-call(bf16[128,1024]{1,0:T(8,128)(2,1)} %block.6.own_ref, bf16[128,1024]{1,0:T(8,128)(2,1)} %copy-done.3, bf16[1,128,4096]{2,1,0:T(8,128)(2,1)} %finish.4.refs_0_), custom_call_target="tpu_custom_call", output_to_operand_aliasing={{}: (2, {})} | custom-call | flops 131072 | bytes 786432 | tf_op jit(solution)/shard_map/finish/pallas_call | solution.py:137
  49.9 0.0 collective-permute-done.2.received_ref
  49.9 0.0 copy-start.1
  49.9 0.7 %copy-done.1 = bf16[128,1024]{1,0:T(8,128)(2,1)} copy-done((bf16[128,1024]{1,0:T(8,128)(2,1)}, bf16[128,1024]{1,0:T(8,128)(2,1)S(1)}, u32[]{:S(2)}) %copy-start.1) | copy-done | bytes 262168
  50.6 1.8 %finish.6.refs_0_ = bf16[1,128,4096]{2,1,0:T(8,128)(2,1)} custom-call(bf16[128,1024]{1,0:T(8,128)(2,1)} %block.5.own_ref, bf16[128,1024]{1,0:T(8,128)(2,1)} %copy-done.1, bf16[1,128,4096]{2,1,0:T(8,128)(2,1)} %finish.5.refs_0_), custom_call_target="tpu_custom_call", output_to_operand_aliasing={{}: (2, {})} | custom-call | flops 131072 | bytes 786432 | tf_op jit(solution)/shard_map/finish/pallas_call | solution.py:137
  52.4 0.0 collective-permute-done.1.received_ref
  52.4 0.0 copy-start.2
  52.4 0.7 %copy-done.2 = bf16[128,1024]{1,0:T(8,128)(2,1)} copy-done((bf16[128,1024]{1,0:T(8,128)(2,1)}, bf16[128,1024]{1,0:T(8,128)(2,1)S(1)}, u32[]{:S(2)}) %copy-start.2) | copy-done | bytes 262168
  53.1 1.8 %finish.7 = bf16[1,128,4096]{2,1,0:T(8,128)(2,1)} custom-call(bf16[128,1024]{1,0:T(8,128)(2,1)} %block.4.own_ref, bf16[128,1024]{1,0:T(8,128)(2,1)} %copy-done.2, bf16[1,128,4096]{2,1,0:T(8,128)(2,1)} %finish.6.refs_0_), custom_call_target="tpu_custom_call", output_to_operand_aliasing={{}: (2, {})} | custom-call | flops 131072 | bytes 786432 | tf_op jit(solution)/shard_map/finish/pallas_call | solution.py:137
Async XLA Ops:
  5.2 21.6 %collective-permute-start = (bf16[128,3072]{1,0:T(8,128)(2,1)}, bf16[128,3072]{1,0:T(8,128)(2,1)S(1)}, u32[]{:S(2)}, u32[]{:S(2)}) collective-permute-start(bf16[128,3072]{1,0:T(8,128)(2,1)} %product.2.product_ref), channel_id=1, source_target_pairs={{0,4},{4,8},{8,12},{12,16},{16,20},{20,24},{24,28},{1,5},{5,9},{9,... | collective-permute-start | bytes 2359304 | tf_op jit(solution)/shard_map/ppermute | solution.py:20
  8.9 12.6 %collective-permute-start.4 = (bf16[128,1024]{1,0:T(8,128)(2,1)}, bf16[128,1024]{1,0:T(8,128)(2,1)S(1)}, u32[]{:S(2)}, u32[]{:S(2)}) collective-permute-start(bf16[128,1024]{1,0:T(8,128)(2,1)} %product.3.product_ref), channel_id=1, source_target_pairs={{0,4},{4,8},{8,12},{12,16},{16,20},{20,24},{24,28},{1,5},{5,9},{9,... | collective-permute-start | bytes 786440 | tf_op jit(solution)/shard_map/ppermute | solution.py:20
  21.5 0.7 %copy-start.4 = (bf16[128,1024]{1,0:T(8,128)(2,1)}, bf16[128,1024]{1,0:T(8,128)(2,1)S(1)}, u32[]{:S(2)}) copy-start(bf16[128,1024]{1,0:T(8,128)(2,1)S(1)} %collective-permute-done.4.behind_ref) | copy-start | bytes 786436
  25.5 16.1 %collective-permute-start.5 = (bf16[128,1024]{1,0:T(8,128)(2,1)}, bf16[128,1024]{1,0:T(8,128)(2,1)S(1)}, u32[]{:S(2)}, u32[]{:S(2)}) collective-permute-start(bf16[128,1024]{1,0:T(8,128)(2,1)} %block.7.own_ref), channel_id=1, source_target_pairs={{0,1},{2,3},{4,5},{6,7},{8,9},{10,11},{12,13},{14,15},{16,17},{18,... | collective-permute-start | bytes 786440 | tf_op jit(solution)/shard_map/ppermute | solution.py:20
  26.8 0.9 %copy-start = (bf16[128,3072]{1,0:T(8,128)(2,1)}, bf16[128,3072]{1,0:T(8,128)(2,1)S(1)}, u32[]{:S(2)}) copy-start(bf16[128,3072]{1,0:T(8,128)(2,1)S(1)} %collective-permute-done.behind_ref) | copy-start | bytes 2359300
  31.0 18.8 %collective-permute-start.2 = (bf16[128,1024]{1,0:T(8,128)(2,1)}, bf16[128,1024]{1,0:T(8,128)(2,1)S(1)}, u32[]{:S(2)}, u32[]{:S(2)}) collective-permute-start(bf16[128,1024]{1,0:T(8,128)(2,1)} %block.5.own_ref), channel_id=1, source_target_pairs={{0,1},{2,3},{4,5},{6,7},{8,9},{10,11},{12,13},{14,15},{16,17},{18,... | collective-permute-start | bytes 786440 | tf_op jit(solution)/shard_map/ppermute | solution.py:20
  35.7 11.7 %collective-permute-start.3 = (bf16[128,1024]{1,0:T(8,128)(2,1)}, bf16[128,1024]{1,0:T(8,128)(2,1)S(1)}, u32[]{:S(2)}, u32[]{:S(2)}) collective-permute-start(bf16[128,1024]{1,0:T(8,128)(2,1)} %block.6.own_ref), channel_id=1, source_target_pairs={{0,1},{2,3},{4,5},{6,7},{8,9},{10,11},{12,13},{14,15},{16,17},{18,... | collective-permute-start | bytes 786440 | tf_op jit(solution)/shard_map/ppermute | solution.py:20
  40.3 12.0 %collective-permute-start.1 = (bf16[128,1024]{1,0:T(8,128)(2,1)}, bf16[128,1024]{1,0:T(8,128)(2,1)S(1)}, u32[]{:S(2)}, u32[]{:S(2)}) collective-permute-start(bf16[128,1024]{1,0:T(8,128)(2,1)} %block.4.own_ref), channel_id=1, source_target_pairs={{0,1},{2,3},{4,5},{6,7},{8,9},{10,11},{12,13},{14,15},{16,17},{18,... | collective-permute-start | bytes 786440 | tf_op jit(solution)/shard_map/ppermute | solution.py:20
  41.6 0.7 %copy-start.5 = (bf16[128,1024]{1,0:T(8,128)(2,1)}, bf16[128,1024]{1,0:T(8,128)(2,1)S(1)}, u32[]{:S(2)}) copy-start(bf16[128,1024]{1,0:T(8,128)(2,1)S(1)} %collective-permute-done.5.received_ref) | copy-start | bytes 786436
  47.4 0.7 %copy-start.3 = (bf16[128,1024]{1,0:T(8,128)(2,1)}, bf16[128,1024]{1,0:T(8,128)(2,1)S(1)}, u32[]{:S(2)}) copy-start(bf16[128,1024]{1,0:T(8,128)(2,1)S(1)} %collective-permute-done.3.received_ref) | copy-start | bytes 786436
  49.9 0.7 %copy-start.1 = (bf16[128,1024]{1,0:T(8,128)(2,1)}, bf16[128,1024]{1,0:T(8,128)(2,1)S(1)}, u32[]{:S(2)}) copy-start(bf16[128,1024]{1,0:T(8,128)(2,1)S(1)} %collective-permute-done.2.received_ref) | copy-start | bytes 786436
  52.4 0.7 %copy-start.2 = (bf16[128,1024]{1,0:T(8,128)(2,1)}, bf16[128,1024]{1,0:T(8,128)(2,1)S(1)}, u32[]{:S(2)}) copy-start(bf16[128,1024]{1,0:T(8,128)(2,1)S(1)} %collective-permute-done.1.received_ref) | copy-start | bytes 786436

commit v2 on v0

v2 whole, which is shorter than its diff:
```python
import functools

import jax
import jax.numpy as jnp
from jax import lax
from jax.experimental import pallas as pl
from jax.experimental.pallas import tpu as pltpu
from jax.sharding import PartitionSpec as P

LANES = 128
ROW_BLOCK = 32
HALOS = (768, 1280, 2048)
CHUNKS = (768, 1280, 1024, 640, 384)
F32 = jnp.float32
BF16 = jnp.bfloat16
MIB = 1024 * 1024

SMEM = pl.BlockSpec(memory_space=pltpu.SMEM)
VMEM = pl.BlockSpec(memory_space=pltpu.VMEM)
ANY = pl.BlockSpec(memory_space=pl.ANY)
HBM = pl.BlockSpec(memory_space=pltpu.HBM)


def from_behind(value, axis, steps):
    count = lax.axis_size(axis)
    first, last = (max(0, -steps), min(count, count - steps))
    return lax.ppermute(value, axis, [(source, source + steps) for source in range(first, last)])


def params(limit=16):
    return pltpu.CompilerParams(vmem_limit_bytes=limit * MIB)


def cost(flops=1024):
    return pl.CostEstimate(flops=flops, bytes_accessed=1024, transcendentals=0)


def product_kernel(first, start_ref, keys_ref, values_ref, *refs):
    out_refs = refs[:-3]
    keys_in, values_in, sems = refs[-3:]
    rows, width = keys_in.shape
    copies = [
        pltpu.make_async_copy(keys_ref.at[0, :, pl.ds(first, width)], keys_in, sems.at[0]),
        pltpu.make_async_copy(values_ref.at[0, :, pl.ds(first, width)], values_in, sems.at[1]),
    ]
    for copy in copies:
        copy.start()
    for copy in copies:
        copy.wait()
    slab = lax.axis_index("ctx") * rows
    offset = 0
    for out_ref in out_refs:
        cols = out_ref.shape[1]
        for tile in range(0, cols, LANES):
            at = slice(offset + tile, offset + tile + LANES)
            positions = slab + lax.broadcasted_iota(jnp.int32, (rows, LANES), 0)
            product = keys_in[:, at].astype(F32) * values_in[:, at].astype(F32)
            out_ref[:, tile : tile + LANES] = jnp.where(positions >= start_ref[0], product, 0.0).astype(BF16)
        offset += cols


def products(context_start, keys, values, first, widths, after=()):
    rows, width = keys.shape[1], sum(widths)

    def kernel(start_ref, keys_ref, values_ref, *refs):
        product_kernel(first, start_ref, keys_ref, values_ref, *refs[len(after) :])

    return pl.pallas_call(
        kernel,
        out_shape=tuple(jax.ShapeDtypeStruct((rows, cols), BF16) for cols in widths),
        in_specs=[SMEM, HBM, HBM] + [ANY] * len(after),
        out_specs=tuple(VMEM for _ in widths),
        scratch_shapes=[
            pltpu.VMEM((rows, width), BF16),
            pltpu.VMEM((rows, width), BF16),
            pltpu.SemaphoreType.DMA((2,)),
        ],
        compiler_params=params(16),
        cost_estimate=cost(),
        name="product",
    )(context_start, keys, values, *after)


def turn_table(lines_ref, row, per_lanes, table_ref, at):
    taps = lines_ref.shape[1]
    upper = lax.broadcasted_iota(jnp.int32, (ROW_BLOCK, taps), 1) > lax.broadcasted_iota(
        jnp.int32, (ROW_BLOCK, taps), 0
    )
    for group in range(per_lanes):
        line = lines_ref[row + group : row + group + 1, :]
        turned = pltpu.roll(jnp.broadcast_to(line, (ROW_BLOCK, taps)), 1, 1, stride=1, stride_axis=0)
        span = slice(at + group * ROW_BLOCK, at + (group + 1) * ROW_BLOCK)
        table_ref[span, :taps] = jnp.where(upper, turned, 0.0).astype(BF16)
        table_ref[span, taps:] = jnp.where(upper, 0.0, turned)[:, :ROW_BLOCK].astype(BF16)


def taps_kernel(bank_ref, scales_ref, assign_ref, *refs):
    lines_ref, table_ref = refs[-2:]
    groups, taps = lines_ref.shape
    size = bank_ref.shape[1]
    per_lanes = LANES * groups // sum(CHUNKS)
    chosen = (lax.broadcasted_iota(jnp.int32, (size, groups), 0) == assign_ref[...]).astype(F32).astype(BF16)
    contract = (((0,), (0,)), ((), ()))
    picked = lax.dot_general(bank_ref[0], chosen, contract, preferred_element_type=F32)
    scaled = (picked * scales_ref[...]).astype(BF16)
    order = lax.broadcasted_iota(jnp.int32, (taps, taps), 0) + lax.broadcasted_iota(jnp.int32, (taps, taps), 1)
    flip = (order == taps - 1).astype(F32).astype(BF16)
    lines_ref[...] = lax.dot_general(scaled, flip, contract, preferred_element_type=F32)
    for tile in range(table_ref.shape[0] // (per_lanes * ROW_BLOCK)):
        turn_table(lines_ref, tile * per_lanes, per_lanes, table_ref, tile * per_lanes * ROW_BLOCK)


def tap_lines(bank, scales, assign, width, after=()):
    groups, taps = assign.shape[1], bank.shape[2]
    rows = width * groups // sum(CHUNKS) * ROW_BLOCK
    return pl.pallas_call(
        taps_kernel,
        out_shape=(
            jax.ShapeDtypeStruct((groups, taps), F32),
            jax.ShapeDtypeStruct((rows, taps + ROW_BLOCK), BF16),
        ),
        in_specs=[VMEM] * 3 + [ANY] * len(after),
        out_specs=(VMEM, VMEM),
        compiler_params=params(),
        cost_estimate=cost(),
        name="taps",
    )(bank, scales, assign, *after)


def mix(table_ref, row, per_lanes, window, queries_ref, cols, store):
    rows = queries_ref.shape[1]
    depth = table_ref.shape[1]
    member = lax.broadcasted_iota(jnp.int32, (ROW_BLOCK, LANES), 1) // (LANES // per_lanes)
    table = table_ref[row : row + per_lanes * ROW_BLOCK, :]
    for first in range(0, rows, ROW_BLOCK):
        span = slice(first, first + ROW_BLOCK)
        sums = jnp.dot(table, window[first : first + depth], preferred_element_type=F32)
        mixed = sums[:ROW_BLOCK]
        for group in range(1, per_lanes):
            mixed = jnp.where(member == group, sums[group * ROW_BLOCK : (group + 1) * ROW_BLOCK], mixed)
        store(span, queries_ref[0, span, cols].astype(F32) * mixed)


def gate(first, local, width, lines_ref, table_ref, made, behind_ref, product_ref, queries_ref, store):
    per_lanes = LANES * lines_ref.shape[0] // queries_ref.shape[2]
    for tile in range(width // LANES):
        at = slice(tile * LANES, (tile + 1) * LANES)
        inner = slice(local + at.start, local + at.stop)
        cols = slice(first + at.start, first + at.stop)
        row = tile * per_lanes * ROW_BLOCK
        if not made:
            turn_table(lines_ref, cols.start // LANES * per_lanes, per_lanes, table_ref, row)
        window = jnp.concatenate([behind_ref[:, inner], product_ref[:, inner]], axis=0)
        mix(table_ref, row, per_lanes, window, queries_ref, cols, functools.partial(store, at, cols))


def own_kernel(first, local, made, *refs):
    lines_ref, behind_ref, product_ref, queries_ref, residual_ref, table_ref, out_ref = refs[:7]
    if not made:
        table_ref = refs[-1]

    @pl.when(lax.axis_index("pipe") == 0)
    def _():
        def store(at, cols, span, gated):
            out_ref[span, at] = (residual_ref[span, cols].astype(F32) + gated).astype(BF16)

        gate(
            first, local, out_ref.shape[1], lines_ref, table_ref, made, behind_ref, product_ref, queries_ref, store
        )


def later_kernel(first, local, *refs):
    lines_ref, behind_ref, product_ref, queries_ref, _, out_ref, table_ref = refs

    @pl.when(lax.axis_index("pipe") != 0)
    def _():
        def store(at, cols, span, gated):
            out_ref[span, at] = gated

        gate(
            first, local, out_ref.shape[1], lines_ref, table_ref, False, behind_ref, product_ref, queries_ref, store
        )


def table_scratch(lines, width, total):
    groups, taps = lines.shape
    return pltpu.VMEM((width * groups // total * ROW_BLOCK, taps + ROW_BLOCK), BF16)


def own_of(lines, behind, product, queries, residual, first, local, width, made, after):
    rows, total = residual.shape
    return pl.pallas_call(
        functools.partial(own_kernel, first, local, made),
        out_shape=jax.ShapeDtypeStruct((rows, width), BF16),
        in_specs=[VMEM] * 5 + [VMEM if made else ANY],
        out_specs=VMEM,
        scratch_shapes=[] if made else [table_scratch(lines, width, total)],
        compiler_params=params(),
        cost_estimate=cost(20_000_000_000),
        name="own",
    )(lines, behind, product, queries, residual, after)


def later_of(lines, behind, product, queries, own, first, local, width):
    rows, total = queries.shape[1:]
    return pl.pallas_call(
        functools.partial(later_kernel, first, local),
        out_shape=jax.ShapeDtypeStruct((rows, width), F32),
        in_specs=[VMEM] * 4 + [ANY],
        out_specs=VMEM,
        scratch_shapes=[table_scratch(lines, width, total)],
        compiler_params=params(),
        cost_estimate=cost(),
        name="later",
    )(lines, behind, product, queries, own)


def send_out(buffer, out_ref, first, sem):
    width = buffer.shape[1]
    copy = pltpu.make_async_copy(buffer, out_ref.at[0, :, pl.ds(first, width)], sem)
    copy.start()
    copy.wait()


def finish_kernel(first, local, *refs):
    own_ref, received_ref, lines_ref, behind_ref, product_ref, queries_ref = refs[:6]
    out_ref, table_ref, buffer, sem = refs[-4:]
    is_first = lax.axis_index("pipe") == 0

    @pl.when(is_first)
    def _():
        send_out(own_ref, out_ref, first, sem)

    @pl.when(jnp.logical_not(is_first))
    def _():
        def store(at, cols, span, gated):
            buffer[span, at] = (received_ref[span, at].astype(F32) + gated).astype(BF16)

        gate(
            first, local, buffer.shape[1], lines_ref, table_ref, False, behind_ref, product_ref, queries_ref, store
        )
        send_out(buffer, out_ref, first, sem)


def last_kernel(first, own_ref, received_ref, gated_ref, *refs):
    out_ref, buffer, sem = refs[-3:]
    is_first = lax.axis_index("pipe") == 0

    @pl.when(is_first)
    def _():
        send_out(own_ref, out_ref, first, sem)

    @pl.when(jnp.logical_not(is_first))
    def _():
        buffer[...] = (received_ref[...].astype(F32) + gated_ref[...]).astype(BF16)
        send_out(buffer, out_ref, first, sem)


def finish(held, after, own, received, lines, behind, product, queries, first, local):
    rows, width = own.shape
    total = queries.shape[2]
    return pl.pallas_call(
        functools.partial(finish_kernel, first, local),
        out_shape=jax.ShapeDtypeStruct((1, rows, total), BF16),
        in_specs=[VMEM] * 6 + [ANY],
        out_specs=ANY,
        scratch_shapes=[
            table_scratch(lines, width, total),
            pltpu.VMEM((rows, width), BF16),
            pltpu.SemaphoreType.DMA(()),
        ],
        input_output_aliases={} if held is None else {6: 0},
        compiler_params=params(),
        cost_estimate=cost(20_000_000_000),
        name="finish",
    )(own, received, lines, behind, product, queries, after if held is None else held)


def last(held, own, received, gated, first):
    rows, width = own.shape
    return pl.pallas_call(
        functools.partial(last_kernel, first),
        out_shape=jax.ShapeDtypeStruct(held.shape, BF16),
        in_specs=[VMEM] * 3 + [ANY],
        out_specs=ANY,
        scratch_shapes=[pltpu.VMEM((rows, width), BF16), pltpu.SemaphoreType.DMA(())],
        input_output_aliases={3: 0},
        compiler_params=params(),
        cost_estimate=cost(20_000_000_000),
        name="last",
    )(own, received, gated, held)


def body(queries, keys, values, residual, filter_bank, filter_scales, group_filter, context_start):
    keys, values = (pltpu.with_memory_space_constraint(array, pltpu.HBM) for array in (keys, values))
    (near,) = products(context_start, keys, values, 0, HALOS[:1])
    pieces = [near, *products(context_start, keys, values, HALOS[0], HALOS[1:], (near,))]
    behinds = [from_behind(piece, "ctx", 1) for piece in pieces]
    lines, table = tap_lines(filter_bank, filter_scales, group_filter, CHUNKS[0], (pieces[1],))
    places = []
    first = 0
    for width in CHUNKS:
        start, piece = 0, 0
        while start + HALOS[piece] <= first:
            start, piece = start + HALOS[piece], piece + 1
        places.append((piece, first, first - start, width))
        first += width
    own, received = [], []
    for chunk, (piece, first, local, width) in enumerate(places):
        after = own[-1] if own else table
        own.append(
            own_of(lines, behinds[piece], pieces[piece], queries, residual, first, local, width, not own, after)
        )
        received.append(from_behind(own[-1], "pipe", 1))
    piece, first, local, width = places[-1]
    gated = later_of(lines, behinds[piece], pieces[piece], queries, own[-1], first, local, width)
    held = None
    for chunk, (piece, first, local, width) in enumerate(places[:-1]):
        held = finish(
            held, gated, own[chunk], received[chunk], lines, behinds[piece], pieces[piece], queries, first, local
        )
    return last(held, own[-1], received[-1], gated, places[-1][1])


def solution(mesh):
    return jax.shard_map(
        body,
        mesh=mesh,
        in_specs=(
            P("pipe", ("dp", "ctx"), None),
            P("pipe", ("dp", "ctx"), None),
            P("pipe", ("dp", "ctx"), None),
            P(("dp", "ctx"), None),
            P("pipe", None, None),
            P("pipe", None),
            P("pipe", None),
            P("dp"),
        ),
        out_specs=P("pipe", ("dp", "ctx"), None),
        check_vma=False,
    )
```

time: 85.6 us -> 41.2 us (0.48)
  the two profiles are of different devices: /device:TPU:12 before, /device:TPU:13 now
where the time goes in v2:
time: 41.2 us; the launch traced here: 40.8 us
  starting transfers between devices  15.9 us (39%)
  Pallas kernels  12.4 us (30%)
  waiting for transfers between devices  11.6 us (28%)
  between operations  0.92 us (2%)
    ppermute x8, starting transfers between devices, from_behind(): lax.ppermute(value, axis, [(source, source + steps) for source in range(f...  15.9 us
    ppermute x8, waiting for transfers between devices, from_behind(): lax.ppermute(value, axis, [(source, source + steps) for source in range(f...  11.6 us
    pallas_call x4, Pallas kernels, finish(): pl.pallas_call(functools.partial(finish_kernel, first, local), out_shape=...  7.63 us
    pallas_call x2, Pallas kernels, products(): pl.pallas_call(kernel, out_shape=tuple((jax.ShapeDtypeStruct((rows, cols)...  2.84 us
  transfers between devices with their start and end apart: 8, of which 4 were waited for; matrix products, arithmetic and copies ran while one was open for 0% of the time, Pallas kernels for 26%

profile of v2, /device:TPU:13, one launch (start us, length us, event | category | flops | bytes accessed | tf_op | source)
XLA Modules:
  0.0 40.8 jit_solution(15760909329217942745)
XLA Ops:
  0.7 1.1 %product.2.refs_0_.refs_2_.refs_4_ = bf16[128,768]{1,0:T(8,128)(2,1)S(1)} custom-call(s32[1]{0:T(128)S(6)} %copy.17.start_ref, bf16[1,128,4096]{2,1,0:T(8,128)(2,1)} %keys_ref.3, bf16[1,128,4096]{2,1,0:T(8,128)(2,1)} %values_ref.3), custom_call_target="tpu_custom_call" | custom-call | flops 1024 | bytes 1024 | tf_op jit(solution)/shard_map/product/pallas_call | solution.py:68
  1.8 0.0 copy-start.1
  1.8 0.0 copy-start
  1.8 0.0 copy-start.4
  1.8 3.9 %collective-permute-start.2 = (bf16[128,768]{1,0:T(8,128)(2,1)S(1)}, bf16[128,768]{1,0:T(8,128)(2,1)S(1)}, u32[]{:S(2)}, u32[]{:S(2)}) collective-permute-start(bf16[128,768]{1,0:T(8,128)(2,1)S(1)} %product.2.refs_0_.refs_2_.refs_4_), channel_id=1, source_target_pairs={{0,4},{4,8},{8,12},{12,16},{16,20},{20,24},{24,28},{1,5},{5,9},{9,... | collective-permute-start | bytes 589832 | tf_op jit(solution)/shard_map/ppermute | solution.py:27
  5.7 1.7 %product.3 = (bf16[128,1280]{1,0:T(8,128)(2,1)S(1)}, bf16[128,2048]{1,0:T(8,128)(2,1)S(1)}) custom-call(s32[1]{0:T(128)S(6)} %copy.17.start_ref, bf16[1,128,4096]{2,1,0:T(8,128)(2,1)} %keys_ref.3, bf16[1,128,4096]{2,1,0:T(8,128)(2,1)} %values_ref.3, bf16[128,768]{1,0:T(8,128)(2,1)S(1)} %product.2.refs_0_.refs_2_.refs_4_), custom_call_target="tpu_custom_call" | custom-call | flops 1024 | bytes 1024 | tf_op jit(solution)/shard_map/product/pallas_call | solution.py:68
  7.4 0.0 copy-start.3
  7.5 0.0 copy-start.2
  7.5 1.9 %collective-permute-start.1 = (bf16[128,1280]{1,0:T(8,128)(2,1)S(1)}, bf16[128,1280]{1,0:T(8,128)(2,1)S(1)}, u32[]{:S(2)}, u32[]{:S(2)}) collective-permute-start(bf16[128,1280]{1,0:T(8,128)(2,1)S(1)} %get-tuple-element.9.refs_0_.refs_2_.refs_4_), channel_id=1, source_target_pairs={{0,4},{4,8},{8,12},{12,16},{16,20},{20,24},{24,28},{1,5},{5,9},{9,... | collective-permute-start | bytes 983048 | tf_op jit(solution)/shard_map/ppermute | solution.py:27
  9.4 3.6 %collective-permute-start = (bf16[128,2048]{1,0:T(8,128)(2,1)S(1)}, bf16[128,2048]{1,0:T(8,128)(2,1)S(1)}, u32[]{:S(2)}, u32[]{:S(2)}) collective-permute-start(bf16[128,2048]{1,0:T(8,128)(2,1)S(1)} %get-tuple-element.11.refs_2_.refs_4_), channel_id=1, source_target_pairs={{0,4},{4,8},{8,12},{12,16},{16,20},{20,24},{24,28},{1,5},{5,9},{9,... | collective-permute-start | bytes 1572872 | tf_op jit(solution)/shard_map/ppermute | solution.py:27
  13.0 0.0 copy-done.1
  13.0 0.0 copy-done.3
  13.0 0.0 copy-done.2
  13.0 0.6 %taps.1 = (f32[256,128]{1,0:T(8,128)S(1)}, bf16[1536,160]{1,0:T(8,128)(2,1)S(1)}) custom-call(bf16[1,256,128]{2,1,0:T(8,128)(2,1)S(1)} %copy-done.1, f32[1,256]{1,0:T(1,128)S(1)} %copy-done.2, s32[1,256]{1,0:T(1,128)S(1)} %copy-done.3, bf16[128,1280]{1,0:T(8,128)(2,1)S(1)} %get-tuple-element.9.refs_0_.refs_2_.refs_4_), custom_call_target="tpu_custom_call" | custom-call | flops 1024 | bytes 1024 | tf_op jit(solution)/shard_map/taps/pallas_call | solution.py:116
  13.6 0.0 collective-permute-done.2.refs_1_.refs_3_
  13.6 0.0 copy-done
  13.6 0.0 copy-done.4
  13.6 1.3 %collective-permute-start.7 = (bf16[128,768]{1,0:T(8,128)(2,1)S(1)}, bf16[128,768]{1,0:T(8,128)(2,1)S(1)}, u32[]{:S(2)}, u32[]{:S(2)}) collective-permute-start(bf16[128,768]{1,0:T(8,128)(2,1)S(1)} %own.5.refs_5_.refs_0_), channel_id=1, source_target_pairs={{0,1},{2,3},{4,5},{6,7},{8,9},{10,11},{12,13},{14,15},{16,17},{18,... | collective-permute-start | bytes 589832 | tf_op jit(solution)/shard_map/ppermute | solution.py:27
  14.9 0.0 collective-permute-done.1.refs_1_.refs_3_
  15.0 1.3 %collective-permute-start.6 = (bf16[128,1280]{1,0:T(8,128)(2,1)S(1)}, bf16[128,1280]{1,0:T(8,128)(2,1)S(1)}, u32[]{:S(2)}, u32[]{:S(2)}) collective-permute-start(bf16[128,1280]{1,0:T(8,128)(2,1)S(1)} %own.6.refs_5_.refs_0_), channel_id=1, source_target_pairs={{0,1},{2,3},{4,5},{6,7},{8,9},{10,11},{12,13},{14,15},{16,17},{18,... | collective-permute-start | bytes 983048 | tf_op jit(solution)/shard_map/ppermute | solution.py:27
  16.3 2.8 %collective-permute-done.refs_1_.refs_3_ = bf16[128,2048]{1,0:T(8,128)(2,1)S(1)} collective-permute-done((bf16[128,2048]{1,0:T(8,128)(2,1)S(1)}, bf16[128,2048]{1,0:T(8,128)(2,1)S(1)}, u32[]{:S(2)}, u32[]{:S(2)}) %collective-permute-start) | collective-permute-done | bytes 524320 | tf_op jit(solution)/shard_map/ppermute | solution.py:27
  19.1 1.3 %collective-permute-start.5 = (bf16[128,1024]{1,0:T(8,128)(2,1)S(1)}, bf16[128,1024]{1,0:T(8,128)(2,1)S(1)}, u32[]{:S(2)}, u32[]{:S(2)}) collective-permute-start(bf16[128,1024]{1,0:T(8,128)(2,1)S(1)} %own.7.refs_5_.refs_0_), channel_id=1, source_target_pairs={{0,1},{2,3},{4,5},{6,7},{8,9},{10,11},{12,13},{14,15},{16,17},{18,... | collective-permute-start | bytes 786440 | tf_op jit(solution)/shard_map/ppermute | solution.py:27
  20.4 1.3 %collective-permute-start.4 = (bf16[128,640]{1,0:T(8,128)(2,1)S(1)}, bf16[128,640]{1,0:T(8,128)(2,1)S(1)}, u32[]{:S(2)}, u32[]{:S(2)}) collective-permute-start(bf16[128,640]{1,0:T(8,128)(2,1)S(1)} %own.8.refs_5_.refs_0_), channel_id=1, source_target_pairs={{0,1},{2,3},{4,5},{6,7},{8,9},{10,11},{12,13},{14,15},{16,17},{18,... | collective-permute-start | bytes 491528 | tf_op jit(solution)/shard_map/ppermute | solution.py:27
  21.7 1.3 %collective-permute-start.3 = (bf16[128,384]{1,0:T(8,128)(2,1)S(1)}, bf16[128,384]{1,0:T(8,128)(2,1)S(1)}, u32[]{:S(2)}, u32[]{:S(2)}) collective-permute-start(bf16[128,384]{1,0:T(8,128)(2,1)S(1)} %own.9.refs_4_.own_ref), channel_id=1, source_target_pairs={{0,1},{2,3},{4,5},{6,7},{8,9},{10,11},{12,13},{14,15},{16,17},{18,... | collective-permute-start | bytes 294920 | tf_op jit(solution)/shard_map/ppermute | solution.py:27
  23.0 0.6 %later.1.refs_6_.gated_ref = f32[128,384]{1,0:T(8,128)S(1)} custom-call(f32[256,128]{1,0:T(8,128)S(1)} %get-tuple-element.10.refs_0_.refs_2_, bf16[128,2048]{1,0:T(8,128)(2,1)S(1)} %collective-permute-done.refs_1_.refs_3_, bf16[128,2048]{1,0:T(8,128)(2,1)S(1)} %get-tuple-element.11.refs_2_.refs_4_, bf16[1,128,4096]{2,1,0:T(8,128)(2,1)S(1)} %copy-done, ...), custom_call_target="tpu_custom_call" | custom-call | flops 1024 | bytes 1024 | tf_op jit(solution)/shard_map/later/pallas_call | solution.py:206
  23.7 0.0 collective-permute-done.7.refs_1_
  23.7 1.7 %finish.4.refs_6_ = bf16[1,128,4096]{2,1,0:T(8,128)(2,1)} custom-call(bf16[128,768]{1,0:T(8,128)(2,1)S(1)} %own.5.refs_5_.refs_0_, bf16[128,768]{1,0:T(8,128)(2,1)S(1)} %collective-permute-done.7.refs_1_, f32[256,128]{1,0:T(8,128)S(1)} %get-tuple-element.10.refs_0_.refs_2_, bf16[128,768]{1,0:T(8,128)(2,1)S(1)} %collective-permute-done.2.refs_1_.refs_3_, ...), custom_call_target="tpu_custom_call" | custom-call | flops 20000000000 | bytes 1024 | tf_op jit(solution)/shard_map/finish/pallas_call | solution.py:262
  25.4 4.0 %collective-permute-done.6.refs_1_ = bf16[128,1280]{1,0:T(8,128)(2,1)S(1)} collective-permute-done((bf16[128,1280]{1,0:T(8,128)(2,1)S(1)}, bf16[128,1280]{1,0:T(8,128)(2,1)S(1)}, u32[]{:S(2)}, u32[]{:S(2)}) %collective-permute-start.6) | collective-permute-done | bytes 327712 | tf_op jit(solution)/shard_map/ppermute | solution.py:27
  29.4 2.3 %finish.5.refs_6_ = bf16[1,128,4096]{2,1,0:T(8,128)(2,1)} custom-call(bf16[128,1280]{1,0:T(8,128)(2,1)S(1)} %own.6.refs_5_.refs_0_, bf16[128,1280]{1,0:T(8,128)(2,1)S(1)} %collective-permute-done.6.refs_1_, f32[256,128]{1,0:T(8,128)S(1)} %get-tuple-element.10.refs_0_.refs_2_, ...), custom_call_target="tpu_custom_call", output_to_operand_aliasing={{}: (6, {})} | custom-call | flops 20000000000 | bytes 1024 | tf_op jit(solution)/shard_map/finish/pallas_call | solution.py:262
  31.8 3.3 %collective-permute-done.5.refs_1_ = bf16[128,1024]{1,0:T(8,128)(2,1)S(1)} collective-permute-done((bf16[128,1024]{1,0:T(8,128)(2,1)S(1)}, bf16[128,1024]{1,0:T(8,128)(2,1)S(1)}, u32[]{:S(2)}, u32[]{:S(2)}) %collective-permute-start.5) | collective-permute-done | bytes 262176 | tf_op jit(solution)/shard_map/ppermute | solution.py:27
  35.1 2.0 %finish.6.refs_6_ = bf16[1,128,4096]{2,1,0:T(8,128)(2,1)} custom-call(bf16[128,1024]{1,0:T(8,128)(2,1)S(1)} %own.7.refs_5_.refs_0_, bf16[128,1024]{1,0:T(8,128)(2,1)S(1)} %collective-permute-done.5.refs_1_, f32[256,128]{1,0:T(8,128)S(1)} %get-tuple-element.10.refs_0_.refs_2_, ...), custom_call_target="tpu_custom_call", output_to_operand_aliasing={{}: (6, {})} | custom-call | flops 20000000000 | bytes 1024 | tf_op jit(solution)/shard_map/finish/pallas_call | solution.py:262
  37.1 1.5 %collective-permute-done.4.refs_1_ = bf16[128,640]{1,0:T(8,128)(2,1)S(1)} collective-permute-done((bf16[128,640]{1,0:T(8,128)(2,1)S(1)}, bf16[128,640]{1,0:T(8,128)(2,1)S(1)}, u32[]{:S(2)}, u32[]{:S(2)}) %collective-permute-start.4) | collective-permute-done | bytes 163872 | tf_op jit(solution)/shard_map/ppermute | solution.py:27
  38.6 1.6 %finish.7.refs_0_ = bf16[1,128,4096]{2,1,0:T(8,128)(2,1)} custom-call(bf16[128,640]{1,0:T(8,128)(2,1)S(1)} %own.8.refs_5_.refs_0_, bf16[128,640]{1,0:T(8,128)(2,1)S(1)} %collective-permute-done.4.refs_1_, f32[256,128]{1,0:T(8,128)S(1)} %get-tuple-element.10.refs_0_.refs_2_, ...), custom_call_target="tpu_custom_call", output_to_operand_aliasing={{}: (6, {})} | custom-call | flops 20000000000 | bytes 1024 | tf_op jit(solution)/shard_map/finish/pallas_call | solution.py:262
  40.1 0.0 collective-permute-done.3.received_ref
  40.2 0.7 %last.1 = bf16[1,128,4096]{2,1,0:T(8,128)(2,1)} custom-call(bf16[128,384]{1,0:T(8,128)(2,1)S(1)} %own.9.refs_4_.own_ref, bf16[128,384]{1,0:T(8,128)(2,1)S(1)} %collective-permute-done.3.received_ref, f32[128,384]{1,0:T(8,128)S(1)} %later.1.refs_6_.gated_ref, bf16[1,128,4096]{2,1,0:T(8,128)(2,1)} %finish.7.refs_0_), custom_call_target="tpu_custom_call", output_to_operand_aliasing={{}: (3, {})} | custom-call | flops 20000000000 | bytes 1024 | tf_op jit(solution)/shard_map/last/pallas_call | solution.py:281
  (5 shorter events, 0.1 us)
Async XLA Ops:
  1.8 11.2 %copy-start.1 = (bf16[1,256,128]{2,1,0:T(8,128)(2,1)S(1)}, bf16[1,256,128]{2,1,0:T(8,128)(2,1)}, u32[]{:S(2)}) copy-start(bf16[1,256,128]{2,1,0:T(8,128)(2,1)} %bank_ref.1) | copy-start | bytes 196612
  1.8 11.8 %copy-start = (bf16[1,128,4096]{2,1,0:T(8,128)(2,1)S(1)}, bf16[1,128,4096]{2,1,0:T(8,128)(2,1)}, u32[]{:S(2)}) copy-start(bf16[1,128,4096]{2,1,0:T(8,128)(2,1)} %refs_5_.7) | copy-start | bytes 3145732
  1.8 11.8 %copy-start.4 = (bf16[128,4096]{1,0:T(8,128)(2,1)S(1)}, bf16[128,4096]{1,0:T(8,128)(2,1)}, u32[]{:S(2)}) copy-start(bf16[128,4096]{1,0:T(8,128)(2,1)} %refs_4_.9) | copy-start | bytes 3145732
  1.8 11.8 %collective-permute-start.2 = (bf16[128,768]{1,0:T(8,128)(2,1)S(1)}, bf16[128,768]{1,0:T(8,128)(2,1)S(1)}, u32[]{:S(2)}, u32[]{:S(2)}) collective-permute-start(bf16[128,768]{1,0:T(8,128)(2,1)S(1)} %product.2.refs_0_.refs_2_.refs_4_), channel_id=1, source_target_pairs={{0,4},{4,8},{8,12},{12,16},{16,20},{20,24},{24,28},{1,5},{5,9},{9,... | collective-permute-start | bytes 589832 | tf_op jit(solution)/shard_map/ppermute | solution.py:27
  7.4 5.6 %copy-start.3 = (s32[1,256]{1,0:T(1,128)S(1)}, s32[1,256]{1,0:T(1,128)}, u32[]{:S(2)}) copy-start(s32[1,256]{1,0:T(1,128)} %assign_ref.1) | copy-start | bytes 3076
  7.5 5.6 %copy-start.2 = (f32[1,256]{1,0:T(1,128)S(1)}, f32[1,256]{1,0:T(1,128)}, u32[]{:S(2)}) copy-start(f32[1,256]{1,0:T(1,128)} %scales_ref.1) | copy-start | bytes 3076
  7.5 7.5 %collective-permute-start.1 = (bf16[128,1280]{1,0:T(8,128)(2,1)S(1)}, bf16[128,1280]{1,0:T(8,128)(2,1)S(1)}, u32[]{:S(2)}, u32[]{:S(2)}) collective-permute-start(bf16[128,1280]{1,0:T(8,128)(2,1)S(1)} %get-tuple-element.9.refs_0_.refs_2_.refs_4_), channel_id=1, source_target_pairs={{0,4},{4,8},{8,12},{12,16},{16,20},{20,24},{24,28},{1,5},{5,9},{9,... | collective-permute-start | bytes 983048 | tf_op jit(solution)/shard_map/ppermute | solution.py:27
  9.4 9.7 %collective-permute-start = (bf16[128,2048]{1,0:T(8,128)(2,1)S(1)}, bf16[128,2048]{1,0:T(8,128)(2,1)S(1)}, u32[]{:S(2)}, u32[]{:S(2)}) collective-permute-start(bf16[128,2048]{1,0:T(8,128)(2,1)S(1)} %get-tuple-element.11.refs_2_.refs_4_), channel_id=1, source_target_pairs={{0,4},{4,8},{8,12},{12,16},{16,20},{20,24},{24,28},{1,5},{5,9},{9,... | collective-permute-start | bytes 1572872 | tf_op jit(solution)/shard_map/ppermute | solution.py:27
  13.6 10.0 %collective-permute-start.7 = (bf16[128,768]{1,0:T(8,128)(2,1)S(1)}, bf16[128,768]{1,0:T(8,128)(2,1)S(1)}, u32[]{:S(2)}, u32[]{:S(2)}) collective-permute-start(bf16[128,768]{1,0:T(8,128)(2,1)S(1)} %own.5.refs_5_.refs_0_), channel_id=1, source_target_pairs={{0,1},{2,3},{4,5},{6,7},{8,9},{10,11},{12,13},{14,15},{16,17},{18,... | collective-permute-start | bytes 589832 | tf_op jit(solution)/shard_map/ppermute | solution.py:27
  15.0 14.5 %collective-permute-start.6 = (bf16[128,1280]{1,0:T(8,128)(2,1)S(1)}, bf16[128,1280]{1,0:T(8,128)(2,1)S(1)}, u32[]{:S(2)}, u32[]{:S(2)}) collective-permute-start(bf16[128,1280]{1,0:T(8,128)(2,1)S(1)} %own.6.refs_5_.refs_0_), channel_id=1, source_target_pairs={{0,1},{2,3},{4,5},{6,7},{8,9},{10,11},{12,13},{14,15},{16,17},{18,... | collective-permute-start | bytes 983048 | tf_op jit(solution)/shard_map/ppermute | solution.py:27
  19.1 16.0 %collective-permute-start.5 = (bf16[128,1024]{1,0:T(8,128)(2,1)S(1)}, bf16[128,1024]{1,0:T(8,128)(2,1)S(1)}, u32[]{:S(2)}, u32[]{:S(2)}) collective-permute-start(bf16[128,1024]{1,0:T(8,128)(2,1)S(1)} %own.7.refs_5_.refs_0_), channel_id=1, source_target_pairs={{0,1},{2,3},{4,5},{6,7},{8,9},{10,11},{12,13},{14,15},{16,17},{18,... | collective-permute-start | bytes 786440 | tf_op jit(solution)/shard_map/ppermute | solution.py:27
  20.4 18.2 %collective-permute-start.4 = (bf16[128,640]{1,0:T(8,128)(2,1)S(1)}, bf16[128,640]{1,0:T(8,128)(2,1)S(1)}, u32[]{:S(2)}, u32[]{:S(2)}) collective-permute-start(bf16[128,640]{1,0:T(8,128)(2,1)S(1)} %own.8.refs_5_.refs_0_), channel_id=1, source_target_pairs={{0,1},{2,3},{4,5},{6,7},{8,9},{10,11},{12,13},{14,15},{16,17},{18,... | collective-permute-start | bytes 491528 | tf_op jit(solution)/shard_map/ppermute | solution.py:27
  21.7 18.4 %collective-permute-start.3 = (bf16[128,384]{1,0:T(8,128)(2,1)S(1)}, bf16[128,384]{1,0:T(8,128)(2,1)S(1)}, u32[]{:S(2)}, u32[]{:S(2)}) collective-permute-start(bf16[128,384]{1,0:T(8,128)(2,1)S(1)} %own.9.refs_4_.own_ref), channel_id=1, source_target_pairs={{0,1},{2,3},{4,5},{6,7},{8,9},{10,11},{12,13},{14,15},{16,17},{18,... | collective-permute-start | bytes 294920 | tf_op jit(solution)/shard_map/ppermute | solution.py:27

commit v3 on v0

v3 whole, which is shorter than its diff:
```python
import functools

import jax
import jax.numpy as jnp
from jax import lax
from jax.experimental import pallas as pl
from jax.experimental.pallas import tpu as pltpu
from jax.sharding import PartitionSpec as P

LANES = 128
ROW_BLOCK = 32
RAW = 1152
CHUNKS = (1408, 1024, 512)
F32 = jnp.float32
BF16 = jnp.bfloat16
MIB = 1024 * 1024
QUICK, SLOW = 1024, 20_000_000_000

SMEM = pl.BlockSpec(memory_space=pltpu.SMEM)
VMEM = pl.BlockSpec(memory_space=pltpu.VMEM)
ANY = pl.BlockSpec(memory_space=pl.ANY)
HBM = pl.BlockSpec(memory_space=pltpu.HBM)


def to_next_slab(value, pipes):
    slabs, depth = lax.axis_size("ctx"), lax.axis_size("pipe")
    pairs = [(slab * depth + pipe, (slab + 1) * depth + pipe) for slab in range(slabs - 1) for pipe in pipes]
    return lax.ppermute(value, ("ctx", "pipe"), pairs)


def to_next_section(value):
    return lax.ppermute(value, "pipe", [(0, 1)])


def call(kernel, name, out_shape, in_specs, out_specs, scratch=(), weight=QUICK, aliases=None):
    return pl.pallas_call(
        kernel,
        out_shape=out_shape,
        in_specs=in_specs,
        out_specs=out_specs,
        scratch_shapes=list(scratch),
        input_output_aliases=aliases or {},
        compiler_params=pltpu.CompilerParams(vmem_limit_bytes=16 * MIB),
        cost_estimate=pl.CostEstimate(flops=weight, bytes_accessed=1024, transcendentals=0),
        name=name,
    )


def is_first():
    return lax.axis_index("pipe") == 0


def array(rows, cols, kind=BF16):
    return jax.ShapeDtypeStruct((rows, cols), kind)


def multiply(start_ref, keys_ref, values_ref, keys_in, values_in, sems, first, targets):
    rows = keys_in.shape[0]
    slab = lax.axis_index("ctx") * rows
    positions = slab + lax.broadcasted_iota(jnp.int32, (rows, LANES), 0)
    inside = positions >= start_ref[0]
    pieces, offset = [], 0
    for piece, (out_ref, row, col, width) in enumerate(targets):
        at = pl.ds(offset, width)
        source = pl.ds(first + offset, width)
        copies = (
            pltpu.make_async_copy(keys_ref.at[0, :, source], keys_in.at[:, at], sems.at[2 * piece]),
            pltpu.make_async_copy(values_ref.at[0, :, source], values_in.at[:, at], sems.at[2 * piece + 1]),
        )
        for copy in copies:
            copy.start()
        pieces.append(copies)
        offset += width
    offset = 0
    for copies, (out_ref, row, col, width) in zip(pieces, targets):
        for copy in copies:
            copy.wait()
        for tile in range(0, width, LANES):
            at = slice(offset + tile, offset + tile + LANES)
            product = keys_in[:, at].astype(F32) * values_in[:, at].astype(F32)
            out_ref[row : row + rows, col + tile : col + tile + LANES] = jnp.where(inside, product, 0.0).astype(BF16)
        offset += width


def lead_kernel(start_ref, queries_ref, keys_ref, values_ref, raw_ref, near_ref, keys_in, values_in, sems, sem):
    rows, width = near_ref.shape

    @pl.when(is_first())
    def _():
        copy = pltpu.make_async_copy(queries_ref.at[0, :, pl.ds(0, RAW)], raw_ref.at[pl.ds(0, rows)], sem)
        copy.start()
        targets = [(raw_ref, rows, 0, RAW), (near_ref, 0, 0, width)]
        multiply(start_ref, keys_ref, values_ref, keys_in, values_in, sems, 0, targets)
        copy.wait()


def lead_of(start, queries, keys, values):
    rows, width = queries.shape[1], CHUNKS[0]
    return call(
        lead_kernel,
        "lead",
        (array(2 * rows, RAW), array(rows, width)),
        [SMEM, HBM, HBM, HBM],
        (VMEM, VMEM),
        [
            pltpu.VMEM((rows, RAW + width), BF16),
            pltpu.VMEM((rows, RAW + width), BF16),
            pltpu.SemaphoreType.DMA((4,)),
            pltpu.SemaphoreType.DMA(()),
        ],
    )(start, queries, keys, values)


def rest_kernel(start_ref, keys_ref, values_ref, _, rest_ref, later_ref, keys_in, values_in, sems):
    width, total = rest_ref.shape[1], later_ref.shape[1]
    half = total // 2

    @pl.when(is_first())
    def _():
        targets = [(rest_ref, 0, 0, width)]
        multiply(start_ref, keys_ref, values_ref, keys_in, values_in, sems, total - width, targets)

    @pl.when(jnp.logical_not(is_first()))
    def _():
        targets = [(later_ref, 0, 0, half), (later_ref, 0, half, total - half)]
        multiply(start_ref, keys_ref, values_ref, keys_in, values_in, sems, 0, targets)


def rest_of(start, keys, values, after):
    rows, total = keys.shape[1:]
    return call(
        rest_kernel,
        "rest",
        (array(rows, total - RAW - CHUNKS[0]), array(rows, total)),
        [SMEM, HBM, HBM, ANY],
        (VMEM, VMEM),
        [pltpu.VMEM((rows, total), BF16), pltpu.VMEM((rows, total), BF16), pltpu.SemaphoreType.DMA((4,))],
    )(start, keys, values, after)


def turn_table(lines_ref, row, count, table_ref, at):
    taps = lines_ref.shape[1]
    upper = lax.broadcasted_iota(jnp.int32, (ROW_BLOCK, taps), 1) > lax.broadcasted_iota(
        jnp.int32, (ROW_BLOCK, taps), 0
    )
    for group in range(count):
        line = lines_ref[row + group : row + group + 1, :]
        turned = pltpu.roll(jnp.broadcast_to(line, (ROW_BLOCK, taps)), 1, 1, stride=1, stride_axis=0)
        span = slice(at + group * ROW_BLOCK, at + (group + 1) * ROW_BLOCK)
        table_ref[span, :taps] = jnp.where(upper, turned, 0.0).astype(BF16)
        table_ref[span, taps:] = jnp.where(upper, 0.0, turned)[:, :ROW_BLOCK].astype(BF16)


def taps_kernel(share, bank_ref, scales_ref, assign_ref, _, lines_ref, table_ref):
    groups, taps = lines_ref.shape
    size = bank_ref.shape[1]
    chosen = (lax.broadcasted_iota(jnp.int32, (size, groups), 0) == assign_ref[...]).astype(F32).astype(BF16)
    contract = (((0,), (0,)), ((), ()))
    picked = lax.dot_general(bank_ref[0], chosen, contract, preferred_element_type=F32)
    scaled = (picked * scales_ref[...]).astype(BF16)
    order = lax.broadcasted_iota(jnp.int32, (taps, taps), 0) + lax.broadcasted_iota(jnp.int32, (taps, taps), 1)
    flip = (order == taps - 1).astype(F32).astype(BF16)
    lines_ref[...] = lax.dot_general(scaled, flip, contract, preferred_element_type=F32)

    @pl.when(is_first())
    def _():
        for tile in range(CHUNKS[0] // LANES):
            turn_table(lines_ref, (RAW // LANES + tile) * share, share, table_ref, tile * share * ROW_BLOCK)


def taps_of(bank, scales, assign, total, after):
    groups, taps = assign.shape[1], bank.shape[2]
    share = LANES * groups // total
    return call(
        functools.partial(taps_kernel, share),
        "taps",
        (array(groups, taps, F32), array(CHUNKS[0] // LANES * share * ROW_BLOCK, taps + ROW_BLOCK)),
        [VMEM] * 3 + [ANY],
        (VMEM, VMEM),
    )(bank, scales, assign, after)


def mix(table_ref, row, share, window, store):
    depth = table_ref.shape[1]
    rows = window.shape[0] - depth + ROW_BLOCK
    member = lax.broadcasted_iota(jnp.int32, (ROW_BLOCK, LANES), 1) // (LANES // share)
    table = table_ref[row : row + share * ROW_BLOCK, :]
    for first in range(0, rows, ROW_BLOCK):
        sums = jnp.dot(table, window[first : first + depth], preferred_element_type=F32)
        mixed = sums[:ROW_BLOCK]
        for group in range(1, share):
            mixed = jnp.where(member == group, sums[group * ROW_BLOCK : (group + 1) * ROW_BLOCK], mixed)
        store(slice(first, first + ROW_BLOCK), mixed)


def mix_all(width, share, lines_ref, line, table_ref, made, behind_ref, product_ref, local, store):
    for tile in range(width // LANES):
        at = slice(tile * LANES, (tile + 1) * LANES)
        inner = slice(local + at.start, local + at.stop)
        row = tile * share * ROW_BLOCK
        if not made:
            turn_table(lines_ref, line + tile * share, share, table_ref, row)
        window = jnp.concatenate([behind_ref[:, inner], product_ref[:, inner]], axis=0)
        mix(table_ref, row, share, window, functools.partial(store, at))


def share_of(lines_ref, total):
    return LANES * lines_ref.shape[0] // total


def own_kernel(first, local, made, *refs):
    lines_ref, behind_ref, product_ref, queries_ref, residual_ref, table_ref, out_ref = refs[:7]
    if not made:
        table_ref = refs[-1]
    width = out_ref.shape[1]
    rows, total = residual_ref.shape
    share = share_of(lines_ref, total)

    @pl.when(is_first())
    def _():
        def store(at, span, mixed):
            cols = slice(first + at.start, first + at.stop)
            gated = queries_ref[0, span, cols].astype(F32) * mixed
            out_ref[span, at] = (residual_ref[span, cols].astype(F32) + gated).astype(BF16)

        line = first // LANES * share
        mix_all(width, share, lines_ref, line, table_ref, made, behind_ref, product_ref, local, store)
        if made:
            extra = out_ref.shape[0] - rows
            for part in range(-(-(RAW // LANES * share) // extra)):
                taken = lines_ref[part * extra : (part + 1) * extra, :].astype(BF16)
                out_ref[rows:, part * LANES : (part + 1) * LANES] = taken


def table_scratch(lines, width, total):
    groups, taps = lines.shape
    return pltpu.VMEM((width * groups // total * ROW_BLOCK, taps + ROW_BLOCK), BF16)


def own_of(lines, behind, product, queries, residual, first, local, width, made, after):
    rows, total = residual.shape
    return call(
        functools.partial(own_kernel, first, local, made),
        "own",
        array(rows + 16 if made else rows, width),
        [VMEM] * 5 + [VMEM if made else ANY],
        VMEM,
        [] if made else [table_scratch(lines, width, total)],
        weight=QUICK if made else SLOW,
    )(lines, behind, product, queries, residual, after)


def pick_kernel(raw_ref, received_ref, _, queries_ref, product_ref):
    rows = queries_ref.shape[0]

    def take(source):
        queries_ref[...] = source[:rows, :]
        product_ref[...] = source[rows:, :]

    pl.when(is_first())(lambda: take(raw_ref))
    pl.when(jnp.logical_not(is_first()))(lambda: take(received_ref))


def pick_of(raw, received, after):
    rows, width = raw.shape[0] // 2, raw.shape[1]
    return call(
        pick_kernel, "pick", (array(rows, width),) * 2, [VMEM, VMEM, ANY], (VMEM, VMEM), weight=SLOW
    )(raw, received, after)


def later_kernel(first, lines_ref, behind_ref, product_ref, queries_ref, _, out_ref, table_ref):
    total = queries_ref.shape[2]
    share = share_of(lines_ref, total)

    @pl.when(jnp.logical_not(is_first()))
    def _():
        def store(at, span, mixed):
            cols = slice(first + at.start, first + at.stop)
            out_ref[span, at] = queries_ref[0, span, cols].astype(F32) * mixed

        line = first // LANES * share
        mix_all(total - first, share, lines_ref, line, table_ref, False, behind_ref, product_ref, first, store)


def later_of(lines, behind, product, queries, first, after):
    rows, total = product.shape
    return call(
        functools.partial(later_kernel, first),
        "later",
        array(rows, total - first, F32),
        [VMEM] * 4 + [ANY],
        VMEM,
        [table_scratch(lines, total - first, total)],
        weight=SLOW,
    )(lines, behind, product, queries, after)


def send_out(buffer, out_ref, first, sem):
    width = out_ref.shape[2] if buffer.shape[1] == out_ref.shape[2] else buffer.shape[1]
    copy = pltpu.make_async_copy(buffer, out_ref.at[0, :, pl.ds(first, width)], sem)
    copy.start()
    copy.wait()


def chunk_kernel(first, *refs):
    own_ref, received_ref, lines_ref, behind_ref, product_ref, queries_ref = refs[:6]
    out_ref, table_ref, buffer, sem = refs[-4:]
    rows, width = buffer.shape
    share = share_of(lines_ref, queries_ref.shape[2])

    @pl.when(is_first())
    def _():
        send_out(own_ref.at[pl.ds(0, rows)], out_ref, first, sem)

    @pl.when(jnp.logical_not(is_first()))
    def _():
        def store(at, span, mixed):
            cols = slice(first + at.start, first + at.stop)
            gated = queries_ref[0, span, cols].astype(F32) * mixed
            buffer[span, at] = (received_ref[span, at].astype(F32) + gated).astype(BF16)

        line = first // LANES * share
        mix_all(width, share, lines_ref, line, table_ref, False, behind_ref, product_ref, first, store)
        send_out(buffer, out_ref, first, sem)


def chunk_finish(own, received, lines, behind, product, queries, first, after):
    rows, total = product.shape
    width = own.shape[1]
    return call(
        functools.partial(chunk_kernel, first),
        "chunk",
        jax.ShapeDtypeStruct((1, rows, total), BF16),
        [VMEM] * 6 + [ANY],
        ANY,
        [table_scratch(lines, width, total), pltpu.VMEM((rows, width), BF16), pltpu.SemaphoreType.DMA(())],
        weight=SLOW,
    )(own, received, lines, behind, product, queries, after)


def raw_kernel(*refs):
    lines_ref, received_ref, raw_behind_ref, raw_product_ref, raw_queries_ref = refs[:5]
    behind_ref, product_ref, queries_ref, residual_ref, _ = refs[5:10]
    out_ref, chosen_ref, table_ref, buffer, sem = refs[10:]
    rows, width = buffer.shape
    share = share_of(lines_ref, queries_ref.shape[2])
    count = chosen_ref.shape[0]

    @pl.when(is_first())
    def _():
        chosen_ref[...] = lines_ref[:count, :]

    @pl.when(jnp.logical_not(is_first()))
    def _():
        extra = received_ref.shape[0] - rows
        for part in range(-(-count // extra)):
            span = slice(part * extra, min((part + 1) * extra, count))
            taken = received_ref[rows:, part * LANES : (part + 1) * LANES].astype(F32)
            chosen_ref[span, :] = taken[: span.stop - span.start]

    def store_first(at, span, mixed):
        gated = raw_queries_ref[span, at].astype(F32) * mixed
        buffer[span, at] = (residual_ref[span, at].astype(F32) + gated).astype(BF16)

    mix_all(width, share, chosen_ref, 0, table_ref, False, raw_behind_ref, raw_product_ref, 0, store_first)

    @pl.when(jnp.logical_not(is_first()))
    def _():
        def store_second(at, span, mixed):
            gated = queries_ref[0, span, at].astype(F32) * mixed
            buffer[span, at] = (buffer[span, at].astype(F32) + gated).astype(BF16)

        mix_all(width, share, lines_ref, 0, table_ref, False, behind_ref, product_ref, 0, store_second)

    send_out(buffer, out_ref, 0, sem)


def raw_finish(held, lines, received, raw_behind, raw_product, raw_queries, behind, product, queries, residual):
    rows, total = residual.shape
    groups, taps = lines.shape
    return call(
        raw_kernel,
        "raw",
        jax.ShapeDtypeStruct(held.shape, BF16),
        [VMEM] * 9 + [ANY],
        ANY,
        [
            pltpu.VMEM((RAW * groups // total, taps), F32),
            table_scratch(lines, RAW, total),
            pltpu.VMEM((rows, RAW), BF16),
            pltpu.SemaphoreType.DMA(()),
        ],
        weight=SLOW,
        aliases={9: 0},
    )(lines, received, raw_behind, raw_product, raw_queries, behind, product, queries, residual, held)


def last_kernel(first, local, own_ref, received_ref, gated_ref, _, out_ref, buffer, sem):
    width = buffer.shape[1]

    @pl.when(is_first())
    def _():
        send_out(own_ref, out_ref, first, sem)

    @pl.when(jnp.logical_not(is_first()))
    def _():
        buffer[...] = (received_ref[...].astype(F32) + gated_ref[:, local : local + width]).astype(BF16)
        send_out(buffer, out_ref, first, sem)


def last_finish(held, own, received, gated, first, local):
    rows, width = own.shape
    return call(
        functools.partial(last_kernel, first, local),
        "last",
        jax.ShapeDtypeStruct(held.shape, BF16),
        [VMEM] * 3 + [ANY],
        ANY,
        [pltpu.VMEM((rows, width), BF16), pltpu.SemaphoreType.DMA(())],
        weight=SLOW,
        aliases={3: 0},
    )(own, received, gated, held)


def body(queries, keys, values, residual, filter_bank, filter_scales, group_filter, context_start):
    total = queries.shape[2]
    far_queries, keys, values = (
        pltpu.with_memory_space_constraint(value, pltpu.HBM) for value in (queries, keys, values)
    )
    raw, near = lead_of(context_start, far_queries, keys, values)
    raw_received = to_next_section(raw)
    near_behind = to_next_slab(near, (0,))
    rest, product = rest_of(context_start, keys, values, near)
    rest_behind = to_next_slab(rest, (0,))
    behind = to_next_slab(product, (1,))
    lines, table = taps_of(filter_bank, filter_scales, group_filter, total, rest)
    own = [own_of(lines, near_behind, near, queries, residual, RAW, 0, CHUNKS[0], True, table)]
    received = [to_next_section(own[0])]
    raw_queries, raw_product = pick_of(raw, raw_received, own[0])
    raw_behind = to_next_slab(raw_product, (0, 1))
    second = RAW + CHUNKS[0]
    first, after = second, raw_product
    for width in CHUNKS[1:]:
        after = own_of(lines, rest_behind, rest, queries, residual, first, first - second, width, False, after)
        own.append(after)
        received.append(to_next_section(after))
        first += width
    gated = later_of(lines, behind, product, queries, second, after)
    held = chunk_finish(own[0], received[0], lines, behind, product, queries, RAW, gated)
    held = raw_finish(
        held, lines, received[0], raw_behind, raw_product, raw_queries, behind, product, queries, residual
    )
    first = second
    for chunk, width in enumerate(CHUNKS[1:], 1):
        held = last_finish(held, own[chunk], received[chunk], gated, first, first - second)
        first += width
    return held


def solution(mesh):
    return jax.shard_map(
        body,
        mesh=mesh,
        in_specs=(
            P("pipe", ("dp", "ctx"), None),
            P("pipe", ("dp", "ctx"), None),
            P("pipe", ("dp", "ctx"), None),
            P(("dp", "ctx"), None),
            P("pipe", None, None),
            P("pipe", None),
            P("pipe", None),
            P("dp"),
        ),
        out_specs=P("pipe", ("dp", "ctx"), None),
        check_vma=False,
    )
```

time: 85.6 us -> 36.3 us (0.42)
  the two profiles are of different devices: /device:TPU:12 before, /device:TPU:0 now
where the time goes in v3:
time: 36.3 us; the launch traced here: 35.9 us
  starting transfers between devices  17 us (47%)
  Pallas kernels  11.6 us (32%)
  waiting for transfers between devices  6.39 us (18%)
  between operations  0.92 us (3%)
    ppermute x4, starting transfers between devices, to_next_section(): return lax.ppermute(value, 'pipe', [(0, 1)])  9.27 us
    ppermute x4, starting transfers between devices, to_next_slab(): return lax.ppermute(value, ('ctx', 'pipe'), pairs)  7.7 us
    ppermute x4, waiting for transfers between devices, to_next_section(): return lax.ppermute(value, 'pipe', [(0, 1)])  6.38 us
    pallas_call x3, Pallas kernels, own_of(): call(functools.partial(own_kernel, first, local, made), 'own', array(rows...  3.73 us
    pallas_call x1, Pallas kernels, raw_finish(): call(raw_kernel, 'raw', jax.ShapeDtypeStruct(held.shape, BF16), [VMEM] *...  2.19 us
    pallas_call x1, Pallas kernels, lead_of(): call(lead_kernel, 'lead', (array(2 * rows, RAW), array(rows, width)), [SM...  1.54 us
    pallas_call x2, Pallas kernels, last_finish(): call(functools.partial(last_kernel, first, local), 'last', jax.ShapeDtype...  1.37 us
    pallas_call x1, Pallas kernels, rest_of(): call(rest_kernel, 'rest', (array(rows, total - RAW - CHUNKS[0]), array(ro...  1.3 us
  transfers between devices with their start and end apart: 8, of which 4 were waited for; matrix products, arithmetic and copies ran while one was open for 0% of the time, Pallas kernels for 26%

profile of v3, /device:TPU:0, one launch (start us, length us, event | category | flops | bytes accessed | tf_op | source)
XLA Modules:
  0.0 35.9 jit_solution(13264177643518212859)
XLA Ops:
  0.7 1.5 %lead.1 = (bf16[256,1152]{1,0:T(8,128)(2,1)S(1)}, bf16[128,1408]{1,0:T(8,128)(2,1)S(1)}) custom-call(s32[1]{0:T(128)S(6)} %copy.15.start_ref, bf16[1,128,4096]{2,1,0:T(8,128)(2,1)} %refs_7_.1, bf16[1,128,4096]{2,1,0:T(8,128)(2,1)} %keys_ref.3, bf16[1,128,4096]{2,1,0:T(8,128)(2,1)} %values_ref.3), custom_call_target="tpu_custom_call" | custom-call | flops 1024 | bytes 1024 | tf_op jit(solution)/shard_map/lead/pallas_call | solution.py:99
  2.2 0.0 copy-start.2
  2.2 0.0 copy-start.3
  2.2 0.0 copy-start.4
  2.2 3.6 %collective-permute-start.1 = (bf16[256,1152]{1,0:T(8,128)(2,1)S(1)}, bf16[256,1152]{1,0:T(8,128)(2,1)S(1)}, u32[]{:S(2)}, u32[]{:S(2)}) collective-permute-start(bf16[256,1152]{1,0:T(8,128)(2,1)S(1)} %get-tuple-element.16.raw_ref), channel_id=1, source_target_pairs={{0,1},{2,3},{4,5},{6,7},{8,9},{10,11},{12,13},{14,15},{16,17},{18,... | collective-permute-start | bytes 1769480 | tf_op jit(solution)/shard_map/ppermute | solution.py:32
  5.8 0.0 copy-start
  5.8 0.0 copy-start.1
  5.8 1.6 %collective-permute-start.2 = (bf16[128,1408]{1,0:T(8,128)(2,1)S(1)}, bf16[128,1408]{1,0:T(8,128)(2,1)S(1)}, u32[]{:S(2)}, u32[]{:S(2)}) collective-permute-start(bf16[128,1408]{1,0:T(8,128)(2,1)S(1)} %get-tuple-element.13._.refs_2_), channel_id=1, source_target_pairs={{0,4},{4,8},{8,12},{12,16},{16,20},{20,24},{24,28},{2,6},{6,10},{1... | collective-permute-start | bytes 1081352 | tf_op jit(solution)/shard_map/ppermute | solution.py:28
  7.4 1.3 %rest.1 = (bf16[128,1536]{1,0:T(8,128)(2,1)S(1)}, bf16[128,4096]{1,0:T(8,128)(2,1)S(1)}) custom-call(s32[1]{0:T(128)S(6)} %copy.15.start_ref, bf16[1,128,4096]{2,1,0:T(8,128)(2,1)} %keys_ref.3, bf16[1,128,4096]{2,1,0:T(8,128)(2,1)} %values_ref.3, bf16[128,1408]{1,0:T(8,128)(2,1)S(1)} %get-tuple-element.13._.refs_2_), custom_call_target="tpu_custom_call" | custom-call | flops 1024 | bytes 1024 | tf_op jit(solution)/shard_map/rest/pallas_call | solution.py:131
  8.8 4.0 %collective-permute-start = (bf16[128,1536]{1,0:T(8,128)(2,1)S(1)}, bf16[128,1536]{1,0:T(8,128)(2,1)S(1)}, u32[]{:S(2)}, u32[]{:S(2)}) collective-permute-start(bf16[128,1536]{1,0:T(8,128)(2,1)S(1)} %get-tuple-element.14._.refs_2_), channel_id=1, source_target_pairs={{0,4},{4,8},{8,12},{12,16},{16,20},{20,24},{24,28},{2,6},{6,10},{1... | collective-permute-start | bytes 1179656 | tf_op jit(solution)/shard_map/ppermute | solution.py:28
  12.8 0.7 %collective-permute-start.4 = (bf16[128,4096]{1,0:T(8,128)(2,1)S(1)}, bf16[128,4096]{1,0:T(8,128)(2,1)S(1)}, u32[]{:S(2)}, u32[]{:S(2)}) collective-permute-start(bf16[128,4096]{1,0:T(8,128)(2,1)S(1)} %get-tuple-element.19.product_ref.refs_4_.refs_6_), channel_id=1, source_target_pairs={{1,5},{5,9},{9,13},{13,17},{17,21},{21,25},{25,29},{3,7},{7,11},{1... | collective-permute-start | bytes 3145736 | tf_op jit(solution)/shard_map/ppermute | solution.py:28
  13.6 0.0 copy-done.2
  13.6 0.0 copy-done.3
  13.6 0.0 copy-done.4
  13.6 0.7 %taps.1 = (f32[256,128]{1,0:T(8,128)S(1)}, bf16[2816,160]{1,0:T(8,128)(2,1)S(1)}) custom-call(bf16[1,256,128]{2,1,0:T(8,128)(2,1)S(1)} %copy-done.2, f32[1,256]{1,0:T(1,128)S(1)} %copy-done.3, s32[1,256]{1,0:T(1,128)S(1)} %copy-done.4, bf16[128,1536]{1,0:T(8,128)(2,1)S(1)} %get-tuple-element.14._.refs_2_), custom_call_target="tpu_custom_call" | custom-call | flops 1024 | bytes 1024 | tf_op jit(solution)/shard_map/taps/pallas_call | solution.py:174
  14.3 0.0 collective-permute-done.2.refs_1_
  14.3 0.0 copy-done
  14.3 0.0 copy-done.1
  14.3 1.7 %own.3._.refs_0_ = bf16[144,1408]{1,0:T(8,128)(2,1)S(1)} custom-call(f32[256,128]{1,0:T(8,128)S(1)} %get-tuple-element.15.refs_0_.lines_ref.refs_2_, bf16[128,1408]{1,0:T(8,128)(2,1)S(1)} %collective-permute-done.2.refs_1_, bf16[128,1408]{1,0:T(8,128)(2,1)S(1)} %get-tuple-element.13._.refs_2_, bf16[1,128,4096]{2,1,0:T(8,128)(2,1)S(1)} %copy-done, ...), custom_call_target="tpu_custom_call" | custom-call | flops 1024 | bytes 1024 | tf_op jit(solution)/shard_map/own/pallas_call | solution.py:242
  16.0 1.3 %collective-permute-start.6 = (bf16[144,1408]{1,0:T(8,128)(2,1)S(1)}, bf16[144,1408]{1,0:T(8,128)(2,1)S(1)}, u32[]{:S(2)}, u32[]{:S(2)}) collective-permute-start(bf16[144,1408]{1,0:T(8,128)(2,1)S(1)} %own.3._.refs_0_), channel_id=1, source_target_pairs={{0,1},{2,3},{4,5},{6,7},{8,9},{10,11},{12,13},{14,15},{16,17},{18,... | collective-permute-start | bytes 1216520 | tf_op jit(solution)/shard_map/ppermute | solution.py:32
  17.3 1.7 %collective-permute-done.1.received_ref = bf16[256,1152]{1,0:T(8,128)(2,1)S(1)} collective-permute-done((bf16[256,1152]{1,0:T(8,128)(2,1)S(1)}, bf16[256,1152]{1,0:T(8,128)(2,1)S(1)}, u32[]{:S(2)}, u32[]{:S(2)}) %collective-permute-start.1) | collective-permute-done | bytes 589856 | tf_op jit(solution)/shard_map/ppermute | solution.py:32
  19.0 1.3 %collective-permute-start.7 = (bf16[128,1152]{1,0:T(8,128)(2,1)S(1)}, bf16[128,1152]{1,0:T(8,128)(2,1)S(1)}, u32[]{:S(2)}, u32[]{:S(2)}) collective-permute-start(bf16[128,1152]{1,0:T(8,128)(2,1)S(1)} %get-tuple-element.18.refs_5_.refs_3_), channel_id=1, source_target_pairs={{0,4},{1,5},{4,8},{5,9},{8,12},{9,13},{12,16},{13,17},{16,20},{17,... | collective-permute-start | bytes 884744 | tf_op jit(solution)/shard_map/ppermute | solution.py:28
  20.3 0.0 collective-permute-done.refs_1_
  20.3 1.3 %own.4.refs_5_.own_ref = bf16[128,1024]{1,0:T(8,128)(2,1)S(1)} custom-call(f32[256,128]{1,0:T(8,128)S(1)} %get-tuple-element.15.refs_0_.lines_ref.refs_2_, bf16[128,1536]{1,0:T(8,128)(2,1)S(1)} %collective-permute-done.refs_1_, bf16[128,1536]{1,0:T(8,128)(2,1)S(1)} %get-tuple-element.14._.refs_2_, bf16[1,128,4096]{2,1,0:T(8,128)(2,1)S(1)} %copy-done, ...), custom_call_target="tpu_custom_call" | custom-call | flops 20000000000 | bytes 1024 | tf_op jit(solution)/shard_map/own/pallas_call | solution.py:242
  21.7 3.1 %collective-permute-start.5 = (bf16[128,1024]{1,0:T(8,128)(2,1)S(1)}, bf16[128,1024]{1,0:T(8,128)(2,1)S(1)}, u32[]{:S(2)}, u32[]{:S(2)}) collective-permute-start(bf16[128,1024]{1,0:T(8,128)(2,1)S(1)} %own.4.refs_5_.own_ref), channel_id=1, source_target_pairs={{0,1},{2,3},{4,5},{6,7},{8,9},{10,11},{12,13},{14,15},{16,17},{18,... | collective-permute-start | bytes 786440 | tf_op jit(solution)/shard_map/ppermute | solution.py:32
  24.8 0.8 %own.5._.own_ref = bf16[128,512]{1,0:T(8,128)(2,1)S(1)} custom-call(f32[256,128]{1,0:T(8,128)S(1)} %get-tuple-element.15.refs_0_.lines_ref.refs_2_, bf16[128,1536]{1,0:T(8,128)(2,1)S(1)} %collective-permute-done.refs_1_, bf16[128,1536]{1,0:T(8,128)(2,1)S(1)} %get-tuple-element.14._.refs_2_, bf16[1,128,4096]{2,1,0:T(8,128)(2,1)S(1)} %copy-done, ...), custom_call_target="tpu_custom_call" | custom-call | flops 20000000000 | bytes 1024 | tf_op jit(solution)/shard_map/own/pallas_call | solution.py:242
  25.5 1.3 %collective-permute-start.3 = (bf16[128,512]{1,0:T(8,128)(2,1)S(1)}, bf16[128,512]{1,0:T(8,128)(2,1)S(1)}, u32[]{:S(2)}, u32[]{:S(2)}) collective-permute-start(bf16[128,512]{1,0:T(8,128)(2,1)S(1)} %own.5._.own_ref), channel_id=1, source_target_pairs={{0,1},{2,3},{4,5},{6,7},{8,9},{10,11},{12,13},{14,15},{16,17},{18,... | collective-permute-start | bytes 393224 | tf_op jit(solution)/shard_map/ppermute | solution.py:32
  26.9 0.0 collective-permute-done.4.behind_ref.refs_3_.refs_5_
  26.9 0.1 collective-permute-done.6.refs_1_
  27.0 0.7 %chunk.1.refs_9_ = bf16[1,128,4096]{2,1,0:T(8,128)(2,1)} custom-call(bf16[144,1408]{1,0:T(8,128)(2,1)S(1)} %own.3._.refs_0_, bf16[144,1408]{1,0:T(8,128)(2,1)S(1)} %collective-permute-done.6.refs_1_, f32[256,128]{1,0:T(8,128)S(1)} %get-tuple-element.15.refs_0_.lines_ref.refs_2_, bf16[128,4096]{1,0:T(8,128)(2,1)S(1)} %collective-permute-done.4.behind_ref.refs_3_.refs_5_, ...), custom_call_target="tpu_custom_call" | custom-call | flops 20000000000 | bytes 1024 | tf_op jit(solution)/shard_map/chunk/pallas_call | solution.py:330
  27.8 0.0 collective-permute-done.7.refs_2_
  27.8 2.2 %raw.1._ = bf16[1,128,4096]{2,1,0:T(8,128)(2,1)} custom-call(f32[256,128]{1,0:T(8,128)S(1)} %get-tuple-element.15.refs_0_.lines_ref.refs_2_, bf16[144,1408]{1,0:T(8,128)(2,1)S(1)} %collective-permute-done.6.refs_1_, bf16[128,1152]{1,0:T(8,128)(2,1)S(1)} %collective-permute-done.7.refs_2_, ...), custom_call_target="tpu_custom_call", output_to_operand_aliasing={{}: (9, {})} | custom-call | flops 20000000000 | bytes 1024 | tf_op jit(solution)/shard_map/raw/pallas_call | solution.py:381
  30.0 2.5 %collective-permute-done.5.received_ref = bf16[128,1024]{1,0:T(8,128)(2,1)S(1)} collective-permute-done((bf16[128,1024]{1,0:T(8,128)(2,1)S(1)}, bf16[128,1024]{1,0:T(8,128)(2,1)S(1)}, u32[]{:S(2)}, u32[]{:S(2)}) %collective-permute-start.5) | collective-permute-done | bytes 262176 | tf_op jit(solution)/shard_map/ppermute | solution.py:32
  32.5 0.7 %last.2._ = bf16[1,128,4096]{2,1,0:T(8,128)(2,1)} custom-call(bf16[128,1024]{1,0:T(8,128)(2,1)S(1)} %own.4.refs_5_.own_ref, bf16[128,1024]{1,0:T(8,128)(2,1)S(1)} %collective-permute-done.5.received_ref, f32[128,1536]{1,0:T(8,128)S(1)} %later.1.refs_6_.gated_ref, bf16[1,128,4096]{2,1,0:T(8,128)(2,1)} %raw.1._), custom_call_target="tpu_custom_call", output_to_operand_aliasing={{}: (3, {})} | custom-call | flops 20000000000 | bytes 1024 | tf_op jit(solution)/shard_map/last/pallas_call | solution.py:413
  33.2 2.1 %collective-permute-done.3.received_ref = bf16[128,512]{1,0:T(8,128)(2,1)S(1)} collective-permute-done((bf16[128,512]{1,0:T(8,128)(2,1)S(1)}, bf16[128,512]{1,0:T(8,128)(2,1)S(1)}, u32[]{:S(2)}, u32[]{:S(2)}) %collective-permute-start.3) | collective-permute-done | bytes 131104 | tf_op jit(solution)/shard_map/ppermute | solution.py:32
  35.3 0.7 %last.3 = bf16[1,128,4096]{2,1,0:T(8,128)(2,1)} custom-call(bf16[128,512]{1,0:T(8,128)(2,1)S(1)} %own.5._.own_ref, bf16[128,512]{1,0:T(8,128)(2,1)S(1)} %collective-permute-done.3.received_ref, f32[128,1536]{1,0:T(8,128)S(1)} %later.1.refs_6_.gated_ref, bf16[1,128,4096]{2,1,0:T(8,128)(2,1)} %last.2._), custom_call_target="tpu_custom_call", output_to_operand_aliasing={{}: (3, {})} | custom-call | flops 20000000000 | bytes 1024 | tf_op jit(solution)/shard_map/last/pallas_call | solution.py:413
  (2 shorter events, 0.1 us)
Async XLA Ops:
  2.2 11.3 %copy-start.2 = (bf16[1,256,128]{2,1,0:T(8,128)(2,1)S(1)}, bf16[1,256,128]{2,1,0:T(8,128)(2,1)}, u32[]{:S(2)}) copy-start(bf16[1,256,128]{2,1,0:T(8,128)(2,1)} %bank_ref.1) | copy-start | bytes 196612
  2.2 11.3 %copy-start.3 = (f32[1,256]{1,0:T(1,128)S(1)}, f32[1,256]{1,0:T(1,128)}, u32[]{:S(2)}) copy-start(f32[1,256]{1,0:T(1,128)} %scales_ref.1) | copy-start | bytes 3076
  2.2 11.3 %copy-start.4 = (s32[1,256]{1,0:T(1,128)S(1)}, s32[1,256]{1,0:T(1,128)}, u32[]{:S(2)}) copy-start(s32[1,256]{1,0:T(1,128)} %assign_ref.1) | copy-start | bytes 3076
  2.2 16.7 %collective-permute-start.1 = (bf16[256,1152]{1,0:T(8,128)(2,1)S(1)}, bf16[256,1152]{1,0:T(8,128)(2,1)S(1)}, u32[]{:S(2)}, u32[]{:S(2)}) collective-permute-start(bf16[256,1152]{1,0:T(8,128)(2,1)S(1)} %get-tuple-element.16.raw_ref), channel_id=1, source_target_pairs={{0,1},{2,3},{4,5},{6,7},{8,9},{10,11},{12,13},{14,15},{16,17},{18,... | collective-permute-start | bytes 1769480 | tf_op jit(solution)/shard_map/ppermute | solution.py:32
  5.8 8.5 %copy-start = (bf16[1,128,4096]{2,1,0:T(8,128)(2,1)S(1)}, bf16[1,128,4096]{2,1,0:T(8,128)(2,1)}, u32[]{:S(2)}) copy-start(bf16[1,128,4096]{2,1,0:T(8,128)(2,1)} %refs_7_.1) | copy-start | bytes 3145732
  5.8 8.5 %copy-start.1 = (bf16[128,4096]{1,0:T(8,128)(2,1)S(1)}, bf16[128,4096]{1,0:T(8,128)(2,1)}, u32[]{:S(2)}) copy-start(bf16[128,4096]{1,0:T(8,128)(2,1)} %refs_8_.1) | copy-start | bytes 3145732
  5.8 8.4 %collective-permute-start.2 = (bf16[128,1408]{1,0:T(8,128)(2,1)S(1)}, bf16[128,1408]{1,0:T(8,128)(2,1)S(1)}, u32[]{:S(2)}, u32[]{:S(2)}) collective-permute-start(bf16[128,1408]{1,0:T(8,128)(2,1)S(1)} %get-tuple-element.13._.refs_2_), channel_id=1, source_target_pairs={{0,4},{4,8},{8,12},{12,16},{16,20},{20,24},{24,28},{2,6},{6,10},{1... | collective-permute-start | bytes 1081352 | tf_op jit(solution)/shard_map/ppermute | solution.py:28
  8.8 11.6 %collective-permute-start = (bf16[128,1536]{1,0:T(8,128)(2,1)S(1)}, bf16[128,1536]{1,0:T(8,128)(2,1)S(1)}, u32[]{:S(2)}, u32[]{:S(2)}) collective-permute-start(bf16[128,1536]{1,0:T(8,128)(2,1)S(1)} %get-tuple-element.14._.refs_2_), channel_id=1, source_target_pairs={{0,4},{4,8},{8,12},{12,16},{16,20},{20,24},{24,28},{2,6},{6,10},{1... | collective-permute-start | bytes 1179656 | tf_op jit(solution)/shard_map/ppermute | solution.py:28
  12.8 14.0 %collective-permute-start.4 = (bf16[128,4096]{1,0:T(8,128)(2,1)S(1)}, bf16[128,4096]{1,0:T(8,128)(2,1)S(1)}, u32[]{:S(2)}, u32[]{:S(2)}) collective-permute-start(bf16[128,4096]{1,0:T(8,128)(2,1)S(1)} %get-tuple-element.19.product_ref.refs_4_.refs_6_), channel_id=1, source_target_pairs={{1,5},{5,9},{9,13},{13,17},{17,21},{21,25},{25,29},{3,7},{7,11},{1... | collective-permute-start | bytes 3145736 | tf_op jit(solution)/shard_map/ppermute | solution.py:28
  16.0 11.1 %collective-permute-start.6 = (bf16[144,1408]{1,0:T(8,128)(2,1)S(1)}, bf16[144,1408]{1,0:T(8,128)(2,1)S(1)}, u32[]{:S(2)}, u32[]{:S(2)}) collective-permute-start(bf16[144,1408]{1,0:T(8,128)(2,1)S(1)} %own.3._.refs_0_), channel_id=1, source_target_pairs={{0,1},{2,3},{4,5},{6,7},{8,9},{10,11},{12,13},{14,15},{16,17},{18,... | collective-permute-start | bytes 1216520 | tf_op jit(solution)/shard_map/ppermute | solution.py:32
  19.0 8.8 %collective-permute-start.7 = (bf16[128,1152]{1,0:T(8,128)(2,1)S(1)}, bf16[128,1152]{1,0:T(8,128)(2,1)S(1)}, u32[]{:S(2)}, u32[]{:S(2)}) collective-permute-start(bf16[128,1152]{1,0:T(8,128)(2,1)S(1)} %get-tuple-element.18.refs_5_.refs_3_), channel_id=1, source_target_pairs={{0,4},{1,5},{4,8},{5,9},{8,12},{9,13},{12,16},{13,17},{16,20},{17,... | collective-permute-start | bytes 884744 | tf_op jit(solution)/shard_map/ppermute | solution.py:28
  21.7 10.8 %collective-permute-start.5 = (bf16[128,1024]{1,0:T(8,128)(2,1)S(1)}, bf16[128,1024]{1,0:T(8,128)(2,1)S(1)}, u32[]{:S(2)}, u32[]{:S(2)}) collective-permute-start(bf16[128,1024]{1,0:T(8,128)(2,1)S(1)} %own.4.refs_5_.own_ref), channel_id=1, source_target_pairs={{0,1},{2,3},{4,5},{6,7},{8,9},{10,11},{12,13},{14,15},{16,17},{18,... | collective-permute-start | bytes 786440 | tf_op jit(solution)/shard_map/ppermute | solution.py:32
  25.5 9.7 %collective-permute-start.3 = (bf16[128,512]{1,0:T(8,128)(2,1)S(1)}, bf16[128,512]{1,0:T(8,128)(2,1)S(1)}, u32[]{:S(2)}, u32[]{:S(2)}) collective-permute-start(bf16[128,512]{1,0:T(8,128)(2,1)S(1)} %own.5._.own_ref), channel_id=1, source_target_pairs={{0,1},{2,3},{4,5},{6,7},{8,9},{10,11},{12,13},{14,15},{16,17},{18,... | collective-permute-start | bytes 393224 | tf_op jit(solution)/shard_map/ppermute | solution.py:32

commit v4 on v3

v4 whole, which is shorter than its diff:
```python
import functools

import jax
import jax.numpy as jnp
from jax import lax
from jax.experimental import pallas as pl
from jax.experimental.pallas import tpu as pltpu
from jax.sharding import PartitionSpec as P

LANES = 128
ROW_BLOCK = 32
RAW = 896
CHUNKS = (896, 768, 1024, 512)
EXTRA = 8
F32 = jnp.float32
BF16 = jnp.bfloat16
MIB = 1024 * 1024
QUICK, SLOW = 1024, 20_000_000_000

SMEM = pl.BlockSpec(memory_space=pltpu.SMEM)
VMEM = pl.BlockSpec(memory_space=pltpu.VMEM)
ANY = pl.BlockSpec(memory_space=pl.ANY)
HBM = pl.BlockSpec(memory_space=pltpu.HBM)


def to_next_slab(value, pipes):
    slabs, depth = lax.axis_size("ctx"), lax.axis_size("pipe")
    pairs = [(slab * depth + pipe, (slab + 1) * depth + pipe) for slab in range(slabs - 1) for pipe in pipes]
    return lax.ppermute(value, ("ctx", "pipe"), pairs)


def to_next_section(value):
    return lax.ppermute(value, "pipe", [(0, 1)])


def call(kernel, name, out_shape, in_specs, out_specs, scratch=(), weight=QUICK, aliases=None):
    return pl.pallas_call(
        kernel,
        out_shape=out_shape,
        in_specs=in_specs,
        out_specs=out_specs,
        scratch_shapes=list(scratch),
        input_output_aliases=aliases or {},
        compiler_params=pltpu.CompilerParams(vmem_limit_bytes=16 * MIB),
        cost_estimate=pl.CostEstimate(flops=weight, bytes_accessed=1024, transcendentals=0),
        name=name,
    )


def is_first():
    return lax.axis_index("pipe") == 0


def array(rows, cols, kind=BF16):
    return jax.ShapeDtypeStruct((rows, cols), kind)


def multiply(keys_ref, values_ref, keys_in, values_in, sems, first, targets):
    rows = keys_in.shape[0]
    pieces, offset = [], 0
    for piece, (out_ref, row, col, width) in enumerate(targets):
        at = pl.ds(offset, width)
        source = pl.ds(first + offset, width)
        copies = (
            pltpu.make_async_copy(keys_ref.at[0, :, source], keys_in.at[:, at], sems.at[2 * piece]),
            pltpu.make_async_copy(values_ref.at[0, :, source], values_in.at[:, at], sems.at[2 * piece + 1]),
        )
        for copy in copies:
            copy.start()
        pieces.append(copies)
        offset += width
    offset = 0
    for copies, (out_ref, row, col, width) in zip(pieces, targets):
        for copy in copies:
            copy.wait()
        for tile in range(0, width, LANES):
            at = slice(offset + tile, offset + tile + LANES)
            product = keys_in[:, at].astype(F32) * values_in[:, at].astype(F32)
            out_ref[row : row + rows, col + tile : col + tile + LANES] = product.astype(BF16)
        offset += width


def lead_kernel(queries_ref, keys_ref, values_ref, raw_ref, near_ref, rest_ref, keys_in, values_in, sems, sem):
    rows, width = near_ref.shape

    @pl.when(is_first())
    def _():
        copy = pltpu.make_async_copy(queries_ref.at[0, :, pl.ds(0, RAW)], raw_ref.at[pl.ds(0, rows)], sem)
        copy.start()
        targets = [(raw_ref, rows, 0, RAW), (near_ref, 0, 0, width), (rest_ref, 0, 0, rest_ref.shape[1])]
        multiply(keys_ref, values_ref, keys_in, values_in, sems, 0, targets)
        copy.wait()


def product_scratch(rows, total, pieces):
    return [pltpu.VMEM((rows, total), BF16), pltpu.VMEM((rows, total), BF16), pltpu.SemaphoreType.DMA((2 * pieces,))]


def lead_of(queries, keys, values):
    rows, total = queries.shape[1:]
    return call(
        lead_kernel,
        "lead",
        (array(2 * rows, RAW), array(rows, CHUNKS[0]), array(rows, total - RAW - CHUNKS[0])),
        [HBM] * 3,
        (VMEM,) * 3,
        product_scratch(rows, total, 3) + [pltpu.SemaphoreType.DMA(())],
    )(queries, keys, values)


def product_kernel(keys_ref, values_ref, _, out_ref, keys_in, values_in, sems):
    half = out_ref.shape[1] // 2

    @pl.when(jnp.logical_not(is_first()))
    def _():
        targets = [(out_ref, 0, 0, half), (out_ref, 0, half, half)]
        multiply(keys_ref, values_ref, keys_in, values_in, sems, 0, targets)


def product_of(keys, values, after):
    rows, total = keys.shape[1:]
    return call(
        product_kernel, "product", array(rows, total), [HBM, HBM, ANY], VMEM, product_scratch(rows, total, 2)
    )(keys, values, after)


def turn_table(lines_ref, row, count, table_ref, at):
    taps = lines_ref.shape[1]
    upper = lax.broadcasted_iota(jnp.int32, (ROW_BLOCK, taps), 1) > lax.broadcasted_iota(
        jnp.int32, (ROW_BLOCK, taps), 0
    )
    for group in range(count):
        line = lines_ref[row + group : row + group + 1, :]
        turned = pltpu.roll(jnp.broadcast_to(line, (ROW_BLOCK, taps)), 1, 1, stride=1, stride_axis=0)
        span = slice(at + group * ROW_BLOCK, at + (group + 1) * ROW_BLOCK)
        table_ref[span, :taps] = jnp.where(upper, turned, 0.0).astype(BF16)
        table_ref[span, taps:] = jnp.where(upper, 0.0, turned)[:, :ROW_BLOCK].astype(BF16)


def taps_kernel(share, bank_ref, scales_ref, assign_ref, _, lines_ref, table_ref):
    groups, taps = lines_ref.shape
    size = bank_ref.shape[1]
    chosen = (lax.broadcasted_iota(jnp.int32, (size, groups), 0) == assign_ref[...]).astype(F32).astype(BF16)
    contract = (((0,), (0,)), ((), ()))
    picked = lax.dot_general(bank_ref[0], chosen, contract, preferred_element_type=F32)
    scaled = (picked * scales_ref[...]).astype(BF16)
    order = lax.broadcasted_iota(jnp.int32, (taps, taps), 0) + lax.broadcasted_iota(jnp.int32, (taps, taps), 1)
    flip = (order == taps - 1).astype(F32).astype(BF16)
    lines_ref[...] = lax.dot_general(scaled, flip, contract, preferred_element_type=F32)

    @pl.when(is_first())
    def _():
        for tile in range(CHUNKS[0] // LANES):
            turn_table(lines_ref, (RAW // LANES + tile) * share, share, table_ref, tile * share * ROW_BLOCK)


def taps_of(bank, scales, assign, total, after):
    groups, taps = assign.shape[1], bank.shape[2]
    share = LANES * groups // total
    return call(
        functools.partial(taps_kernel, share),
        "taps",
        (array(groups, taps, F32), array(CHUNKS[0] // LANES * share * ROW_BLOCK, taps + ROW_BLOCK)),
        [VMEM] * 3 + [ANY],
        (VMEM, VMEM),
    )(bank, scales, assign, after)


def mix(table_ref, row, share, window, store):
    depth = table_ref.shape[1]
    rows = window.shape[0] - depth + ROW_BLOCK
    member = lax.broadcasted_iota(jnp.int32, (ROW_BLOCK, LANES), 1) // (LANES // share)
    table = table_ref[row : row + share * ROW_BLOCK, :]
    for first in range(0, rows, ROW_BLOCK):
        sums = jnp.dot(table, window[first : first + depth], preferred_element_type=F32)
        mixed = sums[:ROW_BLOCK]
        for group in range(1, share):
            mixed = jnp.where(member == group, sums[group * ROW_BLOCK : (group + 1) * ROW_BLOCK], mixed)
        store(slice(first, first + ROW_BLOCK), mixed)


def mix_all(width, share, lines_ref, line, table_ref, made, start_ref, behind_ref, product_ref, local, store):
    rows = product_ref.shape[0]
    first = (lax.axis_index("ctx") - 1) * rows
    inside = first + lax.broadcasted_iota(jnp.int32, (2 * rows, LANES), 0) >= start_ref[0]
    for tile in range(width // LANES):
        at = slice(tile * LANES, (tile + 1) * LANES)
        inner = slice(local + at.start, local + at.stop)
        row = tile * share * ROW_BLOCK
        if not made:
            turn_table(lines_ref, line + tile * share, share, table_ref, row)
        window = jnp.concatenate([behind_ref[:, inner], product_ref[:, inner]], axis=0)
        window = jnp.where(inside, window, jnp.zeros_like(window))
        mix(table_ref, row, share, window, functools.partial(store, at))


def share_of(lines_ref, total):
    return LANES * lines_ref.shape[0] // total


def own_kernel(first, local, made, *refs):
    start_ref, lines_ref, behind_ref, product_ref, queries_ref, residual_ref, table_ref, out_ref = refs[:8]
    if not made:
        table_ref = refs[-1]
    width = out_ref.shape[1]
    rows, total = residual_ref.shape
    share = share_of(lines_ref, total)

    @pl.when(is_first())
    def _():
        def store(at, span, mixed):
            cols = slice(first + at.start, first + at.stop)
            gated = queries_ref[0, span, cols].astype(F32) * mixed
            out_ref[span, at] = (residual_ref[span, cols].astype(F32) + gated).astype(BF16)

        line = first // LANES * share
        mix_all(width, share, lines_ref, line, table_ref, made, start_ref, behind_ref, product_ref, local, store)
        if made:
            for part in range(-(-(RAW // LANES * share) // EXTRA)):
                taken = lines_ref[part * EXTRA : (part + 1) * EXTRA, :].astype(BF16)
                out_ref[rows:, part * LANES : (part + 1) * LANES] = taken


def table_scratch(lines, width, total):
    groups, taps = lines.shape
    return pltpu.VMEM((width * groups // total * ROW_BLOCK, taps + ROW_BLOCK), BF16)


def own_of(start, lines, behind, product, queries, residual, first, local, width, made, after):
    rows, total = residual.shape
    return call(
        functools.partial(own_kernel, first, local, made),
        "own",
        array(rows + EXTRA if made else rows, width),
        [SMEM] + [VMEM] * 5 + [VMEM if made else ANY],
        VMEM,
        [] if made else [table_scratch(lines, width, total)],
        weight=QUICK if made else SLOW,
    )(start, lines, behind, product, queries, residual, after)


def pick_kernel(raw_ref, received_ref, _, queries_ref, product_ref):
    rows = queries_ref.shape[0]

    def take(source):
        queries_ref[...] = source[:rows, :]
        product_ref[...] = source[rows:, :]

    pl.when(is_first())(lambda: take(raw_ref))
    pl.when(jnp.logical_not(is_first()))(lambda: take(received_ref))


def pick_of(raw, received, after):
    rows, width = raw.shape[0] // 2, raw.shape[1]
    return call(
        pick_kernel, "pick", (array(rows, width),) * 2, [VMEM, VMEM, ANY], (VMEM, VMEM), weight=SLOW
    )(raw, received, after)


def hold_kernel(value_ref, _, out_ref):
    pass


def held_back(value, after):
    return call(hold_kernel, "hold", array(*value.shape), [ANY, ANY], ANY, aliases={0: 0})(value, after)


def later_kernel(start_ref, lines_ref, behind_ref, product_ref, queries_ref, _, out_ref, table_ref):
    total = queries_ref.shape[2]
    share = share_of(lines_ref, total)

    @pl.when(jnp.logical_not(is_first()))
    def _():
        def store(at, span, mixed):
            out_ref[span, at] = queries_ref[0, span, at].astype(F32) * mixed

        mix_all(total, share, lines_ref, 0, table_ref, False, start_ref, behind_ref, product_ref, 0, store)


def later_of(start, lines, behind, product, queries, after):
    rows, total = product.shape
    return call(
        later_kernel,
        "later",
        array(rows, total, F32),
        [SMEM] + [VMEM] * 4 + [ANY],
        VMEM,
        [table_scratch(lines, total, total)],
        weight=SLOW,
    )(start, lines, behind, product, queries, after)


def send_out(buffer, out_ref, first, sem):
    copy = pltpu.make_async_copy(buffer, out_ref.at[0, :, pl.ds(first, buffer.shape[1])], sem)
    copy.start()
    copy.wait()


def raw_kernel(*refs):
    start_ref, lines_ref, received_ref, behind_ref, product_ref, queries_ref, gated_ref, residual_ref, _ = refs[:9]
    out_ref, chosen_ref, table_ref, buffer, sem = refs[9:]
    rows, width = buffer.shape
    share = share_of(lines_ref, residual_ref.shape[1])
    count = chosen_ref.shape[0]

    @pl.when(is_first())
    def _():
        chosen_ref[...] = lines_ref[:count, :]

    @pl.when(jnp.logical_not(is_first()))
    def _():
        for part in range(-(-count // EXTRA)):
            span = slice(part * EXTRA, min((part + 1) * EXTRA, count))
            taken = received_ref[rows:, part * LANES : (part + 1) * LANES].astype(F32)
            chosen_ref[span, :] = taken[: span.stop - span.start]

    def store(at, span, mixed):
        gated = queries_ref[span, at].astype(F32) * mixed
        buffer[span, at] = (residual_ref[span, at].astype(F32) + gated).astype(BF16)

    mix_all(width, share, chosen_ref, 0, table_ref, False, start_ref, behind_ref, product_ref, 0, store)

    @pl.when(jnp.logical_not(is_first()))
    def _():
        buffer[...] = (buffer[...].astype(F32) + gated_ref[:, :width]).astype(BF16)

    send_out(buffer, out_ref, 0, sem)


def raw_finish(held, start, lines, received, behind, product, queries, gated, residual):
    rows, total = residual.shape
    groups, taps = lines.shape
    return call(
        raw_kernel,
        "raw",
        jax.ShapeDtypeStruct(held.shape, BF16),
        [SMEM] + [VMEM] * 7 + [ANY],
        ANY,
        [
            pltpu.VMEM((RAW * groups // total, taps), F32),
            table_scratch(lines, RAW, total),
            pltpu.VMEM((rows, RAW), BF16),
            pltpu.SemaphoreType.DMA(()),
        ],
        weight=SLOW,
        aliases={8: 0},
    )(start, lines, received, behind, product, queries, gated, residual, held)


def chunk_kernel(first, own_ref, received_ref, gated_ref, *refs):
    out_ref, buffer, sem = refs[-3:]
    rows, width = buffer.shape

    @pl.when(is_first())
    def _():
        send_out(own_ref.at[pl.ds(0, rows)], out_ref, first, sem)

    @pl.when(jnp.logical_not(is_first()))
    def _():
        total = received_ref[:rows, :].astype(F32) + gated_ref[:, first : first + width]
        buffer[...] = total.astype(BF16)
        send_out(buffer, out_ref, first, sem)


def chunk_finish(held, own, received, gated, first):
    rows, total = gated.shape
    width = own.shape[1]
    return call(
        functools.partial(chunk_kernel, first),
        "chunk",
        jax.ShapeDtypeStruct((1, rows, total), BF16),
        [VMEM] * 3 + ([] if held is None else [ANY]),
        ANY,
        [pltpu.VMEM((rows, width), BF16), pltpu.SemaphoreType.DMA(())],
        weight=SLOW,
        aliases={} if held is None else {3: 0},
    )(own, received, gated, *([] if held is None else [held]))


def body(queries, keys, values, residual, filter_bank, filter_scales, group_filter, context_start):
    total = queries.shape[2]
    far_queries, keys, values = (
        pltpu.with_memory_space_constraint(value, pltpu.HBM) for value in (queries, keys, values)
    )
    raw, near, rest = lead_of(far_queries, keys, values)
    raw_received = to_next_section(raw)
    near_behind = to_next_slab(near, (0,))
    product = product_of(keys, values, near)
    rest_behind = to_next_slab(rest, (0,))
    behind = to_next_slab(product, (1,))
    lines, table = taps_of(filter_bank, filter_scales, group_filter, total, product)
    own = [own_of(context_start, lines, near_behind, near, queries, residual, RAW, 0, CHUNKS[0], True, table)]
    received = [to_next_section(own[0])]
    raw_queries, raw_product = pick_of(raw, raw_received, own[0])
    second = RAW + CHUNKS[0]
    first, after = second, raw_queries
    for chunk, width in enumerate(CHUNKS[1:], 1):
        if chunk == len(CHUNKS) - 1:
            raw_product = held_back(raw_product, after)
            raw_behind = to_next_slab(raw_product, (0, 1))
            after = raw_product
        after = own_of(
            context_start, lines, rest_behind, rest, queries, residual, first, first - second, width, False, after
        )
        own.append(after)
        received.append(to_next_section(after))
        first += width
    gated = later_of(context_start, lines, behind, product, queries, after)
    held, first = None, RAW
    for chunk, width in enumerate(CHUNKS):
        held = chunk_finish(held, own[chunk], received[chunk], gated, first)
        first += width
        if chunk == 0:
            held = raw_finish(
                held, context_start, lines, received[0], raw_behind, raw_product, raw_queries, gated, residual
            )
    return held


def solution(mesh):
    return jax.shard_map(
        body,
        mesh=mesh,
        in_specs=(
            P("pipe", ("dp", "ctx"), None),
            P("pipe", ("dp", "ctx"), None),
            P("pipe", ("dp", "ctx"), None),
            P(("dp", "ctx"), None),
            P("pipe", None, None),
            P("pipe", None),
            P("pipe", None),
            P("dp"),
        ),
        out_specs=P("pipe", ("dp", "ctx"), None),
        check_vma=False,
    )
```

time: 36.3 us -> 34.6 us (0.953)
  waiting for transfers between devices: 6.39 us -> 2.5 us
  starting transfers between devices: 17 us -> 19.2 us
    ppermute x4 -> x5, waiting for transfers between devices: 6.38 us -> 2.49 us  [to_next_section(): return lax.ppermute(value, 'pipe', [(0, 1)])]
    pallas_call x6 -> x5, Pallas kernels: 6.42 us -> 3.9 us  [the longest x1 1.95 us: lead_of(): call(lead_kernel, 'lead', (array(2 * rows, RAW), array(rows, CHUNKS[0]),...]
    pallas_call x1 -> x4, Pallas kernels: 0.74 us -> 2.77 us  [chunk_finish(): call(functools.partial(chunk_kernel, first), 'chunk', jax.ShapeDtypeStruc...]
    ppermute x4, starting transfers between devices: 7.7 us -> 9.34 us  [to_next_slab(): return lax.ppermute(value, ('ctx', 'pipe'), pairs)]
    ppermute x4 -> x5, starting transfers between devices: 9.27 us -> 9.87 us  [to_next_section(): return lax.ppermute(value, 'pipe', [(0, 1)])]
    pallas_call x3 -> x4, Pallas kernels: 3.73 us -> 4.24 us  [own_of(): call(functools.partial(own_kernel, first, local, made), 'own', array(rows...]
  transfers between devices with their start and end apart: 8 -> 9, of which waited for: 4 -> 2; matrix products, arithmetic and copies ran while one was open for 0% -> 0% of each run, Pallas kernels for 26% -> 26%
where the time goes in v4:
time: 34.6 us; the launch traced here: 34.3 us
  starting transfers between devices  19.2 us (55%)
  Pallas kernels  11.6 us (34%)
  waiting for transfers between devices  2.5 us (7%)
  between operations  0.97 us (3%)
    ppermute x5, starting transfers between devices, to_next_section(): return lax.ppermute(value, 'pipe', [(0, 1)])  9.87 us
    ppermute x4, starting transfers between devices, to_next_slab(): return lax.ppermute(value, ('ctx', 'pipe'), pairs)  9.34 us
    pallas_call x4, Pallas kernels, own_of(): call(functools.partial(own_kernel, first, local, made), 'own', array(rows...  4.24 us
    pallas_call x4, Pallas kernels, chunk_finish(): call(functools.partial(chunk_kernel, first), 'chunk', jax.ShapeDtypeStruc...  2.77 us
    ppermute x5, waiting for transfers between devices, to_next_section(): return lax.ppermute(value, 'pipe', [(0, 1)])  2.49 us
    pallas_call x1, Pallas kernels, lead_of(): call(lead_kernel, 'lead', (array(2 * rows, RAW), array(rows, CHUNKS[0]),...  1.95 us
    pallas_call x1, Pallas kernels, raw_finish(): call(raw_kernel, 'raw', jax.ShapeDtypeStruct(held.shape, BF16), [SMEM] +...  1.89 us
  transfers between devices with their start and end apart: 9, of which 2 were waited for; matrix products, arithmetic and copies ran while one was open for 0% of the time, Pallas kernels for 26%

profile of v4, /device:TPU:0, one launch (start us, length us, event | category | flops | bytes accessed | tf_op | source)
XLA Modules:
  0.0 34.3 jit_solution(7460631530418972942)
XLA Ops:
  0.0 2.0 %lead.1 = (bf16[256,896]{1,0:T(8,128)(2,1)S(1)}, bf16[128,896]{1,0:T(8,128)(2,1)S(1)}, bf16[128,2304]{1,0:T(8,128)(2,1)S(1)}) custom-call(bf16[1,128,4096]{2,1,0:T(8,128)(2,1)} %queries_ref.3, bf16[1,128,4096]{2,1,0:T(8,128)(2,1)} %keys_ref.3, bf16[1,128,4096]{2,1,0:T(8,128)(2,1)} %values_ref.3), custom_call_target="tpu_custom_call" | custom-call | flops 1024 | bytes 1024 | tf_op jit(solution)/shard_map/lead/pallas_call | solution.py:101
  2.0 0.0 copy-start.2
  2.0 0.0 copy-start.3
  2.0 0.0 copy-start.4
  2.0 3.1 %collective-permute-start.1 = (bf16[256,896]{1,0:T(8,128)(2,1)S(1)}, bf16[256,896]{1,0:T(8,128)(2,1)S(1)}, u32[]{:S(2)}, u32[]{:S(2)}) collective-permute-start(bf16[256,896]{1,0:T(8,128)(2,1)S(1)} %get-tuple-element.15.raw_ref), channel_id=1, source_target_pairs={{0,1},{2,3},{4,5},{6,7},{8,9},{10,11},{12,13},{14,15},{16,17},{18,... | collective-permute-start | bytes 1376264 | tf_op jit(solution)/shard_map/ppermute | solution.py:33
  5.1 1.5 %collective-permute-start.2 = (bf16[128,896]{1,0:T(8,128)(2,1)S(1)}, bf16[128,896]{1,0:T(8,128)(2,1)S(1)}, u32[]{:S(2)}, u32[]{:S(2)}) collective-permute-start(bf16[128,896]{1,0:T(8,128)(2,1)S(1)} %get-tuple-element.12._.refs_3_), channel_id=1, source_target_pairs={{0,4},{4,8},{8,12},{12,16},{16,20},{20,24},{24,28},{2,6},{6,10},{1... | collective-permute-start | bytes 688136 | tf_op jit(solution)/shard_map/ppermute | solution.py:29
  6.6 0.0 copy-start
  6.6 0.0 copy-start.1
  6.7 4.2 %collective-permute-start = (bf16[128,2304]{1,0:T(8,128)(2,1)S(1)}, bf16[128,2304]{1,0:T(8,128)(2,1)S(1)}, u32[]{:S(2)}, u32[]{:S(2)}) collective-permute-start(bf16[128,2304]{1,0:T(8,128)(2,1)S(1)} %get-tuple-element.14.refs_3_), channel_id=1, source_target_pairs={{0,4},{4,8},{8,12},{12,16},{16,20},{20,24},{24,28},{2,6},{6,10},{1... | collective-permute-start | bytes 1769480 | tf_op jit(solution)/shard_map/ppermute | solution.py:29
  10.9 0.1 product.1._.product_ref
  10.9 0.7 %collective-permute-start.4 = (bf16[128,4096]{1,0:T(8,128)(2,1)S(1)}, bf16[128,4096]{1,0:T(8,128)(2,1)S(1)}, u32[]{:S(2)}, u32[]{:S(2)}) collective-permute-start(bf16[128,4096]{1,0:T(8,128)(2,1)S(1)} %product.1._.product_ref), channel_id=1, source_target_pairs={{1,5},{5,9},{9,13},{13,17},{17,21},{21,25},{25,29},{3,7},{7,11},{1... | collective-permute-start | bytes 3145736 | tf_op jit(solution)/shard_map/ppermute | solution.py:29
  11.7 0.0 copy-done.2
  11.7 0.0 copy-done.3
  11.7 0.0 copy-done.4
  11.7 0.6 %taps.1 = (f32[256,128]{1,0:T(8,128)S(1)}, bf16[1792,160]{1,0:T(8,128)(2,1)S(1)}) custom-call(bf16[1,256,128]{2,1,0:T(8,128)(2,1)S(1)} %copy-done.2, f32[1,256]{1,0:T(1,128)S(1)} %copy-done.3, s32[1,256]{1,0:T(1,128)S(1)} %copy-done.4, bf16[128,4096]{1,0:T(8,128)(2,1)S(1)} %product.1._.product_ref), custom_call_target="tpu_custom_call" | custom-call | flops 1024 | bytes 1024 | tf_op jit(solution)/shard_map/taps/pallas_call | solution.py:160
  12.9 0.0 collective-permute-done.2.refs_2_
  12.9 0.0 copy-done
  12.9 0.0 copy-done.1
  13.0 1.1 %own.4._.own_ref = bf16[136,896]{1,0:T(8,128)(2,1)S(1)} custom-call(s32[1]{0:T(128)S(6)} %copy.19.refs_0_.start_ref, f32[256,128]{1,0:T(8,128)S(1)} %get-tuple-element.13.refs_1_.lines_ref, bf16[128,896]{1,0:T(8,128)(2,1)S(1)} %collective-permute-done.2.refs_2_, bf16[128,896]{1,0:T(8,128)(2,1)S(1)} %get-tuple-element.12._.refs_3_, ...), custom_call_target="tpu_custom_call" | custom-call | flops 1024 | bytes 1024 | tf_op jit(solution)/shard_map/own/pallas_call | solution.py:231
  14.1 1.3 %collective-permute-start.7 = (bf16[136,896]{1,0:T(8,128)(2,1)S(1)}, bf16[136,896]{1,0:T(8,128)(2,1)S(1)}, u32[]{:S(2)}, u32[]{:S(2)}) collective-permute-start(bf16[136,896]{1,0:T(8,128)(2,1)S(1)} %own.4._.own_ref), channel_id=1, source_target_pairs={{0,1},{2,3},{4,5},{6,7},{8,9},{10,11},{12,13},{14,15},{16,17},{18,... | collective-permute-start | bytes 731144 | tf_op jit(solution)/shard_map/ppermute | solution.py:33
  15.4 0.0 collective-permute-done.1.received_ref
  15.5 0.0 collective-permute-done.refs_2_
  15.5 1.0 %own.5.refs_6_.own_ref = bf16[128,768]{1,0:T(8,128)(2,1)S(1)} custom-call(s32[1]{0:T(128)S(6)} %copy.19.refs_0_.start_ref, f32[256,128]{1,0:T(8,128)S(1)} %get-tuple-element.13.refs_1_.lines_ref, bf16[128,2304]{1,0:T(8,128)(2,1)S(1)} %collective-permute-done.refs_2_, bf16[128,2304]{1,0:T(8,128)(2,1)S(1)} %get-tuple-element.14.refs_3_, ...), custom_call_target="tpu_custom_call" | custom-call | flops 20000000000 | bytes 1024 | tf_op jit(solution)/shard_map/own/pallas_call | solution.py:231
  16.5 2.8 %collective-permute-start.6 = (bf16[128,768]{1,0:T(8,128)(2,1)S(1)}, bf16[128,768]{1,0:T(8,128)(2,1)S(1)}, u32[]{:S(2)}, u32[]{:S(2)}) collective-permute-start(bf16[128,768]{1,0:T(8,128)(2,1)S(1)} %own.5.refs_6_.own_ref), channel_id=1, source_target_pairs={{0,1},{2,3},{4,5},{6,7},{8,9},{10,11},{12,13},{14,15},{16,17},{18,... | collective-permute-start | bytes 589832 | tf_op jit(solution)/shard_map/ppermute | solution.py:33
  19.4 1.3 %own.6._.own_ref = bf16[128,1024]{1,0:T(8,128)(2,1)S(1)} custom-call(s32[1]{0:T(128)S(6)} %copy.19.refs_0_.start_ref, f32[256,128]{1,0:T(8,128)S(1)} %get-tuple-element.13.refs_1_.lines_ref, bf16[128,2304]{1,0:T(8,128)(2,1)S(1)} %collective-permute-done.refs_2_, bf16[128,2304]{1,0:T(8,128)(2,1)S(1)} %get-tuple-element.14.refs_3_, ...), custom_call_target="tpu_custom_call" | custom-call | flops 20000000000 | bytes 1024 | tf_op jit(solution)/shard_map/own/pallas_call | solution.py:231
  20.7 1.3 %collective-permute-start.5 = (bf16[128,1024]{1,0:T(8,128)(2,1)S(1)}, bf16[128,1024]{1,0:T(8,128)(2,1)S(1)}, u32[]{:S(2)}, u32[]{:S(2)}) collective-permute-start(bf16[128,1024]{1,0:T(8,128)(2,1)S(1)} %own.6._.own_ref), channel_id=1, source_target_pairs={{0,1},{2,3},{4,5},{6,7},{8,9},{10,11},{12,13},{14,15},{16,17},{18,... | collective-permute-start | bytes 786440 | tf_op jit(solution)/shard_map/ppermute | solution.py:33
  22.0 2.9 %collective-permute-start.8 = (bf16[128,896]{1,0:T(8,128)(2,1)S(1)}, bf16[128,896]{1,0:T(8,128)(2,1)S(1)}, u32[]{:S(2)}, u32[]{:S(2)}) collective-permute-start(bf16[128,896]{1,0:T(8,128)(2,1)S(1)} %hold.1.refs_6_.refs_4_), channel_id=1, source_target_pairs={{0,4},{1,5},{4,8},{5,9},{8,12},{9,13},{12,16},{13,17},{16,20},{17,... | collective-permute-start | bytes 688136 | tf_op jit(solution)/shard_map/ppermute | solution.py:29
  25.0 0.8 %own.7._.own_ref = bf16[128,512]{1,0:T(8,128)(2,1)S(1)} custom-call(s32[1]{0:T(128)S(6)} %copy.19.refs_0_.start_ref, f32[256,128]{1,0:T(8,128)S(1)} %get-tuple-element.13.refs_1_.lines_ref, bf16[128,2304]{1,0:T(8,128)(2,1)S(1)} %collective-permute-done.refs_2_, bf16[128,2304]{1,0:T(8,128)(2,1)S(1)} %get-tuple-element.14.refs_3_, ...), custom_call_target="tpu_custom_call" | custom-call | flops 20000000000 | bytes 1024 | tf_op jit(solution)/shard_map/own/pallas_call | solution.py:231
  25.7 0.0 collective-permute-done.4.behind_ref
  25.7 1.3 %collective-permute-start.3 = (bf16[128,512]{1,0:T(8,128)(2,1)S(1)}, bf16[128,512]{1,0:T(8,128)(2,1)S(1)}, u32[]{:S(2)}, u32[]{:S(2)}) collective-permute-start(bf16[128,512]{1,0:T(8,128)(2,1)S(1)} %own.7._.own_ref), channel_id=1, source_target_pairs={{0,1},{2,3},{4,5},{6,7},{8,9},{10,11},{12,13},{14,15},{16,17},{18,... | collective-permute-start | bytes 393224 | tf_op jit(solution)/shard_map/ppermute | solution.py:33
  27.1 0.0 collective-permute-done.7.received_ref.refs_2_
  27.1 0.7 %chunk.4.refs_8_ = bf16[1,128,4096]{2,1,0:T(8,128)(2,1)} custom-call(bf16[136,896]{1,0:T(8,128)(2,1)S(1)} %own.4._.own_ref, bf16[136,896]{1,0:T(8,128)(2,1)S(1)} %collective-permute-done.7.received_ref.refs_2_, f32[128,4096]{1,0:T(8,128)S(1)} %later.1.gated_ref.refs_6_), custom_call_target="tpu_custom_call" | custom-call | flops 20000000000 | bytes 1024 | tf_op jit(solution)/shard_map/chunk/pallas_call | solution.py:368
  27.8 0.0 collective-permute-done.8.refs_3_
  27.8 1.9 %raw.1.refs_0_ = bf16[1,128,4096]{2,1,0:T(8,128)(2,1)} custom-call(s32[1]{0:T(128)S(6)} %copy.19.refs_0_.start_ref, f32[256,128]{1,0:T(8,128)S(1)} %get-tuple-element.13.refs_1_.lines_ref, bf16[136,896]{1,0:T(8,128)(2,1)S(1)} %collective-permute-done.7.received_ref.refs_2_, ...), custom_call_target="tpu_custom_call", output_to_operand_aliasing={{}: (8, {})} | custom-call | flops 20000000000 | bytes 1024 | tf_op jit(solution)/shard_map/raw/pallas_call | solution.py:333
  29.7 0.0 collective-permute-done.6.received_ref
  29.7 0.7 %chunk.5.refs_0_ = bf16[1,128,4096]{2,1,0:T(8,128)(2,1)} custom-call(bf16[128,768]{1,0:T(8,128)(2,1)S(1)} %own.5.refs_6_.own_ref, bf16[128,768]{1,0:T(8,128)(2,1)S(1)} %collective-permute-done.6.received_ref, f32[128,4096]{1,0:T(8,128)S(1)} %later.1.gated_ref.refs_6_, bf16[1,128,4096]{2,1,0:T(8,128)(2,1)} %raw.1.refs_0_), custom_call_target="tpu_custom_call", output_to_operand_aliasing={{}: (3, {})} | custom-call | flops 20000000000 | bytes 1024 | tf_op jit(solution)/shard_map/chunk/pallas_call | solution.py:368
  30.4 0.5 %collective-permute-done.5.received_ref = bf16[128,1024]{1,0:T(8,128)(2,1)S(1)} collective-permute-done((bf16[128,1024]{1,0:T(8,128)(2,1)S(1)}, bf16[128,1024]{1,0:T(8,128)(2,1)S(1)}, u32[]{:S(2)}, u32[]{:S(2)}) %collective-permute-start.5) | collective-permute-done | bytes 262176 | tf_op jit(solution)/shard_map/ppermute | solution.py:33
  31.0 0.7 %chunk.6.refs_0_ = bf16[1,128,4096]{2,1,0:T(8,128)(2,1)} custom-call(bf16[128,1024]{1,0:T(8,128)(2,1)S(1)} %own.6._.own_ref, bf16[128,1024]{1,0:T(8,128)(2,1)S(1)} %collective-permute-done.5.received_ref, f32[128,4096]{1,0:T(8,128)S(1)} %later.1.gated_ref.refs_6_, bf16[1,128,4096]{2,1,0:T(8,128)(2,1)} %chunk.5.refs_0_), custom_call_target="tpu_custom_call", output_to_operand_aliasing={{}: (3, {})} | custom-call | flops 20000000000 | bytes 1024 | tf_op jit(solution)/shard_map/chunk/pallas_call | solution.py:368
  31.7 1.9 %collective-permute-done.3.received_ref = bf16[128,512]{1,0:T(8,128)(2,1)S(1)} collective-permute-done((bf16[128,512]{1,0:T(8,128)(2,1)S(1)}, bf16[128,512]{1,0:T(8,128)(2,1)S(1)}, u32[]{:S(2)}, u32[]{:S(2)}) %collective-permute-start.3) | collective-permute-done | bytes 131104 | tf_op jit(solution)/shard_map/ppermute | solution.py:33
  33.6 0.7 %chunk.7 = bf16[1,128,4096]{2,1,0:T(8,128)(2,1)} custom-call(bf16[128,512]{1,0:T(8,128)(2,1)S(1)} %own.7._.own_ref, bf16[128,512]{1,0:T(8,128)(2,1)S(1)} %collective-permute-done.3.received_ref, f32[128,4096]{1,0:T(8,128)S(1)} %later.1.gated_ref.refs_6_, bf16[1,128,4096]{2,1,0:T(8,128)(2,1)} %chunk.6.refs_0_), custom_call_target="tpu_custom_call", output_to_operand_aliasing={{}: (3, {})} | custom-call | flops 20000000000 | bytes 1024 | tf_op jit(solution)/shard_map/chunk/pallas_call | solution.py:368
  (3 shorter events, 0.1 us)
Async XLA Ops:
  2.0 9.7 %copy-start.2 = (bf16[1,256,128]{2,1,0:T(8,128)(2,1)S(1)}, bf16[1,256,128]{2,1,0:T(8,128)(2,1)}, u32[]{:S(2)}) copy-start(bf16[1,256,128]{2,1,0:T(8,128)(2,1)} %bank_ref.1) | copy-start | bytes 196612
  2.0 9.7 %copy-start.3 = (f32[1,256]{1,0:T(1,128)S(1)}, f32[1,256]{1,0:T(1,128)}, u32[]{:S(2)}) copy-start(f32[1,256]{1,0:T(1,128)} %scales_ref.1) | copy-start | bytes 3076
  2.0 9.7 %copy-start.4 = (s32[1,256]{1,0:T(1,128)S(1)}, s32[1,256]{1,0:T(1,128)}, u32[]{:S(2)}) copy-start(s32[1,256]{1,0:T(1,128)} %assign_ref.1) | copy-start | bytes 3076
  2.0 13.4 %collective-permute-start.1 = (bf16[256,896]{1,0:T(8,128)(2,1)S(1)}, bf16[256,896]{1,0:T(8,128)(2,1)S(1)}, u32[]{:S(2)}, u32[]{:S(2)}) collective-permute-start(bf16[256,896]{1,0:T(8,128)(2,1)S(1)} %get-tuple-element.15.raw_ref), channel_id=1, source_target_pairs={{0,1},{2,3},{4,5},{6,7},{8,9},{10,11},{12,13},{14,15},{16,17},{18,... | collective-permute-start | bytes 1376264 | tf_op jit(solution)/shard_map/ppermute | solution.py:33
  5.1 7.8 %collective-permute-start.2 = (bf16[128,896]{1,0:T(8,128)(2,1)S(1)}, bf16[128,896]{1,0:T(8,128)(2,1)S(1)}, u32[]{:S(2)}, u32[]{:S(2)}) collective-permute-start(bf16[128,896]{1,0:T(8,128)(2,1)S(1)} %get-tuple-element.12._.refs_3_), channel_id=1, source_target_pairs={{0,4},{4,8},{8,12},{12,16},{16,20},{20,24},{24,28},{2,6},{6,10},{1... | collective-permute-start | bytes 688136 | tf_op jit(solution)/shard_map/ppermute | solution.py:29
  6.6 6.3 %copy-start = (bf16[1,128,4096]{2,1,0:T(8,128)(2,1)S(1)}, bf16[1,128,4096]{2,1,0:T(8,128)(2,1)}, u32[]{:S(2)}) copy-start(bf16[1,128,4096]{2,1,0:T(8,128)(2,1)} %queries_ref.3) | copy-start | bytes 3145732
  6.6 6.3 %copy-start.1 = (bf16[128,4096]{1,0:T(8,128)(2,1)S(1)}, bf16[128,4096]{1,0:T(8,128)(2,1)}, u32[]{:S(2)}) copy-start(bf16[128,4096]{1,0:T(8,128)(2,1)} %refs_7_.1) | copy-start | bytes 3145732
  6.7 8.8 %collective-permute-start = (bf16[128,2304]{1,0:T(8,128)(2,1)S(1)}, bf16[128,2304]{1,0:T(8,128)(2,1)S(1)}, u32[]{:S(2)}, u32[]{:S(2)}) collective-permute-start(bf16[128,2304]{1,0:T(8,128)(2,1)S(1)} %get-tuple-element.14.refs_3_), channel_id=1, source_target_pairs={{0,4},{4,8},{8,12},{12,16},{16,20},{20,24},{24,28},{2,6},{6,10},{1... | collective-permute-start | bytes 1769480 | tf_op jit(solution)/shard_map/ppermute | solution.py:29
  10.9 14.8 %collective-permute-start.4 = (bf16[128,4096]{1,0:T(8,128)(2,1)S(1)}, bf16[128,4096]{1,0:T(8,128)(2,1)S(1)}, u32[]{:S(2)}, u32[]{:S(2)}) collective-permute-start(bf16[128,4096]{1,0:T(8,128)(2,1)S(1)} %product.1._.product_ref), channel_id=1, source_target_pairs={{1,5},{5,9},{9,13},{13,17},{17,21},{21,25},{25,29},{3,7},{7,11},{1... | collective-permute-start | bytes 3145736 | tf_op jit(solution)/shard_map/ppermute | solution.py:29
  14.1 13.0 %collective-permute-start.7 = (bf16[136,896]{1,0:T(8,128)(2,1)S(1)}, bf16[136,896]{1,0:T(8,128)(2,1)S(1)}, u32[]{:S(2)}, u32[]{:S(2)}) collective-permute-start(bf16[136,896]{1,0:T(8,128)(2,1)S(1)} %own.4._.own_ref), channel_id=1, source_target_pairs={{0,1},{2,3},{4,5},{6,7},{8,9},{10,11},{12,13},{14,15},{16,17},{18,... | collective-permute-start | bytes 731144 | tf_op jit(solution)/shard_map/ppermute | solution.py:33
  16.5 13.2 %collective-permute-start.6 = (bf16[128,768]{1,0:T(8,128)(2,1)S(1)}, bf16[128,768]{1,0:T(8,128)(2,1)S(1)}, u32[]{:S(2)}, u32[]{:S(2)}) collective-permute-start(bf16[128,768]{1,0:T(8,128)(2,1)S(1)} %own.5.refs_6_.own_ref), channel_id=1, source_target_pairs={{0,1},{2,3},{4,5},{6,7},{8,9},{10,11},{12,13},{14,15},{16,17},{18,... | collective-permute-start | bytes 589832 | tf_op jit(solution)/shard_map/ppermute | solution.py:33
  20.7 10.3 %collective-permute-start.5 = (bf16[128,1024]{1,0:T(8,128)(2,1)S(1)}, bf16[128,1024]{1,0:T(8,128)(2,1)S(1)}, u32[]{:S(2)}, u32[]{:S(2)}) collective-permute-start(bf16[128,1024]{1,0:T(8,128)(2,1)S(1)} %own.6._.own_ref), channel_id=1, source_target_pairs={{0,1},{2,3},{4,5},{6,7},{8,9},{10,11},{12,13},{14,15},{16,17},{18,... | collective-permute-start | bytes 786440 | tf_op jit(solution)/shard_map/ppermute | solution.py:33
  22.0 5.8 %collective-permute-start.8 = (bf16[128,896]{1,0:T(8,128)(2,1)S(1)}, bf16[128,896]{1,0:T(8,128)(2,1)S(1)}, u32[]{:S(2)}, u32[]{:S(2)}) collective-permute-start(bf16[128,896]{1,0:T(8,128)(2,1)S(1)} %hold.1.refs_6_.refs_4_), channel_id=1, source_target_pairs={{0,4},{1,5},{4,8},{5,9},{8,12},{9,13},{12,16},{13,17},{16,20},{17,... | collective-permute-start | bytes 688136 | tf_op jit(solution)/shard_map/ppermute | solution.py:29
  25.7 7.9 %collective-permute-start.3 = (bf16[128,512]{1,0:T(8,128)(2,1)S(1)}, bf16[128,512]{1,0:T(8,128)(2,1)S(1)}, u32[]{:S(2)}, u32[]{:S(2)}) collective-permute-start(bf16[128,512]{1,0:T(8,128)(2,1)S(1)} %own.7._.own_ref), channel_id=1, source_target_pairs={{0,1},{2,3},{4,5},{6,7},{8,9},{10,11},{12,13},{14,15},{16,17},{18,... | collective-permute-start | bytes 393224 | tf_op jit(solution)/shard_map/ppermute | solution.py:33

commit v5 on v4

v5 whole, which is shorter than its diff:
```python
import functools

import jax
import jax.numpy as jnp
from jax import lax
from jax.experimental import pallas as pl
from jax.experimental.pallas import tpu as pltpu
from jax.sharding import PartitionSpec as P

LANES = 128
ROW_BLOCK = 32
RAW = 896
NEAR = (512, 512)
REST = (512, 1024, 640)
LINES = 8
F32 = jnp.float32
BF16 = jnp.bfloat16
MIB = 1024 * 1024
QUICK, SLOW = 1024, 20_000_000_000

SMEM = pl.BlockSpec(memory_space=pltpu.SMEM)
VMEM = pl.BlockSpec(memory_space=pltpu.VMEM)
ANY = pl.BlockSpec(memory_space=pl.ANY)
HBM = pl.BlockSpec(memory_space=pltpu.HBM)


def to_next_slab(value, pipes):
    slabs, depth = lax.axis_size("ctx"), lax.axis_size("pipe")
    pairs = [(slab * depth + pipe, (slab + 1) * depth + pipe) for slab in range(slabs - 1) for pipe in pipes]
    return lax.ppermute(value, ("ctx", "pipe"), pairs)


def to_next_section(value):
    return lax.ppermute(value, "pipe", [(0, 1)])


def call(kernel, name, out_shape, in_specs, out_specs, scratch=(), weight=QUICK, aliases=None):
    return pl.pallas_call(
        kernel,
        out_shape=out_shape,
        in_specs=in_specs,
        out_specs=out_specs,
        scratch_shapes=list(scratch),
        input_output_aliases=aliases or {},
        compiler_params=pltpu.CompilerParams(vmem_limit_bytes=16 * MIB),
        cost_estimate=pl.CostEstimate(flops=weight, bytes_accessed=1024, transcendentals=0),
        name=name,
    )


def is_first():
    return lax.axis_index("pipe") == 0


def array(rows, cols, kind=BF16):
    return jax.ShapeDtypeStruct((rows, cols), kind)


def multiply(keys_ref, values_ref, keys_in, values_in, sems, first, targets, meanwhile=None):
    rows = keys_in.shape[0]
    pieces, offset = [], 0
    for piece, (out_ref, row, col, width) in enumerate(targets):
        at = pl.ds(offset, width)
        source = pl.ds(first + offset, width)
        copies = (
            pltpu.make_async_copy(keys_ref.at[0, :, source], keys_in.at[:, at], sems.at[2 * piece]),
            pltpu.make_async_copy(values_ref.at[0, :, source], values_in.at[:, at], sems.at[2 * piece + 1]),
        )
        for copy in copies:
            copy.start()
        pieces.append(copies)
        offset += width
    if meanwhile is not None:
        meanwhile()
    offset = 0
    for copies, (out_ref, row, col, width) in zip(pieces, targets):
        for copy in copies:
            copy.wait()
        for tile in range(0, width, LANES):
            at = slice(offset + tile, offset + tile + LANES)
            product = keys_in[:, at].astype(F32) * values_in[:, at].astype(F32)
            out_ref[row : row + rows, col + tile : col + tile + LANES] = product.astype(BF16)
        offset += width


def fill_lines(bank, scales_ref, assign_ref, lines_ref):
    groups, taps = lines_ref.shape
    size = bank.shape[0]
    chosen = (lax.broadcasted_iota(jnp.int32, (size, groups), 0) == assign_ref[...]).astype(F32).astype(BF16)
    contract = (((0,), (0,)), ((), ()))
    picked = lax.dot_general(bank, chosen, contract, preferred_element_type=F32)
    scaled = (picked * scales_ref[...]).astype(BF16)
    order = lax.broadcasted_iota(jnp.int32, (taps, taps), 0) + lax.broadcasted_iota(jnp.int32, (taps, taps), 1)
    flip = (order == taps - 1).astype(F32).astype(BF16)
    lines_ref[...] = lax.dot_general(scaled, flip, contract, preferred_element_type=F32)


def lead_kernel(*refs):
    bank_ref, scales_ref, assign_ref, queries_ref, keys_ref, values_ref = refs[:6]
    raw_ref, near_ref, rest_ref, lines_ref = refs[6:10]
    bank_in, scales_in, assign_in, keys_in, values_in, sems, own_sems = refs[10:]
    rows, width = near_ref.shape
    far = rest_ref.shape[1]
    half = far // 2 // LANES * LANES

    @pl.when(is_first())
    def _():
        copies = [
            pltpu.make_async_copy(bank_ref, bank_in, own_sems.at[0]),
            pltpu.make_async_copy(scales_ref, scales_in, own_sems.at[1]),
            pltpu.make_async_copy(assign_ref, assign_in, own_sems.at[2]),
            pltpu.make_async_copy(queries_ref.at[0, :, pl.ds(0, RAW)], raw_ref.at[pl.ds(0, rows)], own_sems.at[3]),
        ]
        for copy in copies:
            copy.start()

        def taps():
            for copy in copies[:3]:
                copy.wait()
            fill_lines(bank_in[0], scales_in, assign_in, lines_ref)
            for part in range(RAW // LANES):
                taken = lines_ref[part * LINES : (part + 1) * LINES, :].astype(BF16)
                raw_ref[2 * rows :, part * LANES : (part + 1) * LANES] = taken

        targets = [
            (raw_ref, rows, 0, RAW),
            (near_ref, 0, 0, width),
            (rest_ref, 0, 0, half),
            (rest_ref, 0, half, far - half),
        ]
        multiply(keys_ref, values_ref, keys_in, values_in, sems, 0, targets, taps)
        copies[3].wait()


def product_scratch(rows, total, pieces):
    return [pltpu.VMEM((rows, total), BF16), pltpu.VMEM((rows, total), BF16), pltpu.SemaphoreType.DMA((2 * pieces,))]


def lead_of(bank, scales, assign, queries, keys, values):
    rows, total = queries.shape[1:]
    near = sum(NEAR)
    return call(
        lead_kernel,
        "lead",
        (
            array(2 * rows + LINES, RAW),
            array(rows, near),
            array(rows, total - RAW - near),
            array(assign.shape[1], bank.shape[2], F32),
        ),
        [HBM] * 6,
        (VMEM,) * 4,
        [pltpu.VMEM(bank.shape, BF16), pltpu.VMEM(scales.shape, F32), pltpu.VMEM(assign.shape, jnp.int32)]
        + product_scratch(rows, total, 4)
        + [pltpu.SemaphoreType.DMA((4,))],
    )(bank, scales, assign, queries, keys, values)


def turn_table(lines_ref, row, count, table_ref, at):
    taps = lines_ref.shape[1]
    upper = lax.broadcasted_iota(jnp.int32, (ROW_BLOCK, taps), 1) > lax.broadcasted_iota(
        jnp.int32, (ROW_BLOCK, taps), 0
    )
    for group in range(count):
        line = lines_ref[row + group : row + group + 1, :]
        turned = pltpu.roll(jnp.broadcast_to(line, (ROW_BLOCK, taps)), 1, 1, stride=1, stride_axis=0)
        span = slice(at + group * ROW_BLOCK, at + (group + 1) * ROW_BLOCK)
        table_ref[span, :taps] = jnp.where(upper, turned, 0.0).astype(BF16)
        table_ref[span, taps:] = jnp.where(upper, 0.0, turned)[:, :ROW_BLOCK].astype(BF16)


def product_kernel(share, *refs):
    keys_ref, values_ref, bank_ref, scales_ref, assign_ref, held_ref, _ = refs[:7]
    out_ref, lines_ref, table_ref, keys_in, values_in, sems = refs[7:]
    half = out_ref.shape[1] // 2

    @pl.when(is_first())
    def _():
        for tile in range(sum(NEAR) // LANES):
            turn_table(held_ref, (RAW // LANES + tile) * share, share, table_ref, tile * share * ROW_BLOCK)

    @pl.when(jnp.logical_not(is_first()))
    def _():
        targets = [(out_ref, 0, 0, half), (out_ref, 0, half, half)]
        multiply(
            keys_ref,
            values_ref,
            keys_in,
            values_in,
            sems,
            0,
            targets,
            lambda: fill_lines(bank_ref[0], scales_ref, assign_ref, lines_ref),
        )


def product_of(keys, values, bank, scales, assign, lines, after):
    rows, total = keys.shape[1:]
    groups, taps = lines.shape
    share = LANES * groups // total
    return call(
        functools.partial(product_kernel, share),
        "product",
        (
            array(rows, total),
            array(groups, taps, F32),
            array(sum(NEAR) // LANES * share * ROW_BLOCK, taps + ROW_BLOCK),
        ),
        [HBM, HBM] + [VMEM] * 4 + [ANY],
        (VMEM,) * 3,
        product_scratch(rows, total, 2),
        aliases={5: 1},
    )(keys, values, bank, scales, assign, lines, after)


def mix(table_ref, row, share, window, store):
    depth = table_ref.shape[1]
    rows = window.shape[0] - depth + ROW_BLOCK
    member = lax.broadcasted_iota(jnp.int32, (ROW_BLOCK, LANES), 1) // (LANES // share)
    table = table_ref[row : row + share * ROW_BLOCK, :]
    for first in range(0, rows, ROW_BLOCK):
        sums = jnp.dot(table, window[first : first + depth], preferred_element_type=F32)
        mixed = sums[:ROW_BLOCK]
        for group in range(1, share):
            mixed = jnp.where(member == group, sums[group * ROW_BLOCK : (group + 1) * ROW_BLOCK], mixed)
        store(slice(first, first + ROW_BLOCK), mixed)


def mix_all(width, share, lines_ref, line, table_ref, made, start_ref, behind_ref, product_ref, local, store):
    rows = product_ref.shape[0]
    first = (lax.axis_index("ctx") - 1) * rows
    inside = first + lax.broadcasted_iota(jnp.int32, (2 * rows, LANES), 0) >= start_ref[0]
    for tile in range(width // LANES):
        at = slice(tile * LANES, (tile + 1) * LANES)
        inner = slice(local + at.start, local + at.stop)
        row = tile * share * ROW_BLOCK
        if not made:
            turn_table(lines_ref, line + tile * share, share, table_ref, row)
        window = jnp.concatenate([behind_ref[:, inner], product_ref[:, inner]], axis=0)
        window = jnp.where(inside, window, jnp.zeros_like(window))
        mix(table_ref, row, share, window, functools.partial(store, at))


def share_of(lines_ref, total):
    return LANES * lines_ref.shape[0] // total


def own_kernel(first, local, made, *refs):
    start_ref, lines_ref, behind_ref, product_ref, queries_ref, residual_ref, table_ref = refs[:7]
    out_ref = refs[-1] if made else refs[-2]
    width = out_ref.shape[1]
    share = share_of(lines_ref, residual_ref.shape[1])
    if made:
        table_ref = table_ref.at[pl.ds(local // LANES * share * ROW_BLOCK, width // LANES * share * ROW_BLOCK)]
    else:
        table_ref = refs[-1]

    @pl.when(is_first())
    def _():
        def store(at, span, mixed):
            cols = slice(first + at.start, first + at.stop)
            gated = queries_ref[0, span, cols].astype(F32) * mixed
            out_ref[span, at] = (residual_ref[span, cols].astype(F32) + gated).astype(BF16)

        line = first // LANES * share
        mix_all(width, share, lines_ref, line, table_ref, made, start_ref, behind_ref, product_ref, local, store)


def table_scratch(lines, width, total):
    groups, taps = lines.shape
    return pltpu.VMEM((width * groups // total * ROW_BLOCK, taps + ROW_BLOCK), BF16)


def own_of(start, lines, behind, product, queries, residual, first, local, width, table, *after):
    rows, total = residual.shape
    made = table is not None
    return call(
        functools.partial(own_kernel, first, local, made),
        "own",
        array(rows, width),
        [SMEM] + [VMEM] * (6 if made else 5) + [ANY] * len(after),
        VMEM,
        [] if made else [table_scratch(lines, width, total)],
        weight=QUICK if made else SLOW,
    )(start, lines, behind, product, queries, residual, *([table] if made else []), *after)


def pick_kernel(raw_ref, received_ref, _, queries_ref, product_ref, lines_ref):
    rows = queries_ref.shape[0]

    def take(source):
        queries_ref[...] = source[:rows, :]
        product_ref[...] = source[rows : 2 * rows, :]
        for part in range(RAW // LANES):
            taken = source[2 * rows :, part * LANES : (part + 1) * LANES]
            lines_ref[part * LINES : (part + 1) * LINES, :] = taken.astype(F32)

    pl.when(is_first())(lambda: take(raw_ref))
    pl.when(jnp.logical_not(is_first()))(lambda: take(received_ref))


def pick_of(raw, received, taps, after):
    rows, width = (raw.shape[0] - LINES) // 2, raw.shape[1]
    return call(
        pick_kernel,
        "pick",
        (array(rows, width), array(rows, width), array(RAW // LANES * LINES, taps, F32)),
        [VMEM, VMEM, ANY],
        (VMEM,) * 3,
        weight=SLOW,
    )(raw, received, after)


def hold_kernel(value_ref, _, out_ref):
    pass


def held_back(value, after):
    return call(hold_kernel, "hold", array(*value.shape), [ANY, ANY], ANY, aliases={0: 0})(value, after)


def send_out(pieces, out_ref, sems):
    copies = [
        pltpu.make_async_copy(buffer, out_ref.at[0, :, pl.ds(first, buffer.shape[1])], sems.at[place])
        for place, (buffer, first) in enumerate(pieces)
    ]
    for copy in copies:
        copy.start()
    return copies


def wait_all(copies):
    for copy in copies:
        copy.wait()


def later_kernel(places, *refs):
    start_ref, lines_ref, behind_ref, product_ref, queries_ref = refs[:5]
    own_refs = refs[5 : 5 + len(places)]
    out_ref, gated_ref, table_ref, sems = refs[-4:]
    total = queries_ref.shape[2]
    share = share_of(lines_ref, total)

    @pl.when(is_first())
    def _():
        wait_all(send_out([(own_ref, first) for own_ref, (first, _) in zip(own_refs, places)], out_ref, sems))

    @pl.when(jnp.logical_not(is_first()))
    def _():
        def store(at, span, mixed):
            gated_ref[span, at] = queries_ref[0, span, at].astype(F32) * mixed

        mix_all(total, share, lines_ref, 0, table_ref, False, start_ref, behind_ref, product_ref, 0, store)


def later_of(start, lines, behind, product, queries, own, places):
    rows, total = product.shape
    return call(
        functools.partial(later_kernel, places),
        "later",
        (jax.ShapeDtypeStruct((1, rows, total), BF16), array(rows, total, F32)),
        [SMEM] + [VMEM] * (4 + len(own)),
        (ANY, VMEM),
        [table_scratch(lines, total, total), pltpu.SemaphoreType.DMA((len(own),))],
        weight=SLOW,
    )(start, lines, behind, product, queries, *own)


def raw_kernel(start_ref, lines_ref, behind_ref, product_ref, queries_ref, gated_ref, residual_ref, _, *refs):
    out_ref, table_ref, buffer, sems = refs
    width = buffer.shape[1]
    share = share_of(lines_ref, width)

    def store(at, span, mixed):
        gated = queries_ref[span, at].astype(F32) * mixed
        buffer[span, at] = (residual_ref[span, at].astype(F32) + gated).astype(BF16)

    mix_all(width, share, lines_ref, 0, table_ref, False, start_ref, behind_ref, product_ref, 0, store)

    @pl.when(jnp.logical_not(is_first()))
    def _():
        buffer[...] = (buffer[...].astype(F32) + gated_ref[:, :width]).astype(BF16)

    wait_all(send_out([(buffer, 0)], out_ref, sems))


def raw_finish(held, start, lines, behind, product, queries, gated, residual):
    rows, width = product.shape
    return call(
        raw_kernel,
        "raw",
        jax.ShapeDtypeStruct(held.shape, BF16),
        [SMEM] + [VMEM] * 6 + [ANY],
        ANY,
        [table_scratch(lines, width, width), pltpu.VMEM((rows, width), BF16), pltpu.SemaphoreType.DMA((1,))],
        weight=SLOW,
        aliases={7: 0},
    )(start, lines, behind, product, queries, gated, residual, held)


def finish_kernel(places, *refs):
    gated_ref, received_refs = refs[0], refs[1 : 1 + len(places)]
    out_ref, *buffers, sems = refs[2 + len(places) :]

    @pl.when(jnp.logical_not(is_first()))
    def _():
        copies = []
        for place, (first, width) in enumerate(places):
            buffer = buffers[place]
            total = received_refs[place][...].astype(F32) + gated_ref[:, first : first + width]
            buffer[...] = total.astype(BF16)
            copies += send_out([(buffer, first)], out_ref, sems.at[pl.ds(place, 1)])
        wait_all(copies)


def finish(held, gated, received, places):
    rows = gated.shape[0]
    count = len(places)
    return call(
        functools.partial(finish_kernel, places),
        "finish",
        jax.ShapeDtypeStruct(held.shape, BF16),
        [VMEM] * (1 + count) + [ANY],
        ANY,
        [pltpu.VMEM((rows, width), BF16) for _, width in places] + [pltpu.SemaphoreType.DMA((count,))],
        weight=SLOW,
        aliases={1 + count: 0},
    )(gated, *received, held)


def body(queries, keys, values, residual, filter_bank, filter_scales, group_filter, context_start):
    total = queries.shape[2]
    small = (filter_bank, filter_scales, group_filter)
    far_small = [pltpu.with_memory_space_constraint(value, pltpu.HBM) for value in small]
    far_queries, keys, values = (
        pltpu.with_memory_space_constraint(value, pltpu.HBM) for value in (queries, keys, values)
    )
    raw, near, rest, lines = lead_of(*far_small, far_queries, keys, values)
    raw_received = to_next_section(raw)
    near_behind = to_next_slab(near, (0,))
    product, lines, table = product_of(keys, values, *small, lines, near)
    rest_behind = to_next_slab(rest, (0,))
    behind = to_next_slab(product, (1,))
    own, received, places = [], [], []

    def send(made, source, source_behind, origin, first, width, *after):
        piece = own_of(
            context_start, lines, source_behind, source, queries, residual, first, first - origin, width, made, *after
        )
        own.append(piece)
        received.append(to_next_section(piece))
        places.append((first, width))
        return first + width, piece

    first, after = RAW, lines
    for width in NEAR:
        first, after = send(table, near, near_behind, RAW, first, width, after)
    raw_queries, raw_product, raw_lines = pick_of(raw, raw_received, lines.shape[1], after)
    origin, after = first, raw_queries
    for chunk, width in enumerate(REST):
        if chunk == len(REST) - 1:
            raw_product = held_back(raw_product, after)
            raw_behind = to_next_slab(raw_product, (0, 1))
            after = raw_product
        passed = received[chunk - 1 : chunk] if chunk else []
        first, after = send(None, rest, rest_behind, origin, first, width, after, *passed)
    held, gated = later_of(context_start, lines, behind, product, queries, own, places)
    held = finish(held, gated, received[:3], places[:3])
    held = raw_finish(held, context_start, raw_lines, raw_behind, raw_product, raw_queries, gated, residual)
    for chunk in range(3, len(places)):
        held = finish(held, gated, received[chunk : chunk + 1], places[chunk : chunk + 1])
    return held


def solution(mesh):
    return jax.shard_map(
        body,
        mesh=mesh,
        in_specs=(
            P("pipe", ("dp", "ctx"), None),
            P("pipe", ("dp", "ctx"), None),
            P("pipe", ("dp", "ctx"), None),
            P(("dp", "ctx"), None),
            P("pipe", None, None),
            P("pipe", None),
            P("pipe", None),
            P("dp"),
        ),
        out_specs=P("pipe", ("dp", "ctx"), None),
        check_vma=False,
    )
```

time: 34.6 us -> 34.4 us (level)
  the two profiles are of different devices: /device:TPU:0 before, /device:TPU:21 now
where the time goes in v5:
time: 34.4 us; the launch traced here: 34 us
  starting transfers between devices  18.2 us (53%)
  Pallas kernels  10.8 us (31%)
  waiting for transfers between devices  4.12 us (12%)
  between operations  0.94 us (3%)
    ppermute x4, starting transfers between devices, to_next_slab(): return lax.ppermute(value, ('ctx', 'pipe'), pairs)  10.3 us
    ppermute x6, starting transfers between devices, to_next_section(): return lax.ppermute(value, 'pipe', [(0, 1)])  7.87 us
    pallas_call x1, Pallas kernels, later_of(): call(functools.partial(later_kernel, places), 'later', (jax.ShapeDtypeStr...  4.66 us
    ppermute x6, waiting for transfers between devices, to_next_section(): return lax.ppermute(value, 'pipe', [(0, 1)])  4.11 us
    pallas_call x3, Pallas kernels, finish(): call(functools.partial(finish_kernel, places), 'finish', jax.ShapeDtypeSt...  2.29 us
    pallas_call x1, Pallas kernels, raw_finish(): call(raw_kernel, 'raw', jax.ShapeDtypeStruct(held.shape, BF16), [SMEM] +...  1.91 us
    pallas_call x1, Pallas kernels, product_of(): call(functools.partial(product_kernel, share), 'product', (array(rows, to...  1.73 us
  transfers between devices with their start and end apart: 10, of which 2 were waited for; matrix products, arithmetic and copies ran while one was open for 0% of the time, Pallas kernels for 29%

profile of v5, /device:TPU:21, one launch (start us, length us, event | category | flops | bytes accessed | tf_op | source)
XLA Modules:
  0.0 34.0 jit_solution(411372882663729737)
XLA Ops:
  0.0 0.0 copy-start.2
  0.0 0.0 copy-start.3
  0.0 0.0 copy-start.4
  0.0 0.0 copy-start
  0.0 0.0 copy-start.1
  0.0 0.1 lead.1
  0.2 1.4 %collective-permute-start.3 = (bf16[264,896]{1,0:T(8,128)(2,1)S(1)}, bf16[264,896]{1,0:T(8,128)(2,1)S(1)}, u32[]{:S(2)}, u32[]{:S(2)}) collective-permute-start(bf16[264,896]{1,0:T(8,128)(2,1)S(1)} %get-tuple-element.23.raw_ref), channel_id=1, source_target_pairs={{0,1},{2,3},{4,5},{6,7},{8,9},{10,11},{12,13},{14,15},{16,17},{18,... | collective-permute-start | bytes 1419272 | tf_op jit(solution)/shard_map/ppermute | solution.py:34
  1.6 0.7 %collective-permute-start.1 = (bf16[128,1024]{1,0:T(8,128)(2,1)S(1)}, bf16[128,1024]{1,0:T(8,128)(2,1)S(1)}, u32[]{:S(2)}, u32[]{:S(2)}) collective-permute-start(bf16[128,1024]{1,0:T(8,128)(2,1)S(1)} %get-tuple-element.18.refs_6_.refs_3_), channel_id=1, source_target_pairs={{0,4},{4,8},{8,12},{12,16},{16,20},{20,24},{24,28},{2,6},{6,10},{1... | collective-permute-start | bytes 786440 | tf_op jit(solution)/shard_map/ppermute | solution.py:30
  2.3 0.7 %collective-permute-start.2 = (bf16[128,2176]{1,0:T(8,128)(2,1)S(1)}, bf16[128,2176]{1,0:T(8,128)(2,1)S(1)}, u32[]{:S(2)}, u32[]{:S(2)}) collective-permute-start(bf16[128,2176]{1,0:T(8,128)(2,1)S(1)} %get-tuple-element.22.refs_3_), channel_id=1, source_target_pairs={{0,4},{4,8},{8,12},{12,16},{16,20},{20,24},{24,28},{2,6},{6,10},{1... | collective-permute-start | bytes 1671176 | tf_op jit(solution)/shard_map/ppermute | solution.py:30
  3.0 0.0 copy-done.2
  3.0 0.0 copy-done.3
  3.0 0.0 copy-done.4
  3.0 1.7 %product.1 = (bf16[128,4096]{1,0:T(8,128)(2,1)S(1)}, f32[256,128]{1,0:T(8,128)S(1)}, bf16[2048,160]{1,0:T(8,128)(2,1)S(1)}) custom-call(bf16[1,128,4096]{2,1,0:T(8,128)(2,1)} %refs_0_.9, bf16[1,128,4096]{2,1,0:T(8,128)(2,1)} %refs_1_.3, bf16[1,256,128]{2,1,0:T(8,128)(2,1)S(1)} %copy-done.2, f32[1,256]{1,0:T(1,128)S(1)} %copy-done.3, ...), custom_call_target="tpu_custom_call", output_to_operand_aliasing={{1}: (5, {})} | custom-call | flops 1024 | bytes 1024 | tf_op jit(solution)/shard_map/product/pallas_call | solution.py:201
  4.7 3.8 %collective-permute-start = (bf16[128,4096]{1,0:T(8,128)(2,1)S(1)}, bf16[128,4096]{1,0:T(8,128)(2,1)S(1)}, u32[]{:S(2)}, u32[]{:S(2)}) collective-permute-start(bf16[128,4096]{1,0:T(8,128)(2,1)S(1)} %get-tuple-element.20.refs_3_), channel_id=1, source_target_pairs={{1,5},{5,9},{9,13},{13,17},{17,21},{21,25},{25,29},{3,7},{7,11},{1... | collective-permute-start | bytes 3145736 | tf_op jit(solution)/shard_map/ppermute | solution.py:30
  9.2 0.0 collective-permute-done.1.refs_2_
  9.2 0.0 copy-done
  9.2 0.0 copy-done.1
  9.2 1.3 %collective-permute-start.4 = (bf16[128,512]{1,0:T(8,128)(2,1)S(1)}, bf16[128,512]{1,0:T(8,128)(2,1)S(1)}, u32[]{:S(2)}, u32[]{:S(2)}) collective-permute-start(bf16[128,512]{1,0:T(8,128)(2,1)S(1)} %own.5.refs_7_.refs_5_), channel_id=1, source_target_pairs={{0,1},{2,3},{4,5},{6,7},{8,9},{10,11},{12,13},{14,15},{16,17},{18,... | collective-permute-start | bytes 393224 | tf_op jit(solution)/shard_map/ppermute | solution.py:34
  10.5 1.3 %collective-permute-start.5 = (bf16[128,512]{1,0:T(8,128)(2,1)S(1)}, bf16[128,512]{1,0:T(8,128)(2,1)S(1)}, u32[]{:S(2)}, u32[]{:S(2)}) collective-permute-start(bf16[128,512]{1,0:T(8,128)(2,1)S(1)} %own.6._.refs_6_), channel_id=1, source_target_pairs={{0,1},{2,3},{4,5},{6,7},{8,9},{10,11},{12,13},{14,15},{16,17},{18,... | collective-permute-start | bytes 393224 | tf_op jit(solution)/shard_map/ppermute | solution.py:34
  11.8 2.3 %collective-permute-done.3.received_ref = bf16[264,896]{1,0:T(8,128)(2,1)S(1)} collective-permute-done((bf16[264,896]{1,0:T(8,128)(2,1)S(1)}, bf16[264,896]{1,0:T(8,128)(2,1)S(1)}, u32[]{:S(2)}, u32[]{:S(2)}) %collective-permute-start.3) | collective-permute-done | bytes 473120 | tf_op jit(solution)/shard_map/ppermute | solution.py:34
  14.2 0.0 collective-permute-done.2.refs_2_
  14.2 1.3 %collective-permute-start.9 = (bf16[128,512]{1,0:T(8,128)(2,1)S(1)}, bf16[128,512]{1,0:T(8,128)(2,1)S(1)}, u32[]{:S(2)}, u32[]{:S(2)}) collective-permute-start(bf16[128,512]{1,0:T(8,128)(2,1)S(1)} %own.7.refs_6_.refs_7_), channel_id=1, source_target_pairs={{0,1},{2,3},{4,5},{6,7},{8,9},{10,11},{12,13},{14,15},{16,17},{18,... | collective-permute-start | bytes 393224 | tf_op jit(solution)/shard_map/ppermute | solution.py:34
  15.5 1.8 %collective-permute-done.4.refs_7_.refs_1_ = bf16[128,512]{1,0:T(8,128)(2,1)S(1)} collective-permute-done((bf16[128,512]{1,0:T(8,128)(2,1)S(1)}, bf16[128,512]{1,0:T(8,128)(2,1)S(1)}, u32[]{:S(2)}, u32[]{:S(2)}) %collective-permute-start.4) | collective-permute-done | bytes 131104 | tf_op jit(solution)/shard_map/ppermute | solution.py:34
  17.3 1.3 %collective-permute-start.7 = (bf16[128,1024]{1,0:T(8,128)(2,1)S(1)}, bf16[128,1024]{1,0:T(8,128)(2,1)S(1)}, u32[]{:S(2)}, u32[]{:S(2)}) collective-permute-start(bf16[128,1024]{1,0:T(8,128)(2,1)S(1)} %own.8._.refs_8_), channel_id=1, source_target_pairs={{0,1},{2,3},{4,5},{6,7},{8,9},{10,11},{12,13},{14,15},{16,17},{18,... | collective-permute-start | bytes 786440 | tf_op jit(solution)/shard_map/ppermute | solution.py:34
  18.6 5.1 %collective-permute-start.8 = (bf16[128,896]{1,0:T(8,128)(2,1)S(1)}, bf16[128,896]{1,0:T(8,128)(2,1)S(1)}, u32[]{:S(2)}, u32[]{:S(2)}) collective-permute-start(bf16[128,896]{1,0:T(8,128)(2,1)S(1)} %hold.1.refs_6_.product_ref), channel_id=1, source_target_pairs={{0,4},{1,5},{4,8},{5,9},{8,12},{9,13},{12,16},{13,17},{16,20},{17,... | collective-permute-start | bytes 688136 | tf_op jit(solution)/shard_map/ppermute | solution.py:30
  23.8 0.0 collective-permute-done.5.refs_7_.refs_2_
  23.8 1.3 %collective-permute-start.6 = (bf16[128,640]{1,0:T(8,128)(2,1)S(1)}, bf16[128,640]{1,0:T(8,128)(2,1)S(1)}, u32[]{:S(2)}, u32[]{:S(2)}) collective-permute-start(bf16[128,640]{1,0:T(8,128)(2,1)S(1)} %own.9.refs_9_), channel_id=1, source_target_pairs={{0,1},{2,3},{4,5},{6,7},{8,9},{10,11},{12,13},{14,15},{16,17},{18,... | collective-permute-start | bytes 491528 | tf_op jit(solution)/shard_map/ppermute | solution.py:34
  25.1 0.0 collective-permute-done.refs_2_
  25.1 4.7 %later.1 = (bf16[1,128,4096]{2,1,0:T(8,128)(2,1)}, f32[128,4096]{1,0:T(8,128)S(1)}) custom-call(s32[1]{0:T(128)S(6)} %copy.21.refs_0_.start_ref, f32[256,128]{1,0:T(8,128)S(1)} %get-tuple-element.19.refs_1_.refs_7_, bf16[128,4096]{1,0:T(8,128)(2,1)S(1)} %collective-permute-done.refs_2_, bf16[128,4096]{1,0:T(8,128)(2,1)S(1)} %get-tuple-element.20.refs_3_, ...), custom_call_target="tpu_custom_call" | custom-call | flops 20000000000 | bytes 1024 | tf_op jit(solution)/shard_map/later/pallas_call | solution.py:358
  29.8 0.0 collective-permute-done.9.refs_3_
  29.8 0.8 %finish.3._ = bf16[1,128,4096]{2,1,0:T(8,128)(2,1)} custom-call(f32[128,4096]{1,0:T(8,128)S(1)} %get-tuple-element.26.refs_0_.gated_ref, bf16[128,512]{1,0:T(8,128)(2,1)S(1)} %collective-permute-done.4.refs_7_.refs_1_, bf16[128,512]{1,0:T(8,128)(2,1)S(1)} %collective-permute-done.5.refs_7_.refs_2_, ...), custom_call_target="tpu_custom_call", output_to_operand_aliasing={{}: (4, {})} | custom-call | flops 20000000000 | bytes 1024 | tf_op jit(solution)/shard_map/finish/pallas_call | solution.py:419
  30.6 0.0 collective-permute-done.8.behind_ref
  30.6 1.9 %raw.1.refs_2_ = bf16[1,128,4096]{2,1,0:T(8,128)(2,1)} custom-call(s32[1]{0:T(128)S(6)} %copy.21.refs_0_.start_ref, f32[56,128]{1,0:T(8,128)S(1)} %get-tuple-element.27.lines_ref, bf16[128,896]{1,0:T(8,128)(2,1)S(1)} %collective-permute-done.8.behind_ref, bf16[128,896]{1,0:T(8,128)(2,1)S(1)} %hold.1.refs_6_.product_ref, ...), custom_call_target="tpu_custom_call", output_to_operand_aliasing={{}: (7, {})} | custom-call | flops 20000000000 | bytes 1024 | tf_op jit(solution)/shard_map/raw/pallas_call | solution.py:389
  32.5 0.0 collective-permute-done.7.refs_1_
  32.5 0.8 %finish.4.refs_2_ = bf16[1,128,4096]{2,1,0:T(8,128)(2,1)} custom-call(f32[128,4096]{1,0:T(8,128)S(1)} %get-tuple-element.26.refs_0_.gated_ref, bf16[128,1024]{1,0:T(8,128)(2,1)S(1)} %collective-permute-done.7.refs_1_, bf16[1,128,4096]{2,1,0:T(8,128)(2,1)} %raw.1.refs_2_), custom_call_target="tpu_custom_call", output_to_operand_aliasing={{}: (2, {})} | custom-call | flops 20000000000 | bytes 1024 | tf_op jit(solution)/shard_map/finish/pallas_call | solution.py:419
  33.3 0.0 collective-permute-done.6.refs_1_
  33.3 0.7 %finish.5 = bf16[1,128,4096]{2,1,0:T(8,128)(2,1)} custom-call(f32[128,4096]{1,0:T(8,128)S(1)} %get-tuple-element.26.refs_0_.gated_ref, bf16[128,640]{1,0:T(8,128)(2,1)S(1)} %collective-permute-done.6.refs_1_, bf16[1,128,4096]{2,1,0:T(8,128)(2,1)} %finish.4.refs_2_), custom_call_target="tpu_custom_call", output_to_operand_aliasing={{}: (2, {})} | custom-call | flops 20000000000 | bytes 1024 | tf_op jit(solution)/shard_map/finish/pallas_call | solution.py:419
  (7 shorter events, 0.1 us)
Async XLA Ops:
  0.0 3.0 %copy-start.2 = (bf16[1,256,128]{2,1,0:T(8,128)(2,1)S(1)}, bf16[1,256,128]{2,1,0:T(8,128)(2,1)}, u32[]{:S(2)}) copy-start(bf16[1,256,128]{2,1,0:T(8,128)(2,1)} %refs_2_.3) | copy-start | bytes 196612
  0.0 3.0 %copy-start.3 = (f32[1,256]{1,0:T(1,128)S(1)}, f32[1,256]{1,0:T(1,128)}, u32[]{:S(2)}) copy-start(f32[1,256]{1,0:T(1,128)} %refs_3_.3) | copy-start | bytes 3076
  0.0 3.0 %copy-start.4 = (s32[1,256]{1,0:T(1,128)S(1)}, s32[1,256]{1,0:T(1,128)}, u32[]{:S(2)}) copy-start(s32[1,256]{1,0:T(1,128)} %refs_4_.9) | copy-start | bytes 3076
  0.0 9.2 %copy-start = (bf16[1,128,4096]{2,1,0:T(8,128)(2,1)S(1)}, bf16[1,128,4096]{2,1,0:T(8,128)(2,1)}, u32[]{:S(2)}) copy-start(bf16[1,128,4096]{2,1,0:T(8,128)(2,1)} %refs_4_.15) | copy-start | bytes 3145732
  0.0 9.2 %copy-start.1 = (bf16[128,4096]{1,0:T(8,128)(2,1)S(1)}, bf16[128,4096]{1,0:T(8,128)(2,1)}, u32[]{:S(2)}) copy-start(bf16[128,4096]{1,0:T(8,128)(2,1)} %residual_ref.1) | copy-start | bytes 3145732
  0.2 14.0 %collective-permute-start.3 = (bf16[264,896]{1,0:T(8,128)(2,1)S(1)}, bf16[264,896]{1,0:T(8,128)(2,1)S(1)}, u32[]{:S(2)}, u32[]{:S(2)}) collective-permute-start(bf16[264,896]{1,0:T(8,128)(2,1)S(1)} %get-tuple-element.23.raw_ref), channel_id=1, source_target_pairs={{0,1},{2,3},{4,5},{6,7},{8,9},{10,11},{12,13},{14,15},{16,17},{18,... | collective-permute-start | bytes 1419272 | tf_op jit(solution)/shard_map/ppermute | solution.py:34
  1.6 7.6 %collective-permute-start.1 = (bf16[128,1024]{1,0:T(8,128)(2,1)S(1)}, bf16[128,1024]{1,0:T(8,128)(2,1)S(1)}, u32[]{:S(2)}, u32[]{:S(2)}) collective-permute-start(bf16[128,1024]{1,0:T(8,128)(2,1)S(1)} %get-tuple-element.18.refs_6_.refs_3_), channel_id=1, source_target_pairs={{0,4},{4,8},{8,12},{12,16},{16,20},{20,24},{24,28},{2,6},{6,10},{1... | collective-permute-start | bytes 786440 | tf_op jit(solution)/shard_map/ppermute | solution.py:30
  2.3 11.9 %collective-permute-start.2 = (bf16[128,2176]{1,0:T(8,128)(2,1)S(1)}, bf16[128,2176]{1,0:T(8,128)(2,1)S(1)}, u32[]{:S(2)}, u32[]{:S(2)}) collective-permute-start(bf16[128,2176]{1,0:T(8,128)(2,1)S(1)} %get-tuple-element.22.refs_3_), channel_id=1, source_target_pairs={{0,4},{4,8},{8,12},{12,16},{16,20},{20,24},{24,28},{2,6},{6,10},{1... | collective-permute-start | bytes 1671176 | tf_op jit(solution)/shard_map/ppermute | solution.py:30
  4.7 20.4 %collective-permute-start = (bf16[128,4096]{1,0:T(8,128)(2,1)S(1)}, bf16[128,4096]{1,0:T(8,128)(2,1)S(1)}, u32[]{:S(2)}, u32[]{:S(2)}) collective-permute-start(bf16[128,4096]{1,0:T(8,128)(2,1)S(1)} %get-tuple-element.20.refs_3_), channel_id=1, source_target_pairs={{1,5},{5,9},{9,13},{13,17},{17,21},{21,25},{25,29},{3,7},{7,11},{1... | collective-permute-start | bytes 3145736 | tf_op jit(solution)/shard_map/ppermute | solution.py:30
  9.2 8.1 %collective-permute-start.4 = (bf16[128,512]{1,0:T(8,128)(2,1)S(1)}, bf16[128,512]{1,0:T(8,128)(2,1)S(1)}, u32[]{:S(2)}, u32[]{:S(2)}) collective-permute-start(bf16[128,512]{1,0:T(8,128)(2,1)S(1)} %own.5.refs_7_.refs_5_), channel_id=1, source_target_pairs={{0,1},{2,3},{4,5},{6,7},{8,9},{10,11},{12,13},{14,15},{16,17},{18,... | collective-permute-start | bytes 393224 | tf_op jit(solution)/shard_map/ppermute | solution.py:34
  10.5 13.2 %collective-permute-start.5 = (bf16[128,512]{1,0:T(8,128)(2,1)S(1)}, bf16[128,512]{1,0:T(8,128)(2,1)S(1)}, u32[]{:S(2)}, u32[]{:S(2)}) collective-permute-start(bf16[128,512]{1,0:T(8,128)(2,1)S(1)} %own.6._.refs_6_), channel_id=1, source_target_pairs={{0,1},{2,3},{4,5},{6,7},{8,9},{10,11},{12,13},{14,15},{16,17},{18,... | collective-permute-start | bytes 393224 | tf_op jit(solution)/shard_map/ppermute | solution.py:34
  14.2 15.6 %collective-permute-start.9 = (bf16[128,512]{1,0:T(8,128)(2,1)S(1)}, bf16[128,512]{1,0:T(8,128)(2,1)S(1)}, u32[]{:S(2)}, u32[]{:S(2)}) collective-permute-start(bf16[128,512]{1,0:T(8,128)(2,1)S(1)} %own.7.refs_6_.refs_7_), channel_id=1, source_target_pairs={{0,1},{2,3},{4,5},{6,7},{8,9},{10,11},{12,13},{14,15},{16,17},{18,... | collective-permute-start | bytes 393224 | tf_op jit(solution)/shard_map/ppermute | solution.py:34
  17.3 15.2 %collective-permute-start.7 = (bf16[128,1024]{1,0:T(8,128)(2,1)S(1)}, bf16[128,1024]{1,0:T(8,128)(2,1)S(1)}, u32[]{:S(2)}, u32[]{:S(2)}) collective-permute-start(bf16[128,1024]{1,0:T(8,128)(2,1)S(1)} %own.8._.refs_8_), channel_id=1, source_target_pairs={{0,1},{2,3},{4,5},{6,7},{8,9},{10,11},{12,13},{14,15},{16,17},{18,... | collective-permute-start | bytes 786440 | tf_op jit(solution)/shard_map/ppermute | solution.py:34
  18.6 12.0 %collective-permute-start.8 = (bf16[128,896]{1,0:T(8,128)(2,1)S(1)}, bf16[128,896]{1,0:T(8,128)(2,1)S(1)}, u32[]{:S(2)}, u32[]{:S(2)}) collective-permute-start(bf16[128,896]{1,0:T(8,128)(2,1)S(1)} %hold.1.refs_6_.product_ref), channel_id=1, source_target_pairs={{0,4},{1,5},{4,8},{5,9},{8,12},{9,13},{12,16},{13,17},{16,20},{17,... | collective-permute-start | bytes 688136 | tf_op jit(solution)/shard_map/ppermute | solution.py:30
  23.8 9.5 %collective-permute-start.6 = (bf16[128,640]{1,0:T(8,128)(2,1)S(1)}, bf16[128,640]{1,0:T(8,128)(2,1)S(1)}, u32[]{:S(2)}, u32[]{:S(2)}) collective-permute-start(bf16[128,640]{1,0:T(8,128)(2,1)S(1)} %own.9.refs_9_), channel_id=1, source_target_pairs={{0,1},{2,3},{4,5},{6,7},{8,9},{10,11},{12,13},{14,15},{16,17},{18,... | collective-permute-start | bytes 491528 | tf_op jit(solution)/shard_map/ppermute | solution.py:34

commit v6 on v5

--- a/solution.py
+++ b/solution.py
@@ -218,12 +218,16 @@
     rows = window.shape[0] - depth + ROW_BLOCK
     member = lax.broadcasted_iota(jnp.int32, (ROW_BLOCK, LANES), 1) // (LANES // share)
     table = table_ref[row : row + share * ROW_BLOCK, :]
-    for first in range(0, rows, ROW_BLOCK):
-        sums = jnp.dot(table, window[first : first + depth], preferred_element_type=F32)
-        mixed = sums[:ROW_BLOCK]
-        for group in range(1, share):
-            mixed = jnp.where(member == group, sums[group * ROW_BLOCK : (group + 1) * ROW_BLOCK], mixed)
-        store(slice(first, first + ROW_BLOCK), mixed)
+    for first in range(0, rows, 2 * ROW_BLOCK):
+        starts = (first, first + ROW_BLOCK)
+        pair = jnp.concatenate([window[begin : begin + depth] for begin in starts], axis=1)
+        sums = jnp.dot(table, pair, preferred_element_type=F32)
+        for place, begin in enumerate(starts):
+            part = sums[:, place * LANES : (place + 1) * LANES]
+            mixed = part[:ROW_BLOCK]
+            for group in range(1, share):
+                mixed = jnp.where(member == group, part[group * ROW_BLOCK : (group + 1) * ROW_BLOCK], mixed)
+            store(slice(begin, begin + ROW_BLOCK), mixed)
 
 
 def mix_all(width, share, lines_ref, line, table_ref, made, start_ref, behind_ref, product_ref, local, store):

time: 34.4 us -> 33.5 us (0.974)
  the two profiles are of different devices: /device:TPU:21 before, /device:TPU:12 now
where the time goes in v6:
time: 33.5 us; the launch traced here: 33.1 us
  starting transfers between devices  13.1 us (39%)
  waiting for transfers between devices  10.8 us (32%)
  Pallas kernels  8.26 us (25%)
  between operations  0.92 us (3%)
    ppermute x6, waiting for transfers between devices, to_next_section(): return lax.ppermute(value, 'pipe', [(0, 1)])  10.2 us
    ppermute x6, starting transfers between devices, to_next_section(): return lax.ppermute(value, 'pipe', [(0, 1)])  7.87 us
    ppermute x4, starting transfers between devices, to_next_slab(): return lax.ppermute(value, ('ctx', 'pipe'), pairs)  5.21 us
    pallas_call x1, Pallas kernels, later_of(): call(functools.partial(later_kernel, places), 'later', (jax.ShapeDtypeStr...  2.56 us
    pallas_call x3, Pallas kernels, finish(): call(functools.partial(finish_kernel, places), 'finish', jax.ShapeDtypeSt...  2.26 us
    pallas_call x1, Pallas kernels, product_of(): call(functools.partial(product_kernel, share), 'product', (array(rows, to...  1.73 us
    pallas_call x1, Pallas kernels, raw_finish(): call(raw_kernel, 'raw', jax.ShapeDtypeStruct(held.shape, BF16), [SMEM] +...  1.48 us
    ppermute x4, waiting for transfers between devices, to_next_slab(): return lax.ppermute(value, ('ctx', 'pipe'), pairs)  0.68 us
  transfers between devices with their start and end apart: 10, of which 5 were waited for; matrix products, arithmetic and copies ran while one was open for 0% of the time, Pallas kernels for 22%

profile of v6, /device:TPU:12, one launch (start us, length us, event | category | flops | bytes accessed | tf_op | source)
XLA Modules:
  0.0 33.1 jit_solution(14686290040625895425)
XLA Ops:
  0.0 0.0 copy-start.2
  0.0 0.0 copy-start.3
  0.0 0.0 copy-start.4
  0.0 0.0 copy-start
  0.0 0.0 copy-start.1
  0.0 0.1 lead.1
  0.2 1.4 %collective-permute-start.3 = (bf16[264,896]{1,0:T(8,128)(2,1)S(1)}, bf16[264,896]{1,0:T(8,128)(2,1)S(1)}, u32[]{:S(2)}, u32[]{:S(2)}) collective-permute-start(bf16[264,896]{1,0:T(8,128)(2,1)S(1)} %get-tuple-element.23.raw_ref), channel_id=1, source_target_pairs={{0,1},{2,3},{4,5},{6,7},{8,9},{10,11},{12,13},{14,15},{16,17},{18,... | collective-permute-start | bytes 1419272 | tf_op jit(solution)/shard_map/ppermute | solution.py:34
  1.6 0.7 %collective-permute-start.1 = (bf16[128,1024]{1,0:T(8,128)(2,1)S(1)}, bf16[128,1024]{1,0:T(8,128)(2,1)S(1)}, u32[]{:S(2)}, u32[]{:S(2)}) collective-permute-start(bf16[128,1024]{1,0:T(8,128)(2,1)S(1)} %get-tuple-element.18.refs_6_.refs_3_), channel_id=1, source_target_pairs={{0,4},{4,8},{8,12},{12,16},{16,20},{20,24},{24,28},{2,6},{6,10},{1... | collective-permute-start | bytes 786440 | tf_op jit(solution)/shard_map/ppermute | solution.py:30
  2.3 0.7 %collective-permute-start.2 = (bf16[128,2176]{1,0:T(8,128)(2,1)S(1)}, bf16[128,2176]{1,0:T(8,128)(2,1)S(1)}, u32[]{:S(2)}, u32[]{:S(2)}) collective-permute-start(bf16[128,2176]{1,0:T(8,128)(2,1)S(1)} %get-tuple-element.22.refs_3_), channel_id=1, source_target_pairs={{0,4},{4,8},{8,12},{12,16},{16,20},{20,24},{24,28},{2,6},{6,10},{1... | collective-permute-start | bytes 1671176 | tf_op jit(solution)/shard_map/ppermute | solution.py:30
  3.0 0.0 copy-done.2
  3.0 0.0 copy-done.3
  3.0 0.0 copy-done.4
  3.0 1.7 %product.1 = (bf16[128,4096]{1,0:T(8,128)(2,1)S(1)}, f32[256,128]{1,0:T(8,128)S(1)}, bf16[2048,160]{1,0:T(8,128)(2,1)S(1)}) custom-call(bf16[1,128,4096]{2,1,0:T(8,128)(2,1)} %refs_0_.9, bf16[1,128,4096]{2,1,0:T(8,128)(2,1)} %refs_1_.3, bf16[1,256,128]{2,1,0:T(8,128)(2,1)S(1)} %copy-done.2, f32[1,256]{1,0:T(1,128)S(1)} %copy-done.3, ...), custom_call_target="tpu_custom_call", output_to_operand_aliasing={{1}: (5, {})} | custom-call | flops 1024 | bytes 1024 | tf_op jit(solution)/shard_map/product/pallas_call | solution.py:201
  4.7 1.9 %collective-permute-start = (bf16[128,4096]{1,0:T(8,128)(2,1)S(1)}, bf16[128,4096]{1,0:T(8,128)(2,1)S(1)}, u32[]{:S(2)}, u32[]{:S(2)}) collective-permute-start(bf16[128,4096]{1,0:T(8,128)(2,1)S(1)} %get-tuple-element.20.refs_3_), channel_id=1, source_target_pairs={{1,5},{5,9},{9,13},{13,17},{17,21},{21,25},{25,29},{3,7},{7,11},{1... | collective-permute-start | bytes 3145736 | tf_op jit(solution)/shard_map/ppermute | solution.py:30
  7.3 0.0 collective-permute-done.1.refs_2_
  7.3 0.0 copy-done
  7.3 0.0 copy-done.1
  7.4 1.3 %collective-permute-start.4 = (bf16[128,512]{1,0:T(8,128)(2,1)S(1)}, bf16[128,512]{1,0:T(8,128)(2,1)S(1)}, u32[]{:S(2)}, u32[]{:S(2)}) collective-permute-start(bf16[128,512]{1,0:T(8,128)(2,1)S(1)} %own.5.refs_7_.refs_5_), channel_id=1, source_target_pairs={{0,1},{2,3},{4,5},{6,7},{8,9},{10,11},{12,13},{14,15},{16,17},{18,... | collective-permute-start | bytes 393224 | tf_op jit(solution)/shard_map/ppermute | solution.py:34
  8.7 1.3 %collective-permute-start.5 = (bf16[128,512]{1,0:T(8,128)(2,1)S(1)}, bf16[128,512]{1,0:T(8,128)(2,1)S(1)}, u32[]{:S(2)}, u32[]{:S(2)}) collective-permute-start(bf16[128,512]{1,0:T(8,128)(2,1)S(1)} %own.6._.refs_6_), channel_id=1, source_target_pairs={{0,1},{2,3},{4,5},{6,7},{8,9},{10,11},{12,13},{14,15},{16,17},{18,... | collective-permute-start | bytes 393224 | tf_op jit(solution)/shard_map/ppermute | solution.py:34
  10.0 5.5 %collective-permute-done.3.received_ref = bf16[264,896]{1,0:T(8,128)(2,1)S(1)} collective-permute-done((bf16[264,896]{1,0:T(8,128)(2,1)S(1)}, bf16[264,896]{1,0:T(8,128)(2,1)S(1)}, u32[]{:S(2)}, u32[]{:S(2)}) %collective-permute-start.3) | collective-permute-done | bytes 473120 | tf_op jit(solution)/shard_map/ppermute | solution.py:34
  15.6 0.0 collective-permute-done.2.refs_2_
  15.6 1.3 %collective-permute-start.9 = (bf16[128,512]{1,0:T(8,128)(2,1)S(1)}, bf16[128,512]{1,0:T(8,128)(2,1)S(1)}, u32[]{:S(2)}, u32[]{:S(2)}) collective-permute-start(bf16[128,512]{1,0:T(8,128)(2,1)S(1)} %own.7.refs_6_.refs_7_), channel_id=1, source_target_pairs={{0,1},{2,3},{4,5},{6,7},{8,9},{10,11},{12,13},{14,15},{16,17},{18,... | collective-permute-start | bytes 393224 | tf_op jit(solution)/shard_map/ppermute | solution.py:34
  16.9 1.4 %collective-permute-done.4.refs_7_.refs_1_ = bf16[128,512]{1,0:T(8,128)(2,1)S(1)} collective-permute-done((bf16[128,512]{1,0:T(8,128)(2,1)S(1)}, bf16[128,512]{1,0:T(8,128)(2,1)S(1)}, u32[]{:S(2)}, u32[]{:S(2)}) %collective-permute-start.4) | collective-permute-done | bytes 131104 | tf_op jit(solution)/shard_map/ppermute | solution.py:34
  18.3 1.3 %collective-permute-start.7 = (bf16[128,1024]{1,0:T(8,128)(2,1)S(1)}, bf16[128,1024]{1,0:T(8,128)(2,1)S(1)}, u32[]{:S(2)}, u32[]{:S(2)}) collective-permute-start(bf16[128,1024]{1,0:T(8,128)(2,1)S(1)} %own.8._.refs_8_), channel_id=1, source_target_pairs={{0,1},{2,3},{4,5},{6,7},{8,9},{10,11},{12,13},{14,15},{16,17},{18,... | collective-permute-start | bytes 786440 | tf_op jit(solution)/shard_map/ppermute | solution.py:34
  19.6 1.9 %collective-permute-start.8 = (bf16[128,896]{1,0:T(8,128)(2,1)S(1)}, bf16[128,896]{1,0:T(8,128)(2,1)S(1)}, u32[]{:S(2)}, u32[]{:S(2)}) collective-permute-start(bf16[128,896]{1,0:T(8,128)(2,1)S(1)} %hold.1.refs_6_.product_ref), channel_id=1, source_target_pairs={{0,4},{1,5},{4,8},{5,9},{8,12},{9,13},{12,16},{13,17},{16,20},{17,... | collective-permute-start | bytes 688136 | tf_op jit(solution)/shard_map/ppermute | solution.py:30
  21.6 0.0 collective-permute-done.5.refs_7_.refs_2_
  21.6 1.3 %collective-permute-start.6 = (bf16[128,640]{1,0:T(8,128)(2,1)S(1)}, bf16[128,640]{1,0:T(8,128)(2,1)S(1)}, u32[]{:S(2)}, u32[]{:S(2)}) collective-permute-start(bf16[128,640]{1,0:T(8,128)(2,1)S(1)} %own.9.refs_9_), channel_id=1, source_target_pairs={{0,1},{2,3},{4,5},{6,7},{8,9},{10,11},{12,13},{14,15},{16,17},{18,... | collective-permute-start | bytes 491528 | tf_op jit(solution)/shard_map/ppermute | solution.py:34
  22.9 0.0 collective-permute-done.refs_2_
  22.9 2.6 %later.1 = (bf16[1,128,4096]{2,1,0:T(8,128)(2,1)}, f32[128,4096]{1,0:T(8,128)S(1)}) custom-call(s32[1]{0:T(128)S(6)} %copy.21.refs_0_.start_ref, f32[256,128]{1,0:T(8,128)S(1)} %get-tuple-element.19.refs_1_.refs_7_, bf16[128,4096]{1,0:T(8,128)(2,1)S(1)} %collective-permute-done.refs_2_, bf16[128,4096]{1,0:T(8,128)(2,1)S(1)} %get-tuple-element.20.refs_3_, ...), custom_call_target="tpu_custom_call" | custom-call | flops 20000000000 | bytes 1024 | tf_op jit(solution)/shard_map/later/pallas_call | solution.py:362
  25.5 0.0 collective-permute-done.9.refs_3_
  25.5 0.8 %finish.3._ = bf16[1,128,4096]{2,1,0:T(8,128)(2,1)} custom-call(f32[128,4096]{1,0:T(8,128)S(1)} %get-tuple-element.26.refs_0_.gated_ref, bf16[128,512]{1,0:T(8,128)(2,1)S(1)} %collective-permute-done.4.refs_7_.refs_1_, bf16[128,512]{1,0:T(8,128)(2,1)S(1)} %collective-permute-done.5.refs_7_.refs_2_, ...), custom_call_target="tpu_custom_call", output_to_operand_aliasing={{}: (4, {})} | custom-call | flops 20000000000 | bytes 1024 | tf_op jit(solution)/shard_map/finish/pallas_call | solution.py:423
  26.3 0.7 %collective-permute-done.8.behind_ref = bf16[128,896]{1,0:T(8,128)(2,1)S(1)} collective-permute-done((bf16[128,896]{1,0:T(8,128)(2,1)S(1)}, bf16[128,896]{1,0:T(8,128)(2,1)S(1)}, u32[]{:S(2)}, u32[]{:S(2)}) %collective-permute-start.8) | collective-permute-done | bytes 229408 | tf_op jit(solution)/shard_map/ppermute | solution.py:30
  27.0 1.5 %raw.1.refs_2_ = bf16[1,128,4096]{2,1,0:T(8,128)(2,1)} custom-call(s32[1]{0:T(128)S(6)} %copy.21.refs_0_.start_ref, f32[56,128]{1,0:T(8,128)S(1)} %get-tuple-element.27.lines_ref, bf16[128,896]{1,0:T(8,128)(2,1)S(1)} %collective-permute-done.8.behind_ref, bf16[128,896]{1,0:T(8,128)(2,1)S(1)} %hold.1.refs_6_.product_ref, ...), custom_call_target="tpu_custom_call", output_to_operand_aliasing={{}: (7, {})} | custom-call | flops 20000000000 | bytes 1024 | tf_op jit(solution)/shard_map/raw/pallas_call | solution.py:393
  28.5 0.6 %collective-permute-done.7.refs_1_ = bf16[128,1024]{1,0:T(8,128)(2,1)S(1)} collective-permute-done((bf16[128,1024]{1,0:T(8,128)(2,1)S(1)}, bf16[128,1024]{1,0:T(8,128)(2,1)S(1)}, u32[]{:S(2)}, u32[]{:S(2)}) %collective-permute-start.7) | collective-permute-done | bytes 262176 | tf_op jit(solution)/shard_map/ppermute | solution.py:34
  29.1 0.8 %finish.4.refs_2_ = bf16[1,128,4096]{2,1,0:T(8,128)(2,1)} custom-call(f32[128,4096]{1,0:T(8,128)S(1)} %get-tuple-element.26.refs_0_.gated_ref, bf16[128,1024]{1,0:T(8,128)(2,1)S(1)} %collective-permute-done.7.refs_1_, bf16[1,128,4096]{2,1,0:T(8,128)(2,1)} %raw.1.refs_2_), custom_call_target="tpu_custom_call", output_to_operand_aliasing={{}: (2, {})} | custom-call | flops 20000000000 | bytes 1024 | tf_op jit(solution)/shard_map/finish/pallas_call | solution.py:423
  29.9 2.6 %collective-permute-done.6.refs_1_ = bf16[128,640]{1,0:T(8,128)(2,1)S(1)} collective-permute-done((bf16[128,640]{1,0:T(8,128)(2,1)S(1)}, bf16[128,640]{1,0:T(8,128)(2,1)S(1)}, u32[]{:S(2)}, u32[]{:S(2)}) %collective-permute-start.6) | collective-permute-done | bytes 163872 | tf_op jit(solution)/shard_map/ppermute | solution.py:34
  32.4 0.7 %finish.5 = bf16[1,128,4096]{2,1,0:T(8,128)(2,1)} custom-call(f32[128,4096]{1,0:T(8,128)S(1)} %get-tuple-element.26.refs_0_.gated_ref, bf16[128,640]{1,0:T(8,128)(2,1)S(1)} %collective-permute-done.6.refs_1_, bf16[1,128,4096]{2,1,0:T(8,128)(2,1)} %finish.4.refs_2_), custom_call_target="tpu_custom_call", output_to_operand_aliasing={{}: (2, {})} | custom-call | flops 20000000000 | bytes 1024 | tf_op jit(solution)/shard_map/finish/pallas_call | solution.py:423
  (7 shorter events, 0.1 us)
Async XLA Ops:
  0.0 3.0 %copy-start.2 = (bf16[1,256,128]{2,1,0:T(8,128)(2,1)S(1)}, bf16[1,256,128]{2,1,0:T(8,128)(2,1)}, u32[]{:S(2)}) copy-start(bf16[1,256,128]{2,1,0:T(8,128)(2,1)} %refs_2_.3) | copy-start | bytes 196612
  0.0 3.0 %copy-start.3 = (f32[1,256]{1,0:T(1,128)S(1)}, f32[1,256]{1,0:T(1,128)}, u32[]{:S(2)}) copy-start(f32[1,256]{1,0:T(1,128)} %refs_3_.3) | copy-start | bytes 3076
  0.0 3.0 %copy-start.4 = (s32[1,256]{1,0:T(1,128)S(1)}, s32[1,256]{1,0:T(1,128)}, u32[]{:S(2)}) copy-start(s32[1,256]{1,0:T(1,128)} %refs_4_.9) | copy-start | bytes 3076
  0.0 7.3 %copy-start = (bf16[1,128,4096]{2,1,0:T(8,128)(2,1)S(1)}, bf16[1,128,4096]{2,1,0:T(8,128)(2,1)}, u32[]{:S(2)}) copy-start(bf16[1,128,4096]{2,1,0:T(8,128)(2,1)} %refs_4_.15) | copy-start | bytes 3145732
  0.0 7.3 %copy-start.1 = (bf16[128,4096]{1,0:T(8,128)(2,1)S(1)}, bf16[128,4096]{1,0:T(8,128)(2,1)}, u32[]{:S(2)}) copy-start(bf16[128,4096]{1,0:T(8,128)(2,1)} %residual_ref.1) | copy-start | bytes 3145732
  0.2 15.4 %collective-permute-start.3 = (bf16[264,896]{1,0:T(8,128)(2,1)S(1)}, bf16[264,896]{1,0:T(8,128)(2,1)S(1)}, u32[]{:S(2)}, u32[]{:S(2)}) collective-permute-start(bf16[264,896]{1,0:T(8,128)(2,1)S(1)} %get-tuple-element.23.raw_ref), channel_id=1, source_target_pairs={{0,1},{2,3},{4,5},{6,7},{8,9},{10,11},{12,13},{14,15},{16,17},{18,... | collective-permute-start | bytes 1419272 | tf_op jit(solution)/shard_map/ppermute | solution.py:34
  1.6 5.7 %collective-permute-start.1 = (bf16[128,1024]{1,0:T(8,128)(2,1)S(1)}, bf16[128,1024]{1,0:T(8,128)(2,1)S(1)}, u32[]{:S(2)}, u32[]{:S(2)}) collective-permute-start(bf16[128,1024]{1,0:T(8,128)(2,1)S(1)} %get-tuple-element.18.refs_6_.refs_3_), channel_id=1, source_target_pairs={{0,4},{4,8},{8,12},{12,16},{16,20},{20,24},{24,28},{2,6},{6,10},{1... | collective-permute-start | bytes 786440 | tf_op jit(solution)/shard_map/ppermute | solution.py:30
  2.3 13.3 %collective-permute-start.2 = (bf16[128,2176]{1,0:T(8,128)(2,1)S(1)}, bf16[128,2176]{1,0:T(8,128)(2,1)S(1)}, u32[]{:S(2)}, u32[]{:S(2)}) collective-permute-start(bf16[128,2176]{1,0:T(8,128)(2,1)S(1)} %get-tuple-element.22.refs_3_), channel_id=1, source_target_pairs={{0,4},{4,8},{8,12},{12,16},{16,20},{20,24},{24,28},{2,6},{6,10},{1... | collective-permute-start | bytes 1671176 | tf_op jit(solution)/shard_map/ppermute | solution.py:30
  4.7 18.2 %collective-permute-start = (bf16[128,4096]{1,0:T(8,128)(2,1)S(1)}, bf16[128,4096]{1,0:T(8,128)(2,1)S(1)}, u32[]{:S(2)}, u32[]{:S(2)}) collective-permute-start(bf16[128,4096]{1,0:T(8,128)(2,1)S(1)} %get-tuple-element.20.refs_3_), channel_id=1, source_target_pairs={{1,5},{5,9},{9,13},{13,17},{17,21},{21,25},{25,29},{3,7},{7,11},{1... | collective-permute-start | bytes 3145736 | tf_op jit(solution)/shard_map/ppermute | solution.py:30
  7.4 11.0 %collective-permute-start.4 = (bf16[128,512]{1,0:T(8,128)(2,1)S(1)}, bf16[128,512]{1,0:T(8,128)(2,1)S(1)}, u32[]{:S(2)}, u32[]{:S(2)}) collective-permute-start(bf16[128,512]{1,0:T(8,128)(2,1)S(1)} %own.5.refs_7_.refs_5_), channel_id=1, source_target_pairs={{0,1},{2,3},{4,5},{6,7},{8,9},{10,11},{12,13},{14,15},{16,17},{18,... | collective-permute-start | bytes 393224 | tf_op jit(solution)/shard_map/ppermute | solution.py:34
  8.7 12.9 %collective-permute-start.5 = (bf16[128,512]{1,0:T(8,128)(2,1)S(1)}, bf16[128,512]{1,0:T(8,128)(2,1)S(1)}, u32[]{:S(2)}, u32[]{:S(2)}) collective-permute-start(bf16[128,512]{1,0:T(8,128)(2,1)S(1)} %own.6._.refs_6_), channel_id=1, source_target_pairs={{0,1},{2,3},{4,5},{6,7},{8,9},{10,11},{12,13},{14,15},{16,17},{18,... | collective-permute-start | bytes 393224 | tf_op jit(solution)/shard_map/ppermute | solution.py:34
  15.6 9.9 %collective-permute-start.9 = (bf16[128,512]{1,0:T(8,128)(2,1)S(1)}, bf16[128,512]{1,0:T(8,128)(2,1)S(1)}, u32[]{:S(2)}, u32[]{:S(2)}) collective-permute-start(bf16[128,512]{1,0:T(8,128)(2,1)S(1)} %own.7.refs_6_.refs_7_), channel_id=1, source_target_pairs={{0,1},{2,3},{4,5},{6,7},{8,9},{10,11},{12,13},{14,15},{16,17},{18,... | collective-permute-start | bytes 393224 | tf_op jit(solution)/shard_map/ppermute | solution.py:34
  18.3 10.8 %collective-permute-start.7 = (bf16[128,1024]{1,0:T(8,128)(2,1)S(1)}, bf16[128,1024]{1,0:T(8,128)(2,1)S(1)}, u32[]{:S(2)}, u32[]{:S(2)}) collective-permute-start(bf16[128,1024]{1,0:T(8,128)(2,1)S(1)} %own.8._.refs_8_), channel_id=1, source_target_pairs={{0,1},{2,3},{4,5},{6,7},{8,9},{10,11},{12,13},{14,15},{16,17},{18,... | collective-permute-start | bytes 786440 | tf_op jit(solution)/shard_map/ppermute | solution.py:34
  19.6 7.3 %collective-permute-start.8 = (bf16[128,896]{1,0:T(8,128)(2,1)S(1)}, bf16[128,896]{1,0:T(8,128)(2,1)S(1)}, u32[]{:S(2)}, u32[]{:S(2)}) collective-permute-start(bf16[128,896]{1,0:T(8,128)(2,1)S(1)} %hold.1.refs_6_.product_ref), channel_id=1, source_target_pairs={{0,4},{1,5},{4,8},{5,9},{8,12},{9,13},{12,16},{13,17},{16,20},{17,... | collective-permute-start | bytes 688136 | tf_op jit(solution)/shard_map/ppermute | solution.py:30
  21.6 10.8 %collective-permute-start.6 = (bf16[128,640]{1,0:T(8,128)(2,1)S(1)}, bf16[128,640]{1,0:T(8,128)(2,1)S(1)}, u32[]{:S(2)}, u32[]{:S(2)}) collective-permute-start(bf16[128,640]{1,0:T(8,128)(2,1)S(1)} %own.9.refs_9_), channel_id=1, source_target_pairs={{0,1},{2,3},{4,5},{6,7},{8,9},{10,11},{12,13},{14,15},{16,17},{18,... | collective-permute-start | bytes 491528 | tf_op jit(solution)/shard_map/ppermute | solution.py:34

commit v7 on v6

--- a/solution.py
+++ b/solution.py
@@ -9,9 +9,9 @@
 
 LANES = 128
 ROW_BLOCK = 32
-RAW = 896
-NEAR = (512, 512)
-REST = (512, 1024, 640)
+RAW = 512
+ODD = (1536, 2048)
+EVEN = (1408, 768, 768, 640)
 LINES = 8
 F32 = jnp.float32
 BF16 = jnp.bfloat16
@@ -24,14 +24,17 @@
 HBM = pl.BlockSpec(memory_space=pltpu.HBM)
 
 
-def to_next_slab(value, pipes):
+def to_next_slab(value, pipes, from_odd=(0, 1)):
     slabs, depth = lax.axis_size("ctx"), lax.axis_size("pipe")
-    pairs = [(slab * depth + pipe, (slab + 1) * depth + pipe) for slab in range(slabs - 1) for pipe in pipes]
+    sources = [slab for slab in range(slabs - 1) if slab % 2 in from_odd]
+    pairs = [(slab * depth + pipe, (slab + 1) * depth + pipe) for slab in sources for pipe in pipes]
     return lax.ppermute(value, ("ctx", "pipe"), pairs)
 
 
-def to_next_section(value):
-    return lax.ppermute(value, "pipe", [(0, 1)])
+def to_next_section(value, slabs=(0, 1)):
+    depth = lax.axis_size("pipe")
+    pairs = [(slab * depth, slab * depth + 1) for slab in range(lax.axis_size("ctx")) if slab % 2 in slabs]
+    return lax.ppermute(value, ("ctx", "pipe"), pairs)
 
 
 def call(kernel, name, out_shape, in_specs, out_specs, scratch=(), weight=QUICK, aliases=None):
@@ -50,6 +53,10 @@
 
 def is_first():
     return lax.axis_index("pipe") == 0
+
+
+def is_slab(odd):
+    return lax.axis_index("ctx") % 2 == odd
 
 
 def array(rows, cols, kind=BF16):
@@ -97,11 +104,10 @@
 
 def lead_kernel(*refs):
     bank_ref, scales_ref, assign_ref, queries_ref, keys_ref, values_ref = refs[:6]
-    raw_ref, near_ref, rest_ref, lines_ref = refs[6:10]
-    bank_in, scales_in, assign_in, keys_in, values_in, sems, own_sems = refs[10:]
-    rows, width = near_ref.shape
-    far = rest_ref.shape[1]
-    half = far // 2 // LANES * LANES
+    raw_ref, rest_ref, lines_ref = refs[6:9]
+    bank_in, scales_in, assign_in, keys_in, values_in, sems, own_sems = refs[9:]
+    rows, far = rest_ref.shape
+    step = far // 3 // LANES * LANES
 
     @pl.when(is_first())
     def _():
@@ -124,9 +130,9 @@
 
         targets = [
             (raw_ref, rows, 0, RAW),
-            (near_ref, 0, 0, width),
-            (rest_ref, 0, 0, half),
-            (rest_ref, 0, half, far - half),
+            (rest_ref, 0, 0, step),
+            (rest_ref, 0, step, step),
+            (rest_ref, 0, 2 * step, far - 2 * step),
         ]
         multiply(keys_ref, values_ref, keys_in, values_in, sems, 0, targets, taps)
         copies[3].wait()
@@ -138,18 +144,16 @@
 
 def lead_of(bank, scales, assign, queries, keys, values):
     rows, total = queries.shape[1:]
-    near = sum(NEAR)
     return call(
         lead_kernel,
         "lead",
         (
             array(2 * rows + LINES, RAW),
-            array(rows, near),
-            array(rows, total - RAW - near),
+            array(rows, total - RAW),
             array(assign.shape[1], bank.shape[2], F32),
         ),
         [HBM] * 6,
-        (VMEM,) * 4,
+        (VMEM,) * 3,
         [pltpu.VMEM(bank.shape, BF16), pltpu.VMEM(scales.shape, F32), pltpu.VMEM(assign.shape, jnp.int32)]
         + product_scratch(rows, total, 4)
         + [pltpu.SemaphoreType.DMA((4,))],
@@ -169,15 +173,16 @@
         table_ref[span, taps:] = jnp.where(upper, 0.0, turned)[:, :ROW_BLOCK].astype(BF16)
 
 
-def product_kernel(share, *refs):
-    keys_ref, values_ref, bank_ref, scales_ref, assign_ref, held_ref, _ = refs[:7]
-    out_ref, lines_ref, table_ref, keys_in, values_in, sems = refs[7:]
+def product_kernel(*refs):
+    keys_ref, values_ref, bank_ref, scales_ref, assign_ref, _, rest_ref = refs[:7]
+    out_ref, lines_ref, near_ref, far_ref, keys_in, values_in, sems = refs[7:]
     half = out_ref.shape[1] // 2
-
-    @pl.when(is_first())
-    def _():
-        for tile in range(sum(NEAR) // LANES):
-            turn_table(held_ref, (RAW // LANES + tile) * share, share, table_ref, tile * share * ROW_BLOCK)
+    near = near_ref.shape[1]
+
+    @pl.when(jnp.logical_and(is_first(), is_slab(1)))
+    def _():
+        near_ref[...] = rest_ref[:, :near]
+        far_ref[...] = rest_ref[:, near:]
 
     @pl.when(jnp.logical_not(is_first()))
     def _():
@@ -194,23 +199,18 @@
         )
 
 
-def product_of(keys, values, bank, scales, assign, lines, after):
+def product_of(keys, values, bank, scales, assign, lines, rest):
     rows, total = keys.shape[1:]
-    groups, taps = lines.shape
-    share = LANES * groups // total
-    return call(
-        functools.partial(product_kernel, share),
+    near = EVEN[0]
+    return call(
+        product_kernel,
         "product",
-        (
-            array(rows, total),
-            array(groups, taps, F32),
-            array(sum(NEAR) // LANES * share * ROW_BLOCK, taps + ROW_BLOCK),
-        ),
-        [HBM, HBM] + [VMEM] * 4 + [ANY],
-        (VMEM,) * 3,
+        (array(rows, total), array(*lines.shape, F32), array(rows, near), array(rows, total - RAW - near)),
+        [HBM, HBM] + [VMEM] * 5,
+        (VMEM,) * 4,
         product_scratch(rows, total, 2),
         aliases={5: 1},
-    )(keys, values, bank, scales, assign, lines, after)
+    )(keys, values, bank, scales, assign, lines, rest)
 
 
 def mix(table_ref, row, share, window, store):
@@ -230,17 +230,16 @@
             store(slice(begin, begin + ROW_BLOCK), mixed)
 
 
-def mix_all(width, share, lines_ref, line, table_ref, made, start_ref, behind_ref, product_ref, local, store):
+def mix_all(width, share, lines_ref, line, table_ref, start_ref, behind_ref, product_ref, local, store):
     rows = product_ref.shape[0]
     first = (lax.axis_index("ctx") - 1) * rows
     inside = first + lax.broadcasted_iota(jnp.int32, (2 * rows, LANES), 0) >= start_ref[0]
     for tile in range(width // LANES):
         at = slice(tile * LANES, (tile + 1) * LANES)
-        inner = slice(local + at.start, local + at.stop)
+        near, inner = (slice(begin + at.start, begin + at.stop) for begin in local)
         row = tile * share * ROW_BLOCK
-        if not made:
-            turn_table(lines_ref, line + tile * share, share, table_ref, row)
-        window = jnp.concatenate([behind_ref[:, inner], product_ref[:, inner]], axis=0)
+        turn_table(lines_ref, line + tile * share, share, table_ref, row)
+        window = jnp.concatenate([behind_ref[:, near], product_ref[:, inner]], axis=0)
         window = jnp.where(inside, window, jnp.zeros_like(window))
         mix(table_ref, row, share, window, functools.partial(store, at))
 
@@ -249,17 +248,13 @@
     return LANES * lines_ref.shape[0] // total
 
 
-def own_kernel(first, local, made, *refs):
-    start_ref, lines_ref, behind_ref, product_ref, queries_ref, residual_ref, table_ref = refs[:7]
-    out_ref = refs[-1] if made else refs[-2]
+def own_kernel(odd, first, shift, local, *refs):
+    start_ref, lines_ref, behind_ref, product_ref, queries_ref, residual_ref = refs[:6]
+    out_ref, table_ref = refs[-2:]
     width = out_ref.shape[1]
     share = share_of(lines_ref, residual_ref.shape[1])
-    if made:
-        table_ref = table_ref.at[pl.ds(local // LANES * share * ROW_BLOCK, width // LANES * share * ROW_BLOCK)]
-    else:
-        table_ref = refs[-1]
-
-    @pl.when(is_first())
+
+    @pl.when(jnp.logical_and(is_first(), is_slab(odd)))
     def _():
         def store(at, span, mixed):
             cols = slice(first + at.start, first + at.stop)
@@ -267,7 +262,8 @@
             out_ref[span, at] = (residual_ref[span, cols].astype(F32) + gated).astype(BF16)
 
         line = first // LANES * share
-        mix_all(width, share, lines_ref, line, table_ref, made, start_ref, behind_ref, product_ref, local, store)
+        at = (shift, local)
+        mix_all(width, share, lines_ref, line, table_ref, start_ref, behind_ref, product_ref, at, store)
 
 
 def table_scratch(lines, width, total):
@@ -275,18 +271,17 @@
     return pltpu.VMEM((width * groups // total * ROW_BLOCK, taps + ROW_BLOCK), BF16)
 
 
-def own_of(start, lines, behind, product, queries, residual, first, local, width, table, *after):
+def own_of(odd, origin, start, lines, behind, product, queries, residual, first, width, weight, *after):
     rows, total = residual.shape
-    made = table is not None
-    return call(
-        functools.partial(own_kernel, first, local, made),
+    return call(
+        functools.partial(own_kernel, odd, first, first - origin, first - RAW),
         "own",
         array(rows, width),
-        [SMEM] + [VMEM] * (6 if made else 5) + [ANY] * len(after),
+        [SMEM] + [VMEM] * 5 + [ANY] * len(after),
         VMEM,
-        [] if made else [table_scratch(lines, width, total)],
-        weight=QUICK if made else SLOW,
-    )(start, lines, behind, product, queries, residual, *([table] if made else []), *after)
+        [table_scratch(lines, width, total)],
+        weight=weight,
+    )(start, lines, behind, product, queries, residual, *after)
 
 
 def pick_kernel(raw_ref, received_ref, _, queries_ref, product_ref, lines_ref):
@@ -319,8 +314,10 @@
     pass
 
 
-def held_back(value, after):
-    return call(hold_kernel, "hold", array(*value.shape), [ANY, ANY], ANY, aliases={0: 0})(value, after)
+def held_back(value, after, weight=QUICK):
+    return call(
+        hold_kernel, "hold", array(*value.shape), [ANY, ANY], ANY, weight=weight, aliases={0: 0}
+    )(value, after)
 
 
 def send_out(pieces, out_ref, sems):
@@ -345,16 +342,19 @@
     total = queries_ref.shape[2]
     share = share_of(lines_ref, total)
 
-    @pl.when(is_first())
-    def _():
-        wait_all(send_out([(own_ref, first) for own_ref, (first, _) in zip(own_refs, places)], out_ref, sems))
+    for odd in (0, 1):
+
+        @pl.when(jnp.logical_and(is_first(), is_slab(odd)))
+        def _():
+            pieces = [(own_ref, first) for own_ref, (side, first, _) in zip(own_refs, places) if side == odd]
+            wait_all(send_out(pieces, out_ref, sems))
 
     @pl.when(jnp.logical_not(is_first()))
     def _():
         def store(at, span, mixed):
             gated_ref[span, at] = queries_ref[0, span, at].astype(F32) * mixed
 
-        mix_all(total, share, lines_ref, 0, table_ref, False, start_ref, behind_ref, product_ref, 0, store)
+        mix_all(total, share, lines_ref, 0, table_ref, start_ref, behind_ref, product_ref, (0, 0), store)
 
 
 def later_of(start, lines, behind, product, queries, own, places):
@@ -379,7 +379,7 @@
         gated = queries_ref[span, at].astype(F32) * mixed
         buffer[span, at] = (residual_ref[span, at].astype(F32) + gated).astype(BF16)
 
-    mix_all(width, share, lines_ref, 0, table_ref, False, start_ref, behind_ref, product_ref, 0, store)
+    mix_all(width, share, lines_ref, 0, table_ref, start_ref, behind_ref, product_ref, (0, 0), store)
 
     @pl.when(jnp.logical_not(is_first()))
     def _():
@@ -402,14 +402,14 @@
     )(start, lines, behind, product, queries, gated, residual, held)
 
 
-def finish_kernel(places, *refs):
+def finish_kernel(odd, places, *refs):
     gated_ref, received_refs = refs[0], refs[1 : 1 + len(places)]
     out_ref, *buffers, sems = refs[2 + len(places) :]
 
-    @pl.when(jnp.logical_not(is_first()))
+    @pl.when(jnp.logical_and(jnp.logical_not(is_first()), is_slab(odd)))
     def _():
         copies = []
-        for place, (first, width) in enumerate(places):
+        for place, (_, first, width) in enumerate(places):
             buffer = buffers[place]
             total = received_refs[place][...].astype(F32) + gated_ref[:, first : first + width]
             buffer[...] = total.astype(BF16)
@@ -421,12 +421,12 @@
     rows = gated.shape[0]
     count = len(places)
     return call(
-        functools.partial(finish_kernel, places),
+        functools.partial(finish_kernel, places[0][0], places),
         "finish",
         jax.ShapeDtypeStruct(held.shape, BF16),
         [VMEM] * (1 + count) + [ANY],
         ANY,
-        [pltpu.VMEM((rows, width), BF16) for _, width in places] + [pltpu.SemaphoreType.DMA((count,))],
+        [pltpu.VMEM((rows, width), BF16) for _, _, width in places] + [pltpu.SemaphoreType.DMA((count,))],
         weight=SLOW,
         aliases={1 + count: 0},
     )(gated, *received, held)
@@ -439,40 +439,43 @@
     far_queries, keys, values = (
         pltpu.with_memory_space_constraint(value, pltpu.HBM) for value in (queries, keys, values)
     )
-    raw, near, rest, lines = lead_of(*far_small, far_queries, keys, values)
+    raw, rest, lines = lead_of(*far_small, far_queries, keys, values)
     raw_received = to_next_section(raw)
-    near_behind = to_next_slab(near, (0,))
-    product, lines, table = product_of(keys, values, *small, lines, near)
-    rest_behind = to_next_slab(rest, (0,))
-    behind = to_next_slab(product, (1,))
+    chip_behind = to_next_slab(rest, (0,), (0,))
+    product, lines, near, far = product_of(keys, values, *small, lines, rest)
     own, received, places = [], [], []
 
-    def send(made, source, source_behind, origin, first, width, *after):
+    def send(odd, behind, origin, first, width, weight, *after):
         piece = own_of(
-            context_start, lines, source_behind, source, queries, residual, first, first - origin, width, made, *after
+            odd, origin, context_start, lines, behind, rest, queries, residual, first, width, weight, *after
         )
         own.append(piece)
-        received.append(to_next_section(piece))
-        places.append((first, width))
+        received.append(to_next_section(piece, (odd,)))
+        places.append((odd, first, width))
         return first + width, piece
 
-    first, after = RAW, lines
-    for width in NEAR:
-        first, after = send(table, near, near_behind, RAW, first, width, after)
-    raw_queries, raw_product, raw_lines = pick_of(raw, raw_received, lines.shape[1], after)
-    origin, after = first, raw_queries
-    for chunk, width in enumerate(REST):
-        if chunk == len(REST) - 1:
-            raw_product = held_back(raw_product, after)
-            raw_behind = to_next_slab(raw_product, (0, 1))
-            after = raw_product
-        passed = received[chunk - 1 : chunk] if chunk else []
-        first, after = send(None, rest, rest_behind, origin, first, width, after, *passed)
+    first, after = send(1, chip_behind, RAW, RAW, ODD[0], QUICK, lines)
+    near = held_back(near, after)
+    near_behind = to_next_slab(near, (0,), (1,))
+    first, after = send(1, chip_behind, RAW, first, ODD[1], QUICK, near)
+    product = held_back(product, after)
+    behind = to_next_slab(product, (1,))
+    raw_queries, raw_product, raw_lines = pick_of(raw, raw_received, lines.shape[1], product)
+    far_behind = to_next_slab(held_back(far, raw_queries), (0,), (1,))
+    raw_queries = held_back(raw_queries, received[0], SLOW)
+    first, after = send(0, near_behind, RAW, RAW, EVEN[0], SLOW, raw_queries)
+    raw_product = held_back(raw_product, after)
+    raw_behind = to_next_slab(raw_product, (0, 1))
+    origin, after = first, raw_product
+    for width, passed in zip(EVEN[1:], (received[1], after, behind)):
+        first, after = send(0, far_behind, origin, first, width, SLOW, after, passed)
     held, gated = later_of(context_start, lines, behind, product, queries, own, places)
-    held = finish(held, gated, received[:3], places[:3])
+    odd = len(ODD)
+    held = finish(held, gated, received[:odd], places[:odd])
     held = raw_finish(held, context_start, raw_lines, raw_behind, raw_product, raw_queries, gated, residual)
-    for chunk in range(3, len(places)):
-        held = finish(held, gated, received[chunk : chunk + 1], places[chunk : chunk + 1])
+    for last in (odd + 2, odd + 3, odd + 4):
+        begin = odd if last == odd + 2 else last - 1
+        held = finish(held, gated, received[begin:last], places[begin:last])
     return held
 
 

time: 33.5 us -> 34.2 us (1.021)
  starting transfers between devices: 13.1 us -> 16.4 us
  waiting for transfers between devices: 10.8 us -> 8.32 us
    ppermute x6 -> x7, waiting for transfers between devices: 10.2 us -> 6.77 us  [to_next_section(): return lax.ppermute(value, ('ctx', 'pipe'), pairs)]
    ppermute x4 -> x5, starting transfers between devices: 5.21 us -> 8.6 us  [to_next_slab(): return lax.ppermute(value, ('ctx', 'pipe'), pairs)]
    ppermute x4 -> x5, waiting for transfers between devices: 0.68 us -> 1.55 us  [to_next_slab(): return lax.ppermute(value, ('ctx', 'pipe'), pairs)]
    pallas_call x11 -> x17, Pallas kernels: 4.18 us -> 4.32 us  [the longest x4 2.34 us: finish(): call(functools.partial(finish_kernel, places[0][0], places), 'finish', ja...]
    ppermute x6 -> x7, starting transfers between devices: 7.87 us -> 7.83 us  [to_next_section(): return lax.ppermute(value, ('ctx', 'pipe'), pairs)]
  transfers between devices with their start and end apart: 10 -> 12, of which waited for: 5 -> 5; matrix products, arithmetic and copies ran while one was open for 0% -> 0% of each run, Pallas kernels for 22% -> 22%
where the time goes in v7:
time: 34.2 us; the launch traced here: 33.9 us
  starting transfers between devices  16.4 us (48%)
  waiting for transfers between devices  8.32 us (24%)
  Pallas kernels  8.13 us (24%)
  between operations  1 us (3%)
    ppermute x5, starting transfers between devices, to_next_slab(): return lax.ppermute(value, ('ctx', 'pipe'), pairs)  8.6 us
    ppermute x7, starting transfers between devices, to_next_section(): return lax.ppermute(value, ('ctx', 'pipe'), pairs)  7.83 us
    ppermute x7, waiting for transfers between devices, to_next_section(): return lax.ppermute(value, ('ctx', 'pipe'), pairs)  6.77 us
    pallas_call x1, Pallas kernels, later_of(): call(functools.partial(later_kernel, places), 'later', (jax.ShapeDtypeStr...  2.59 us
    pallas_call x4, Pallas kernels, finish(): call(functools.partial(finish_kernel, places[0][0], places), 'finish', ja...  2.34 us
    pallas_call x1, Pallas kernels, product_of(): call(product_kernel, 'product', (array(rows, total), array(*lines.shape,...  1.74 us
    ppermute x5, waiting for transfers between devices, to_next_slab(): return lax.ppermute(value, ('ctx', 'pipe'), pairs)  1.55 us
    pallas_call x1, Pallas kernels, raw_finish(): call(raw_kernel, 'raw', jax.ShapeDtypeStruct(held.shape, BF16), [SMEM] +...  1.2 us
  transfers between devices with their start and end apart: 12, of which 5 were waited for; matrix products, arithmetic and copies ran while one was open for 0% of the time, Pallas kernels for 22%

profile of v7, /device:TPU:12, one launch (start us, length us, event | category | flops | bytes accessed | tf_op | source)
XLA Modules:
  0.0 33.9 jit_solution(14113365446788548431)
XLA Ops:
  0.0 0.0 copy-start.2
  0.0 0.0 copy-start.3
  0.0 0.0 copy-start.4
  0.0 0.1 lead.1
  0.1 0.0 copy-start
  0.2 0.0 copy-start.1
  0.2 0.9 %collective-permute-start = (bf16[128,3584]{1,0:T(8,128)(2,1)S(1)}, bf16[128,3584]{1,0:T(8,128)(2,1)S(1)}, u32[]{:S(2)}, u32[]{:S(2)}) collective-permute-start(bf16[128,3584]{1,0:T(8,128)(2,1)S(1)} %get-tuple-element.18.refs_6_.refs_3_), channel_id=1, source_target_pairs={{0,4},{8,12},{16,20},{24,28},{2,6},{10,14},{18,22},{26,30}} | collective-permute-start | bytes 2752520 | tf_op jit(solution)/shard_map/ppermute | solution.py:31
  1.0 1.3 %collective-permute-start.3 = (bf16[264,512]{1,0:T(8,128)(2,1)S(1)}, bf16[264,512]{1,0:T(8,128)(2,1)S(1)}, u32[]{:S(2)}, u32[]{:S(2)}) collective-permute-start(bf16[264,512]{1,0:T(8,128)(2,1)S(1)} %get-tuple-element.22.raw_ref), channel_id=1, source_target_pairs={{0,1},{4,5},{8,9},{12,13},{16,17},{20,21},{24,25},{28,29},{2,3},{6... | collective-permute-start | bytes 811016 | tf_op jit(solution)/shard_map/ppermute | solution.py:37
  2.3 0.0 copy-done.2
  2.3 0.0 copy-done.3
  2.3 0.0 copy-done.4
  2.4 1.7 %product.1 = (bf16[128,4096]{1,0:T(8,128)(2,1)S(1)}, f32[256,128]{1,0:T(8,128)S(1)}, bf16[128,1408]{1,0:T(8,128)(2,1)S(1)}, bf16[128,2176]{1,0:T(8,128)(2,1)S(1)}) custom-call(bf16[1,128,4096]{2,1,0:T(8,128)(2,1)} %refs_0_.10, bf16[1,128,4096]{2,1,0:T(8,128)(2,1)} %refs_1_.3, bf16[1,256,128]{2,1,0:T(8,128)(2,1)S(1)} %copy-done.2, ...), custom_call_target="tpu_custom_call", output_to_operand_aliasing={{1}: (5, {})} | custom-call | flops 1024 | bytes 1024 | tf_op jit(solution)/shard_map/product/pallas_call | solution.py:205
  4.7 0.0 collective-permute-done.refs_2_
  4.8 0.0 copy-done
  4.8 0.0 copy-done.1
  4.8 0.7 %collective-permute-start.4 = (bf16[128,1536]{1,0:T(8,128)(2,1)S(1)}, bf16[128,1536]{1,0:T(8,128)(2,1)S(1)}, u32[]{:S(2)}, u32[]{:S(2)}) collective-permute-start(bf16[128,1536]{1,0:T(8,128)(2,1)S(1)} %own.6._.refs_5_), channel_id=1, source_target_pairs={{4,5},{12,13},{20,21},{28,29},{6,7},{14,15},{22,23},{30,31}} | collective-permute-start | bytes 1179656 | tf_op jit(solution)/shard_map/ppermute | solution.py:37
  5.5 0.7 %collective-permute-start.2 = (bf16[128,1408]{1,0:T(8,128)(2,1)S(1)}, bf16[128,1408]{1,0:T(8,128)(2,1)S(1)}, u32[]{:S(2)}, u32[]{:S(2)}) collective-permute-start(bf16[128,1408]{1,0:T(8,128)(2,1)S(1)} %hold.5.refs_6_), channel_id=1, source_target_pairs={{4,8},{12,16},{20,24},{6,10},{14,18},{22,26}} | collective-permute-start | bytes 1081352 | tf_op jit(solution)/shard_map/ppermute | solution.py:31
  6.2 0.7 %collective-permute-start.6 = (bf16[128,2048]{1,0:T(8,128)(2,1)S(1)}, bf16[128,2048]{1,0:T(8,128)(2,1)S(1)}, u32[]{:S(2)}, u32[]{:S(2)}) collective-permute-start(bf16[128,2048]{1,0:T(8,128)(2,1)S(1)} %own.7._.refs_6_), channel_id=1, source_target_pairs={{4,5},{12,13},{20,21},{28,29},{6,7},{14,15},{22,23},{30,31}} | collective-permute-start | bytes 1572872 | tf_op jit(solution)/shard_map/ppermute | solution.py:37
  6.9 2.9 %collective-permute-start.1 = (bf16[128,4096]{1,0:T(8,128)(2,1)S(1)}, bf16[128,4096]{1,0:T(8,128)(2,1)S(1)}, u32[]{:S(2)}, u32[]{:S(2)}) collective-permute-start(bf16[128,4096]{1,0:T(8,128)(2,1)S(1)} %hold.6._.refs_3_), channel_id=1, source_target_pairs={{1,5},{5,9},{9,13},{13,17},{17,21},{21,25},{25,29},{3,7},{7,11},{1... | collective-permute-start | bytes 3145736 | tf_op jit(solution)/shard_map/ppermute | solution.py:31
  9.9 3.4 %collective-permute-done.3.received_ref = bf16[264,512]{1,0:T(8,128)(2,1)S(1)} collective-permute-done((bf16[264,512]{1,0:T(8,128)(2,1)S(1)}, bf16[264,512]{1,0:T(8,128)(2,1)S(1)}, u32[]{:S(2)}, u32[]{:S(2)}) %collective-permute-start.3) | collective-permute-done | bytes 270368 | tf_op jit(solution)/shard_map/ppermute | solution.py:37
  13.3 0.7 %collective-permute-start.5 = (bf16[128,2176]{1,0:T(8,128)(2,1)S(1)}, bf16[128,2176]{1,0:T(8,128)(2,1)S(1)}, u32[]{:S(2)}, u32[]{:S(2)}) collective-permute-start(bf16[128,2176]{1,0:T(8,128)(2,1)S(1)} %hold.8), channel_id=1, source_target_pairs={{4,8},{12,16},{20,24},{6,10},{14,18},{22,26}} | collective-permute-start | bytes 1671176 | tf_op jit(solution)/shard_map/ppermute | solution.py:31
  14.0 0.0 collective-permute-done.4._.refs_1_
  14.1 0.0 collective-permute-done.2.refs_2_
  14.1 1.3 %collective-permute-start.9 = (bf16[128,1408]{1,0:T(8,128)(2,1)S(1)}, bf16[128,1408]{1,0:T(8,128)(2,1)S(1)}, u32[]{:S(2)}, u32[]{:S(2)}) collective-permute-start(bf16[128,1408]{1,0:T(8,128)(2,1)S(1)} %own.8._.refs_7_), channel_id=1, source_target_pairs={{0,1},{8,9},{16,17},{24,25},{2,3},{10,11},{18,19},{26,27}} | collective-permute-start | bytes 1081352 | tf_op jit(solution)/shard_map/ppermute | solution.py:37
  15.4 3.4 %collective-permute-start.11 = (bf16[128,512]{1,0:T(8,128)(2,1)S(1)}, bf16[128,512]{1,0:T(8,128)(2,1)S(1)}, u32[]{:S(2)}, u32[]{:S(2)}) collective-permute-start(bf16[128,512]{1,0:T(8,128)(2,1)S(1)} %hold.9.refs_6_.refs_7_.product_ref), channel_id=1, source_target_pairs={{0,4},{1,5},{4,8},{5,9},{8,12},{9,13},{12,16},{13,17},{16,20},{17,... | collective-permute-start | bytes 393224 | tf_op jit(solution)/shard_map/ppermute | solution.py:31
  18.8 0.0 collective-permute-done.6.refs_7_.refs_2_
  18.9 0.0 collective-permute-done.5.refs_2_
  18.9 1.3 %collective-permute-start.10 = (bf16[128,768]{1,0:T(8,128)(2,1)S(1)}, bf16[128,768]{1,0:T(8,128)(2,1)S(1)}, u32[]{:S(2)}, u32[]{:S(2)}) collective-permute-start(bf16[128,768]{1,0:T(8,128)(2,1)S(1)} %own.9.refs_6_.refs_8_), channel_id=1, source_target_pairs={{0,1},{8,9},{16,17},{24,25},{2,3},{10,11},{18,19},{26,27}} | collective-permute-start | bytes 589832 | tf_op jit(solution)/shard_map/ppermute | solution.py:37
  20.2 1.3 %collective-permute-start.8 = (bf16[128,768]{1,0:T(8,128)(2,1)S(1)}, bf16[128,768]{1,0:T(8,128)(2,1)S(1)}, u32[]{:S(2)}, u32[]{:S(2)}) collective-permute-start(bf16[128,768]{1,0:T(8,128)(2,1)S(1)} %own.10.refs_6_.refs_9_), channel_id=1, source_target_pairs={{0,1},{8,9},{16,17},{24,25},{2,3},{10,11},{18,19},{26,27}} | collective-permute-start | bytes 589832 | tf_op jit(solution)/shard_map/ppermute | solution.py:37
  21.5 1.5 %collective-permute-done.1.refs_7_.refs_2_ = bf16[128,4096]{1,0:T(8,128)(2,1)S(1)} collective-permute-done((bf16[128,4096]{1,0:T(8,128)(2,1)S(1)}, bf16[128,4096]{1,0:T(8,128)(2,1)S(1)}, u32[]{:S(2)}, u32[]{:S(2)}) %collective-permute-start.1) | collective-permute-done | bytes 1048608 | tf_op jit(solution)/shard_map/ppermute | solution.py:31
  23.1 1.3 %collective-permute-start.7 = (bf16[128,640]{1,0:T(8,128)(2,1)S(1)}, bf16[128,640]{1,0:T(8,128)(2,1)S(1)}, u32[]{:S(2)}, u32[]{:S(2)}) collective-permute-start(bf16[128,640]{1,0:T(8,128)(2,1)S(1)} %own.11.refs_10_), channel_id=1, source_target_pairs={{0,1},{8,9},{16,17},{24,25},{2,3},{10,11},{18,19},{26,27}} | collective-permute-start | bytes 491528 | tf_op jit(solution)/shard_map/ppermute | solution.py:37
  24.4 2.6 %later.1 = (bf16[1,128,4096]{2,1,0:T(8,128)(2,1)}, f32[128,4096]{1,0:T(8,128)S(1)}) custom-call(s32[1]{0:T(128)S(6)} %copy.31.refs_0_.start_ref, f32[256,128]{1,0:T(8,128)S(1)} %get-tuple-element.19.refs_1_.refs_6_, bf16[128,4096]{1,0:T(8,128)(2,1)S(1)} %collective-permute-done.1.refs_7_.refs_2_, bf16[128,4096]{1,0:T(8,128)(2,1)S(1)} %hold.6._.refs_3_, ...), custom_call_target="tpu_custom_call" | custom-call | flops 20000000000 | bytes 1024 | tf_op jit(solution)/shard_map/later/pallas_call | solution.py:362
  27.0 0.0 collective-permute-done.11.behind_ref
  27.0 1.2 %raw.1.refs_3_ = bf16[1,128,4096]{2,1,0:T(8,128)(2,1)} custom-call(s32[1]{0:T(128)S(6)} %copy.31.refs_0_.start_ref, f32[32,128]{1,0:T(8,128)S(1)} %get-tuple-element.27.lines_ref, bf16[128,512]{1,0:T(8,128)(2,1)S(1)} %collective-permute-done.11.behind_ref, bf16[128,512]{1,0:T(8,128)(2,1)S(1)} %hold.9.refs_6_.refs_7_.product_ref, ...), custom_call_target="tpu_custom_call", output_to_operand_aliasing={{}: (7, {})} | custom-call | flops 20000000000 | bytes 1024 | tf_op jit(solution)/shard_map/raw/pallas_call | solution.py:393
  28.2 0.0 collective-permute-done.9.refs_1_
  28.2 1.1 %collective-permute-done.10.refs_2_ = bf16[128,768]{1,0:T(8,128)(2,1)S(1)} collective-permute-done((bf16[128,768]{1,0:T(8,128)(2,1)S(1)}, bf16[128,768]{1,0:T(8,128)(2,1)S(1)}, u32[]{:S(2)}, u32[]{:S(2)}) %collective-permute-start.10) | collective-permute-done | bytes 196640 | tf_op jit(solution)/shard_map/ppermute | solution.py:37
  29.3 0.9 %finish.5.refs_2_ = bf16[1,128,4096]{2,1,0:T(8,128)(2,1)} custom-call(f32[128,4096]{1,0:T(8,128)S(1)} %get-tuple-element.26.refs_0_.gated_ref, bf16[128,1408]{1,0:T(8,128)(2,1)S(1)} %collective-permute-done.9.refs_1_, bf16[128,768]{1,0:T(8,128)(2,1)S(1)} %collective-permute-done.10.refs_2_, ...), custom_call_target="tpu_custom_call", output_to_operand_aliasing={{}: (3, {})} | custom-call | flops 20000000000 | bytes 1024 | tf_op jit(solution)/shard_map/finish/pallas_call | solution.py:423
  30.2 1.2 %collective-permute-done.8.refs_1_ = bf16[128,768]{1,0:T(8,128)(2,1)S(1)} collective-permute-done((bf16[128,768]{1,0:T(8,128)(2,1)S(1)}, bf16[128,768]{1,0:T(8,128)(2,1)S(1)}, u32[]{:S(2)}, u32[]{:S(2)}) %collective-permute-start.8) | collective-permute-done | bytes 196640 | tf_op jit(solution)/shard_map/ppermute | solution.py:37
  31.4 0.7 %finish.6.refs_2_ = bf16[1,128,4096]{2,1,0:T(8,128)(2,1)} custom-call(f32[128,4096]{1,0:T(8,128)S(1)} %get-tuple-element.26.refs_0_.gated_ref, bf16[128,768]{1,0:T(8,128)(2,1)S(1)} %collective-permute-done.8.refs_1_, bf16[1,128,4096]{2,1,0:T(8,128)(2,1)} %finish.5.refs_2_), custom_call_target="tpu_custom_call", output_to_operand_aliasing={{}: (2, {})} | custom-call | flops 20000000000 | bytes 1024 | tf_op jit(solution)/shard_map/finish/pallas_call | solution.py:423
  32.2 1.0 %collective-permute-done.7.refs_1_ = bf16[128,640]{1,0:T(8,128)(2,1)S(1)} collective-permute-done((bf16[128,640]{1,0:T(8,128)(2,1)S(1)}, bf16[128,640]{1,0:T(8,128)(2,1)S(1)}, u32[]{:S(2)}, u32[]{:S(2)}) %collective-permute-start.7) | collective-permute-done | bytes 163872 | tf_op jit(solution)/shard_map/ppermute | solution.py:37
  33.2 0.7 %finish.7 = bf16[1,128,4096]{2,1,0:T(8,128)(2,1)} custom-call(f32[128,4096]{1,0:T(8,128)S(1)} %get-tuple-element.26.refs_0_.gated_ref, bf16[128,640]{1,0:T(8,128)(2,1)S(1)} %collective-permute-done.7.refs_1_, bf16[1,128,4096]{2,1,0:T(8,128)(2,1)} %finish.6.refs_2_), custom_call_target="tpu_custom_call", output_to_operand_aliasing={{}: (2, {})} | custom-call | flops 20000000000 | bytes 1024 | tf_op jit(solution)/shard_map/finish/pallas_call | solution.py:423
  (13 shorter events, 0.2 us)
Async XLA Ops:
  0.0 2.3 %copy-start.2 = (bf16[1,256,128]{2,1,0:T(8,128)(2,1)S(1)}, bf16[1,256,128]{2,1,0:T(8,128)(2,1)}, u32[]{:S(2)}) copy-start(bf16[1,256,128]{2,1,0:T(8,128)(2,1)} %refs_2_.3) | copy-start | bytes 196612
  0.0 2.3 %copy-start.3 = (f32[1,256]{1,0:T(1,128)S(1)}, f32[1,256]{1,0:T(1,128)}, u32[]{:S(2)}) copy-start(f32[1,256]{1,0:T(1,128)} %refs_3_.3) | copy-start | bytes 3076
  0.0 2.3 %copy-start.4 = (s32[1,256]{1,0:T(1,128)S(1)}, s32[1,256]{1,0:T(1,128)}, u32[]{:S(2)}) copy-start(s32[1,256]{1,0:T(1,128)} %refs_4_.10) | copy-start | bytes 3076
  0.1 4.6 %copy-start = (bf16[1,128,4096]{2,1,0:T(8,128)(2,1)S(1)}, bf16[1,128,4096]{2,1,0:T(8,128)(2,1)}, u32[]{:S(2)}) copy-start(bf16[1,128,4096]{2,1,0:T(8,128)(2,1)} %refs_4_.17) | copy-start | bytes 3145732
  0.2 4.6 %copy-start.1 = (bf16[128,4096]{1,0:T(8,128)(2,1)S(1)}, bf16[128,4096]{1,0:T(8,128)(2,1)}, u32[]{:S(2)}) copy-start(bf16[128,4096]{1,0:T(8,128)(2,1)} %residual_ref.1) | copy-start | bytes 3145732
  0.2 4.6 %collective-permute-start = (bf16[128,3584]{1,0:T(8,128)(2,1)S(1)}, bf16[128,3584]{1,0:T(8,128)(2,1)S(1)}, u32[]{:S(2)}, u32[]{:S(2)}) collective-permute-start(bf16[128,3584]{1,0:T(8,128)(2,1)S(1)} %get-tuple-element.18.refs_6_.refs_3_), channel_id=1, source_target_pairs={{0,4},{8,12},{16,20},{24,28},{2,6},{10,14},{18,22},{26,30}} | collective-permute-start | bytes 2752520 | tf_op jit(solution)/shard_map/ppermute | solution.py:31
  1.0 12.3 %collective-permute-start.3 = (bf16[264,512]{1,0:T(8,128)(2,1)S(1)}, bf16[264,512]{1,0:T(8,128)(2,1)S(1)}, u32[]{:S(2)}, u32[]{:S(2)}) collective-permute-start(bf16[264,512]{1,0:T(8,128)(2,1)S(1)} %get-tuple-element.22.raw_ref), channel_id=1, source_target_pairs={{0,1},{4,5},{8,9},{12,13},{16,17},{20,21},{24,25},{28,29},{2,3},{6... | collective-permute-start | bytes 811016 | tf_op jit(solution)/shard_map/ppermute | solution.py:37
  4.8 9.2 %collective-permute-start.4 = (bf16[128,1536]{1,0:T(8,128)(2,1)S(1)}, bf16[128,1536]{1,0:T(8,128)(2,1)S(1)}, u32[]{:S(2)}, u32[]{:S(2)}) collective-permute-start(bf16[128,1536]{1,0:T(8,128)(2,1)S(1)} %own.6._.refs_5_), channel_id=1, source_target_pairs={{4,5},{12,13},{20,21},{28,29},{6,7},{14,15},{22,23},{30,31}} | collective-permute-start | bytes 1179656 | tf_op jit(solution)/shard_map/ppermute | solution.py:37
  5.5 8.6 %collective-permute-start.2 = (bf16[128,1408]{1,0:T(8,128)(2,1)S(1)}, bf16[128,1408]{1,0:T(8,128)(2,1)S(1)}, u32[]{:S(2)}, u32[]{:S(2)}) collective-permute-start(bf16[128,1408]{1,0:T(8,128)(2,1)S(1)} %hold.5.refs_6_), channel_id=1, source_target_pairs={{4,8},{12,16},{20,24},{6,10},{14,18},{22,26}} | collective-permute-start | bytes 1081352 | tf_op jit(solution)/shard_map/ppermute | solution.py:31
  6.2 12.6 %collective-permute-start.6 = (bf16[128,2048]{1,0:T(8,128)(2,1)S(1)}, bf16[128,2048]{1,0:T(8,128)(2,1)S(1)}, u32[]{:S(2)}, u32[]{:S(2)}) collective-permute-start(bf16[128,2048]{1,0:T(8,128)(2,1)S(1)} %own.7._.refs_6_), channel_id=1, source_target_pairs={{4,5},{12,13},{20,21},{28,29},{6,7},{14,15},{22,23},{30,31}} | collective-permute-start | bytes 1572872 | tf_op jit(solution)/shard_map/ppermute | solution.py:37
  6.9 16.1 %collective-permute-start.1 = (bf16[128,4096]{1,0:T(8,128)(2,1)S(1)}, bf16[128,4096]{1,0:T(8,128)(2,1)S(1)}, u32[]{:S(2)}, u32[]{:S(2)}) collective-permute-start(bf16[128,4096]{1,0:T(8,128)(2,1)S(1)} %hold.6._.refs_3_), channel_id=1, source_target_pairs={{1,5},{5,9},{9,13},{13,17},{17,21},{21,25},{25,29},{3,7},{7,11},{1... | collective-permute-start | bytes 3145736 | tf_op jit(solution)/shard_map/ppermute | solution.py:31
  13.3 5.5 %collective-permute-start.5 = (bf16[128,2176]{1,0:T(8,128)(2,1)S(1)}, bf16[128,2176]{1,0:T(8,128)(2,1)S(1)}, u32[]{:S(2)}, u32[]{:S(2)}) collective-permute-start(bf16[128,2176]{1,0:T(8,128)(2,1)S(1)} %hold.8), channel_id=1, source_target_pairs={{4,8},{12,16},{20,24},{6,10},{14,18},{22,26}} | collective-permute-start | bytes 1671176 | tf_op jit(solution)/shard_map/ppermute | solution.py:31
  14.1 14.1 %collective-permute-start.9 = (bf16[128,1408]{1,0:T(8,128)(2,1)S(1)}, bf16[128,1408]{1,0:T(8,128)(2,1)S(1)}, u32[]{:S(2)}, u32[]{:S(2)}) collective-permute-start(bf16[128,1408]{1,0:T(8,128)(2,1)S(1)} %own.8._.refs_7_), channel_id=1, source_target_pairs={{0,1},{8,9},{16,17},{24,25},{2,3},{10,11},{18,19},{26,27}} | collective-permute-start | bytes 1081352 | tf_op jit(solution)/shard_map/ppermute | solution.py:37
  15.4 11.6 %collective-permute-start.11 = (bf16[128,512]{1,0:T(8,128)(2,1)S(1)}, bf16[128,512]{1,0:T(8,128)(2,1)S(1)}, u32[]{:S(2)}, u32[]{:S(2)}) collective-permute-start(bf16[128,512]{1,0:T(8,128)(2,1)S(1)} %hold.9.refs_6_.refs_7_.product_ref), channel_id=1, source_target_pairs={{0,4},{1,5},{4,8},{5,9},{8,12},{9,13},{12,16},{13,17},{16,20},{17,... | collective-permute-start | bytes 393224 | tf_op jit(solution)/shard_map/ppermute | solution.py:31
  18.9 10.4 %collective-permute-start.10 = (bf16[128,768]{1,0:T(8,128)(2,1)S(1)}, bf16[128,768]{1,0:T(8,128)(2,1)S(1)}, u32[]{:S(2)}, u32[]{:S(2)}) collective-permute-start(bf16[128,768]{1,0:T(8,128)(2,1)S(1)} %own.9.refs_6_.refs_8_), channel_id=1, source_target_pairs={{0,1},{8,9},{16,17},{24,25},{2,3},{10,11},{18,19},{26,27}} | collective-permute-start | bytes 589832 | tf_op jit(solution)/shard_map/ppermute | solution.py:37
  20.2 11.2 %collective-permute-start.8 = (bf16[128,768]{1,0:T(8,128)(2,1)S(1)}, bf16[128,768]{1,0:T(8,128)(2,1)S(1)}, u32[]{:S(2)}, u32[]{:S(2)}) collective-permute-start(bf16[128,768]{1,0:T(8,128)(2,1)S(1)} %own.10.refs_6_.refs_9_), channel_id=1, source_target_pairs={{0,1},{8,9},{16,17},{24,25},{2,3},{10,11},{18,19},{26,27}} | collective-permute-start | bytes 589832 | tf_op jit(solution)/shard_map/ppermute | solution.py:37
  23.1 10.1 %collective-permute-start.7 = (bf16[128,640]{1,0:T(8,128)(2,1)S(1)}, bf16[128,640]{1,0:T(8,128)(2,1)S(1)}, u32[]{:S(2)}, u32[]{:S(2)}) collective-permute-start(bf16[128,640]{1,0:T(8,128)(2,1)S(1)} %own.11.refs_10_), channel_id=1, source_target_pairs={{0,1},{8,9},{16,17},{24,25},{2,3},{10,11},{18,19},{26,27}} | collective-permute-start | bytes 491528 | tf_op jit(solution)/shard_map/ppermute | solution.py:37

commit v8 on v7

--- a/solution.py
+++ b/solution.py
@@ -9,9 +9,10 @@
 
 LANES = 128
 ROW_BLOCK = 32
-RAW = 512
-ODD = (1536, 2048)
-EVEN = (1408, 768, 768, 640)
+RAW = 384
+ODD = (1536, 2176)
+EVEN = (1024, 1024, 768, 896)
+NEAR = 2048
 LINES = 8
 F32 = jnp.float32
 BF16 = jnp.bfloat16
@@ -104,10 +105,10 @@
 
 def lead_kernel(*refs):
     bank_ref, scales_ref, assign_ref, queries_ref, keys_ref, values_ref = refs[:6]
-    raw_ref, rest_ref, lines_ref = refs[6:9]
+    raw_ref, whole_ref, lines_ref = refs[6:9]
     bank_in, scales_in, assign_in, keys_in, values_in, sems, own_sems = refs[9:]
-    rows, far = rest_ref.shape
-    step = far // 3 // LANES * LANES
+    rows, total = whole_ref.shape
+    step = total // 4 // LANES * LANES
 
     @pl.when(is_first())
     def _():
@@ -129,12 +130,13 @@
                 raw_ref[2 * rows :, part * LANES : (part + 1) * LANES] = taken
 
         targets = [
-            (raw_ref, rows, 0, RAW),
-            (rest_ref, 0, 0, step),
-            (rest_ref, 0, step, step),
-            (rest_ref, 0, 2 * step, far - 2 * step),
+            (whole_ref, 0, 0, step),
+            (whole_ref, 0, step, step),
+            (whole_ref, 0, 2 * step, step),
+            (whole_ref, 0, 3 * step, total - 3 * step),
         ]
         multiply(keys_ref, values_ref, keys_in, values_in, sems, 0, targets, taps)
+        raw_ref[rows : 2 * rows, :] = whole_ref[:, :RAW]
         copies[3].wait()
 
 
@@ -149,7 +151,7 @@
         "lead",
         (
             array(2 * rows + LINES, RAW),
-            array(rows, total - RAW),
+            array(rows, total),
             array(assign.shape[1], bank.shape[2], F32),
         ),
         [HBM] * 6,
@@ -174,15 +176,16 @@
 
 
 def product_kernel(*refs):
-    keys_ref, values_ref, bank_ref, scales_ref, assign_ref, _, rest_ref = refs[:7]
+    keys_ref, values_ref, bank_ref, scales_ref, assign_ref, _, whole_ref = refs[:7]
     out_ref, lines_ref, near_ref, far_ref, keys_in, values_in, sems = refs[7:]
     half = out_ref.shape[1] // 2
     near = near_ref.shape[1]
 
     @pl.when(jnp.logical_and(is_first(), is_slab(1)))
     def _():
-        near_ref[...] = rest_ref[:, :near]
-        far_ref[...] = rest_ref[:, near:]
+        near_ref[...] = whole_ref[:, RAW : RAW + near]
+        far_ref[:, : far_ref.shape[1] - RAW] = whole_ref[:, RAW + near :]
+        far_ref[:, far_ref.shape[1] - RAW :] = whole_ref[:, :RAW]
 
     @pl.when(jnp.logical_not(is_first()))
     def _():
@@ -199,18 +202,17 @@
         )
 
 
-def product_of(keys, values, bank, scales, assign, lines, rest):
+def product_of(keys, values, bank, scales, assign, lines, whole):
     rows, total = keys.shape[1:]
-    near = EVEN[0]
     return call(
         product_kernel,
         "product",
-        (array(rows, total), array(*lines.shape, F32), array(rows, near), array(rows, total - RAW - near)),
+        (array(rows, total), array(*lines.shape, F32), array(rows, NEAR), array(rows, total - NEAR)),
         [HBM, HBM] + [VMEM] * 5,
         (VMEM,) * 4,
         product_scratch(rows, total, 2),
         aliases={5: 1},
-    )(keys, values, bank, scales, assign, lines, rest)
+    )(keys, values, bank, scales, assign, lines, whole)
 
 
 def mix(table_ref, row, share, window, store):
@@ -274,7 +276,7 @@
 def own_of(odd, origin, start, lines, behind, product, queries, residual, first, width, weight, *after):
     rows, total = residual.shape
     return call(
-        functools.partial(own_kernel, odd, first, first - origin, first - RAW),
+        functools.partial(own_kernel, odd, first, first - origin, first),
         "own",
         array(rows, width),
         [SMEM] + [VMEM] * 5 + [ANY] * len(after),
@@ -370,16 +372,28 @@
     )(start, lines, behind, product, queries, *own)
 
 
-def raw_kernel(start_ref, lines_ref, behind_ref, product_ref, queries_ref, gated_ref, residual_ref, _, *refs):
-    out_ref, table_ref, buffer, sems = refs
+def raw_kernel(*refs):
+    start_ref, lines_ref, behind_ref, chip_ref, far_ref, product_ref, queries_ref, gated_ref, residual_ref = refs[:9]
+    out_ref, chosen_ref, table_ref, buffer, sems = refs[10:]
     width = buffer.shape[1]
     share = share_of(lines_ref, width)
+    far = far_ref.shape[1]
+    sources = (
+        (jnp.logical_and(is_first(), is_slab(0)), far_ref, slice(far - width, far)),
+        (jnp.logical_and(is_first(), is_slab(1)), chip_ref, slice(0, width)),
+        (jnp.logical_not(is_first()), behind_ref, slice(0, width)),
+    )
+    for wanted, source, cols in sources:
+
+        @pl.when(wanted)
+        def _():
+            chosen_ref[...] = source[:, cols]
 
     def store(at, span, mixed):
         gated = queries_ref[span, at].astype(F32) * mixed
         buffer[span, at] = (residual_ref[span, at].astype(F32) + gated).astype(BF16)
 
-    mix_all(width, share, lines_ref, 0, table_ref, start_ref, behind_ref, product_ref, (0, 0), store)
+    mix_all(width, share, lines_ref, 0, table_ref, start_ref, chosen_ref, product_ref, (0, 0), store)
 
     @pl.when(jnp.logical_not(is_first()))
     def _():
@@ -388,18 +402,23 @@
     wait_all(send_out([(buffer, 0)], out_ref, sems))
 
 
-def raw_finish(held, start, lines, behind, product, queries, gated, residual):
+def raw_finish(held, start, lines, behind, chip_behind, far_behind, product, queries, gated, residual):
     rows, width = product.shape
     return call(
         raw_kernel,
         "raw",
         jax.ShapeDtypeStruct(held.shape, BF16),
-        [SMEM] + [VMEM] * 6 + [ANY],
+        [SMEM] + [VMEM] * 8 + [ANY],
         ANY,
-        [table_scratch(lines, width, width), pltpu.VMEM((rows, width), BF16), pltpu.SemaphoreType.DMA((1,))],
+        [
+            pltpu.VMEM((rows, width), BF16),
+            table_scratch(lines, width, width),
+            pltpu.VMEM((rows, width), BF16),
+            pltpu.SemaphoreType.DMA((1,)),
+        ],
         weight=SLOW,
-        aliases={7: 0},
-    )(start, lines, behind, product, queries, gated, residual, held)
+        aliases={9: 0},
+    )(start, lines, behind, chip_behind, far_behind, product, queries, gated, residual, held)
 
 
 def finish_kernel(odd, places, *refs):
@@ -439,25 +458,25 @@
     far_queries, keys, values = (
         pltpu.with_memory_space_constraint(value, pltpu.HBM) for value in (queries, keys, values)
     )
-    raw, rest, lines = lead_of(*far_small, far_queries, keys, values)
+    raw, whole, lines = lead_of(*far_small, far_queries, keys, values)
     raw_received = to_next_section(raw)
-    chip_behind = to_next_slab(rest, (0,), (0,))
-    product, lines, near, far = product_of(keys, values, *small, lines, rest)
+    chip_behind = to_next_slab(whole, (0,), (0,))
+    product, lines, near, far = product_of(keys, values, *small, lines, whole)
     own, received, places = [], [], []
 
     def send(odd, behind, origin, first, width, weight, *after):
         piece = own_of(
-            odd, origin, context_start, lines, behind, rest, queries, residual, first, width, weight, *after
+            odd, origin, context_start, lines, behind, whole, queries, residual, first, width, weight, *after
         )
         own.append(piece)
         received.append(to_next_section(piece, (odd,)))
         places.append((odd, first, width))
         return first + width, piece
 
-    first, after = send(1, chip_behind, RAW, RAW, ODD[0], QUICK, lines)
+    first, after = send(1, chip_behind, 0, RAW, ODD[0], QUICK, lines)
     near = held_back(near, after)
     near_behind = to_next_slab(near, (0,), (1,))
-    first, after = send(1, chip_behind, RAW, first, ODD[1], QUICK, near)
+    first, after = send(1, chip_behind, 0, first, ODD[1], QUICK, near)
     product = held_back(product, after)
     behind = to_next_slab(product, (1,))
     raw_queries, raw_product, raw_lines = pick_of(raw, raw_received, lines.shape[1], product)
@@ -465,14 +484,27 @@
     raw_queries = held_back(raw_queries, received[0], SLOW)
     first, after = send(0, near_behind, RAW, RAW, EVEN[0], SLOW, raw_queries)
     raw_product = held_back(raw_product, after)
-    raw_behind = to_next_slab(raw_product, (0, 1))
-    origin, after = first, raw_product
+    raw_behind = to_next_slab(raw_product, (1,))
+    after = raw_product
     for width, passed in zip(EVEN[1:], (received[1], after, behind)):
-        first, after = send(0, far_behind, origin, first, width, SLOW, after, passed)
+        origin = RAW if first < RAW + NEAR else RAW + NEAR
+        source = near_behind if first < RAW + NEAR else far_behind
+        first, after = send(0, source, origin, first, width, SLOW, after, passed)
     held, gated = later_of(context_start, lines, behind, product, queries, own, places)
     odd = len(ODD)
     held = finish(held, gated, received[:odd], places[:odd])
-    held = raw_finish(held, context_start, raw_lines, raw_behind, raw_product, raw_queries, gated, residual)
+    held = raw_finish(
+        held,
+        context_start,
+        raw_lines,
+        raw_behind,
+        chip_behind,
+        far_behind,
+        raw_product,
+        raw_queries,
+        gated,
+        residual,
+    )
     for last in (odd + 2, odd + 3, odd + 4):
         begin = odd if last == odd + 2 else last - 1
         held = finish(held, gated, received[begin:last], places[begin:last])

time: 34.2 us -> 33.1 us (0.968)
  waiting for transfers between devices: 8.32 us -> 5.69 us
  starting transfers between devices: 16.4 us -> 17.9 us
    ppermute x7, waiting for transfers between devices: 6.77 us -> 2.76 us  [to_next_section(): return lax.ppermute(value, ('ctx', 'pipe'), pairs)]
    ppermute x5, starting transfers between devices: 8.6 us -> 10 us  [to_next_slab(): return lax.ppermute(value, ('ctx', 'pipe'), pairs)]
    ppermute x5, waiting for transfers between devices: 1.55 us -> 2.93 us  [to_next_slab(): return lax.ppermute(value, ('ctx', 'pipe'), pairs)]
  transfers between devices with their start and end apart: 12 -> 12, of which waited for: 5 -> 4; matrix products, arithmetic and copies ran while one was open for 0% -> 0% of each run, Pallas kernels for 22% -> 22%
where the time goes in v8:
time: 33.1 us; the launch traced here: 32.7 us
  starting transfers between devices  17.9 us (54%)
  Pallas kernels  8.16 us (25%)
  waiting for transfers between devices  5.69 us (17%)
  between operations  1.01 us (3%)
    ppermute x5, starting transfers between devices, to_next_slab(): return lax.ppermute(value, ('ctx', 'pipe'), pairs)  10 us
    ppermute x7, starting transfers between devices, to_next_section(): return lax.ppermute(value, ('ctx', 'pipe'), pairs)  7.83 us
    ppermute x5, waiting for transfers between devices, to_next_slab(): return lax.ppermute(value, ('ctx', 'pipe'), pairs)  2.93 us
    ppermute x7, waiting for transfers between devices, to_next_section(): return lax.ppermute(value, ('ctx', 'pipe'), pairs)  2.76 us
    pallas_call x1, Pallas kernels, later_of(): call(functools.partial(later_kernel, places), 'later', (jax.ShapeDtypeStr...  2.59 us
    pallas_call x4, Pallas kernels, finish(): call(functools.partial(finish_kernel, places[0][0], places), 'finish', ja...  2.41 us
    pallas_call x1, Pallas kernels, product_of(): call(product_kernel, 'product', (array(rows, total), array(*lines.shape,...  1.74 us
    pallas_call x1, Pallas kernels, raw_finish(): call(raw_kernel, 'raw', jax.ShapeDtypeStruct(held.shape, BF16), [SMEM] +...  1.15 us
  transfers between devices with their start and end apart: 12, of which 4 were waited for; matrix products, arithmetic and copies ran while one was open for 0% of the time, Pallas kernels for 22%

profile of v8, /device:TPU:12, one launch (start us, length us, event | category | flops | bytes accessed | tf_op | source)
XLA Modules:
  0.0 32.7 jit_solution(877285871212337035)
XLA Ops:
  0.0 0.0 copy-start.2
  0.0 0.0 copy-start.3
  0.0 0.0 copy-start.4
  0.0 0.1 lead.1
  0.1 0.0 copy-start
  0.2 0.0 copy-start.1
  0.2 0.9 %collective-permute-start = (bf16[128,4096]{1,0:T(8,128)(2,1)S(1)}, bf16[128,4096]{1,0:T(8,128)(2,1)S(1)}, u32[]{:S(2)}, u32[]{:S(2)}) collective-permute-start(bf16[128,4096]{1,0:T(8,128)(2,1)S(1)} %get-tuple-element.18.refs_6_.refs_3_), channel_id=1, source_target_pairs={{0,4},{8,12},{16,20},{24,28},{2,6},{10,14},{18,22},{26,30}} | collective-permute-start | bytes 3145736 | tf_op jit(solution)/shard_map/ppermute | solution.py:32
  1.0 1.3 %collective-permute-start.3 = (bf16[264,384]{1,0:T(8,128)(2,1)S(1)}, bf16[264,384]{1,0:T(8,128)(2,1)S(1)}, u32[]{:S(2)}, u32[]{:S(2)}) collective-permute-start(bf16[264,384]{1,0:T(8,128)(2,1)S(1)} %get-tuple-element.22.raw_ref), channel_id=1, source_target_pairs={{0,1},{4,5},{8,9},{12,13},{16,17},{20,21},{24,25},{28,29},{2,3},{6... | collective-permute-start | bytes 608264 | tf_op jit(solution)/shard_map/ppermute | solution.py:38
  2.3 0.0 copy-done.2
  2.3 0.0 copy-done.3
  2.4 0.0 copy-done.4
  2.4 1.7 %product.1 = (bf16[128,4096]{1,0:T(8,128)(2,1)S(1)}, f32[256,128]{1,0:T(8,128)S(1)}, bf16[128,2048]{1,0:T(8,128)(2,1)S(1)}, bf16[128,2048]{1,0:T(8,128)(2,1)S(1)}) custom-call(bf16[1,128,4096]{2,1,0:T(8,128)(2,1)} %refs_0_.11, bf16[1,128,4096]{2,1,0:T(8,128)(2,1)} %refs_1_.3, bf16[1,256,128]{2,1,0:T(8,128)(2,1)S(1)} %copy-done.2, ...), custom_call_target="tpu_custom_call", output_to_operand_aliasing={{1}: (5, {})} | custom-call | flops 1024 | bytes 1024 | tf_op jit(solution)/shard_map/product/pallas_call | solution.py:207
  4.8 0.0 collective-permute-done.refs_2_.refs_3_
  4.8 0.0 copy-done
  4.8 0.0 copy-done.1
  4.8 0.7 %collective-permute-start.4 = (bf16[128,1536]{1,0:T(8,128)(2,1)S(1)}, bf16[128,1536]{1,0:T(8,128)(2,1)S(1)}, u32[]{:S(2)}, u32[]{:S(2)}) collective-permute-start(bf16[128,1536]{1,0:T(8,128)(2,1)S(1)} %own.6._.refs_5_), channel_id=1, source_target_pairs={{4,5},{12,13},{20,21},{28,29},{6,7},{14,15},{22,23},{30,31}} | collective-permute-start | bytes 1179656 | tf_op jit(solution)/shard_map/ppermute | solution.py:38
  5.5 0.7 %collective-permute-start.2 = (bf16[128,2048]{1,0:T(8,128)(2,1)S(1)}, bf16[128,2048]{1,0:T(8,128)(2,1)S(1)}, u32[]{:S(2)}, u32[]{:S(2)}) collective-permute-start(bf16[128,2048]{1,0:T(8,128)(2,1)S(1)} %hold.5.refs_6_), channel_id=1, source_target_pairs={{4,8},{12,16},{20,24},{6,10},{14,18},{22,26}} | collective-permute-start | bytes 1572872 | tf_op jit(solution)/shard_map/ppermute | solution.py:32
  6.2 0.7 %collective-permute-start.5 = (bf16[128,2176]{1,0:T(8,128)(2,1)S(1)}, bf16[128,2176]{1,0:T(8,128)(2,1)S(1)}, u32[]{:S(2)}, u32[]{:S(2)}) collective-permute-start(bf16[128,2176]{1,0:T(8,128)(2,1)S(1)} %own.7._.refs_6_), channel_id=1, source_target_pairs={{4,5},{12,13},{20,21},{28,29},{6,7},{14,15},{22,23},{30,31}} | collective-permute-start | bytes 1671176 | tf_op jit(solution)/shard_map/ppermute | solution.py:38
  7.0 2.9 %collective-permute-start.1 = (bf16[128,4096]{1,0:T(8,128)(2,1)S(1)}, bf16[128,4096]{1,0:T(8,128)(2,1)S(1)}, u32[]{:S(2)}, u32[]{:S(2)}) collective-permute-start(bf16[128,4096]{1,0:T(8,128)(2,1)S(1)} %hold.6._.refs_3_), channel_id=1, source_target_pairs={{1,5},{5,9},{9,13},{13,17},{17,21},{21,25},{25,29},{3,7},{7,11},{1... | collective-permute-start | bytes 3145736 | tf_op jit(solution)/shard_map/ppermute | solution.py:32
  9.9 0.6 %collective-permute-done.3.received_ref = bf16[264,384]{1,0:T(8,128)(2,1)S(1)} collective-permute-done((bf16[264,384]{1,0:T(8,128)(2,1)S(1)}, bf16[264,384]{1,0:T(8,128)(2,1)S(1)}, u32[]{:S(2)}, u32[]{:S(2)}) %collective-permute-start.3) | collective-permute-done | bytes 202784 | tf_op jit(solution)/shard_map/ppermute | solution.py:38
  10.6 0.7 %collective-permute-start.6 = (bf16[128,2048]{1,0:T(8,128)(2,1)S(1)}, bf16[128,2048]{1,0:T(8,128)(2,1)S(1)}, u32[]{:S(2)}, u32[]{:S(2)}) collective-permute-start(bf16[128,2048]{1,0:T(8,128)(2,1)S(1)} %hold.9), channel_id=1, source_target_pairs={{4,8},{12,16},{20,24},{6,10},{14,18},{22,26}} | collective-permute-start | bytes 1572872 | tf_op jit(solution)/shard_map/ppermute | solution.py:32
  11.3 0.0 collective-permute-done.4._.refs_1_
  11.3 0.0 collective-permute-done.2.refs_2_
  11.3 1.3 %collective-permute-start.9 = (bf16[128,1024]{1,0:T(8,128)(2,1)S(1)}, bf16[128,1024]{1,0:T(8,128)(2,1)S(1)}, u32[]{:S(2)}, u32[]{:S(2)}) collective-permute-start(bf16[128,1024]{1,0:T(8,128)(2,1)S(1)} %own.8._.refs_7_), channel_id=1, source_target_pairs={{0,1},{8,9},{16,17},{24,25},{2,3},{10,11},{18,19},{26,27}} | collective-permute-start | bytes 786440 | tf_op jit(solution)/shard_map/ppermute | solution.py:38
  12.6 4.8 %collective-permute-start.11 = (bf16[128,384]{1,0:T(8,128)(2,1)S(1)}, bf16[128,384]{1,0:T(8,128)(2,1)S(1)}, u32[]{:S(2)}, u32[]{:S(2)}) collective-permute-start(bf16[128,384]{1,0:T(8,128)(2,1)S(1)} %hold.8.refs_6_.refs_7_.refs_5_), channel_id=1, source_target_pairs={{1,5},{5,9},{9,13},{13,17},{17,21},{21,25},{25,29},{3,7},{7,11},{1... | collective-permute-start | bytes 294920 | tf_op jit(solution)/shard_map/ppermute | solution.py:32
  17.5 0.0 collective-permute-done.5.refs_7_.refs_2_
  17.5 1.3 %collective-permute-start.10 = (bf16[128,1024]{1,0:T(8,128)(2,1)S(1)}, bf16[128,1024]{1,0:T(8,128)(2,1)S(1)}, u32[]{:S(2)}, u32[]{:S(2)}) collective-permute-start(bf16[128,1024]{1,0:T(8,128)(2,1)S(1)} %own.9.refs_6_.refs_8_), channel_id=1, source_target_pairs={{0,1},{8,9},{16,17},{24,25},{2,3},{10,11},{18,19},{26,27}} | collective-permute-start | bytes 786440 | tf_op jit(solution)/shard_map/ppermute | solution.py:38
  18.8 0.0 collective-permute-done.6.refs_2_.refs_4_
  18.9 1.3 %collective-permute-start.8 = (bf16[128,768]{1,0:T(8,128)(2,1)S(1)}, bf16[128,768]{1,0:T(8,128)(2,1)S(1)}, u32[]{:S(2)}, u32[]{:S(2)}) collective-permute-start(bf16[128,768]{1,0:T(8,128)(2,1)S(1)} %own.10.refs_6_.refs_9_), channel_id=1, source_target_pairs={{0,1},{8,9},{16,17},{24,25},{2,3},{10,11},{18,19},{26,27}} | collective-permute-start | bytes 589832 | tf_op jit(solution)/shard_map/ppermute | solution.py:38
  20.2 2.9 %collective-permute-done.1.refs_7_.refs_2_ = bf16[128,4096]{1,0:T(8,128)(2,1)S(1)} collective-permute-done((bf16[128,4096]{1,0:T(8,128)(2,1)S(1)}, bf16[128,4096]{1,0:T(8,128)(2,1)S(1)}, u32[]{:S(2)}, u32[]{:S(2)}) %collective-permute-start.1) | collective-permute-done | bytes 1048608 | tf_op jit(solution)/shard_map/ppermute | solution.py:32
  23.1 1.3 %collective-permute-start.7 = (bf16[128,896]{1,0:T(8,128)(2,1)S(1)}, bf16[128,896]{1,0:T(8,128)(2,1)S(1)}, u32[]{:S(2)}, u32[]{:S(2)}) collective-permute-start(bf16[128,896]{1,0:T(8,128)(2,1)S(1)} %own.11.refs_10_), channel_id=1, source_target_pairs={{0,1},{8,9},{16,17},{24,25},{2,3},{10,11},{18,19},{26,27}} | collective-permute-start | bytes 688136 | tf_op jit(solution)/shard_map/ppermute | solution.py:38
  24.4 2.6 %later.1 = (bf16[1,128,4096]{2,1,0:T(8,128)(2,1)}, f32[128,4096]{1,0:T(8,128)S(1)}) custom-call(s32[1]{0:T(128)S(6)} %copy.31.refs_0_, f32[256,128]{1,0:T(8,128)S(1)} %get-tuple-element.19.refs_1_.refs_6_, bf16[128,4096]{1,0:T(8,128)(2,1)S(1)} %collective-permute-done.1.refs_7_.refs_2_, bf16[128,4096]{1,0:T(8,128)(2,1)S(1)} %hold.6._.refs_3_, ...), custom_call_target="tpu_custom_call" | custom-call | flops 20000000000 | bytes 1024 | tf_op jit(solution)/shard_map/later/pallas_call | solution.py:364
  27.0 0.0 collective-permute-done.11.refs_2_
  27.0 1.2 %raw.1.refs_3_ = bf16[1,128,4096]{2,1,0:T(8,128)(2,1)} custom-call(s32[1]{0:T(128)S(6)} %copy.31.refs_0_, f32[24,128]{1,0:T(8,128)S(1)} %get-tuple-element.27.refs_1_, bf16[128,384]{1,0:T(8,128)(2,1)S(1)} %collective-permute-done.11.refs_2_, bf16[128,4096]{1,0:T(8,128)(2,1)S(1)} %collective-permute-done.refs_2_.refs_3_, ...), custom_call_target="tpu_custom_call", output_to_operand_aliasing={{}: (9, {})} | custom-call | flops 20000000000 | bytes 1024 | tf_op jit(solution)/shard_map/raw/pallas_call | solution.py:407
  28.2 0.0 collective-permute-done.9.refs_1_
  28.2 0.0 collective-permute-done.10.refs_2_
  28.2 0.9 %finish.5.refs_2_ = bf16[1,128,4096]{2,1,0:T(8,128)(2,1)} custom-call(f32[128,4096]{1,0:T(8,128)S(1)} %get-tuple-element.26.refs_0_.refs_7_, bf16[128,1024]{1,0:T(8,128)(2,1)S(1)} %collective-permute-done.9.refs_1_, bf16[128,1024]{1,0:T(8,128)(2,1)S(1)} %collective-permute-done.10.refs_2_, ...), custom_call_target="tpu_custom_call", output_to_operand_aliasing={{}: (3, {})} | custom-call | flops 20000000000 | bytes 1024 | tf_op jit(solution)/shard_map/finish/pallas_call | solution.py:442
  29.1 0.4 %collective-permute-done.8.refs_1_ = bf16[128,768]{1,0:T(8,128)(2,1)S(1)} collective-permute-done((bf16[128,768]{1,0:T(8,128)(2,1)S(1)}, bf16[128,768]{1,0:T(8,128)(2,1)S(1)}, u32[]{:S(2)}, u32[]{:S(2)}) %collective-permute-start.8) | collective-permute-done | bytes 196640 | tf_op jit(solution)/shard_map/ppermute | solution.py:38
  29.5 0.7 %finish.6.refs_2_ = bf16[1,128,4096]{2,1,0:T(8,128)(2,1)} custom-call(f32[128,4096]{1,0:T(8,128)S(1)} %get-tuple-element.26.refs_0_.refs_7_, bf16[128,768]{1,0:T(8,128)(2,1)S(1)} %collective-permute-done.8.refs_1_, bf16[1,128,4096]{2,1,0:T(8,128)(2,1)} %finish.5.refs_2_), custom_call_target="tpu_custom_call", output_to_operand_aliasing={{}: (2, {})} | custom-call | flops 20000000000 | bytes 1024 | tf_op jit(solution)/shard_map/finish/pallas_call | solution.py:442
  30.3 1.7 %collective-permute-done.7.refs_1_ = bf16[128,896]{1,0:T(8,128)(2,1)S(1)} collective-permute-done((bf16[128,896]{1,0:T(8,128)(2,1)S(1)}, bf16[128,896]{1,0:T(8,128)(2,1)S(1)}, u32[]{:S(2)}, u32[]{:S(2)}) %collective-permute-start.7) | collective-permute-done | bytes 229408 | tf_op jit(solution)/shard_map/ppermute | solution.py:38
  32.0 0.8 %finish.7 = bf16[1,128,4096]{2,1,0:T(8,128)(2,1)} custom-call(f32[128,4096]{1,0:T(8,128)S(1)} %get-tuple-element.26.refs_0_.refs_7_, bf16[128,896]{1,0:T(8,128)(2,1)S(1)} %collective-permute-done.7.refs_1_, bf16[1,128,4096]{2,1,0:T(8,128)(2,1)} %finish.6.refs_2_), custom_call_target="tpu_custom_call", output_to_operand_aliasing={{}: (2, {})} | custom-call | flops 20000000000 | bytes 1024 | tf_op jit(solution)/shard_map/finish/pallas_call | solution.py:442
  (13 shorter events, 0.2 us)
Async XLA Ops:
  0.0 2.3 %copy-start.2 = (bf16[1,256,128]{2,1,0:T(8,128)(2,1)S(1)}, bf16[1,256,128]{2,1,0:T(8,128)(2,1)}, u32[]{:S(2)}) copy-start(bf16[1,256,128]{2,1,0:T(8,128)(2,1)} %refs_2_.3) | copy-start | bytes 196612
  0.0 2.3 %copy-start.3 = (f32[1,256]{1,0:T(1,128)S(1)}, f32[1,256]{1,0:T(1,128)}, u32[]{:S(2)}) copy-start(f32[1,256]{1,0:T(1,128)} %refs_3_.3) | copy-start | bytes 3076
  0.0 2.3 %copy-start.4 = (s32[1,256]{1,0:T(1,128)S(1)}, s32[1,256]{1,0:T(1,128)}, u32[]{:S(2)}) copy-start(s32[1,256]{1,0:T(1,128)} %refs_4_.10) | copy-start | bytes 3076
  0.1 4.6 %copy-start = (bf16[1,128,4096]{2,1,0:T(8,128)(2,1)S(1)}, bf16[1,128,4096]{2,1,0:T(8,128)(2,1)}, u32[]{:S(2)}) copy-start(bf16[1,128,4096]{2,1,0:T(8,128)(2,1)} %refs_4_.17) | copy-start | bytes 3145732
  0.2 4.6 %copy-start.1 = (bf16[128,4096]{1,0:T(8,128)(2,1)S(1)}, bf16[128,4096]{1,0:T(8,128)(2,1)}, u32[]{:S(2)}) copy-start(bf16[128,4096]{1,0:T(8,128)(2,1)} %refs_8_.1) | copy-start | bytes 3145732
  0.2 4.6 %collective-permute-start = (bf16[128,4096]{1,0:T(8,128)(2,1)S(1)}, bf16[128,4096]{1,0:T(8,128)(2,1)S(1)}, u32[]{:S(2)}, u32[]{:S(2)}) collective-permute-start(bf16[128,4096]{1,0:T(8,128)(2,1)S(1)} %get-tuple-element.18.refs_6_.refs_3_), channel_id=1, source_target_pairs={{0,4},{8,12},{16,20},{24,28},{2,6},{10,14},{18,22},{26,30}} | collective-permute-start | bytes 3145736 | tf_op jit(solution)/shard_map/ppermute | solution.py:32
  1.0 9.5 %collective-permute-start.3 = (bf16[264,384]{1,0:T(8,128)(2,1)S(1)}, bf16[264,384]{1,0:T(8,128)(2,1)S(1)}, u32[]{:S(2)}, u32[]{:S(2)}) collective-permute-start(bf16[264,384]{1,0:T(8,128)(2,1)S(1)} %get-tuple-element.22.raw_ref), channel_id=1, source_target_pairs={{0,1},{4,5},{8,9},{12,13},{16,17},{20,21},{24,25},{28,29},{2,3},{6... | collective-permute-start | bytes 608264 | tf_op jit(solution)/shard_map/ppermute | solution.py:38
  4.8 6.4 %collective-permute-start.4 = (bf16[128,1536]{1,0:T(8,128)(2,1)S(1)}, bf16[128,1536]{1,0:T(8,128)(2,1)S(1)}, u32[]{:S(2)}, u32[]{:S(2)}) collective-permute-start(bf16[128,1536]{1,0:T(8,128)(2,1)S(1)} %own.6._.refs_5_), channel_id=1, source_target_pairs={{4,5},{12,13},{20,21},{28,29},{6,7},{14,15},{22,23},{30,31}} | collective-permute-start | bytes 1179656 | tf_op jit(solution)/shard_map/ppermute | solution.py:38
  5.5 5.8 %collective-permute-start.2 = (bf16[128,2048]{1,0:T(8,128)(2,1)S(1)}, bf16[128,2048]{1,0:T(8,128)(2,1)S(1)}, u32[]{:S(2)}, u32[]{:S(2)}) collective-permute-start(bf16[128,2048]{1,0:T(8,128)(2,1)S(1)} %hold.5.refs_6_), channel_id=1, source_target_pairs={{4,8},{12,16},{20,24},{6,10},{14,18},{22,26}} | collective-permute-start | bytes 1572872 | tf_op jit(solution)/shard_map/ppermute | solution.py:32
  6.2 11.2 %collective-permute-start.5 = (bf16[128,2176]{1,0:T(8,128)(2,1)S(1)}, bf16[128,2176]{1,0:T(8,128)(2,1)S(1)}, u32[]{:S(2)}, u32[]{:S(2)}) collective-permute-start(bf16[128,2176]{1,0:T(8,128)(2,1)S(1)} %own.7._.refs_6_), channel_id=1, source_target_pairs={{4,5},{12,13},{20,21},{28,29},{6,7},{14,15},{22,23},{30,31}} | collective-permute-start | bytes 1671176 | tf_op jit(solution)/shard_map/ppermute | solution.py:38
  7.0 16.1 %collective-permute-start.1 = (bf16[128,4096]{1,0:T(8,128)(2,1)S(1)}, bf16[128,4096]{1,0:T(8,128)(2,1)S(1)}, u32[]{:S(2)}, u32[]{:S(2)}) collective-permute-start(bf16[128,4096]{1,0:T(8,128)(2,1)S(1)} %hold.6._.refs_3_), channel_id=1, source_target_pairs={{1,5},{5,9},{9,13},{13,17},{17,21},{21,25},{25,29},{3,7},{7,11},{1... | collective-permute-start | bytes 3145736 | tf_op jit(solution)/shard_map/ppermute | solution.py:32
  10.6 8.3 %collective-permute-start.6 = (bf16[128,2048]{1,0:T(8,128)(2,1)S(1)}, bf16[128,2048]{1,0:T(8,128)(2,1)S(1)}, u32[]{:S(2)}, u32[]{:S(2)}) collective-permute-start(bf16[128,2048]{1,0:T(8,128)(2,1)S(1)} %hold.9), channel_id=1, source_target_pairs={{4,8},{12,16},{20,24},{6,10},{14,18},{22,26}} | collective-permute-start | bytes 1572872 | tf_op jit(solution)/shard_map/ppermute | solution.py:32
  11.3 16.9 %collective-permute-start.9 = (bf16[128,1024]{1,0:T(8,128)(2,1)S(1)}, bf16[128,1024]{1,0:T(8,128)(2,1)S(1)}, u32[]{:S(2)}, u32[]{:S(2)}) collective-permute-start(bf16[128,1024]{1,0:T(8,128)(2,1)S(1)} %own.8._.refs_7_), channel_id=1, source_target_pairs={{0,1},{8,9},{16,17},{24,25},{2,3},{10,11},{18,19},{26,27}} | collective-permute-start | bytes 786440 | tf_op jit(solution)/shard_map/ppermute | solution.py:38
  12.6 14.4 %collective-permute-start.11 = (bf16[128,384]{1,0:T(8,128)(2,1)S(1)}, bf16[128,384]{1,0:T(8,128)(2,1)S(1)}, u32[]{:S(2)}, u32[]{:S(2)}) collective-permute-start(bf16[128,384]{1,0:T(8,128)(2,1)S(1)} %hold.8.refs_6_.refs_7_.refs_5_), channel_id=1, source_target_pairs={{1,5},{5,9},{9,13},{13,17},{17,21},{21,25},{25,29},{3,7},{7,11},{1... | collective-permute-start | bytes 294920 | tf_op jit(solution)/shard_map/ppermute | solution.py:32
  17.5 10.7 %collective-permute-start.10 = (bf16[128,1024]{1,0:T(8,128)(2,1)S(1)}, bf16[128,1024]{1,0:T(8,128)(2,1)S(1)}, u32[]{:S(2)}, u32[]{:S(2)}) collective-permute-start(bf16[128,1024]{1,0:T(8,128)(2,1)S(1)} %own.9.refs_6_.refs_8_), channel_id=1, source_target_pairs={{0,1},{8,9},{16,17},{24,25},{2,3},{10,11},{18,19},{26,27}} | collective-permute-start | bytes 786440 | tf_op jit(solution)/shard_map/ppermute | solution.py:38
  18.9 10.7 %collective-permute-start.8 = (bf16[128,768]{1,0:T(8,128)(2,1)S(1)}, bf16[128,768]{1,0:T(8,128)(2,1)S(1)}, u32[]{:S(2)}, u32[]{:S(2)}) collective-permute-start(bf16[128,768]{1,0:T(8,128)(2,1)S(1)} %own.10.refs_6_.refs_9_), channel_id=1, source_target_pairs={{0,1},{8,9},{16,17},{24,25},{2,3},{10,11},{18,19},{26,27}} | collective-permute-start | bytes 589832 | tf_op jit(solution)/shard_map/ppermute | solution.py:38
  23.1 8.9 %collective-permute-start.7 = (bf16[128,896]{1,0:T(8,128)(2,1)S(1)}, bf16[128,896]{1,0:T(8,128)(2,1)S(1)}, u32[]{:S(2)}, u32[]{:S(2)}) collective-permute-start(bf16[128,896]{1,0:T(8,128)(2,1)S(1)} %own.11.refs_10_), channel_id=1, source_target_pairs={{0,1},{8,9},{16,17},{24,25},{2,3},{10,11},{18,19},{26,27}} | collective-permute-start | bytes 688136 | tf_op jit(solution)/shard_map/ppermute | solution.py:38

commit v9 on v8

--- a/solution.py
+++ b/solution.py
@@ -11,7 +11,8 @@
 ROW_BLOCK = 32
 RAW = 384
 ODD = (1536, 2176)
-EVEN = (1024, 1024, 768, 896)
+EVEN = (1280, 768, 768, 896)
+PIECES = 4
 NEAR = 2048
 LINES = 8
 F32 = jnp.float32
@@ -64,31 +65,27 @@
     return jax.ShapeDtypeStruct((rows, cols), kind)
 
 
-def multiply(keys_ref, values_ref, keys_in, values_in, sems, first, targets, meanwhile=None):
-    rows = keys_in.shape[0]
-    pieces, offset = [], 0
-    for piece, (out_ref, row, col, width) in enumerate(targets):
-        at = pl.ds(offset, width)
-        source = pl.ds(first + offset, width)
-        copies = (
-            pltpu.make_async_copy(keys_ref.at[0, :, source], keys_in.at[:, at], sems.at[2 * piece]),
-            pltpu.make_async_copy(values_ref.at[0, :, source], values_in.at[:, at], sems.at[2 * piece + 1]),
+def multiply(keys_ref, values_ref, keys_in, values_in, sems, out_ref, meanwhile):
+    rows, cols = out_ref.shape
+    step = rows // PIECES
+    spans = [pl.ds(piece * step, step) for piece in range(PIECES)]
+    copies = []
+    for piece, span in enumerate(spans):
+        copies.append(
+            (
+                pltpu.make_async_copy(keys_ref.at[0, span], keys_in.at[span], sems.at[2 * piece]),
+                pltpu.make_async_copy(values_ref.at[0, span], values_in.at[span], sems.at[2 * piece + 1]),
+            )
         )
-        for copy in copies:
+        for copy in copies[-1]:
             copy.start()
-        pieces.append(copies)
-        offset += width
-    if meanwhile is not None:
-        meanwhile()
-    offset = 0
-    for copies, (out_ref, row, col, width) in zip(pieces, targets):
-        for copy in copies:
+    meanwhile()
+    for span, pair in zip(spans, copies):
+        for copy in pair:
             copy.wait()
-        for tile in range(0, width, LANES):
-            at = slice(offset + tile, offset + tile + LANES)
-            product = keys_in[:, at].astype(F32) * values_in[:, at].astype(F32)
-            out_ref[row : row + rows, col + tile : col + tile + LANES] = product.astype(BF16)
-        offset += width
+        for tile in range(0, cols, 4 * LANES):
+            at = slice(tile, tile + 4 * LANES)
+            out_ref[span, at] = (keys_in[span, at].astype(F32) * values_in[span, at].astype(F32)).astype(BF16)
 
 
 def fill_lines(bank, scales_ref, assign_ref, lines_ref):
@@ -107,8 +104,7 @@
     bank_ref, scales_ref, assign_ref, queries_ref, keys_ref, values_ref = refs[:6]
     raw_ref, whole_ref, lines_ref = refs[6:9]
     bank_in, scales_in, assign_in, keys_in, values_in, sems, own_sems = refs[9:]
-    rows, total = whole_ref.shape
-    step = total // 4 // LANES * LANES
+    rows = whole_ref.shape[0]
 
     @pl.when(is_first())
     def _():
@@ -129,19 +125,13 @@
                 taken = lines_ref[part * LINES : (part + 1) * LINES, :].astype(BF16)
                 raw_ref[2 * rows :, part * LANES : (part + 1) * LANES] = taken
 
-        targets = [
-            (whole_ref, 0, 0, step),
-            (whole_ref, 0, step, step),
-            (whole_ref, 0, 2 * step, step),
-            (whole_ref, 0, 3 * step, total - 3 * step),
-        ]
-        multiply(keys_ref, values_ref, keys_in, values_in, sems, 0, targets, taps)
+        multiply(keys_ref, values_ref, keys_in, values_in, sems, whole_ref, taps)
         raw_ref[rows : 2 * rows, :] = whole_ref[:, :RAW]
         copies[3].wait()
 
 
-def product_scratch(rows, total, pieces):
-    return [pltpu.VMEM((rows, total), BF16), pltpu.VMEM((rows, total), BF16), pltpu.SemaphoreType.DMA((2 * pieces,))]
+def product_scratch(rows, total):
+    return [pltpu.VMEM((rows, total), BF16), pltpu.VMEM((rows, total), BF16), pltpu.SemaphoreType.DMA((2 * PIECES,))]
 
 
 def lead_of(bank, scales, assign, queries, keys, values):
@@ -157,7 +147,7 @@
         [HBM] * 6,
         (VMEM,) * 3,
         [pltpu.VMEM(bank.shape, BF16), pltpu.VMEM(scales.shape, F32), pltpu.VMEM(assign.shape, jnp.int32)]
-        + product_scratch(rows, total, 4)
+        + product_scratch(rows, total)
         + [pltpu.SemaphoreType.DMA((4,))],
     )(bank, scales, assign, queries, keys, values)
 
@@ -178,7 +168,6 @@
 def product_kernel(*refs):
     keys_ref, values_ref, bank_ref, scales_ref, assign_ref, _, whole_ref = refs[:7]
     out_ref, lines_ref, near_ref, far_ref, keys_in, values_in, sems = refs[7:]
-    half = out_ref.shape[1] // 2
     near = near_ref.shape[1]
 
     @pl.when(jnp.logical_and(is_first(), is_slab(1)))
@@ -189,15 +178,13 @@
 
     @pl.when(jnp.logical_not(is_first()))
     def _():
-        targets = [(out_ref, 0, 0, half), (out_ref, 0, half, half)]
         multiply(
             keys_ref,
             values_ref,
             keys_in,
             values_in,
             sems,
-            0,
-            targets,
+            out_ref,
             lambda: fill_lines(bank_ref[0], scales_ref, assign_ref, lines_ref),
         )
 
@@ -210,7 +197,7 @@
         (array(rows, total), array(*lines.shape, F32), array(rows, NEAR), array(rows, total - NEAR)),
         [HBM, HBM] + [VMEM] * 5,
         (VMEM,) * 4,
-        product_scratch(rows, total, 2),
+        product_scratch(rows, total),
         aliases={5: 1},
     )(keys, values, bank, scales, assign, lines, whole)
 

time: 33.1 us -> 33.1 us (level)
  no operation moved by 1% of the time
where the time goes in v9:
time: 33.1 us; the launch traced here: 32.8 us
  starting transfers between devices  17.9 us (54%)
  Pallas kernels  8.08 us (24%)
  waiting for transfers between devices  5.78 us (17%)
  between operations  1.01 us (3%)
    ppermute x5, starting transfers between devices, to_next_slab(): return lax.ppermute(value, ('ctx', 'pipe'), pairs)  10 us
    ppermute x7, starting transfers between devices, to_next_section(): return lax.ppermute(value, ('ctx', 'pipe'), pairs)  7.83 us
    ppermute x5, waiting for transfers between devices, to_next_slab(): return lax.ppermute(value, ('ctx', 'pipe'), pairs)  2.94 us
    ppermute x7, waiting for transfers between devices, to_next_section(): return lax.ppermute(value, ('ctx', 'pipe'), pairs)  2.84 us
    pallas_call x1, Pallas kernels, later_of(): call(functools.partial(later_kernel, places), 'later', (jax.ShapeDtypeStr...  2.59 us
    pallas_call x4, Pallas kernels, finish(): call(functools.partial(finish_kernel, places[0][0], places), 'finish', ja...  2.42 us
    pallas_call x1, Pallas kernels, product_of(): call(product_kernel, 'product', (array(rows, total), array(*lines.shape,...  1.67 us
    pallas_call x1, Pallas kernels, raw_finish(): call(raw_kernel, 'raw', jax.ShapeDtypeStruct(held.shape, BF16), [SMEM] +...  1.14 us
  transfers between devices with their start and end apart: 12, of which 4 were waited for; matrix products, arithmetic and copies ran while one was open for 0% of the time, Pallas kernels for 22%

profile of v9, /device:TPU:12, one launch (start us, length us, event | category | flops | bytes accessed | tf_op | source)
XLA Modules:
  0.0 32.8 jit_solution(16194175884621253665)
XLA Ops:
  0.0 0.0 copy-start.2
  0.0 0.0 copy-start.3
  0.0 0.0 copy-start.4
  0.0 0.1 lead.1
  0.1 0.0 copy-start
  0.2 0.0 copy-start.1
  0.2 0.9 %collective-permute-start = (bf16[128,4096]{1,0:T(8,128)(2,1)S(1)}, bf16[128,4096]{1,0:T(8,128)(2,1)S(1)}, u32[]{:S(2)}, u32[]{:S(2)}) collective-permute-start(bf16[128,4096]{1,0:T(8,128)(2,1)S(1)} %get-tuple-element.18.refs_6_.refs_3_), channel_id=1, source_target_pairs={{0,4},{8,12},{16,20},{24,28},{2,6},{10,14},{18,22},{26,30}} | collective-permute-start | bytes 3145736 | tf_op jit(solution)/shard_map/ppermute | solution.py:33
  1.0 1.3 %collective-permute-start.3 = (bf16[264,384]{1,0:T(8,128)(2,1)S(1)}, bf16[264,384]{1,0:T(8,128)(2,1)S(1)}, u32[]{:S(2)}, u32[]{:S(2)}) collective-permute-start(bf16[264,384]{1,0:T(8,128)(2,1)S(1)} %get-tuple-element.22.raw_ref), channel_id=1, source_target_pairs={{0,1},{4,5},{8,9},{12,13},{16,17},{20,21},{24,25},{28,29},{2,3},{6... | collective-permute-start | bytes 608264 | tf_op jit(solution)/shard_map/ppermute | solution.py:39
  2.3 0.0 copy-done.2
  2.3 0.0 copy-done.3
  2.4 0.0 copy-done.4
  2.4 1.7 %product.1 = (bf16[128,4096]{1,0:T(8,128)(2,1)S(1)}, f32[256,128]{1,0:T(8,128)S(1)}, bf16[128,2048]{1,0:T(8,128)(2,1)S(1)}, bf16[128,2048]{1,0:T(8,128)(2,1)S(1)}) custom-call(bf16[1,128,4096]{2,1,0:T(8,128)(2,1)} %refs_0_.11, bf16[1,128,4096]{2,1,0:T(8,128)(2,1)} %refs_1_.3, bf16[1,256,128]{2,1,0:T(8,128)(2,1)S(1)} %copy-done.2, ...), custom_call_target="tpu_custom_call", output_to_operand_aliasing={{1}: (5, {})} | custom-call | flops 1024 | bytes 1024 | tf_op jit(solution)/shard_map/product/pallas_call | solution.py:194
  4.7 0.0 collective-permute-done.refs_2_.refs_3_
  4.7 0.0 copy-done
  4.7 0.0 copy-done.1
  4.7 0.7 %collective-permute-start.4 = (bf16[128,1536]{1,0:T(8,128)(2,1)S(1)}, bf16[128,1536]{1,0:T(8,128)(2,1)S(1)}, u32[]{:S(2)}, u32[]{:S(2)}) collective-permute-start(bf16[128,1536]{1,0:T(8,128)(2,1)S(1)} %own.6._.refs_5_), channel_id=1, source_target_pairs={{4,5},{12,13},{20,21},{28,29},{6,7},{14,15},{22,23},{30,31}} | collective-permute-start | bytes 1179656 | tf_op jit(solution)/shard_map/ppermute | solution.py:39
  5.4 0.7 %collective-permute-start.2 = (bf16[128,2048]{1,0:T(8,128)(2,1)S(1)}, bf16[128,2048]{1,0:T(8,128)(2,1)S(1)}, u32[]{:S(2)}, u32[]{:S(2)}) collective-permute-start(bf16[128,2048]{1,0:T(8,128)(2,1)S(1)} %hold.5.refs_6_), channel_id=1, source_target_pairs={{4,8},{12,16},{20,24},{6,10},{14,18},{22,26}} | collective-permute-start | bytes 1572872 | tf_op jit(solution)/shard_map/ppermute | solution.py:33
  6.2 0.7 %collective-permute-start.5 = (bf16[128,2176]{1,0:T(8,128)(2,1)S(1)}, bf16[128,2176]{1,0:T(8,128)(2,1)S(1)}, u32[]{:S(2)}, u32[]{:S(2)}) collective-permute-start(bf16[128,2176]{1,0:T(8,128)(2,1)S(1)} %own.7._.refs_6_), channel_id=1, source_target_pairs={{4,5},{12,13},{20,21},{28,29},{6,7},{14,15},{22,23},{30,31}} | collective-permute-start | bytes 1671176 | tf_op jit(solution)/shard_map/ppermute | solution.py:39
  6.9 2.9 %collective-permute-start.1 = (bf16[128,4096]{1,0:T(8,128)(2,1)S(1)}, bf16[128,4096]{1,0:T(8,128)(2,1)S(1)}, u32[]{:S(2)}, u32[]{:S(2)}) collective-permute-start(bf16[128,4096]{1,0:T(8,128)(2,1)S(1)} %hold.6._.refs_3_), channel_id=1, source_target_pairs={{1,5},{5,9},{9,13},{13,17},{17,21},{21,25},{25,29},{3,7},{7,11},{1... | collective-permute-start | bytes 3145736 | tf_op jit(solution)/shard_map/ppermute | solution.py:33
  9.8 0.6 %collective-permute-done.3.received_ref = bf16[264,384]{1,0:T(8,128)(2,1)S(1)} collective-permute-done((bf16[264,384]{1,0:T(8,128)(2,1)S(1)}, bf16[264,384]{1,0:T(8,128)(2,1)S(1)}, u32[]{:S(2)}, u32[]{:S(2)}) %collective-permute-start.3) | collective-permute-done | bytes 202784 | tf_op jit(solution)/shard_map/ppermute | solution.py:39
  10.5 0.7 %collective-permute-start.6 = (bf16[128,2048]{1,0:T(8,128)(2,1)S(1)}, bf16[128,2048]{1,0:T(8,128)(2,1)S(1)}, u32[]{:S(2)}, u32[]{:S(2)}) collective-permute-start(bf16[128,2048]{1,0:T(8,128)(2,1)S(1)} %hold.9), channel_id=1, source_target_pairs={{4,8},{12,16},{20,24},{6,10},{14,18},{22,26}} | collective-permute-start | bytes 1572872 | tf_op jit(solution)/shard_map/ppermute | solution.py:33
  11.2 0.0 collective-permute-done.4._.refs_1_
  11.2 0.0 collective-permute-done.2.refs_2_
  11.2 1.3 %collective-permute-start.9 = (bf16[128,1280]{1,0:T(8,128)(2,1)S(1)}, bf16[128,1280]{1,0:T(8,128)(2,1)S(1)}, u32[]{:S(2)}, u32[]{:S(2)}) collective-permute-start(bf16[128,1280]{1,0:T(8,128)(2,1)S(1)} %own.8._.refs_7_), channel_id=1, source_target_pairs={{0,1},{8,9},{16,17},{24,25},{2,3},{10,11},{18,19},{26,27}} | collective-permute-start | bytes 983048 | tf_op jit(solution)/shard_map/ppermute | solution.py:39
  12.5 4.8 %collective-permute-start.11 = (bf16[128,384]{1,0:T(8,128)(2,1)S(1)}, bf16[128,384]{1,0:T(8,128)(2,1)S(1)}, u32[]{:S(2)}, u32[]{:S(2)}) collective-permute-start(bf16[128,384]{1,0:T(8,128)(2,1)S(1)} %hold.8.refs_6_.refs_7_.refs_5_), channel_id=1, source_target_pairs={{1,5},{5,9},{9,13},{13,17},{17,21},{21,25},{25,29},{3,7},{7,11},{1... | collective-permute-start | bytes 294920 | tf_op jit(solution)/shard_map/ppermute | solution.py:33
  17.4 0.0 collective-permute-done.5.refs_7_.refs_2_
  17.4 1.3 %collective-permute-start.10 = (bf16[128,768]{1,0:T(8,128)(2,1)S(1)}, bf16[128,768]{1,0:T(8,128)(2,1)S(1)}, u32[]{:S(2)}, u32[]{:S(2)}) collective-permute-start(bf16[128,768]{1,0:T(8,128)(2,1)S(1)} %own.9.refs_6_.refs_8_), channel_id=1, source_target_pairs={{0,1},{8,9},{16,17},{24,25},{2,3},{10,11},{18,19},{26,27}} | collective-permute-start | bytes 589832 | tf_op jit(solution)/shard_map/ppermute | solution.py:39
  18.7 0.0 collective-permute-done.6.refs_2_.refs_4_
  18.8 1.3 %collective-permute-start.8 = (bf16[128,768]{1,0:T(8,128)(2,1)S(1)}, bf16[128,768]{1,0:T(8,128)(2,1)S(1)}, u32[]{:S(2)}, u32[]{:S(2)}) collective-permute-start(bf16[128,768]{1,0:T(8,128)(2,1)S(1)} %own.10.refs_6_.refs_9_), channel_id=1, source_target_pairs={{0,1},{8,9},{16,17},{24,25},{2,3},{10,11},{18,19},{26,27}} | collective-permute-start | bytes 589832 | tf_op jit(solution)/shard_map/ppermute | solution.py:39
  20.1 2.9 %collective-permute-done.1.refs_7_.refs_2_ = bf16[128,4096]{1,0:T(8,128)(2,1)S(1)} collective-permute-done((bf16[128,4096]{1,0:T(8,128)(2,1)S(1)}, bf16[128,4096]{1,0:T(8,128)(2,1)S(1)}, u32[]{:S(2)}, u32[]{:S(2)}) %collective-permute-start.1) | collective-permute-done | bytes 1048608 | tf_op jit(solution)/shard_map/ppermute | solution.py:33
  23.0 1.3 %collective-permute-start.7 = (bf16[128,896]{1,0:T(8,128)(2,1)S(1)}, bf16[128,896]{1,0:T(8,128)(2,1)S(1)}, u32[]{:S(2)}, u32[]{:S(2)}) collective-permute-start(bf16[128,896]{1,0:T(8,128)(2,1)S(1)} %own.11.refs_10_), channel_id=1, source_target_pairs={{0,1},{8,9},{16,17},{24,25},{2,3},{10,11},{18,19},{26,27}} | collective-permute-start | bytes 688136 | tf_op jit(solution)/shard_map/ppermute | solution.py:39
  24.3 2.6 %later.1 = (bf16[1,128,4096]{2,1,0:T(8,128)(2,1)}, f32[128,4096]{1,0:T(8,128)S(1)}) custom-call(s32[1]{0:T(128)S(6)} %copy.31.refs_0_, f32[256,128]{1,0:T(8,128)S(1)} %get-tuple-element.19.refs_1_.refs_6_, bf16[128,4096]{1,0:T(8,128)(2,1)S(1)} %collective-permute-done.1.refs_7_.refs_2_, bf16[128,4096]{1,0:T(8,128)(2,1)S(1)} %hold.6._.refs_3_, ...), custom_call_target="tpu_custom_call" | custom-call | flops 20000000000 | bytes 1024 | tf_op jit(solution)/shard_map/later/pallas_call | solution.py:351
  26.9 0.0 collective-permute-done.11.refs_2_
  27.0 1.1 %raw.1.refs_3_ = bf16[1,128,4096]{2,1,0:T(8,128)(2,1)} custom-call(s32[1]{0:T(128)S(6)} %copy.31.refs_0_, f32[24,128]{1,0:T(8,128)S(1)} %get-tuple-element.27.refs_1_, bf16[128,384]{1,0:T(8,128)(2,1)S(1)} %collective-permute-done.11.refs_2_, bf16[128,4096]{1,0:T(8,128)(2,1)S(1)} %collective-permute-done.refs_2_.refs_3_, ...), custom_call_target="tpu_custom_call", output_to_operand_aliasing={{}: (9, {})} | custom-call | flops 20000000000 | bytes 1024 | tf_op jit(solution)/shard_map/raw/pallas_call | solution.py:394
  28.1 0.0 collective-permute-done.10.refs_2_
  28.1 0.0 collective-permute-done.9.refs_1_
  28.1 0.9 %finish.5.refs_2_ = bf16[1,128,4096]{2,1,0:T(8,128)(2,1)} custom-call(f32[128,4096]{1,0:T(8,128)S(1)} %get-tuple-element.26.refs_0_.refs_7_, bf16[128,1280]{1,0:T(8,128)(2,1)S(1)} %collective-permute-done.9.refs_1_, bf16[128,768]{1,0:T(8,128)(2,1)S(1)} %collective-permute-done.10.refs_2_, ...), custom_call_target="tpu_custom_call", output_to_operand_aliasing={{}: (3, {})} | custom-call | flops 20000000000 | bytes 1024 | tf_op jit(solution)/shard_map/finish/pallas_call | solution.py:429
  29.0 0.5 %collective-permute-done.8.refs_1_ = bf16[128,768]{1,0:T(8,128)(2,1)S(1)} collective-permute-done((bf16[128,768]{1,0:T(8,128)(2,1)S(1)}, bf16[128,768]{1,0:T(8,128)(2,1)S(1)}, u32[]{:S(2)}, u32[]{:S(2)}) %collective-permute-start.8) | collective-permute-done | bytes 196640 | tf_op jit(solution)/shard_map/ppermute | solution.py:39
  29.6 0.7 %finish.6.refs_2_ = bf16[1,128,4096]{2,1,0:T(8,128)(2,1)} custom-call(f32[128,4096]{1,0:T(8,128)S(1)} %get-tuple-element.26.refs_0_.refs_7_, bf16[128,768]{1,0:T(8,128)(2,1)S(1)} %collective-permute-done.8.refs_1_, bf16[1,128,4096]{2,1,0:T(8,128)(2,1)} %finish.5.refs_2_), custom_call_target="tpu_custom_call", output_to_operand_aliasing={{}: (2, {})} | custom-call | flops 20000000000 | bytes 1024 | tf_op jit(solution)/shard_map/finish/pallas_call | solution.py:429
  30.3 1.7 %collective-permute-done.7.refs_1_ = bf16[128,896]{1,0:T(8,128)(2,1)S(1)} collective-permute-done((bf16[128,896]{1,0:T(8,128)(2,1)S(1)}, bf16[128,896]{1,0:T(8,128)(2,1)S(1)}, u32[]{:S(2)}, u32[]{:S(2)}) %collective-permute-start.7) | collective-permute-done | bytes 229408 | tf_op jit(solution)/shard_map/ppermute | solution.py:39
  32.0 0.8 %finish.7 = bf16[1,128,4096]{2,1,0:T(8,128)(2,1)} custom-call(f32[128,4096]{1,0:T(8,128)S(1)} %get-tuple-element.26.refs_0_.refs_7_, bf16[128,896]{1,0:T(8,128)(2,1)S(1)} %collective-permute-done.7.refs_1_, bf16[1,128,4096]{2,1,0:T(8,128)(2,1)} %finish.6.refs_2_), custom_call_target="tpu_custom_call", output_to_operand_aliasing={{}: (2, {})} | custom-call | flops 20000000000 | bytes 1024 | tf_op jit(solution)/shard_map/finish/pallas_call | solution.py:429
  (13 shorter events, 0.2 us)
Async XLA Ops:
  0.0 2.3 %copy-start.2 = (bf16[1,256,128]{2,1,0:T(8,128)(2,1)S(1)}, bf16[1,256,128]{2,1,0:T(8,128)(2,1)}, u32[]{:S(2)}) copy-start(bf16[1,256,128]{2,1,0:T(8,128)(2,1)} %refs_2_.3) | copy-start | bytes 196612
  0.0 2.3 %copy-start.3 = (f32[1,256]{1,0:T(1,128)S(1)}, f32[1,256]{1,0:T(1,128)}, u32[]{:S(2)}) copy-start(f32[1,256]{1,0:T(1,128)} %refs_3_.3) | copy-start | bytes 3076
  0.0 2.3 %copy-start.4 = (s32[1,256]{1,0:T(1,128)S(1)}, s32[1,256]{1,0:T(1,128)}, u32[]{:S(2)}) copy-start(s32[1,256]{1,0:T(1,128)} %refs_4_.10) | copy-start | bytes 3076
  0.1 4.6 %copy-start = (bf16[1,128,4096]{2,1,0:T(8,128)(2,1)S(1)}, bf16[1,128,4096]{2,1,0:T(8,128)(2,1)}, u32[]{:S(2)}) copy-start(bf16[1,128,4096]{2,1,0:T(8,128)(2,1)} %refs_4_.17) | copy-start | bytes 3145732
  0.2 4.6 %copy-start.1 = (bf16[128,4096]{1,0:T(8,128)(2,1)S(1)}, bf16[128,4096]{1,0:T(8,128)(2,1)}, u32[]{:S(2)}) copy-start(bf16[128,4096]{1,0:T(8,128)(2,1)} %refs_8_.1) | copy-start | bytes 3145732
  0.2 4.5 %collective-permute-start = (bf16[128,4096]{1,0:T(8,128)(2,1)S(1)}, bf16[128,4096]{1,0:T(8,128)(2,1)S(1)}, u32[]{:S(2)}, u32[]{:S(2)}) collective-permute-start(bf16[128,4096]{1,0:T(8,128)(2,1)S(1)} %get-tuple-element.18.refs_6_.refs_3_), channel_id=1, source_target_pairs={{0,4},{8,12},{16,20},{24,28},{2,6},{10,14},{18,22},{26,30}} | collective-permute-start | bytes 3145736 | tf_op jit(solution)/shard_map/ppermute | solution.py:33
  1.0 9.4 %collective-permute-start.3 = (bf16[264,384]{1,0:T(8,128)(2,1)S(1)}, bf16[264,384]{1,0:T(8,128)(2,1)S(1)}, u32[]{:S(2)}, u32[]{:S(2)}) collective-permute-start(bf16[264,384]{1,0:T(8,128)(2,1)S(1)} %get-tuple-element.22.raw_ref), channel_id=1, source_target_pairs={{0,1},{4,5},{8,9},{12,13},{16,17},{20,21},{24,25},{28,29},{2,3},{6... | collective-permute-start | bytes 608264 | tf_op jit(solution)/shard_map/ppermute | solution.py:39
  4.7 6.4 %collective-permute-start.4 = (bf16[128,1536]{1,0:T(8,128)(2,1)S(1)}, bf16[128,1536]{1,0:T(8,128)(2,1)S(1)}, u32[]{:S(2)}, u32[]{:S(2)}) collective-permute-start(bf16[128,1536]{1,0:T(8,128)(2,1)S(1)} %own.6._.refs_5_), channel_id=1, source_target_pairs={{4,5},{12,13},{20,21},{28,29},{6,7},{14,15},{22,23},{30,31}} | collective-permute-start | bytes 1179656 | tf_op jit(solution)/shard_map/ppermute | solution.py:39
  5.4 5.8 %collective-permute-start.2 = (bf16[128,2048]{1,0:T(8,128)(2,1)S(1)}, bf16[128,2048]{1,0:T(8,128)(2,1)S(1)}, u32[]{:S(2)}, u32[]{:S(2)}) collective-permute-start(bf16[128,2048]{1,0:T(8,128)(2,1)S(1)} %hold.5.refs_6_), channel_id=1, source_target_pairs={{4,8},{12,16},{20,24},{6,10},{14,18},{22,26}} | collective-permute-start | bytes 1572872 | tf_op jit(solution)/shard_map/ppermute | solution.py:33
  6.2 11.2 %collective-permute-start.5 = (bf16[128,2176]{1,0:T(8,128)(2,1)S(1)}, bf16[128,2176]{1,0:T(8,128)(2,1)S(1)}, u32[]{:S(2)}, u32[]{:S(2)}) collective-permute-start(bf16[128,2176]{1,0:T(8,128)(2,1)S(1)} %own.7._.refs_6_), channel_id=1, source_target_pairs={{4,5},{12,13},{20,21},{28,29},{6,7},{14,15},{22,23},{30,31}} | collective-permute-start | bytes 1671176 | tf_op jit(solution)/shard_map/ppermute | solution.py:39
  6.9 16.1 %collective-permute-start.1 = (bf16[128,4096]{1,0:T(8,128)(2,1)S(1)}, bf16[128,4096]{1,0:T(8,128)(2,1)S(1)}, u32[]{:S(2)}, u32[]{:S(2)}) collective-permute-start(bf16[128,4096]{1,0:T(8,128)(2,1)S(1)} %hold.6._.refs_3_), channel_id=1, source_target_pairs={{1,5},{5,9},{9,13},{13,17},{17,21},{21,25},{25,29},{3,7},{7,11},{1... | collective-permute-start | bytes 3145736 | tf_op jit(solution)/shard_map/ppermute | solution.py:33
  10.5 8.3 %collective-permute-start.6 = (bf16[128,2048]{1,0:T(8,128)(2,1)S(1)}, bf16[128,2048]{1,0:T(8,128)(2,1)S(1)}, u32[]{:S(2)}, u32[]{:S(2)}) collective-permute-start(bf16[128,2048]{1,0:T(8,128)(2,1)S(1)} %hold.9), channel_id=1, source_target_pairs={{4,8},{12,16},{20,24},{6,10},{14,18},{22,26}} | collective-permute-start | bytes 1572872 | tf_op jit(solution)/shard_map/ppermute | solution.py:33
  11.2 16.9 %collective-permute-start.9 = (bf16[128,1280]{1,0:T(8,128)(2,1)S(1)}, bf16[128,1280]{1,0:T(8,128)(2,1)S(1)}, u32[]{:S(2)}, u32[]{:S(2)}) collective-permute-start(bf16[128,1280]{1,0:T(8,128)(2,1)S(1)} %own.8._.refs_7_), channel_id=1, source_target_pairs={{0,1},{8,9},{16,17},{24,25},{2,3},{10,11},{18,19},{26,27}} | collective-permute-start | bytes 983048 | tf_op jit(solution)/shard_map/ppermute | solution.py:39
  12.5 14.4 %collective-permute-start.11 = (bf16[128,384]{1,0:T(8,128)(2,1)S(1)}, bf16[128,384]{1,0:T(8,128)(2,1)S(1)}, u32[]{:S(2)}, u32[]{:S(2)}) collective-permute-start(bf16[128,384]{1,0:T(8,128)(2,1)S(1)} %hold.8.refs_6_.refs_7_.refs_5_), channel_id=1, source_target_pairs={{1,5},{5,9},{9,13},{13,17},{17,21},{21,25},{25,29},{3,7},{7,11},{1... | collective-permute-start | bytes 294920 | tf_op jit(solution)/shard_map/ppermute | solution.py:33
  17.4 10.7 %collective-permute-start.10 = (bf16[128,768]{1,0:T(8,128)(2,1)S(1)}, bf16[128,768]{1,0:T(8,128)(2,1)S(1)}, u32[]{:S(2)}, u32[]{:S(2)}) collective-permute-start(bf16[128,768]{1,0:T(8,128)(2,1)S(1)} %own.9.refs_6_.refs_8_), channel_id=1, source_target_pairs={{0,1},{8,9},{16,17},{24,25},{2,3},{10,11},{18,19},{26,27}} | collective-permute-start | bytes 589832 | tf_op jit(solution)/shard_map/ppermute | solution.py:39
  18.8 10.8 %collective-permute-start.8 = (bf16[128,768]{1,0:T(8,128)(2,1)S(1)}, bf16[128,768]{1,0:T(8,128)(2,1)S(1)}, u32[]{:S(2)}, u32[]{:S(2)}) collective-permute-start(bf16[128,768]{1,0:T(8,128)(2,1)S(1)} %own.10.refs_6_.refs_9_), channel_id=1, source_target_pairs={{0,1},{8,9},{16,17},{24,25},{2,3},{10,11},{18,19},{26,27}} | collective-permute-start | bytes 589832 | tf_op jit(solution)/shard_map/ppermute | solution.py:39
  23.0 9.0 %collective-permute-start.7 = (bf16[128,896]{1,0:T(8,128)(2,1)S(1)}, bf16[128,896]{1,0:T(8,128)(2,1)S(1)}, u32[]{:S(2)}, u32[]{:S(2)}) collective-permute-start(bf16[128,896]{1,0:T(8,128)(2,1)S(1)} %own.11.refs_10_), channel_id=1, source_target_pairs={{0,1},{8,9},{16,17},{24,25},{2,3},{10,11},{18,19},{26,27}} | collective-permute-start | bytes 688136 | tf_op jit(solution)/shard_map/ppermute | solution.py:39

commit v10 on v9

--- a/solution.py
+++ b/solution.py
@@ -11,7 +11,7 @@
 ROW_BLOCK = 32
 RAW = 384
 ODD = (1536, 2176)
-EVEN = (1280, 768, 768, 896)
+EVEN = (1024, 1024, 768, 896)
 PIECES = 4
 NEAR = 2048
 LINES = 8
@@ -26,10 +26,14 @@
 HBM = pl.BlockSpec(memory_space=pltpu.HBM)
 
 
-def to_next_slab(value, pipes, from_odd=(0, 1)):
+def to_next_slab(value, *links):
     slabs, depth = lax.axis_size("ctx"), lax.axis_size("pipe")
-    sources = [slab for slab in range(slabs - 1) if slab % 2 in from_odd]
-    pairs = [(slab * depth + pipe, (slab + 1) * depth + pipe) for slab in sources for pipe in pipes]
+    pairs = [
+        (slab * depth + pipe, (slab + 1) * depth + pipe)
+        for odd, pipe in links
+        for slab in range(slabs - 1)
+        if slab % 2 == odd
+    ]
     return lax.ppermute(value, ("ctx", "pipe"), pairs)
 
 
@@ -65,8 +69,8 @@
     return jax.ShapeDtypeStruct((rows, cols), kind)
 
 
-def multiply(keys_ref, values_ref, keys_in, values_in, sems, out_ref, meanwhile):
-    rows, cols = out_ref.shape
+def multiply(keys_ref, values_ref, keys_in, values_in, sems, out_refs, meanwhile):
+    rows = out_refs[0].shape[0]
     step = rows // PIECES
     spans = [pl.ds(piece * step, step) for piece in range(PIECES)]
     copies = []
@@ -83,9 +87,13 @@
     for span, pair in zip(spans, copies):
         for copy in pair:
             copy.wait()
-        for tile in range(0, cols, 4 * LANES):
-            at = slice(tile, tile + 4 * LANES)
-            out_ref[span, at] = (keys_in[span, at].astype(F32) * values_in[span, at].astype(F32)).astype(BF16)
+        first = 0
+        for out_ref in out_refs:
+            for tile in range(0, out_ref.shape[1], 4 * LANES):
+                at = slice(first + tile, first + tile + 4 * LANES)
+                product = keys_in[span, at].astype(F32) * values_in[span, at].astype(F32)
+                out_ref[span, tile : tile + 4 * LANES] = product.astype(BF16)
+            first += out_ref.shape[1]
 
 
 def fill_lines(bank, scales_ref, assign_ref, lines_ref):
@@ -125,7 +133,7 @@
                 taken = lines_ref[part * LINES : (part + 1) * LINES, :].astype(BF16)
                 raw_ref[2 * rows :, part * LANES : (part + 1) * LANES] = taken
 
-        multiply(keys_ref, values_ref, keys_in, values_in, sems, whole_ref, taps)
+        multiply(keys_ref, values_ref, keys_in, values_in, sems, [whole_ref], taps)
         raw_ref[rows : 2 * rows, :] = whole_ref[:, :RAW]
         copies[3].wait()
 
@@ -167,7 +175,7 @@
 
 def product_kernel(*refs):
     keys_ref, values_ref, bank_ref, scales_ref, assign_ref, _, whole_ref = refs[:7]
-    out_ref, lines_ref, near_ref, far_ref, keys_in, values_in, sems = refs[7:]
+    lines_ref, near_ref, far_ref, keys_in, values_in, sems = refs[7:]
     near = near_ref.shape[1]
 
     @pl.when(jnp.logical_and(is_first(), is_slab(1)))
@@ -184,7 +192,7 @@
             keys_in,
             values_in,
             sems,
-            out_ref,
+            [near_ref, far_ref],
             lambda: fill_lines(bank_ref[0], scales_ref, assign_ref, lines_ref),
         )
 
@@ -194,11 +202,11 @@
     return call(
         product_kernel,
         "product",
-        (array(rows, total), array(*lines.shape, F32), array(rows, NEAR), array(rows, total - NEAR)),
+        (array(*lines.shape, F32), array(rows, NEAR), array(rows, total - NEAR)),
         [HBM, HBM] + [VMEM] * 5,
-        (VMEM,) * 4,
+        (VMEM,) * 3,
         product_scratch(rows, total),
-        aliases={5: 1},
+        aliases={5: 0},
     )(keys, values, bank, scales, assign, lines, whole)
 
 
@@ -325,8 +333,8 @@
 
 
 def later_kernel(places, *refs):
-    start_ref, lines_ref, behind_ref, product_ref, queries_ref = refs[:5]
-    own_refs = refs[5 : 5 + len(places)]
+    start_ref, lines_ref, near_behind, near_ref, far_behind, far_ref, queries_ref = refs[:7]
+    own_refs = refs[7 : 7 + len(places)]
     out_ref, gated_ref, table_ref, sems = refs[-4:]
     total = queries_ref.shape[2]
     share = share_of(lines_ref, total)
@@ -340,23 +348,27 @@
 
     @pl.when(jnp.logical_not(is_first()))
     def _():
-        def store(at, span, mixed):
-            gated_ref[span, at] = queries_ref[0, span, at].astype(F32) * mixed
-
-        mix_all(total, share, lines_ref, 0, table_ref, start_ref, behind_ref, product_ref, (0, 0), store)
-
-
-def later_of(start, lines, behind, product, queries, own, places):
-    rows, total = product.shape
+        for first, behind_ref, product_ref in ((0, near_behind, near_ref), (NEAR, far_behind, far_ref)):
+
+            def store(at, span, mixed):
+                cols = slice(first + at.start, first + at.stop)
+                gated_ref[span, cols] = queries_ref[0, span, cols].astype(F32) * mixed
+
+            width, line = product_ref.shape[1], first // LANES * share
+            mix_all(width, share, lines_ref, line, table_ref, start_ref, behind_ref, product_ref, (0, 0), store)
+
+
+def later_of(start, lines, near_behind, near, far_behind, far, queries, own, places):
+    rows, total = queries.shape[1:]
     return call(
         functools.partial(later_kernel, places),
         "later",
         (jax.ShapeDtypeStruct((1, rows, total), BF16), array(rows, total, F32)),
-        [SMEM] + [VMEM] * (4 + len(own)),
+        [SMEM] + [VMEM] * (6 + len(own)),
         (ANY, VMEM),
-        [table_scratch(lines, total, total), pltpu.SemaphoreType.DMA((len(own),))],
+        [table_scratch(lines, NEAR, total), pltpu.SemaphoreType.DMA((len(own),))],
         weight=SLOW,
-    )(start, lines, behind, product, queries, *own)
+    )(start, lines, near_behind, near, far_behind, far, queries, *own)
 
 
 def raw_kernel(*refs):
@@ -447,8 +459,8 @@
     )
     raw, whole, lines = lead_of(*far_small, far_queries, keys, values)
     raw_received = to_next_section(raw)
-    chip_behind = to_next_slab(whole, (0,), (0,))
-    product, lines, near, far = product_of(keys, values, *small, lines, whole)
+    chip_behind = to_next_slab(whole, (0, 0))
+    lines, near, far = product_of(keys, values, *small, lines, whole)
     own, received, places = [], [], []
 
     def send(odd, behind, origin, first, width, weight, *after):
@@ -462,22 +474,23 @@
 
     first, after = send(1, chip_behind, 0, RAW, ODD[0], QUICK, lines)
     near = held_back(near, after)
-    near_behind = to_next_slab(near, (0,), (1,))
+    near_behind = to_next_slab(near, (1, 0), (0, 1), (1, 1))
     first, after = send(1, chip_behind, 0, first, ODD[1], QUICK, near)
-    product = held_back(product, after)
-    behind = to_next_slab(product, (1,))
-    raw_queries, raw_product, raw_lines = pick_of(raw, raw_received, lines.shape[1], product)
-    far_behind = to_next_slab(held_back(far, raw_queries), (0,), (1,))
+    raw_queries, raw_product, raw_lines = pick_of(raw, raw_received, lines.shape[1], after)
+    far = held_back(far, raw_queries)
+    far_behind = to_next_slab(far, (1, 0), (0, 1), (1, 1))
     raw_queries = held_back(raw_queries, received[0], SLOW)
     first, after = send(0, near_behind, RAW, RAW, EVEN[0], SLOW, raw_queries)
     raw_product = held_back(raw_product, after)
-    raw_behind = to_next_slab(raw_product, (1,))
+    raw_behind = to_next_slab(raw_product, (0, 1), (1, 1))
     after = raw_product
-    for width, passed in zip(EVEN[1:], (received[1], after, behind)):
+    for width, passed in zip(EVEN[1:], (after, received[1], after)):
         origin = RAW if first < RAW + NEAR else RAW + NEAR
         source = near_behind if first < RAW + NEAR else far_behind
         first, after = send(0, source, origin, first, width, SLOW, after, passed)
-    held, gated = later_of(context_start, lines, behind, product, queries, own, places)
+    held, gated = later_of(
+        context_start, lines, near_behind, near, far_behind, far, queries, own, places
+    )
     odd = len(ODD)
     held = finish(held, gated, received[:odd], places[:odd])
     held = raw_finish(

time: 33.1 us -> 33.1 us (level)
  waiting for transfers between devices: 5.78 us -> 8.82 us
  starting transfers between devices: 17.9 us -> 14.9 us
    ppermute x5 -> x4, starting transfers between devices: 10 us -> 7.05 us  [to_next_slab(): return lax.ppermute(value, ('ctx', 'pipe'), pairs)]
    ppermute x5 -> x4, waiting for transfers between devices: 2.94 us -> 4.59 us  [to_next_slab(): return lax.ppermute(value, ('ctx', 'pipe'), pairs)]
    ppermute x7, waiting for transfers between devices: 2.84 us -> 4.23 us  [to_next_section(): return lax.ppermute(value, ('ctx', 'pipe'), pairs)]
  transfers between devices with their start and end apart: 12 -> 11, of which waited for: 4 -> 5; matrix products, arithmetic and copies ran while one was open for 0% -> 0% of each run, Pallas kernels for 22% -> 22%
where the time goes in v10:
time: 33.1 us; the launch traced here: 32.8 us
  starting transfers between devices  14.9 us (45%)
  waiting for transfers between devices  8.82 us (27%)
  Pallas kernels  8.12 us (25%)
  between operations  0.96 us (3%)
    ppermute x7, starting transfers between devices, to_next_section(): return lax.ppermute(value, ('ctx', 'pipe'), pairs)  7.82 us
    ppermute x4, starting transfers between devices, to_next_slab(): return lax.ppermute(value, ('ctx', 'pipe'), pairs)  7.05 us
    ppermute x4, waiting for transfers between devices, to_next_slab(): return lax.ppermute(value, ('ctx', 'pipe'), pairs)  4.59 us
    ppermute x7, waiting for transfers between devices, to_next_section(): return lax.ppermute(value, ('ctx', 'pipe'), pairs)  4.23 us
    pallas_call x1, Pallas kernels, later_of(): call(functools.partial(later_kernel, places), 'later', (jax.ShapeDtypeStr...  2.65 us
    pallas_call x4, Pallas kernels, finish(): call(functools.partial(finish_kernel, places[0][0], places), 'finish', ja...  2.41 us
    pallas_call x1, Pallas kernels, product_of(): call(product_kernel, 'product', (array(*lines.shape, F32), array(rows, NE...  1.67 us
    pallas_call x1, Pallas kernels, raw_finish(): call(raw_kernel, 'raw', jax.ShapeDtypeStruct(held.shape, BF16), [SMEM] +...  1.15 us
  transfers between devices with their start and end apart: 11, of which 5 were waited for; matrix products, arithmetic and copies ran while one was open for 0% of the time, Pallas kernels for 22%

profile of v10, /device:TPU:12, one launch (start us, length us, event | category | flops | bytes accessed | tf_op | source)
XLA Modules:
  0.0 32.8 jit_solution(14824866276330447540)
XLA Ops:
  0.0 0.0 copy-start.2
  0.0 0.0 copy-start.3
  0.0 0.0 copy-start.4
  0.0 0.1 lead.1
  0.1 0.0 copy-start
  0.2 0.0 copy-start.1
  0.2 0.9 %collective-permute-start = (bf16[128,4096]{1,0:T(8,128)(2,1)S(1)}, bf16[128,4096]{1,0:T(8,128)(2,1)S(1)}, u32[]{:S(2)}, u32[]{:S(2)}) collective-permute-start(bf16[128,4096]{1,0:T(8,128)(2,1)S(1)} %get-tuple-element.17.refs_6_.refs_3_), channel_id=1, source_target_pairs={{0,4},{8,12},{16,20},{24,28},{2,6},{10,14},{18,22},{26,30}} | collective-permute-start | bytes 3145736 | tf_op jit(solution)/shard_map/ppermute | solution.py:37
  1.0 1.3 %collective-permute-start.2 = (bf16[264,384]{1,0:T(8,128)(2,1)S(1)}, bf16[264,384]{1,0:T(8,128)(2,1)S(1)}, u32[]{:S(2)}, u32[]{:S(2)}) collective-permute-start(bf16[264,384]{1,0:T(8,128)(2,1)S(1)} %get-tuple-element.21.raw_ref), channel_id=1, source_target_pairs={{0,1},{4,5},{8,9},{12,13},{16,17},{20,21},{24,25},{28,29},{2,3},{6... | collective-permute-start | bytes 608264 | tf_op jit(solution)/shard_map/ppermute | solution.py:43
  2.3 0.0 copy-done.2
  2.3 0.0 copy-done.3
  2.4 0.0 copy-done.4
  2.4 1.7 %product.1 = (f32[256,128]{1,0:T(8,128)S(1)}, bf16[128,2048]{1,0:T(8,128)(2,1)S(1)}, bf16[128,2048]{1,0:T(8,128)(2,1)S(1)}) custom-call(bf16[1,128,4096]{2,1,0:T(8,128)(2,1)} %refs_0_.11, bf16[1,128,4096]{2,1,0:T(8,128)(2,1)} %refs_1_.3, bf16[1,256,128]{2,1,0:T(8,128)(2,1)S(1)} %copy-done.2, ...), custom_call_target="tpu_custom_call", output_to_operand_aliasing={{0}: (5, {})} | custom-call | flops 1024 | bytes 1024 | tf_op jit(solution)/shard_map/product/pallas_call | solution.py:202
  4.7 0.0 collective-permute-done.refs_2_.refs_3_
  4.7 0.0 copy-done
  4.7 0.0 copy-done.1
  4.7 0.7 %collective-permute-start.4 = (bf16[128,1536]{1,0:T(8,128)(2,1)S(1)}, bf16[128,1536]{1,0:T(8,128)(2,1)S(1)}, u32[]{:S(2)}, u32[]{:S(2)}) collective-permute-start(bf16[128,1536]{1,0:T(8,128)(2,1)S(1)} %own.6._.refs_7_), channel_id=1, source_target_pairs={{4,5},{12,13},{20,21},{28,29},{6,7},{14,15},{22,23},{30,31}} | collective-permute-start | bytes 1179656 | tf_op jit(solution)/shard_map/ppermute | solution.py:43
  5.4 2.3 %collective-permute-start.1 = (bf16[128,2048]{1,0:T(8,128)(2,1)S(1)}, bf16[128,2048]{1,0:T(8,128)(2,1)S(1)}, u32[]{:S(2)}, u32[]{:S(2)}) collective-permute-start(bf16[128,2048]{1,0:T(8,128)(2,1)S(1)} %hold.4.refs_6_.refs_3_), channel_id=1, source_target_pairs={{4,8},{12,16},{20,24},{1,5},{9,13},{17,21},{25,29},{5,9},{13,17},{... | collective-permute-start | bytes 1572872 | tf_op jit(solution)/shard_map/ppermute | solution.py:37
  7.8 0.7 %collective-permute-start.5 = (bf16[128,2176]{1,0:T(8,128)(2,1)S(1)}, bf16[128,2176]{1,0:T(8,128)(2,1)S(1)}, u32[]{:S(2)}, u32[]{:S(2)}) collective-permute-start(bf16[128,2176]{1,0:T(8,128)(2,1)S(1)} %own.7._.refs_8_), channel_id=1, source_target_pairs={{4,5},{12,13},{20,21},{28,29},{6,7},{14,15},{22,23},{30,31}} | collective-permute-start | bytes 1671176 | tf_op jit(solution)/shard_map/ppermute | solution.py:43
  8.5 1.9 %collective-permute-done.2.received_ref = bf16[264,384]{1,0:T(8,128)(2,1)S(1)} collective-permute-done((bf16[264,384]{1,0:T(8,128)(2,1)S(1)}, bf16[264,384]{1,0:T(8,128)(2,1)S(1)}, u32[]{:S(2)}, u32[]{:S(2)}) %collective-permute-start.2) | collective-permute-done | bytes 202784 | tf_op jit(solution)/shard_map/ppermute | solution.py:43
  10.5 1.9 %collective-permute-start.3 = (bf16[128,2048]{1,0:T(8,128)(2,1)S(1)}, bf16[128,2048]{1,0:T(8,128)(2,1)S(1)}, u32[]{:S(2)}, u32[]{:S(2)}) collective-permute-start(bf16[128,2048]{1,0:T(8,128)(2,1)S(1)} %hold.5.refs_5_), channel_id=1, source_target_pairs={{4,8},{12,16},{20,24},{1,5},{9,13},{17,21},{25,29},{5,9},{13,17},{... | collective-permute-start | bytes 1572872 | tf_op jit(solution)/shard_map/ppermute | solution.py:37
  12.4 0.0 collective-permute-done.4._.refs_1_
  12.4 3.5 %collective-permute-done.1.refs_2_ = bf16[128,2048]{1,0:T(8,128)(2,1)S(1)} collective-permute-done((bf16[128,2048]{1,0:T(8,128)(2,1)S(1)}, bf16[128,2048]{1,0:T(8,128)(2,1)S(1)}, u32[]{:S(2)}, u32[]{:S(2)}) %collective-permute-start.1) | collective-permute-done | bytes 524320 | tf_op jit(solution)/shard_map/ppermute | solution.py:37
  15.9 1.3 %collective-permute-start.8 = (bf16[128,1024]{1,0:T(8,128)(2,1)S(1)}, bf16[128,1024]{1,0:T(8,128)(2,1)S(1)}, u32[]{:S(2)}, u32[]{:S(2)}) collective-permute-start(bf16[128,1024]{1,0:T(8,128)(2,1)S(1)} %own.8._.refs_9_), channel_id=1, source_target_pairs={{0,1},{8,9},{16,17},{24,25},{2,3},{10,11},{18,19},{26,27}} | collective-permute-start | bytes 786440 | tf_op jit(solution)/shard_map/ppermute | solution.py:43
  17.2 1.9 %collective-permute-start.10 = (bf16[128,384]{1,0:T(8,128)(2,1)S(1)}, bf16[128,384]{1,0:T(8,128)(2,1)S(1)}, u32[]{:S(2)}, u32[]{:S(2)}) collective-permute-start(bf16[128,384]{1,0:T(8,128)(2,1)S(1)} %hold.7.refs_6_.refs_7_.refs_5_), channel_id=1, source_target_pairs={{1,5},{9,13},{17,21},{25,29},{5,9},{13,17},{21,25},{3,7},{11,15},{... | collective-permute-start | bytes 294920 | tf_op jit(solution)/shard_map/ppermute | solution.py:37
  19.2 1.3 %collective-permute-start.9 = (bf16[128,1024]{1,0:T(8,128)(2,1)S(1)}, bf16[128,1024]{1,0:T(8,128)(2,1)S(1)}, u32[]{:S(2)}, u32[]{:S(2)}) collective-permute-start(bf16[128,1024]{1,0:T(8,128)(2,1)S(1)} %own.9.refs_6_.refs_10_), channel_id=1, source_target_pairs={{0,1},{8,9},{16,17},{24,25},{2,3},{10,11},{18,19},{26,27}} | collective-permute-start | bytes 786440 | tf_op jit(solution)/shard_map/ppermute | solution.py:43
  20.5 1.1 %collective-permute-done.3.refs_2_.refs_4_ = bf16[128,2048]{1,0:T(8,128)(2,1)S(1)} collective-permute-done((bf16[128,2048]{1,0:T(8,128)(2,1)S(1)}, bf16[128,2048]{1,0:T(8,128)(2,1)S(1)}, u32[]{:S(2)}, u32[]{:S(2)}) %collective-permute-start.3) | collective-permute-done | bytes 524320 | tf_op jit(solution)/shard_map/ppermute | solution.py:37
  21.6 0.0 collective-permute-done.5.refs_7_.refs_2_
  21.6 1.3 %collective-permute-start.7 = (bf16[128,768]{1,0:T(8,128)(2,1)S(1)}, bf16[128,768]{1,0:T(8,128)(2,1)S(1)}, u32[]{:S(2)}, u32[]{:S(2)}) collective-permute-start(bf16[128,768]{1,0:T(8,128)(2,1)S(1)} %own.10.refs_6_.refs_11_), channel_id=1, source_target_pairs={{0,1},{8,9},{16,17},{24,25},{2,3},{10,11},{18,19},{26,27}} | collective-permute-start | bytes 589832 | tf_op jit(solution)/shard_map/ppermute | solution.py:43
  22.9 1.3 %collective-permute-start.6 = (bf16[128,896]{1,0:T(8,128)(2,1)S(1)}, bf16[128,896]{1,0:T(8,128)(2,1)S(1)}, u32[]{:S(2)}, u32[]{:S(2)}) collective-permute-start(bf16[128,896]{1,0:T(8,128)(2,1)S(1)} %own.11.refs_12_), channel_id=1, source_target_pairs={{0,1},{8,9},{16,17},{24,25},{2,3},{10,11},{18,19},{26,27}} | collective-permute-start | bytes 688136 | tf_op jit(solution)/shard_map/ppermute | solution.py:43
  24.2 2.7 %later.1 = (bf16[1,128,4096]{2,1,0:T(8,128)(2,1)}, f32[128,4096]{1,0:T(8,128)S(1)}) custom-call(s32[1]{0:T(128)S(6)} %copy.29.refs_0_, f32[256,128]{1,0:T(8,128)S(1)} %get-tuple-element.18.refs_1_.refs_6_, bf16[128,2048]{1,0:T(8,128)(2,1)S(1)} %collective-permute-done.1.refs_2_, bf16[128,2048]{1,0:T(8,128)(2,1)S(1)} %hold.4.refs_6_.refs_3_, ...), custom_call_target="tpu_custom_call" | custom-call | flops 20000000000 | bytes 1024 | tf_op jit(solution)/shard_map/later/pallas_call | solution.py:363
  26.9 0.0 collective-permute-done.10.refs_2_
  26.9 1.1 %raw.1.refs_3_ = bf16[1,128,4096]{2,1,0:T(8,128)(2,1)} custom-call(s32[1]{0:T(128)S(6)} %copy.29.refs_0_, f32[24,128]{1,0:T(8,128)S(1)} %get-tuple-element.25.refs_1_, bf16[128,384]{1,0:T(8,128)(2,1)S(1)} %collective-permute-done.10.refs_2_, bf16[128,4096]{1,0:T(8,128)(2,1)S(1)} %collective-permute-done.refs_2_.refs_3_, ...), custom_call_target="tpu_custom_call", output_to_operand_aliasing={{}: (9, {})} | custom-call | flops 20000000000 | bytes 1024 | tf_op jit(solution)/shard_map/raw/pallas_call | solution.py:406
  28.1 0.0 collective-permute-done.9.refs_2_
  28.1 0.0 collective-permute-done.8.refs_1_
  28.1 0.9 %finish.5.refs_2_ = bf16[1,128,4096]{2,1,0:T(8,128)(2,1)} custom-call(f32[128,4096]{1,0:T(8,128)S(1)} %get-tuple-element.24.refs_0_.refs_7_, bf16[128,1024]{1,0:T(8,128)(2,1)S(1)} %collective-permute-done.8.refs_1_, bf16[128,1024]{1,0:T(8,128)(2,1)S(1)} %collective-permute-done.9.refs_2_, ...), custom_call_target="tpu_custom_call", output_to_operand_aliasing={{}: (3, {})} | custom-call | flops 20000000000 | bytes 1024 | tf_op jit(solution)/shard_map/finish/pallas_call | solution.py:441
  29.0 0.6 %collective-permute-done.7.refs_1_ = bf16[128,768]{1,0:T(8,128)(2,1)S(1)} collective-permute-done((bf16[128,768]{1,0:T(8,128)(2,1)S(1)}, bf16[128,768]{1,0:T(8,128)(2,1)S(1)}, u32[]{:S(2)}, u32[]{:S(2)}) %collective-permute-start.7) | collective-permute-done | bytes 196640 | tf_op jit(solution)/shard_map/ppermute | solution.py:43
  29.6 0.7 %finish.6.refs_2_ = bf16[1,128,4096]{2,1,0:T(8,128)(2,1)} custom-call(f32[128,4096]{1,0:T(8,128)S(1)} %get-tuple-element.24.refs_0_.refs_7_, bf16[128,768]{1,0:T(8,128)(2,1)S(1)} %collective-permute-done.7.refs_1_, bf16[1,128,4096]{2,1,0:T(8,128)(2,1)} %finish.5.refs_2_), custom_call_target="tpu_custom_call", output_to_operand_aliasing={{}: (2, {})} | custom-call | flops 20000000000 | bytes 1024 | tf_op jit(solution)/shard_map/finish/pallas_call | solution.py:441
  30.3 1.7 %collective-permute-done.6.refs_1_ = bf16[128,896]{1,0:T(8,128)(2,1)S(1)} collective-permute-done((bf16[128,896]{1,0:T(8,128)(2,1)S(1)}, bf16[128,896]{1,0:T(8,128)(2,1)S(1)}, u32[]{:S(2)}, u32[]{:S(2)}) %collective-permute-start.6) | collective-permute-done | bytes 229408 | tf_op jit(solution)/shard_map/ppermute | solution.py:43
  32.0 0.8 %finish.7 = bf16[1,128,4096]{2,1,0:T(8,128)(2,1)} custom-call(f32[128,4096]{1,0:T(8,128)S(1)} %get-tuple-element.24.refs_0_.refs_7_, bf16[128,896]{1,0:T(8,128)(2,1)S(1)} %collective-permute-done.6.refs_1_, bf16[1,128,4096]{2,1,0:T(8,128)(2,1)} %finish.6.refs_2_), custom_call_target="tpu_custom_call", output_to_operand_aliasing={{}: (2, {})} | custom-call | flops 20000000000 | bytes 1024 | tf_op jit(solution)/shard_map/finish/pallas_call | solution.py:441
  (12 shorter events, 0.2 us)
Async XLA Ops:
  0.0 2.3 %copy-start.2 = (bf16[1,256,128]{2,1,0:T(8,128)(2,1)S(1)}, bf16[1,256,128]{2,1,0:T(8,128)(2,1)}, u32[]{:S(2)}) copy-start(bf16[1,256,128]{2,1,0:T(8,128)(2,1)} %refs_2_.3) | copy-start | bytes 196612
  0.0 2.3 %copy-start.3 = (f32[1,256]{1,0:T(1,128)S(1)}, f32[1,256]{1,0:T(1,128)}, u32[]{:S(2)}) copy-start(f32[1,256]{1,0:T(1,128)} %refs_3_.3) | copy-start | bytes 3076
  0.0 2.3 %copy-start.4 = (s32[1,256]{1,0:T(1,128)S(1)}, s32[1,256]{1,0:T(1,128)}, u32[]{:S(2)}) copy-start(s32[1,256]{1,0:T(1,128)} %refs_4_.9) | copy-start | bytes 3076
  0.1 4.6 %copy-start = (bf16[1,128,4096]{2,1,0:T(8,128)(2,1)S(1)}, bf16[1,128,4096]{2,1,0:T(8,128)(2,1)}, u32[]{:S(2)}) copy-start(bf16[1,128,4096]{2,1,0:T(8,128)(2,1)} %refs_6_.1) | copy-start | bytes 3145732
  0.2 4.6 %copy-start.1 = (bf16[128,4096]{1,0:T(8,128)(2,1)S(1)}, bf16[128,4096]{1,0:T(8,128)(2,1)}, u32[]{:S(2)}) copy-start(bf16[128,4096]{1,0:T(8,128)(2,1)} %refs_8_.1) | copy-start | bytes 3145732
  0.2 4.5 %collective-permute-start = (bf16[128,4096]{1,0:T(8,128)(2,1)S(1)}, bf16[128,4096]{1,0:T(8,128)(2,1)S(1)}, u32[]{:S(2)}, u32[]{:S(2)}) collective-permute-start(bf16[128,4096]{1,0:T(8,128)(2,1)S(1)} %get-tuple-element.17.refs_6_.refs_3_), channel_id=1, source_target_pairs={{0,4},{8,12},{16,20},{24,28},{2,6},{10,14},{18,22},{26,30}} | collective-permute-start | bytes 3145736 | tf_op jit(solution)/shard_map/ppermute | solution.py:37
  1.0 9.4 %collective-permute-start.2 = (bf16[264,384]{1,0:T(8,128)(2,1)S(1)}, bf16[264,384]{1,0:T(8,128)(2,1)S(1)}, u32[]{:S(2)}, u32[]{:S(2)}) collective-permute-start(bf16[264,384]{1,0:T(8,128)(2,1)S(1)} %get-tuple-element.21.raw_ref), channel_id=1, source_target_pairs={{0,1},{4,5},{8,9},{12,13},{16,17},{20,21},{24,25},{28,29},{2,3},{6... | collective-permute-start | bytes 608264 | tf_op jit(solution)/shard_map/ppermute | solution.py:43
  4.7 7.7 %collective-permute-start.4 = (bf16[128,1536]{1,0:T(8,128)(2,1)S(1)}, bf16[128,1536]{1,0:T(8,128)(2,1)S(1)}, u32[]{:S(2)}, u32[]{:S(2)}) collective-permute-start(bf16[128,1536]{1,0:T(8,128)(2,1)S(1)} %own.6._.refs_7_), channel_id=1, source_target_pairs={{4,5},{12,13},{20,21},{28,29},{6,7},{14,15},{22,23},{30,31}} | collective-permute-start | bytes 1179656 | tf_op jit(solution)/shard_map/ppermute | solution.py:43
  5.4 10.5 %collective-permute-start.1 = (bf16[128,2048]{1,0:T(8,128)(2,1)S(1)}, bf16[128,2048]{1,0:T(8,128)(2,1)S(1)}, u32[]{:S(2)}, u32[]{:S(2)}) collective-permute-start(bf16[128,2048]{1,0:T(8,128)(2,1)S(1)} %hold.4.refs_6_.refs_3_), channel_id=1, source_target_pairs={{4,8},{12,16},{20,24},{1,5},{9,13},{17,21},{25,29},{5,9},{13,17},{... | collective-permute-start | bytes 1572872 | tf_op jit(solution)/shard_map/ppermute | solution.py:37
  7.8 13.7 %collective-permute-start.5 = (bf16[128,2176]{1,0:T(8,128)(2,1)S(1)}, bf16[128,2176]{1,0:T(8,128)(2,1)S(1)}, u32[]{:S(2)}, u32[]{:S(2)}) collective-permute-start(bf16[128,2176]{1,0:T(8,128)(2,1)S(1)} %own.7._.refs_8_), channel_id=1, source_target_pairs={{4,5},{12,13},{20,21},{28,29},{6,7},{14,15},{22,23},{30,31}} | collective-permute-start | bytes 1671176 | tf_op jit(solution)/shard_map/ppermute | solution.py:43
  10.5 11.1 %collective-permute-start.3 = (bf16[128,2048]{1,0:T(8,128)(2,1)S(1)}, bf16[128,2048]{1,0:T(8,128)(2,1)S(1)}, u32[]{:S(2)}, u32[]{:S(2)}) collective-permute-start(bf16[128,2048]{1,0:T(8,128)(2,1)S(1)} %hold.5.refs_5_), channel_id=1, source_target_pairs={{4,8},{12,16},{20,24},{1,5},{9,13},{17,21},{25,29},{5,9},{13,17},{... | collective-permute-start | bytes 1572872 | tf_op jit(solution)/shard_map/ppermute | solution.py:37
  15.9 12.1 %collective-permute-start.8 = (bf16[128,1024]{1,0:T(8,128)(2,1)S(1)}, bf16[128,1024]{1,0:T(8,128)(2,1)S(1)}, u32[]{:S(2)}, u32[]{:S(2)}) collective-permute-start(bf16[128,1024]{1,0:T(8,128)(2,1)S(1)} %own.8._.refs_9_), channel_id=1, source_target_pairs={{0,1},{8,9},{16,17},{24,25},{2,3},{10,11},{18,19},{26,27}} | collective-permute-start | bytes 786440 | tf_op jit(solution)/shard_map/ppermute | solution.py:43
  17.2 9.7 %collective-permute-start.10 = (bf16[128,384]{1,0:T(8,128)(2,1)S(1)}, bf16[128,384]{1,0:T(8,128)(2,1)S(1)}, u32[]{:S(2)}, u32[]{:S(2)}) collective-permute-start(bf16[128,384]{1,0:T(8,128)(2,1)S(1)} %hold.7.refs_6_.refs_7_.refs_5_), channel_id=1, source_target_pairs={{1,5},{9,13},{17,21},{25,29},{5,9},{13,17},{21,25},{3,7},{11,15},{... | collective-permute-start | bytes 294920 | tf_op jit(solution)/shard_map/ppermute | solution.py:37
  19.2 8.9 %collective-permute-start.9 = (bf16[128,1024]{1,0:T(8,128)(2,1)S(1)}, bf16[128,1024]{1,0:T(8,128)(2,1)S(1)}, u32[]{:S(2)}, u32[]{:S(2)}) collective-permute-start(bf16[128,1024]{1,0:T(8,128)(2,1)S(1)} %own.9.refs_6_.refs_10_), channel_id=1, source_target_pairs={{0,1},{8,9},{16,17},{24,25},{2,3},{10,11},{18,19},{26,27}} | collective-permute-start | bytes 786440 | tf_op jit(solution)/shard_map/ppermute | solution.py:43
  21.6 8.0 %collective-permute-start.7 = (bf16[128,768]{1,0:T(8,128)(2,1)S(1)}, bf16[128,768]{1,0:T(8,128)(2,1)S(1)}, u32[]{:S(2)}, u32[]{:S(2)}) collective-permute-start(bf16[128,768]{1,0:T(8,128)(2,1)S(1)} %own.10.refs_6_.refs_11_), channel_id=1, source_target_pairs={{0,1},{8,9},{16,17},{24,25},{2,3},{10,11},{18,19},{26,27}} | collective-permute-start | bytes 589832 | tf_op jit(solution)/shard_map/ppermute | solution.py:43
  22.9 9.1 %collective-permute-start.6 = (bf16[128,896]{1,0:T(8,128)(2,1)S(1)}, bf16[128,896]{1,0:T(8,128)(2,1)S(1)}, u32[]{:S(2)}, u32[]{:S(2)}) collective-permute-start(bf16[128,896]{1,0:T(8,128)(2,1)S(1)} %own.11.refs_12_), channel_id=1, source_target_pairs={{0,1},{8,9},{16,17},{24,25},{2,3},{10,11},{18,19},{26,27}} | collective-permute-start | bytes 688136 | tf_op jit(solution)/shard_map/ppermute | solution.py:43

commit v11 on v10

--- a/solution.py
+++ b/solution.py
@@ -67,6 +67,21 @@
 
 def array(rows, cols, kind=BF16):
     return jax.ShapeDtypeStruct((rows, cols), kind)
+
+
+def send_out(pieces, out_ref, sems):
+    copies = [
+        pltpu.make_async_copy(buffer, out_ref.at[0, :, pl.ds(first, buffer.shape[1])], sems.at[place])
+        for place, (buffer, first) in enumerate(pieces)
+    ]
+    for copy in copies:
+        copy.start()
+    return copies
+
+
+def wait_all(copies):
+    for copy in copies:
+        copy.wait()
 
 
 def multiply(keys_ref, values_ref, keys_in, values_in, sems, out_refs, meanwhile):
@@ -83,10 +98,8 @@
         )
         for copy in copies[-1]:
             copy.start()
-    meanwhile()
-    for span, pair in zip(spans, copies):
-        for copy in pair:
-            copy.wait()
+
+    def piece_product(span):
         first = 0
         for out_ref in out_refs:
             for tile in range(0, out_ref.shape[1], 4 * LANES):
@@ -94,6 +107,16 @@
                 product = keys_in[span, at].astype(F32) * values_in[span, at].astype(F32)
                 out_ref[span, tile : tile + 4 * LANES] = product.astype(BF16)
             first += out_ref.shape[1]
+
+    beside = PIECES // 2
+    for piece in range(beside):
+        wait_all(copies[piece])
+        piece_product(spans[piece])
+    for pair in copies[beside:]:
+        wait_all(pair)
+    meanwhile()
+    for span in spans[beside:]:
+        piece_product(span)
 
 
 def fill_lines(bank, scales_ref, assign_ref, lines_ref):
@@ -317,21 +340,6 @@
     )(value, after)
 
 
-def send_out(pieces, out_ref, sems):
-    copies = [
-        pltpu.make_async_copy(buffer, out_ref.at[0, :, pl.ds(first, buffer.shape[1])], sems.at[place])
-        for place, (buffer, first) in enumerate(pieces)
-    ]
-    for copy in copies:
-        copy.start()
-    return copies
-
-
-def wait_all(copies):
-    for copy in copies:
-        copy.wait()
-
-
 def later_kernel(places, *refs):
     start_ref, lines_ref, near_behind, near_ref, far_behind, far_ref, queries_ref = refs[:7]
     own_refs = refs[7 : 7 + len(places)]
@@ -429,9 +437,15 @@
         copies = []
         for place, (_, first, width) in enumerate(places):
             buffer = buffers[place]
-            total = received_refs[place][...].astype(F32) + gated_ref[:, first : first + width]
-            buffer[...] = total.astype(BF16)
-            copies += send_out([(buffer, first)], out_ref, sems.at[pl.ds(place, 1)])
+            half = buffer.shape[0] // 2
+            for part in range(2):
+                span = slice(part * half, (part + 1) * half)
+                total = received_refs[place][span, :].astype(F32) + gated_ref[span, first : first + width]
+                buffer[span, :] = total.astype(BF16)
+                target = out_ref.at[0, pl.ds(part * half, half), pl.ds(first, width)]
+                sem = sems.at[2 * place + part]
+                copies.append(pltpu.make_async_copy(buffer.at[pl.ds(part * half, half)], target, sem))
+                copies[-1].start()
         wait_all(copies)
 
 
@@ -444,7 +458,7 @@
         jax.ShapeDtypeStruct(held.shape, BF16),
         [VMEM] * (1 + count) + [ANY],
         ANY,
-        [pltpu.VMEM((rows, width), BF16) for _, _, width in places] + [pltpu.SemaphoreType.DMA((count,))],
+        [pltpu.VMEM((rows, width), BF16) for _, _, width in places] + [pltpu.SemaphoreType.DMA((2 * count,))],
         weight=SLOW,
         aliases={1 + count: 0},
     )(gated, *received, held)

time: 33.1 us -> 33.5 us (1.012)
  Pallas kernels: 8.12 us -> 8.51 us
    pallas_call x1, Pallas kernels: 1.67 us -> 2.09 us  [product_of(): call(product_kernel, 'product', (array(*lines.shape, F32), array(rows, NE...]
    ppermute x7, waiting for transfers between devices: 4.23 us -> 3.87 us  [to_next_section(): return lax.ppermute(value, ('ctx', 'pipe'), pairs)]
  transfers between devices with their start and end apart: 11 -> 11, of which waited for: 5 -> 5; matrix products, arithmetic and copies ran while one was open for 0% -> 0% of each run, Pallas kernels for 22% -> 23%
where the time goes in v11:
time: 33.5 us; the launch traced here: 33.2 us
  starting transfers between devices  15.2 us (45%)
  Pallas kernels  8.51 us (25%)
  waiting for transfers between devices  8.5 us (25%)
  between operations  0.96 us (3%)
    ppermute x7, starting transfers between devices, to_next_section(): return lax.ppermute(value, ('ctx', 'pipe'), pairs)  7.82 us
    ppermute x4, starting transfers between devices, to_next_slab(): return lax.ppermute(value, ('ctx', 'pipe'), pairs)  7.37 us
    ppermute x4, waiting for transfers between devices, to_next_slab(): return lax.ppermute(value, ('ctx', 'pipe'), pairs)  4.63 us
    ppermute x7, waiting for transfers between devices, to_next_section(): return lax.ppermute(value, ('ctx', 'pipe'), pairs)  3.87 us
    pallas_call x1, Pallas kernels, later_of(): call(functools.partial(later_kernel, places), 'later', (jax.ShapeDtypeStr...  2.66 us
    pallas_call x4, Pallas kernels, finish(): call(functools.partial(finish_kernel, places[0][0], places), 'finish', ja...  2.38 us
    pallas_call x1, Pallas kernels, product_of(): call(product_kernel, 'product', (array(*lines.shape, F32), array(rows, NE...  2.09 us
    pallas_call x1, Pallas kernels, raw_finish(): call(raw_kernel, 'raw', jax.ShapeDtypeStruct(held.shape, BF16), [SMEM] +...  1.15 us
  transfers between devices with their start and end apart: 11, of which 5 were waited for; matrix products, arithmetic and copies ran while one was open for 0% of the time, Pallas kernels for 23%

profile of v11, /device:TPU:12, one launch (start us, length us, event | category | flops | bytes accessed | tf_op | source)
XLA Modules:
  0.0 33.2 jit_solution(4931578201696448510)
XLA Ops:
  0.0 0.0 copy-start.2
  0.0 0.0 copy-start.3
  0.0 0.0 copy-start.4
  0.0 0.1 lead.1
  0.1 0.0 copy-start
  0.2 0.0 copy-start.1
  0.2 0.9 %collective-permute-start = (bf16[128,4096]{1,0:T(8,128)(2,1)S(1)}, bf16[128,4096]{1,0:T(8,128)(2,1)S(1)}, u32[]{:S(2)}, u32[]{:S(2)}) collective-permute-start(bf16[128,4096]{1,0:T(8,128)(2,1)S(1)} %get-tuple-element.17.refs_6_.refs_3_), channel_id=1, source_target_pairs={{0,4},{8,12},{16,20},{24,28},{2,6},{10,14},{18,22},{26,30}} | collective-permute-start | bytes 3145736 | tf_op jit(solution)/shard_map/ppermute | solution.py:37
  1.0 1.3 %collective-permute-start.2 = (bf16[264,384]{1,0:T(8,128)(2,1)S(1)}, bf16[264,384]{1,0:T(8,128)(2,1)S(1)}, u32[]{:S(2)}, u32[]{:S(2)}) collective-permute-start(bf16[264,384]{1,0:T(8,128)(2,1)S(1)} %get-tuple-element.21.raw_ref), channel_id=1, source_target_pairs={{0,1},{4,5},{8,9},{12,13},{16,17},{20,21},{24,25},{28,29},{2,3},{6... | collective-permute-start | bytes 608264 | tf_op jit(solution)/shard_map/ppermute | solution.py:43
  2.3 0.0 copy-done.2
  2.3 0.0 copy-done.3
  2.4 0.0 copy-done.4
  2.4 2.1 %product.1 = (f32[256,128]{1,0:T(8,128)S(1)}, bf16[128,2048]{1,0:T(8,128)(2,1)S(1)}, bf16[128,2048]{1,0:T(8,128)(2,1)S(1)}) custom-call(bf16[1,128,4096]{2,1,0:T(8,128)(2,1)} %refs_0_.11, bf16[1,128,4096]{2,1,0:T(8,128)(2,1)} %refs_1_.3, bf16[1,256,128]{2,1,0:T(8,128)(2,1)S(1)} %copy-done.2, ...), custom_call_target="tpu_custom_call", output_to_operand_aliasing={{0}: (5, {})} | custom-call | flops 1024 | bytes 1024 | tf_op jit(solution)/shard_map/product/pallas_call | solution.py:225
  5.1 0.0 collective-permute-done.refs_2_.refs_3_
  5.1 0.0 copy-done
  5.1 0.0 copy-done.1
  5.2 0.7 %collective-permute-start.4 = (bf16[128,1536]{1,0:T(8,128)(2,1)S(1)}, bf16[128,1536]{1,0:T(8,128)(2,1)S(1)}, u32[]{:S(2)}, u32[]{:S(2)}) collective-permute-start(bf16[128,1536]{1,0:T(8,128)(2,1)S(1)} %own.6._.refs_7_), channel_id=1, source_target_pairs={{4,5},{12,13},{20,21},{28,29},{6,7},{14,15},{22,23},{30,31}} | collective-permute-start | bytes 1179656 | tf_op jit(solution)/shard_map/ppermute | solution.py:43
  5.9 2.4 %collective-permute-start.1 = (bf16[128,2048]{1,0:T(8,128)(2,1)S(1)}, bf16[128,2048]{1,0:T(8,128)(2,1)S(1)}, u32[]{:S(2)}, u32[]{:S(2)}) collective-permute-start(bf16[128,2048]{1,0:T(8,128)(2,1)S(1)} %hold.4.refs_6_.refs_3_), channel_id=1, source_target_pairs={{4,8},{12,16},{20,24},{1,5},{9,13},{17,21},{25,29},{5,9},{13,17},{... | collective-permute-start | bytes 1572872 | tf_op jit(solution)/shard_map/ppermute | solution.py:37
  8.3 0.7 %collective-permute-start.5 = (bf16[128,2176]{1,0:T(8,128)(2,1)S(1)}, bf16[128,2176]{1,0:T(8,128)(2,1)S(1)}, u32[]{:S(2)}, u32[]{:S(2)}) collective-permute-start(bf16[128,2176]{1,0:T(8,128)(2,1)S(1)} %own.7._.refs_8_), channel_id=1, source_target_pairs={{4,5},{12,13},{20,21},{28,29},{6,7},{14,15},{22,23},{30,31}} | collective-permute-start | bytes 1671176 | tf_op jit(solution)/shard_map/ppermute | solution.py:43
  9.0 1.5 %collective-permute-done.2.received_ref = bf16[264,384]{1,0:T(8,128)(2,1)S(1)} collective-permute-done((bf16[264,384]{1,0:T(8,128)(2,1)S(1)}, bf16[264,384]{1,0:T(8,128)(2,1)S(1)}, u32[]{:S(2)}, u32[]{:S(2)}) %collective-permute-start.2) | collective-permute-done | bytes 202784 | tf_op jit(solution)/shard_map/ppermute | solution.py:43
  10.5 2.2 %collective-permute-start.3 = (bf16[128,2048]{1,0:T(8,128)(2,1)S(1)}, bf16[128,2048]{1,0:T(8,128)(2,1)S(1)}, u32[]{:S(2)}, u32[]{:S(2)}) collective-permute-start(bf16[128,2048]{1,0:T(8,128)(2,1)S(1)} %hold.5.refs_5_), channel_id=1, source_target_pairs={{4,8},{12,16},{20,24},{1,5},{9,13},{17,21},{25,29},{5,9},{13,17},{... | collective-permute-start | bytes 1572872 | tf_op jit(solution)/shard_map/ppermute | solution.py:37
  12.8 0.0 collective-permute-done.4._.refs_1_
  12.8 3.6 %collective-permute-done.1.refs_2_ = bf16[128,2048]{1,0:T(8,128)(2,1)S(1)} collective-permute-done((bf16[128,2048]{1,0:T(8,128)(2,1)S(1)}, bf16[128,2048]{1,0:T(8,128)(2,1)S(1)}, u32[]{:S(2)}, u32[]{:S(2)}) %collective-permute-start.1) | collective-permute-done | bytes 524320 | tf_op jit(solution)/shard_map/ppermute | solution.py:37
  16.4 1.3 %collective-permute-start.8 = (bf16[128,1024]{1,0:T(8,128)(2,1)S(1)}, bf16[128,1024]{1,0:T(8,128)(2,1)S(1)}, u32[]{:S(2)}, u32[]{:S(2)}) collective-permute-start(bf16[128,1024]{1,0:T(8,128)(2,1)S(1)} %own.8._.refs_9_), channel_id=1, source_target_pairs={{0,1},{8,9},{16,17},{24,25},{2,3},{10,11},{18,19},{26,27}} | collective-permute-start | bytes 786440 | tf_op jit(solution)/shard_map/ppermute | solution.py:43
  17.7 1.9 %collective-permute-start.10 = (bf16[128,384]{1,0:T(8,128)(2,1)S(1)}, bf16[128,384]{1,0:T(8,128)(2,1)S(1)}, u32[]{:S(2)}, u32[]{:S(2)}) collective-permute-start(bf16[128,384]{1,0:T(8,128)(2,1)S(1)} %hold.7.refs_6_.refs_7_.refs_5_), channel_id=1, source_target_pairs={{1,5},{9,13},{17,21},{25,29},{5,9},{13,17},{21,25},{3,7},{11,15},{... | collective-permute-start | bytes 294920 | tf_op jit(solution)/shard_map/ppermute | solution.py:37
  19.6 1.3 %collective-permute-start.9 = (bf16[128,1024]{1,0:T(8,128)(2,1)S(1)}, bf16[128,1024]{1,0:T(8,128)(2,1)S(1)}, u32[]{:S(2)}, u32[]{:S(2)}) collective-permute-start(bf16[128,1024]{1,0:T(8,128)(2,1)S(1)} %own.9.refs_6_.refs_10_), channel_id=1, source_target_pairs={{0,1},{8,9},{16,17},{24,25},{2,3},{10,11},{18,19},{26,27}} | collective-permute-start | bytes 786440 | tf_op jit(solution)/shard_map/ppermute | solution.py:43
  20.9 1.1 %collective-permute-done.3.refs_2_.refs_4_ = bf16[128,2048]{1,0:T(8,128)(2,1)S(1)} collective-permute-done((bf16[128,2048]{1,0:T(8,128)(2,1)S(1)}, bf16[128,2048]{1,0:T(8,128)(2,1)S(1)}, u32[]{:S(2)}, u32[]{:S(2)}) %collective-permute-start.3) | collective-permute-done | bytes 524320 | tf_op jit(solution)/shard_map/ppermute | solution.py:37
  22.0 0.0 collective-permute-done.5.refs_7_.refs_2_
  22.0 1.3 %collective-permute-start.7 = (bf16[128,768]{1,0:T(8,128)(2,1)S(1)}, bf16[128,768]{1,0:T(8,128)(2,1)S(1)}, u32[]{:S(2)}, u32[]{:S(2)}) collective-permute-start(bf16[128,768]{1,0:T(8,128)(2,1)S(1)} %own.10.refs_6_.refs_11_), channel_id=1, source_target_pairs={{0,1},{8,9},{16,17},{24,25},{2,3},{10,11},{18,19},{26,27}} | collective-permute-start | bytes 589832 | tf_op jit(solution)/shard_map/ppermute | solution.py:43
  23.3 1.3 %collective-permute-start.6 = (bf16[128,896]{1,0:T(8,128)(2,1)S(1)}, bf16[128,896]{1,0:T(8,128)(2,1)S(1)}, u32[]{:S(2)}, u32[]{:S(2)}) collective-permute-start(bf16[128,896]{1,0:T(8,128)(2,1)S(1)} %own.11.refs_12_), channel_id=1, source_target_pairs={{0,1},{8,9},{16,17},{24,25},{2,3},{10,11},{18,19},{26,27}} | collective-permute-start | bytes 688136 | tf_op jit(solution)/shard_map/ppermute | solution.py:43
  24.6 2.7 %later.1 = (bf16[1,128,4096]{2,1,0:T(8,128)(2,1)}, f32[128,4096]{1,0:T(8,128)S(1)}) custom-call(s32[1]{0:T(128)S(6)} %copy.29.refs_0_, f32[256,128]{1,0:T(8,128)S(1)} %get-tuple-element.18.refs_1_.refs_6_, bf16[128,2048]{1,0:T(8,128)(2,1)S(1)} %collective-permute-done.1.refs_2_, bf16[128,2048]{1,0:T(8,128)(2,1)S(1)} %hold.4.refs_6_.refs_3_, ...), custom_call_target="tpu_custom_call" | custom-call | flops 20000000000 | bytes 1024 | tf_op jit(solution)/shard_map/later/pallas_call | solution.py:371
  27.3 0.1 finish.4.refs_9_
  27.3 0.0 collective-permute-done.10.refs_2_
  27.4 1.1 %raw.1.refs_3_ = bf16[1,128,4096]{2,1,0:T(8,128)(2,1)} custom-call(s32[1]{0:T(128)S(6)} %copy.29.refs_0_, f32[24,128]{1,0:T(8,128)S(1)} %get-tuple-element.25.refs_1_, bf16[128,384]{1,0:T(8,128)(2,1)S(1)} %collective-permute-done.10.refs_2_, bf16[128,4096]{1,0:T(8,128)(2,1)S(1)} %collective-permute-done.refs_2_.refs_3_, ...), custom_call_target="tpu_custom_call", output_to_operand_aliasing={{}: (9, {})} | custom-call | flops 20000000000 | bytes 1024 | tf_op jit(solution)/shard_map/raw/pallas_call | solution.py:414
  28.5 0.0 collective-permute-done.9.refs_2_
  28.5 0.0 collective-permute-done.8.refs_1_
  28.5 0.9 %finish.5.refs_2_ = bf16[1,128,4096]{2,1,0:T(8,128)(2,1)} custom-call(f32[128,4096]{1,0:T(8,128)S(1)} %get-tuple-element.24.refs_0_.refs_7_, bf16[128,1024]{1,0:T(8,128)(2,1)S(1)} %collective-permute-done.8.refs_1_, bf16[128,1024]{1,0:T(8,128)(2,1)S(1)} %collective-permute-done.9.refs_2_, ...), custom_call_target="tpu_custom_call", output_to_operand_aliasing={{}: (3, {})} | custom-call | flops 20000000000 | bytes 1024 | tf_op jit(solution)/shard_map/finish/pallas_call | solution.py:455
  29.4 0.6 %collective-permute-done.7.refs_1_ = bf16[128,768]{1,0:T(8,128)(2,1)S(1)} collective-permute-done((bf16[128,768]{1,0:T(8,128)(2,1)S(1)}, bf16[128,768]{1,0:T(8,128)(2,1)S(1)}, u32[]{:S(2)}, u32[]{:S(2)}) %collective-permute-start.7) | collective-permute-done | bytes 196640 | tf_op jit(solution)/shard_map/ppermute | solution.py:43
  30.0 0.7 %finish.6.refs_2_ = bf16[1,128,4096]{2,1,0:T(8,128)(2,1)} custom-call(f32[128,4096]{1,0:T(8,128)S(1)} %get-tuple-element.24.refs_0_.refs_7_, bf16[128,768]{1,0:T(8,128)(2,1)S(1)} %collective-permute-done.7.refs_1_, bf16[1,128,4096]{2,1,0:T(8,128)(2,1)} %finish.5.refs_2_), custom_call_target="tpu_custom_call", output_to_operand_aliasing={{}: (2, {})} | custom-call | flops 20000000000 | bytes 1024 | tf_op jit(solution)/shard_map/finish/pallas_call | solution.py:455
  30.7 1.7 %collective-permute-done.6.refs_1_ = bf16[128,896]{1,0:T(8,128)(2,1)S(1)} collective-permute-done((bf16[128,896]{1,0:T(8,128)(2,1)S(1)}, bf16[128,896]{1,0:T(8,128)(2,1)S(1)}, u32[]{:S(2)}, u32[]{:S(2)}) %collective-permute-start.6) | collective-permute-done | bytes 229408 | tf_op jit(solution)/shard_map/ppermute | solution.py:43
  32.5 0.7 %finish.7 = bf16[1,128,4096]{2,1,0:T(8,128)(2,1)} custom-call(f32[128,4096]{1,0:T(8,128)S(1)} %get-tuple-element.24.refs_0_.refs_7_, bf16[128,896]{1,0:T(8,128)(2,1)S(1)} %collective-permute-done.6.refs_1_, bf16[1,128,4096]{2,1,0:T(8,128)(2,1)} %finish.6.refs_2_), custom_call_target="tpu_custom_call", output_to_operand_aliasing={{}: (2, {})} | custom-call | flops 20000000000 | bytes 1024 | tf_op jit(solution)/shard_map/finish/pallas_call | solution.py:455
  (11 shorter events, 0.1 us)
Async XLA Ops:
  0.0 2.3 %copy-start.2 = (bf16[1,256,128]{2,1,0:T(8,128)(2,1)S(1)}, bf16[1,256,128]{2,1,0:T(8,128)(2,1)}, u32[]{:S(2)}) copy-start(bf16[1,256,128]{2,1,0:T(8,128)(2,1)} %refs_2_.3) | copy-start | bytes 196612
  0.0 2.3 %copy-start.3 = (f32[1,256]{1,0:T(1,128)S(1)}, f32[1,256]{1,0:T(1,128)}, u32[]{:S(2)}) copy-start(f32[1,256]{1,0:T(1,128)} %refs_3_.3) | copy-start | bytes 3076
  0.0 2.3 %copy-start.4 = (s32[1,256]{1,0:T(1,128)S(1)}, s32[1,256]{1,0:T(1,128)}, u32[]{:S(2)}) copy-start(s32[1,256]{1,0:T(1,128)} %refs_4_.9) | copy-start | bytes 3076
  0.1 5.0 %copy-start = (bf16[1,128,4096]{2,1,0:T(8,128)(2,1)S(1)}, bf16[1,128,4096]{2,1,0:T(8,128)(2,1)}, u32[]{:S(2)}) copy-start(bf16[1,128,4096]{2,1,0:T(8,128)(2,1)} %refs_6_.1) | copy-start | bytes 3145732
  0.2 5.0 %copy-start.1 = (bf16[128,4096]{1,0:T(8,128)(2,1)S(1)}, bf16[128,4096]{1,0:T(8,128)(2,1)}, u32[]{:S(2)}) copy-start(bf16[128,4096]{1,0:T(8,128)(2,1)} %refs_8_.1) | copy-start | bytes 3145732
  0.2 4.9 %collective-permute-start = (bf16[128,4096]{1,0:T(8,128)(2,1)S(1)}, bf16[128,4096]{1,0:T(8,128)(2,1)S(1)}, u32[]{:S(2)}, u32[]{:S(2)}) collective-permute-start(bf16[128,4096]{1,0:T(8,128)(2,1)S(1)} %get-tuple-element.17.refs_6_.refs_3_), channel_id=1, source_target_pairs={{0,4},{8,12},{16,20},{24,28},{2,6},{10,14},{18,22},{26,30}} | collective-permute-start | bytes 3145736 | tf_op jit(solution)/shard_map/ppermute | solution.py:37
  1.0 9.5 %collective-permute-start.2 = (bf16[264,384]{1,0:T(8,128)(2,1)S(1)}, bf16[264,384]{1,0:T(8,128)(2,1)S(1)}, u32[]{:S(2)}, u32[]{:S(2)}) collective-permute-start(bf16[264,384]{1,0:T(8,128)(2,1)S(1)} %get-tuple-element.21.raw_ref), channel_id=1, source_target_pairs={{0,1},{4,5},{8,9},{12,13},{16,17},{20,21},{24,25},{28,29},{2,3},{6... | collective-permute-start | bytes 608264 | tf_op jit(solution)/shard_map/ppermute | solution.py:43
  5.2 7.6 %collective-permute-start.4 = (bf16[128,1536]{1,0:T(8,128)(2,1)S(1)}, bf16[128,1536]{1,0:T(8,128)(2,1)S(1)}, u32[]{:S(2)}, u32[]{:S(2)}) collective-permute-start(bf16[128,1536]{1,0:T(8,128)(2,1)S(1)} %own.6._.refs_7_), channel_id=1, source_target_pairs={{4,5},{12,13},{20,21},{28,29},{6,7},{14,15},{22,23},{30,31}} | collective-permute-start | bytes 1179656 | tf_op jit(solution)/shard_map/ppermute | solution.py:43
  5.9 10.5 %collective-permute-start.1 = (bf16[128,2048]{1,0:T(8,128)(2,1)S(1)}, bf16[128,2048]{1,0:T(8,128)(2,1)S(1)}, u32[]{:S(2)}, u32[]{:S(2)}) collective-permute-start(bf16[128,2048]{1,0:T(8,128)(2,1)S(1)} %hold.4.refs_6_.refs_3_), channel_id=1, source_target_pairs={{4,8},{12,16},{20,24},{1,5},{9,13},{17,21},{25,29},{5,9},{13,17},{... | collective-permute-start | bytes 1572872 | tf_op jit(solution)/shard_map/ppermute | solution.py:37
  8.3 13.7 %collective-permute-start.5 = (bf16[128,2176]{1,0:T(8,128)(2,1)S(1)}, bf16[128,2176]{1,0:T(8,128)(2,1)S(1)}, u32[]{:S(2)}, u32[]{:S(2)}) collective-permute-start(bf16[128,2176]{1,0:T(8,128)(2,1)S(1)} %own.7._.refs_8_), channel_id=1, source_target_pairs={{4,5},{12,13},{20,21},{28,29},{6,7},{14,15},{22,23},{30,31}} | collective-permute-start | bytes 1671176 | tf_op jit(solution)/shard_map/ppermute | solution.py:43
  10.5 11.5 %collective-permute-start.3 = (bf16[128,2048]{1,0:T(8,128)(2,1)S(1)}, bf16[128,2048]{1,0:T(8,128)(2,1)S(1)}, u32[]{:S(2)}, u32[]{:S(2)}) collective-permute-start(bf16[128,2048]{1,0:T(8,128)(2,1)S(1)} %hold.5.refs_5_), channel_id=1, source_target_pairs={{4,8},{12,16},{20,24},{1,5},{9,13},{17,21},{25,29},{5,9},{13,17},{... | collective-permute-start | bytes 1572872 | tf_op jit(solution)/shard_map/ppermute | solution.py:37
  16.4 12.2 %collective-permute-start.8 = (bf16[128,1024]{1,0:T(8,128)(2,1)S(1)}, bf16[128,1024]{1,0:T(8,128)(2,1)S(1)}, u32[]{:S(2)}, u32[]{:S(2)}) collective-permute-start(bf16[128,1024]{1,0:T(8,128)(2,1)S(1)} %own.8._.refs_9_), channel_id=1, source_target_pairs={{0,1},{8,9},{16,17},{24,25},{2,3},{10,11},{18,19},{26,27}} | collective-permute-start | bytes 786440 | tf_op jit(solution)/shard_map/ppermute | solution.py:43
  17.7 9.7 %collective-permute-start.10 = (bf16[128,384]{1,0:T(8,128)(2,1)S(1)}, bf16[128,384]{1,0:T(8,128)(2,1)S(1)}, u32[]{:S(2)}, u32[]{:S(2)}) collective-permute-start(bf16[128,384]{1,0:T(8,128)(2,1)S(1)} %hold.7.refs_6_.refs_7_.refs_5_), channel_id=1, source_target_pairs={{1,5},{9,13},{17,21},{25,29},{5,9},{13,17},{21,25},{3,7},{11,15},{... | collective-permute-start | bytes 294920 | tf_op jit(solution)/shard_map/ppermute | solution.py:37
  19.6 8.9 %collective-permute-start.9 = (bf16[128,1024]{1,0:T(8,128)(2,1)S(1)}, bf16[128,1024]{1,0:T(8,128)(2,1)S(1)}, u32[]{:S(2)}, u32[]{:S(2)}) collective-permute-start(bf16[128,1024]{1,0:T(8,128)(2,1)S(1)} %own.9.refs_6_.refs_10_), channel_id=1, source_target_pairs={{0,1},{8,9},{16,17},{24,25},{2,3},{10,11},{18,19},{26,27}} | collective-permute-start | bytes 786440 | tf_op jit(solution)/shard_map/ppermute | solution.py:43
  22.0 8.0 %collective-permute-start.7 = (bf16[128,768]{1,0:T(8,128)(2,1)S(1)}, bf16[128,768]{1,0:T(8,128)(2,1)S(1)}, u32[]{:S(2)}, u32[]{:S(2)}) collective-permute-start(bf16[128,768]{1,0:T(8,128)(2,1)S(1)} %own.10.refs_6_.refs_11_), channel_id=1, source_target_pairs={{0,1},{8,9},{16,17},{24,25},{2,3},{10,11},{18,19},{26,27}} | collective-permute-start | bytes 589832 | tf_op jit(solution)/shard_map/ppermute | solution.py:43
  23.3 9.1 %collective-permute-start.6 = (bf16[128,896]{1,0:T(8,128)(2,1)S(1)}, bf16[128,896]{1,0:T(8,128)(2,1)S(1)}, u32[]{:S(2)}, u32[]{:S(2)}) collective-permute-start(bf16[128,896]{1,0:T(8,128)(2,1)S(1)} %own.11.refs_12_), channel_id=1, source_target_pairs={{0,1},{8,9},{16,17},{24,25},{2,3},{10,11},{18,19},{26,27}} | collective-permute-start | bytes 688136 | tf_op jit(solution)/shard_map/ppermute | solution.py:43

commit v12 on v10

--- a/solution.py
+++ b/solution.py
@@ -96,13 +96,13 @@
             first += out_ref.shape[1]
 
 
-def fill_lines(bank, scales_ref, assign_ref, lines_ref):
+def fill_lines(bank, scales, assign, lines_ref):
     groups, taps = lines_ref.shape
     size = bank.shape[0]
-    chosen = (lax.broadcasted_iota(jnp.int32, (size, groups), 0) == assign_ref[...]).astype(F32).astype(BF16)
+    chosen = (lax.broadcasted_iota(jnp.int32, (size, groups), 0) == assign).astype(F32).astype(BF16)
     contract = (((0,), (0,)), ((), ()))
     picked = lax.dot_general(bank, chosen, contract, preferred_element_type=F32)
-    scaled = (picked * scales_ref[...]).astype(BF16)
+    scaled = (picked * scales).astype(BF16)
     order = lax.broadcasted_iota(jnp.int32, (taps, taps), 0) + lax.broadcasted_iota(jnp.int32, (taps, taps), 1)
     flip = (order == taps - 1).astype(F32).astype(BF16)
     lines_ref[...] = lax.dot_general(scaled, flip, contract, preferred_element_type=F32)
@@ -110,8 +110,9 @@
 
 def lead_kernel(*refs):
     bank_ref, scales_ref, assign_ref, queries_ref, keys_ref, values_ref = refs[:6]
-    raw_ref, whole_ref, lines_ref = refs[6:9]
-    bank_in, scales_in, assign_in, keys_in, values_in, sems, own_sems = refs[9:]
+    raw_ref, whole_ref = refs[6:8]
+    bank_in, scales_in, assign_in, lines_ref, keys_in, values_in, sems, own_sems = refs[8:]
+    count = lines_ref.shape[0]
     rows = whole_ref.shape[0]
 
     @pl.when(is_first())
@@ -128,7 +129,7 @@
         def taps():
             for copy in copies[:3]:
                 copy.wait()
-            fill_lines(bank_in[0], scales_in, assign_in, lines_ref)
+            fill_lines(bank_in[0], scales_in[:, :count], assign_in[:, :count], lines_ref)
             for part in range(RAW // LANES):
                 taken = lines_ref[part * LINES : (part + 1) * LINES, :].astype(BF16)
                 raw_ref[2 * rows :, part * LANES : (part + 1) * LANES] = taken
@@ -150,11 +151,15 @@
         (
             array(2 * rows + LINES, RAW),
             array(rows, total),
-            array(assign.shape[1], bank.shape[2], F32),
         ),
         [HBM] * 6,
-        (VMEM,) * 3,
-        [pltpu.VMEM(bank.shape, BF16), pltpu.VMEM(scales.shape, F32), pltpu.VMEM(assign.shape, jnp.int32)]
+        (VMEM,) * 2,
+        [
+            pltpu.VMEM(bank.shape, BF16),
+            pltpu.VMEM(scales.shape, F32),
+            pltpu.VMEM(assign.shape, jnp.int32),
+            pltpu.VMEM((min(LANES, assign.shape[1]), bank.shape[2]), F32),
+        ]
         + product_scratch(rows, total)
         + [pltpu.SemaphoreType.DMA((4,))],
     )(bank, scales, assign, queries, keys, values)
@@ -174,9 +179,16 @@
 
 
 def product_kernel(*refs):
-    keys_ref, values_ref, bank_ref, scales_ref, assign_ref, _, whole_ref = refs[:7]
-    lines_ref, near_ref, far_ref, keys_in, values_in, sems = refs[7:]
+    keys_ref, values_ref, bank_ref, scales_ref, assign_ref, whole_ref = refs[:6]
+    lines_ref, near_ref, far_ref, keys_in, values_in, sems = refs[6:]
     near = near_ref.shape[1]
+
+    def taps():
+        fill_lines(bank_ref[0], scales_ref[...], assign_ref[...], lines_ref)
+
+    @pl.when(is_first())
+    def _():
+        taps()
 
     @pl.when(jnp.logical_and(is_first(), is_slab(1)))
     def _():
@@ -186,28 +198,20 @@
 
     @pl.when(jnp.logical_not(is_first()))
     def _():
-        multiply(
-            keys_ref,
-            values_ref,
-            keys_in,
-            values_in,
-            sems,
-            [near_ref, far_ref],
-            lambda: fill_lines(bank_ref[0], scales_ref, assign_ref, lines_ref),
-        )
-
-
-def product_of(keys, values, bank, scales, assign, lines, whole):
+        multiply(keys_ref, values_ref, keys_in, values_in, sems, [near_ref, far_ref], taps)
+
+
+def product_of(keys, values, bank, scales, assign, whole):
     rows, total = keys.shape[1:]
+    groups, taps = assign.shape[1], bank.shape[2]
     return call(
         product_kernel,
         "product",
-        (array(*lines.shape, F32), array(rows, NEAR), array(rows, total - NEAR)),
-        [HBM, HBM] + [VMEM] * 5,
+        (array(groups, taps, F32), array(rows, NEAR), array(rows, total - NEAR)),
+        [HBM, HBM] + [VMEM] * 4,
         (VMEM,) * 3,
         product_scratch(rows, total),
-        aliases={5: 0},
-    )(keys, values, bank, scales, assign, lines, whole)
+    )(keys, values, bank, scales, assign, whole)
 
 
 def mix(table_ref, row, share, window, store):
@@ -457,10 +461,10 @@
     far_queries, keys, values = (
         pltpu.with_memory_space_constraint(value, pltpu.HBM) for value in (queries, keys, values)
     )
-    raw, whole, lines = lead_of(*far_small, far_queries, keys, values)
+    raw, whole = lead_of(*far_small, far_queries, keys, values)
     raw_received = to_next_section(raw)
     chip_behind = to_next_slab(whole, (0, 0))
-    lines, near, far = product_of(keys, values, *small, lines, whole)
+    lines, near, far = product_of(keys, values, *small, whole)
     own, received, places = [], [], []
 
     def send(odd, behind, origin, first, width, weight, *after):
@@ -481,13 +485,12 @@
     far_behind = to_next_slab(far, (1, 0), (0, 1), (1, 1))
     raw_queries = held_back(raw_queries, received[0], SLOW)
     first, after = send(0, near_behind, RAW, RAW, EVEN[0], SLOW, raw_queries)
+    first, after = send(0, near_behind, RAW, first, EVEN[1], SLOW, after)
     raw_product = held_back(raw_product, after)
     raw_behind = to_next_slab(raw_product, (0, 1), (1, 1))
-    after = raw_product
-    for width, passed in zip(EVEN[1:], (after, received[1], after)):
-        origin = RAW if first < RAW + NEAR else RAW + NEAR
-        source = near_behind if first < RAW + NEAR else far_behind
-        first, after = send(0, source, origin, first, width, SLOW, after, passed)
+    origin, after = first, raw_product
+    for width in EVEN[2:]:
+        first, after = send(0, far_behind, origin, first, width, SLOW, after, received[1])
     held, gated = later_of(
         context_start, lines, near_behind, near, far_behind, far, queries, own, places
     )

time: 33.1 us -> 33.2 us (level)
  no operation moved by 1% of the time
where the time goes in v12:
time: 33.2 us; the launch traced here: 32.9 us
  starting transfers between devices  14.9 us (45%)
  waiting for transfers between devices  8.96 us (27%)
  Pallas kernels  8.12 us (24%)
  between operations  0.96 us (3%)
    ppermute x7, starting transfers between devices, to_next_section(): return lax.ppermute(value, ('ctx', 'pipe'), pairs)  7.82 us
    ppermute x4, starting transfers between devices, to_next_slab(): return lax.ppermute(value, ('ctx', 'pipe'), pairs)  7.05 us
    ppermute x4, waiting for transfers between devices, to_next_slab(): return lax.ppermute(value, ('ctx', 'pipe'), pairs)  4.61 us
    ppermute x7, waiting for transfers between devices, to_next_section(): return lax.ppermute(value, ('ctx', 'pipe'), pairs)  4.35 us
    pallas_call x1, Pallas kernels, later_of(): call(functools.partial(later_kernel, places), 'later', (jax.ShapeDtypeStr...  2.65 us
    pallas_call x4, Pallas kernels, finish(): call(functools.partial(finish_kernel, places[0][0], places), 'finish', ja...  2.41 us
    pallas_call x1, Pallas kernels, product_of(): call(product_kernel, 'product', (array(groups, taps, F32), array(rows, NE...  1.67 us
    pallas_call x1, Pallas kernels, raw_finish(): call(raw_kernel, 'raw', jax.ShapeDtypeStruct(held.shape, BF16), [SMEM] +...  1.14 us
  transfers between devices with their start and end apart: 11, of which 5 were waited for; matrix products, arithmetic and copies ran while one was open for 0% of the time, Pallas kernels for 22%

profile of v12, /device:TPU:12, one launch (start us, length us, event | category | flops | bytes accessed | tf_op | source)
XLA Modules:
  0.0 32.9 jit_solution(15878891664172935380)
XLA Ops:
  0.0 0.0 copy-start.2
  0.0 0.0 copy-start.3
  0.0 0.0 copy-start.4
  0.0 0.1 lead.1
  0.1 0.0 copy-start
  0.2 0.0 copy-start.1
  0.2 0.9 %collective-permute-start = (bf16[128,4096]{1,0:T(8,128)(2,1)S(1)}, bf16[128,4096]{1,0:T(8,128)(2,1)S(1)}, u32[]{:S(2)}, u32[]{:S(2)}) collective-permute-start(bf16[128,4096]{1,0:T(8,128)(2,1)S(1)} %get-tuple-element.15.refs_5_.refs_3_), channel_id=1, source_target_pairs={{0,4},{8,12},{16,20},{24,28},{2,6},{10,14},{18,22},{26,30}} | collective-permute-start | bytes 3145736 | tf_op jit(solution)/shard_map/ppermute | solution.py:37
  1.0 1.3 %collective-permute-start.2 = (bf16[264,384]{1,0:T(8,128)(2,1)S(1)}, bf16[264,384]{1,0:T(8,128)(2,1)S(1)}, u32[]{:S(2)}, u32[]{:S(2)}) collective-permute-start(bf16[264,384]{1,0:T(8,128)(2,1)S(1)} %get-tuple-element.19.raw_ref), channel_id=1, source_target_pairs={{0,1},{4,5},{8,9},{12,13},{16,17},{20,21},{24,25},{28,29},{2,3},{6... | collective-permute-start | bytes 608264 | tf_op jit(solution)/shard_map/ppermute | solution.py:43
  2.3 0.0 copy-done.2
  2.3 0.0 copy-done.3
  2.4 0.0 copy-done.4
  2.4 1.7 %product.1 = (f32[256,128]{1,0:T(8,128)S(1)}, bf16[128,2048]{1,0:T(8,128)(2,1)S(1)}, bf16[128,2048]{1,0:T(8,128)(2,1)S(1)}) custom-call(bf16[1,128,4096]{2,1,0:T(8,128)(2,1)} %refs_0_.11, bf16[1,128,4096]{2,1,0:T(8,128)(2,1)} %refs_1_.3, bf16[1,256,128]{2,1,0:T(8,128)(2,1)S(1)} %copy-done.2, f32[1,256]{1,0:T(1,128)S(1)} %copy-done.3, ...), custom_call_target="tpu_custom_call" | custom-call | flops 1024 | bytes 1024 | tf_op jit(solution)/shard_map/product/pallas_call | solution.py:207
  4.7 0.0 collective-permute-done.refs_2_.refs_3_
  4.7 0.0 copy-done
  4.7 0.0 copy-done.1
  4.7 0.7 %collective-permute-start.4 = (bf16[128,1536]{1,0:T(8,128)(2,1)S(1)}, bf16[128,1536]{1,0:T(8,128)(2,1)S(1)}, u32[]{:S(2)}, u32[]{:S(2)}) collective-permute-start(bf16[128,1536]{1,0:T(8,128)(2,1)S(1)} %own.6._.refs_7_), channel_id=1, source_target_pairs={{4,5},{12,13},{20,21},{28,29},{6,7},{14,15},{22,23},{30,31}} | collective-permute-start | bytes 1179656 | tf_op jit(solution)/shard_map/ppermute | solution.py:43
  5.5 2.3 %collective-permute-start.1 = (bf16[128,2048]{1,0:T(8,128)(2,1)S(1)}, bf16[128,2048]{1,0:T(8,128)(2,1)S(1)}, u32[]{:S(2)}, u32[]{:S(2)}) collective-permute-start(bf16[128,2048]{1,0:T(8,128)(2,1)S(1)} %hold.4.refs_6_.refs_3_), channel_id=1, source_target_pairs={{4,8},{12,16},{20,24},{1,5},{9,13},{17,21},{25,29},{5,9},{13,17},{... | collective-permute-start | bytes 1572872 | tf_op jit(solution)/shard_map/ppermute | solution.py:37
  7.8 0.7 %collective-permute-start.5 = (bf16[128,2176]{1,0:T(8,128)(2,1)S(1)}, bf16[128,2176]{1,0:T(8,128)(2,1)S(1)}, u32[]{:S(2)}, u32[]{:S(2)}) collective-permute-start(bf16[128,2176]{1,0:T(8,128)(2,1)S(1)} %own.7._.refs_8_), channel_id=1, source_target_pairs={{4,5},{12,13},{20,21},{28,29},{6,7},{14,15},{22,23},{30,31}} | collective-permute-start | bytes 1671176 | tf_op jit(solution)/shard_map/ppermute | solution.py:43
  8.5 1.9 %collective-permute-done.2.received_ref = bf16[264,384]{1,0:T(8,128)(2,1)S(1)} collective-permute-done((bf16[264,384]{1,0:T(8,128)(2,1)S(1)}, bf16[264,384]{1,0:T(8,128)(2,1)S(1)}, u32[]{:S(2)}, u32[]{:S(2)}) %collective-permute-start.2) | collective-permute-done | bytes 202784 | tf_op jit(solution)/shard_map/ppermute | solution.py:43
  10.5 1.9 %collective-permute-start.3 = (bf16[128,2048]{1,0:T(8,128)(2,1)S(1)}, bf16[128,2048]{1,0:T(8,128)(2,1)S(1)}, u32[]{:S(2)}, u32[]{:S(2)}) collective-permute-start(bf16[128,2048]{1,0:T(8,128)(2,1)S(1)} %hold.5.refs_5_), channel_id=1, source_target_pairs={{4,8},{12,16},{20,24},{1,5},{9,13},{17,21},{25,29},{5,9},{13,17},{... | collective-permute-start | bytes 1572872 | tf_op jit(solution)/shard_map/ppermute | solution.py:37
  12.4 0.0 collective-permute-done.4._.refs_1_
  12.4 3.5 %collective-permute-done.1.refs_2_ = bf16[128,2048]{1,0:T(8,128)(2,1)S(1)} collective-permute-done((bf16[128,2048]{1,0:T(8,128)(2,1)S(1)}, bf16[128,2048]{1,0:T(8,128)(2,1)S(1)}, u32[]{:S(2)}, u32[]{:S(2)}) %collective-permute-start.1) | collective-permute-done | bytes 524320 | tf_op jit(solution)/shard_map/ppermute | solution.py:37
  16.0 1.3 %collective-permute-start.8 = (bf16[128,1024]{1,0:T(8,128)(2,1)S(1)}, bf16[128,1024]{1,0:T(8,128)(2,1)S(1)}, u32[]{:S(2)}, u32[]{:S(2)}) collective-permute-start(bf16[128,1024]{1,0:T(8,128)(2,1)S(1)} %own.8.refs_6_.refs_9_), channel_id=1, source_target_pairs={{0,1},{8,9},{16,17},{24,25},{2,3},{10,11},{18,19},{26,27}} | collective-permute-start | bytes 786440 | tf_op jit(solution)/shard_map/ppermute | solution.py:43
  17.3 1.3 %collective-permute-start.9 = (bf16[128,1024]{1,0:T(8,128)(2,1)S(1)}, bf16[128,1024]{1,0:T(8,128)(2,1)S(1)}, u32[]{:S(2)}, u32[]{:S(2)}) collective-permute-start(bf16[128,1024]{1,0:T(8,128)(2,1)S(1)} %own.9._.refs_10_), channel_id=1, source_target_pairs={{0,1},{8,9},{16,17},{24,25},{2,3},{10,11},{18,19},{26,27}} | collective-permute-start | bytes 786440 | tf_op jit(solution)/shard_map/ppermute | solution.py:43
  18.6 1.9 %collective-permute-start.10 = (bf16[128,384]{1,0:T(8,128)(2,1)S(1)}, bf16[128,384]{1,0:T(8,128)(2,1)S(1)}, u32[]{:S(2)}, u32[]{:S(2)}) collective-permute-start(bf16[128,384]{1,0:T(8,128)(2,1)S(1)} %hold.7.refs_6_.refs_5_), channel_id=1, source_target_pairs={{1,5},{9,13},{17,21},{25,29},{5,9},{13,17},{21,25},{3,7},{11,15},{... | collective-permute-start | bytes 294920 | tf_op jit(solution)/shard_map/ppermute | solution.py:37
  20.5 1.1 %collective-permute-done.3.refs_2_.refs_4_ = bf16[128,2048]{1,0:T(8,128)(2,1)S(1)} collective-permute-done((bf16[128,2048]{1,0:T(8,128)(2,1)S(1)}, bf16[128,2048]{1,0:T(8,128)(2,1)S(1)}, u32[]{:S(2)}, u32[]{:S(2)}) %collective-permute-start.3) | collective-permute-done | bytes 524320 | tf_op jit(solution)/shard_map/ppermute | solution.py:37
  21.6 0.0 collective-permute-done.5.refs_7_.refs_2_
  21.6 1.3 %collective-permute-start.7 = (bf16[128,768]{1,0:T(8,128)(2,1)S(1)}, bf16[128,768]{1,0:T(8,128)(2,1)S(1)}, u32[]{:S(2)}, u32[]{:S(2)}) collective-permute-start(bf16[128,768]{1,0:T(8,128)(2,1)S(1)} %own.10.refs_6_.refs_11_), channel_id=1, source_target_pairs={{0,1},{8,9},{16,17},{24,25},{2,3},{10,11},{18,19},{26,27}} | collective-permute-start | bytes 589832 | tf_op jit(solution)/shard_map/ppermute | solution.py:43
  22.9 1.3 %collective-permute-start.6 = (bf16[128,896]{1,0:T(8,128)(2,1)S(1)}, bf16[128,896]{1,0:T(8,128)(2,1)S(1)}, u32[]{:S(2)}, u32[]{:S(2)}) collective-permute-start(bf16[128,896]{1,0:T(8,128)(2,1)S(1)} %own.11.refs_12_), channel_id=1, source_target_pairs={{0,1},{8,9},{16,17},{24,25},{2,3},{10,11},{18,19},{26,27}} | collective-permute-start | bytes 688136 | tf_op jit(solution)/shard_map/ppermute | solution.py:43
  24.2 2.7 %later.1 = (bf16[1,128,4096]{2,1,0:T(8,128)(2,1)}, f32[128,4096]{1,0:T(8,128)S(1)}) custom-call(s32[1]{0:T(128)S(6)} %copy.27.refs_0_, f32[256,128]{1,0:T(8,128)S(1)} %get-tuple-element.16.refs_1_.refs_6_, bf16[128,2048]{1,0:T(8,128)(2,1)S(1)} %collective-permute-done.1.refs_2_, bf16[128,2048]{1,0:T(8,128)(2,1)S(1)} %hold.4.refs_6_.refs_3_, ...), custom_call_target="tpu_custom_call" | custom-call | flops 20000000000 | bytes 1024 | tf_op jit(solution)/shard_map/later/pallas_call | solution.py:367
  26.9 0.0 collective-permute-done.10.refs_2_
  26.9 1.1 %raw.1.refs_3_ = bf16[1,128,4096]{2,1,0:T(8,128)(2,1)} custom-call(s32[1]{0:T(128)S(6)} %copy.27.refs_0_, f32[24,128]{1,0:T(8,128)S(1)} %get-tuple-element.23.refs_1_, bf16[128,384]{1,0:T(8,128)(2,1)S(1)} %collective-permute-done.10.refs_2_, bf16[128,4096]{1,0:T(8,128)(2,1)S(1)} %collective-permute-done.refs_2_.refs_3_, ...), custom_call_target="tpu_custom_call", output_to_operand_aliasing={{}: (9, {})} | custom-call | flops 20000000000 | bytes 1024 | tf_op jit(solution)/shard_map/raw/pallas_call | solution.py:410
  28.1 0.0 collective-permute-done.9.refs_2_
  28.1 0.0 collective-permute-done.8.refs_1_
  28.1 0.9 %finish.5.refs_2_ = bf16[1,128,4096]{2,1,0:T(8,128)(2,1)} custom-call(f32[128,4096]{1,0:T(8,128)S(1)} %get-tuple-element.22.refs_0_.refs_7_, bf16[128,1024]{1,0:T(8,128)(2,1)S(1)} %collective-permute-done.8.refs_1_, bf16[128,1024]{1,0:T(8,128)(2,1)S(1)} %collective-permute-done.9.refs_2_, ...), custom_call_target="tpu_custom_call", output_to_operand_aliasing={{}: (3, {})} | custom-call | flops 20000000000 | bytes 1024 | tf_op jit(solution)/shard_map/finish/pallas_call | solution.py:445
  29.0 0.7 %collective-permute-done.7.refs_1_ = bf16[128,768]{1,0:T(8,128)(2,1)S(1)} collective-permute-done((bf16[128,768]{1,0:T(8,128)(2,1)S(1)}, bf16[128,768]{1,0:T(8,128)(2,1)S(1)}, u32[]{:S(2)}, u32[]{:S(2)}) %collective-permute-start.7) | collective-permute-done | bytes 196640 | tf_op jit(solution)/shard_map/ppermute | solution.py:43
  29.7 0.7 %finish.6.refs_2_ = bf16[1,128,4096]{2,1,0:T(8,128)(2,1)} custom-call(f32[128,4096]{1,0:T(8,128)S(1)} %get-tuple-element.22.refs_0_.refs_7_, bf16[128,768]{1,0:T(8,128)(2,1)S(1)} %collective-permute-done.7.refs_1_, bf16[1,128,4096]{2,1,0:T(8,128)(2,1)} %finish.5.refs_2_), custom_call_target="tpu_custom_call", output_to_operand_aliasing={{}: (2, {})} | custom-call | flops 20000000000 | bytes 1024 | tf_op jit(solution)/shard_map/finish/pallas_call | solution.py:445
  30.5 1.7 %collective-permute-done.6.refs_1_ = bf16[128,896]{1,0:T(8,128)(2,1)S(1)} collective-permute-done((bf16[128,896]{1,0:T(8,128)(2,1)S(1)}, bf16[128,896]{1,0:T(8,128)(2,1)S(1)}, u32[]{:S(2)}, u32[]{:S(2)}) %collective-permute-start.6) | collective-permute-done | bytes 229408 | tf_op jit(solution)/shard_map/ppermute | solution.py:43
  32.2 0.8 %finish.7 = bf16[1,128,4096]{2,1,0:T(8,128)(2,1)} custom-call(f32[128,4096]{1,0:T(8,128)S(1)} %get-tuple-element.22.refs_0_.refs_7_, bf16[128,896]{1,0:T(8,128)(2,1)S(1)} %collective-permute-done.6.refs_1_, bf16[1,128,4096]{2,1,0:T(8,128)(2,1)} %finish.6.refs_2_), custom_call_target="tpu_custom_call", output_to_operand_aliasing={{}: (2, {})} | custom-call | flops 20000000000 | bytes 1024 | tf_op jit(solution)/shard_map/finish/pallas_call | solution.py:445
  (12 shorter events, 0.2 us)
Async XLA Ops:
  0.0 2.3 %copy-start.2 = (bf16[1,256,128]{2,1,0:T(8,128)(2,1)S(1)}, bf16[1,256,128]{2,1,0:T(8,128)(2,1)}, u32[]{:S(2)}) copy-start(bf16[1,256,128]{2,1,0:T(8,128)(2,1)} %refs_2_.3) | copy-start | bytes 196612
  0.0 2.3 %copy-start.3 = (f32[1,256]{1,0:T(1,128)S(1)}, f32[1,256]{1,0:T(1,128)}, u32[]{:S(2)}) copy-start(f32[1,256]{1,0:T(1,128)} %refs_3_.3) | copy-start | bytes 3076
  0.0 2.3 %copy-start.4 = (s32[1,256]{1,0:T(1,128)S(1)}, s32[1,256]{1,0:T(1,128)}, u32[]{:S(2)}) copy-start(s32[1,256]{1,0:T(1,128)} %refs_4_.9) | copy-start | bytes 3076
  0.1 4.6 %copy-start = (bf16[1,128,4096]{2,1,0:T(8,128)(2,1)S(1)}, bf16[1,128,4096]{2,1,0:T(8,128)(2,1)}, u32[]{:S(2)}) copy-start(bf16[1,128,4096]{2,1,0:T(8,128)(2,1)} %refs_6_.1) | copy-start | bytes 3145732
  0.2 4.6 %copy-start.1 = (bf16[128,4096]{1,0:T(8,128)(2,1)S(1)}, bf16[128,4096]{1,0:T(8,128)(2,1)}, u32[]{:S(2)}) copy-start(bf16[128,4096]{1,0:T(8,128)(2,1)} %refs_8_.1) | copy-start | bytes 3145732
  0.2 4.5 %collective-permute-start = (bf16[128,4096]{1,0:T(8,128)(2,1)S(1)}, bf16[128,4096]{1,0:T(8,128)(2,1)S(1)}, u32[]{:S(2)}, u32[]{:S(2)}) collective-permute-start(bf16[128,4096]{1,0:T(8,128)(2,1)S(1)} %get-tuple-element.15.refs_5_.refs_3_), channel_id=1, source_target_pairs={{0,4},{8,12},{16,20},{24,28},{2,6},{10,14},{18,22},{26,30}} | collective-permute-start | bytes 3145736 | tf_op jit(solution)/shard_map/ppermute | solution.py:37
  1.0 9.4 %collective-permute-start.2 = (bf16[264,384]{1,0:T(8,128)(2,1)S(1)}, bf16[264,384]{1,0:T(8,128)(2,1)S(1)}, u32[]{:S(2)}, u32[]{:S(2)}) collective-permute-start(bf16[264,384]{1,0:T(8,128)(2,1)S(1)} %get-tuple-element.19.raw_ref), channel_id=1, source_target_pairs={{0,1},{4,5},{8,9},{12,13},{16,17},{20,21},{24,25},{28,29},{2,3},{6... | collective-permute-start | bytes 608264 | tf_op jit(solution)/shard_map/ppermute | solution.py:43
  4.7 7.6 %collective-permute-start.4 = (bf16[128,1536]{1,0:T(8,128)(2,1)S(1)}, bf16[128,1536]{1,0:T(8,128)(2,1)S(1)}, u32[]{:S(2)}, u32[]{:S(2)}) collective-permute-start(bf16[128,1536]{1,0:T(8,128)(2,1)S(1)} %own.6._.refs_7_), channel_id=1, source_target_pairs={{4,5},{12,13},{20,21},{28,29},{6,7},{14,15},{22,23},{30,31}} | collective-permute-start | bytes 1179656 | tf_op jit(solution)/shard_map/ppermute | solution.py:43
  5.5 10.5 %collective-permute-start.1 = (bf16[128,2048]{1,0:T(8,128)(2,1)S(1)}, bf16[128,2048]{1,0:T(8,128)(2,1)S(1)}, u32[]{:S(2)}, u32[]{:S(2)}) collective-permute-start(bf16[128,2048]{1,0:T(8,128)(2,1)S(1)} %hold.4.refs_6_.refs_3_), channel_id=1, source_target_pairs={{4,8},{12,16},{20,24},{1,5},{9,13},{17,21},{25,29},{5,9},{13,17},{... | collective-permute-start | bytes 1572872 | tf_op jit(solution)/shard_map/ppermute | solution.py:37
  7.8 13.7 %collective-permute-start.5 = (bf16[128,2176]{1,0:T(8,128)(2,1)S(1)}, bf16[128,2176]{1,0:T(8,128)(2,1)S(1)}, u32[]{:S(2)}, u32[]{:S(2)}) collective-permute-start(bf16[128,2176]{1,0:T(8,128)(2,1)S(1)} %own.7._.refs_8_), channel_id=1, source_target_pairs={{4,5},{12,13},{20,21},{28,29},{6,7},{14,15},{22,23},{30,31}} | collective-permute-start | bytes 1671176 | tf_op jit(solution)/shard_map/ppermute | solution.py:43
  10.5 11.1 %collective-permute-start.3 = (bf16[128,2048]{1,0:T(8,128)(2,1)S(1)}, bf16[128,2048]{1,0:T(8,128)(2,1)S(1)}, u32[]{:S(2)}, u32[]{:S(2)}) collective-permute-start(bf16[128,2048]{1,0:T(8,128)(2,1)S(1)} %hold.5.refs_5_), channel_id=1, source_target_pairs={{4,8},{12,16},{20,24},{1,5},{9,13},{17,21},{25,29},{5,9},{13,17},{... | collective-permute-start | bytes 1572872 | tf_op jit(solution)/shard_map/ppermute | solution.py:37
  16.0 12.1 %collective-permute-start.8 = (bf16[128,1024]{1,0:T(8,128)(2,1)S(1)}, bf16[128,1024]{1,0:T(8,128)(2,1)S(1)}, u32[]{:S(2)}, u32[]{:S(2)}) collective-permute-start(bf16[128,1024]{1,0:T(8,128)(2,1)S(1)} %own.8.refs_6_.refs_9_), channel_id=1, source_target_pairs={{0,1},{8,9},{16,17},{24,25},{2,3},{10,11},{18,19},{26,27}} | collective-permute-start | bytes 786440 | tf_op jit(solution)/shard_map/ppermute | solution.py:43
  17.3 10.8 %collective-permute-start.9 = (bf16[128,1024]{1,0:T(8,128)(2,1)S(1)}, bf16[128,1024]{1,0:T(8,128)(2,1)S(1)}, u32[]{:S(2)}, u32[]{:S(2)}) collective-permute-start(bf16[128,1024]{1,0:T(8,128)(2,1)S(1)} %own.9._.refs_10_), channel_id=1, source_target_pairs={{0,1},{8,9},{16,17},{24,25},{2,3},{10,11},{18,19},{26,27}} | collective-permute-start | bytes 786440 | tf_op jit(solution)/shard_map/ppermute | solution.py:43
  18.6 8.3 %collective-permute-start.10 = (bf16[128,384]{1,0:T(8,128)(2,1)S(1)}, bf16[128,384]{1,0:T(8,128)(2,1)S(1)}, u32[]{:S(2)}, u32[]{:S(2)}) collective-permute-start(bf16[128,384]{1,0:T(8,128)(2,1)S(1)} %hold.7.refs_6_.refs_5_), channel_id=1, source_target_pairs={{1,5},{9,13},{17,21},{25,29},{5,9},{13,17},{21,25},{3,7},{11,15},{... | collective-permute-start | bytes 294920 | tf_op jit(solution)/shard_map/ppermute | solution.py:37
  21.6 8.2 %collective-permute-start.7 = (bf16[128,768]{1,0:T(8,128)(2,1)S(1)}, bf16[128,768]{1,0:T(8,128)(2,1)S(1)}, u32[]{:S(2)}, u32[]{:S(2)}) collective-permute-start(bf16[128,768]{1,0:T(8,128)(2,1)S(1)} %own.10.refs_6_.refs_11_), channel_id=1, source_target_pairs={{0,1},{8,9},{16,17},{24,25},{2,3},{10,11},{18,19},{26,27}} | collective-permute-start | bytes 589832 | tf_op jit(solution)/shard_map/ppermute | solution.py:43
  22.9 9.3 %collective-permute-start.6 = (bf16[128,896]{1,0:T(8,128)(2,1)S(1)}, bf16[128,896]{1,0:T(8,128)(2,1)S(1)}, u32[]{:S(2)}, u32[]{:S(2)}) collective-permute-start(bf16[128,896]{1,0:T(8,128)(2,1)S(1)} %own.11.refs_12_), channel_id=1, source_target_pairs={{0,1},{8,9},{16,17},{24,25},{2,3},{10,11},{18,19},{26,27}} | collective-permute-start | bytes 688136 | tf_op jit(solution)/shard_map/ppermute | solution.py:43

commit v13 on v12

--- a/solution.py
+++ b/solution.py
@@ -11,9 +11,9 @@
 ROW_BLOCK = 32
 RAW = 384
 ODD = (1536, 2176)
-EVEN = (1024, 1024, 768, 896)
+EVEN = (1024, 768, 896, 1024)
 PIECES = 4
-NEAR = 2048
+NEAR = 1792
 LINES = 8
 F32 = jnp.float32
 BF16 = jnp.bfloat16
@@ -89,10 +89,10 @@
             copy.wait()
         first = 0
         for out_ref in out_refs:
-            for tile in range(0, out_ref.shape[1], 4 * LANES):
-                at = slice(first + tile, first + tile + 4 * LANES)
+            for tile in range(0, out_ref.shape[1], LANES):
+                at = slice(first + tile, first + tile + LANES)
                 product = keys_in[span, at].astype(F32) * values_in[span, at].astype(F32)
-                out_ref[span, tile : tile + 4 * LANES] = product.astype(BF16)
+                out_ref[span, tile : tile + LANES] = product.astype(BF16)
             first += out_ref.shape[1]
 
 
@@ -110,10 +110,10 @@
 
 def lead_kernel(*refs):
     bank_ref, scales_ref, assign_ref, queries_ref, keys_ref, values_ref = refs[:6]
-    raw_ref, whole_ref = refs[6:8]
+    raw_ref, rest_ref = refs[6:8]
     bank_in, scales_in, assign_in, lines_ref, keys_in, values_in, sems, own_sems = refs[8:]
     count = lines_ref.shape[0]
-    rows = whole_ref.shape[0]
+    rows = rest_ref.shape[0]
 
     @pl.when(is_first())
     def _():
@@ -134,8 +134,7 @@
                 taken = lines_ref[part * LINES : (part + 1) * LINES, :].astype(BF16)
                 raw_ref[2 * rows :, part * LANES : (part + 1) * LANES] = taken
 
-        multiply(keys_ref, values_ref, keys_in, values_in, sems, [whole_ref], taps)
-        raw_ref[rows : 2 * rows, :] = whole_ref[:, :RAW]
+        multiply(keys_ref, values_ref, keys_in, values_in, sems, [raw_ref.at[pl.ds(rows, rows)], rest_ref], taps)
         copies[3].wait()
 
 
@@ -150,7 +149,7 @@
         "lead",
         (
             array(2 * rows + LINES, RAW),
-            array(rows, total),
+            array(rows, total - RAW),
         ),
         [HBM] * 6,
         (VMEM,) * 2,
@@ -179,9 +178,8 @@
 
 
 def product_kernel(*refs):
-    keys_ref, values_ref, bank_ref, scales_ref, assign_ref, whole_ref = refs[:6]
-    lines_ref, near_ref, far_ref, keys_in, values_in, sems = refs[6:]
-    near = near_ref.shape[1]
+    keys_ref, values_ref, bank_ref, scales_ref, assign_ref, rest_ref = refs[:6]
+    lines_ref, near_ref, far_ref, tail_ref, keys_in, values_in, sems = refs[6:]
 
     def taps():
         fill_lines(bank_ref[0], scales_ref[...], assign_ref[...], lines_ref)
@@ -192,26 +190,25 @@
 
     @pl.when(jnp.logical_and(is_first(), is_slab(1)))
     def _():
-        near_ref[...] = whole_ref[:, RAW : RAW + near]
-        far_ref[:, : far_ref.shape[1] - RAW] = whole_ref[:, RAW + near :]
-        far_ref[:, far_ref.shape[1] - RAW :] = whole_ref[:, :RAW]
+        near_ref[...] = rest_ref[:, :NEAR]
+        far_ref[...] = rest_ref[:, NEAR:]
 
     @pl.when(jnp.logical_not(is_first()))
     def _():
-        multiply(keys_ref, values_ref, keys_in, values_in, sems, [near_ref, far_ref], taps)
-
-
-def product_of(keys, values, bank, scales, assign, whole):
+        multiply(keys_ref, values_ref, keys_in, values_in, sems, [near_ref, far_ref, tail_ref], taps)
+
+
+def product_of(keys, values, bank, scales, assign, rest):
     rows, total = keys.shape[1:]
     groups, taps = assign.shape[1], bank.shape[2]
     return call(
         product_kernel,
         "product",
-        (array(groups, taps, F32), array(rows, NEAR), array(rows, total - NEAR)),
+        (array(groups, taps, F32), array(rows, NEAR), array(rows, total - RAW - NEAR), array(rows, RAW)),
         [HBM, HBM] + [VMEM] * 4,
-        (VMEM,) * 3,
+        (VMEM,) * 4,
         product_scratch(rows, total),
-    )(keys, values, bank, scales, assign, whole)
+    )(keys, values, bank, scales, assign, rest)
 
 
 def mix(table_ref, row, share, window, store):
@@ -275,7 +272,7 @@
 def own_of(odd, origin, start, lines, behind, product, queries, residual, first, width, weight, *after):
     rows, total = residual.shape
     return call(
-        functools.partial(own_kernel, odd, first, first - origin, first),
+        functools.partial(own_kernel, odd, first, first - origin, first - RAW),
         "own",
         array(rows, width),
         [SMEM] + [VMEM] * 5 + [ANY] * len(after),
@@ -285,30 +282,34 @@
     )(start, lines, behind, product, queries, residual, *after)
 
 
-def pick_kernel(raw_ref, received_ref, _, queries_ref, product_ref, lines_ref):
+def pick_kernel(raw_ref, received_ref, tail_ref, _, queries_ref, product_ref, lines_ref):
     rows = queries_ref.shape[0]
 
     def take(source):
         queries_ref[...] = source[:rows, :]
-        product_ref[...] = source[rows : 2 * rows, :]
+        product_ref[:, :RAW] = source[rows : 2 * rows, :]
         for part in range(RAW // LANES):
             taken = source[2 * rows :, part * LANES : (part + 1) * LANES]
             lines_ref[part * LINES : (part + 1) * LINES, :] = taken.astype(F32)
 
     pl.when(is_first())(lambda: take(raw_ref))
-    pl.when(jnp.logical_not(is_first()))(lambda: take(received_ref))
-
-
-def pick_of(raw, received, taps, after):
+
+    @pl.when(jnp.logical_not(is_first()))
+    def _():
+        take(received_ref)
+        product_ref[:, RAW:] = tail_ref[...]
+
+
+def pick_of(raw, received, tail, taps, after):
     rows, width = (raw.shape[0] - LINES) // 2, raw.shape[1]
     return call(
         pick_kernel,
         "pick",
-        (array(rows, width), array(rows, width), array(RAW // LANES * LINES, taps, F32)),
-        [VMEM, VMEM, ANY],
+        (array(rows, width), array(rows, 2 * width), array(RAW // LANES * LINES, taps, F32)),
+        [VMEM, VMEM, VMEM, ANY],
         (VMEM,) * 3,
         weight=SLOW,
-    )(raw, received, after)
+    )(raw, received, tail, after)
 
 
 def hold_kernel(value_ref, _, out_ref):
@@ -337,8 +338,8 @@
 
 
 def later_kernel(places, *refs):
-    start_ref, lines_ref, near_behind, near_ref, far_behind, far_ref, queries_ref = refs[:7]
-    own_refs = refs[7 : 7 + len(places)]
+    start_ref, lines_ref, near_behind, near_ref, far_behind, far_ref, raw_behind, tail_ref, queries_ref = refs[:9]
+    own_refs = refs[9 : 9 + len(places)]
     out_ref, gated_ref, table_ref, sems = refs[-4:]
     total = queries_ref.shape[2]
     share = share_of(lines_ref, total)
@@ -352,51 +353,45 @@
 
     @pl.when(jnp.logical_not(is_first()))
     def _():
-        for first, behind_ref, product_ref in ((0, near_behind, near_ref), (NEAR, far_behind, far_ref)):
+        parts = (
+            (0, 0, near_behind, near_ref),
+            (NEAR, 0, far_behind, far_ref),
+            (total - RAW, RAW, raw_behind, tail_ref),
+        )
+        for first, skip, behind_ref, product_ref in parts:
 
             def store(at, span, mixed):
                 cols = slice(first + at.start, first + at.stop)
                 gated_ref[span, cols] = queries_ref[0, span, cols].astype(F32) * mixed
 
             width, line = product_ref.shape[1], first // LANES * share
-            mix_all(width, share, lines_ref, line, table_ref, start_ref, behind_ref, product_ref, (0, 0), store)
-
-
-def later_of(start, lines, near_behind, near, far_behind, far, queries, own, places):
+            at = (skip, 0)
+            mix_all(width, share, lines_ref, line, table_ref, start_ref, behind_ref, product_ref, at, store)
+
+
+def later_of(start, lines, near_behind, near, far_behind, far, raw_behind, tail, queries, own, places):
     rows, total = queries.shape[1:]
     return call(
         functools.partial(later_kernel, places),
         "later",
         (jax.ShapeDtypeStruct((1, rows, total), BF16), array(rows, total, F32)),
-        [SMEM] + [VMEM] * (6 + len(own)),
+        [SMEM] + [VMEM] * (8 + len(own)),
         (ANY, VMEM),
-        [table_scratch(lines, NEAR, total), pltpu.SemaphoreType.DMA((len(own),))],
+        [table_scratch(lines, total - RAW - NEAR, total), pltpu.SemaphoreType.DMA((len(own),))],
         weight=SLOW,
-    )(start, lines, near_behind, near, far_behind, far, queries, *own)
-
-
-def raw_kernel(*refs):
-    start_ref, lines_ref, behind_ref, chip_ref, far_ref, product_ref, queries_ref, gated_ref, residual_ref = refs[:9]
-    out_ref, chosen_ref, table_ref, buffer, sems = refs[10:]
+    )(start, lines, near_behind, near, far_behind, far, raw_behind, tail, queries, *own)
+
+
+def raw_kernel(start_ref, lines_ref, behind_ref, product_ref, queries_ref, gated_ref, residual_ref, _, *refs):
+    out_ref, table_ref, buffer, sems = refs
     width = buffer.shape[1]
     share = share_of(lines_ref, width)
-    far = far_ref.shape[1]
-    sources = (
-        (jnp.logical_and(is_first(), is_slab(0)), far_ref, slice(far - width, far)),
-        (jnp.logical_and(is_first(), is_slab(1)), chip_ref, slice(0, width)),
-        (jnp.logical_not(is_first()), behind_ref, slice(0, width)),
-    )
-    for wanted, source, cols in sources:
-
-        @pl.when(wanted)
-        def _():
-            chosen_ref[...] = source[:, cols]
 
     def store(at, span, mixed):
         gated = queries_ref[span, at].astype(F32) * mixed
         buffer[span, at] = (residual_ref[span, at].astype(F32) + gated).astype(BF16)
 
-    mix_all(width, share, lines_ref, 0, table_ref, start_ref, chosen_ref, product_ref, (0, 0), store)
+    mix_all(width, share, lines_ref, 0, table_ref, start_ref, behind_ref, product_ref, (0, 0), store)
 
     @pl.when(jnp.logical_not(is_first()))
     def _():
@@ -405,23 +400,18 @@
     wait_all(send_out([(buffer, 0)], out_ref, sems))
 
 
-def raw_finish(held, start, lines, behind, chip_behind, far_behind, product, queries, gated, residual):
-    rows, width = product.shape
+def raw_finish(held, start, lines, behind, product, queries, gated, residual):
+    rows, width = queries.shape
     return call(
         raw_kernel,
         "raw",
         jax.ShapeDtypeStruct(held.shape, BF16),
-        [SMEM] + [VMEM] * 8 + [ANY],
+        [SMEM] + [VMEM] * 6 + [ANY],
         ANY,
-        [
-            pltpu.VMEM((rows, width), BF16),
-            table_scratch(lines, width, width),
-            pltpu.VMEM((rows, width), BF16),
-            pltpu.SemaphoreType.DMA((1,)),
-        ],
+        [table_scratch(lines, width, width), pltpu.VMEM((rows, width), BF16), pltpu.SemaphoreType.DMA((1,))],
         weight=SLOW,
-        aliases={9: 0},
-    )(start, lines, behind, chip_behind, far_behind, product, queries, gated, residual, held)
+        aliases={7: 0},
+    )(start, lines, behind, product, queries, gated, residual, held)
 
 
 def finish_kernel(odd, places, *refs):
@@ -461,53 +451,53 @@
     far_queries, keys, values = (
         pltpu.with_memory_space_constraint(value, pltpu.HBM) for value in (queries, keys, values)
     )
-    raw, whole = lead_of(*far_small, far_queries, keys, values)
+    raw, rest = lead_of(*far_small, far_queries, keys, values)
     raw_received = to_next_section(raw)
-    chip_behind = to_next_slab(whole, (0, 0))
-    lines, near, far = product_of(keys, values, *small, whole)
+    chip_behind = to_next_slab(rest, (0, 0))
+    lines, near, far, tail = product_of(keys, values, *small, rest)
     own, received, places = [], [], []
 
-    def send(odd, behind, origin, first, width, weight, *after):
+    def send(odd, behind, origin, first, width, *after):
         piece = own_of(
-            odd, origin, context_start, lines, behind, whole, queries, residual, first, width, weight, *after
+            odd, origin, context_start, lines, behind, rest, queries, residual, first, width, QUICK, *after
         )
         own.append(piece)
         received.append(to_next_section(piece, (odd,)))
         places.append((odd, first, width))
         return first + width, piece
 
-    first, after = send(1, chip_behind, 0, RAW, ODD[0], QUICK, lines)
+    links = ((1, 0), (0, 1), (1, 1))
+    first, after = send(1, chip_behind, RAW, RAW, ODD[0], lines)
     near = held_back(near, after)
-    near_behind = to_next_slab(near, (1, 0), (0, 1), (1, 1))
-    first, after = send(1, chip_behind, 0, first, ODD[1], QUICK, near)
-    raw_queries, raw_product, raw_lines = pick_of(raw, raw_received, lines.shape[1], after)
+    near_behind = to_next_slab(near, *links)
+    first, after = send(1, chip_behind, RAW, first, ODD[1], near)
+    raw_queries, raw_product, raw_lines = pick_of(raw, raw_received, tail, lines.shape[1], after)
     far = held_back(far, raw_queries)
-    far_behind = to_next_slab(far, (1, 0), (0, 1), (1, 1))
+    far_behind = to_next_slab(far, *links)
+    raw_product = held_back(raw_product, far)
+    raw_behind = to_next_slab(raw_product, (0, 0), *links)
     raw_queries = held_back(raw_queries, received[0], SLOW)
-    first, after = send(0, near_behind, RAW, RAW, EVEN[0], SLOW, raw_queries)
-    first, after = send(0, near_behind, RAW, first, EVEN[1], SLOW, after)
-    raw_product = held_back(raw_product, after)
-    raw_behind = to_next_slab(raw_product, (0, 1), (1, 1))
-    origin, after = first, raw_product
-    for width in EVEN[2:]:
-        first, after = send(0, far_behind, origin, first, width, SLOW, after, received[1])
+    first, after = send(0, near_behind, RAW, RAW, EVEN[0], raw_queries)
+    first, after = send(0, near_behind, RAW, first, EVEN[1], after)
+    origin = first
+    first, after = send(0, far_behind, origin, first, EVEN[2], after, received[1])
+    first, after = send(0, far_behind, origin, first, EVEN[3], after, raw_behind)
     held, gated = later_of(
-        context_start, lines, near_behind, near, far_behind, far, queries, own, places
+        context_start,
+        lines,
+        near_behind,
+        near,
+        far_behind,
+        far,
+        raw_behind,
+        tail,
+        queries,
+        own,
+        places,
     )
     odd = len(ODD)
     held = finish(held, gated, received[:odd], places[:odd])
-    held = raw_finish(
-        held,
-        context_start,
-        raw_lines,
-        raw_behind,
-        chip_behind,
-        far_behind,
-        raw_product,
-        raw_queries,
-        gated,
-        residual,
-    )
+    held = raw_finish(held, context_start, raw_lines, raw_behind, raw_product, raw_queries, gated, residual)
     for last in (odd + 2, odd + 3, odd + 4):
         begin = odd if last == odd + 2 else last - 1
         held = finish(held, gated, received[begin:last], places[begin:last])

time: 33.2 us -> 32.9 us (level)
  waiting for transfers between devices: 8.96 us -> 6.95 us
  starting transfers between devices: 14.9 us -> 16.5 us
    ppermute x4, waiting for transfers between devices: 4.61 us -> 2.74 us  [to_next_slab(): return lax.ppermute(value, ('ctx', 'pipe'), pairs)]
    ppermute x4, starting transfers between devices: 7.05 us -> 8.71 us  [to_next_slab(): return lax.ppermute(value, ('ctx', 'pipe'), pairs)]
where the time goes in v13:
time: 32.9 us; the launch traced here: 32.5 us
  starting transfers between devices  16.5 us (50%)
  Pallas kernels  8.07 us (25%)
  waiting for transfers between devices  6.95 us (21%)
  between operations  0.96 us (3%)
    ppermute x4, starting transfers between devices, to_next_slab(): return lax.ppermute(value, ('ctx', 'pipe'), pairs)  8.71 us
    ppermute x7, starting transfers between devices, to_next_section(): return lax.ppermute(value, ('ctx', 'pipe'), pairs)  7.82 us
    ppermute x7, waiting for transfers between devices, to_next_section(): return lax.ppermute(value, ('ctx', 'pipe'), pairs)  4.21 us
    ppermute x4, waiting for transfers between devices, to_next_slab(): return lax.ppermute(value, ('ctx', 'pipe'), pairs)  2.74 us
    pallas_call x1, Pallas kernels, later_of(): call(functools.partial(later_kernel, places), 'later', (jax.ShapeDtypeStr...  2.66 us
    pallas_call x4, Pallas kernels, finish(): call(functools.partial(finish_kernel, places[0][0], places), 'finish', ja...  2.38 us
    pallas_call x1, Pallas kernels, product_of(): call(product_kernel, 'product', (array(groups, taps, F32), array(rows, NE...  1.68 us
    pallas_call x1, Pallas kernels, raw_finish(): call(raw_kernel, 'raw', jax.ShapeDtypeStruct(held.shape, BF16), [SMEM] +...  1.11 us
  transfers between devices with their start and end apart: 11, of which 5 were waited for; matrix products, arithmetic and copies ran while one was open for 0% of the time, Pallas kernels for 22%

profile of v13, /device:TPU:12, one launch (start us, length us, event | category | flops | bytes accessed | tf_op | source)
XLA Modules:
  0.0 32.5 jit_solution(3435652879353731963)
XLA Ops:
  0.0 0.0 copy-start.2
  0.0 0.0 copy-start.3
  0.0 0.0 copy-start.4
  0.0 0.1 lead.1
  0.1 0.0 copy-start
  0.2 0.0 copy-start.1
  0.2 0.9 %collective-permute-start = (bf16[128,3712]{1,0:T(8,128)(2,1)S(1)}, bf16[128,3712]{1,0:T(8,128)(2,1)S(1)}, u32[]{:S(2)}, u32[]{:S(2)}) collective-permute-start(bf16[128,3712]{1,0:T(8,128)(2,1)S(1)} %get-tuple-element.16.refs_5_.refs_3_), channel_id=1, source_target_pairs={{0,4},{8,12},{16,20},{24,28},{2,6},{10,14},{18,22},{26,30}} | collective-permute-start | bytes 2850824 | tf_op jit(solution)/shard_map/ppermute | solution.py:37
  1.0 1.3 %collective-permute-start.2 = (bf16[264,384]{1,0:T(8,128)(2,1)S(1)}, bf16[264,384]{1,0:T(8,128)(2,1)S(1)}, u32[]{:S(2)}, u32[]{:S(2)}) collective-permute-start(bf16[264,384]{1,0:T(8,128)(2,1)S(1)} %get-tuple-element.20.raw_ref), channel_id=1, source_target_pairs={{0,1},{4,5},{8,9},{12,13},{16,17},{20,21},{24,25},{28,29},{2,3},{6... | collective-permute-start | bytes 608264 | tf_op jit(solution)/shard_map/ppermute | solution.py:43
  2.3 0.0 copy-done.2
  2.3 0.0 copy-done.3
  2.3 0.0 copy-done.4
  2.4 1.7 %product.1 = (f32[256,128]{1,0:T(8,128)S(1)}, bf16[128,1792]{1,0:T(8,128)(2,1)S(1)}, bf16[128,1920]{1,0:T(8,128)(2,1)S(1)}, bf16[128,384]{1,0:T(8,128)(2,1)S(1)}) custom-call(bf16[1,128,4096]{2,1,0:T(8,128)(2,1)} %refs_0_.10, bf16[1,128,4096]{2,1,0:T(8,128)(2,1)} %refs_1_.3, bf16[1,256,128]{2,1,0:T(8,128)(2,1)S(1)} %copy-done.2, f32[1,256]{1,0:T(1,128)S(1)} %copy-done.3, ...), custom_call_target="tpu_custom_call" | custom-call | flops 1024 | bytes 1024 | tf_op jit(solution)/shard_map/product/pallas_call | solution.py:204
  4.7 0.0 collective-permute-done.refs_2_
  4.7 0.0 copy-done
  4.7 0.0 copy-done.1
  4.8 0.7 %collective-permute-start.5 = (bf16[128,1536]{1,0:T(8,128)(2,1)S(1)}, bf16[128,1536]{1,0:T(8,128)(2,1)S(1)}, u32[]{:S(2)}, u32[]{:S(2)}) collective-permute-start(bf16[128,1536]{1,0:T(8,128)(2,1)S(1)} %own.6._.refs_9_), channel_id=1, source_target_pairs={{4,5},{12,13},{20,21},{28,29},{6,7},{14,15},{22,23},{30,31}} | collective-permute-start | bytes 1179656 | tf_op jit(solution)/shard_map/ppermute | solution.py:43
  5.5 2.3 %collective-permute-start.1 = (bf16[128,1792]{1,0:T(8,128)(2,1)S(1)}, bf16[128,1792]{1,0:T(8,128)(2,1)S(1)}, u32[]{:S(2)}, u32[]{:S(2)}) collective-permute-start(bf16[128,1792]{1,0:T(8,128)(2,1)S(1)} %hold.4.refs_6_.refs_3_), channel_id=1, source_target_pairs={{4,8},{12,16},{20,24},{1,5},{9,13},{17,21},{25,29},{5,9},{13,17},{... | collective-permute-start | bytes 1376264 | tf_op jit(solution)/shard_map/ppermute | solution.py:37
  7.8 0.7 %collective-permute-start.6 = (bf16[128,2176]{1,0:T(8,128)(2,1)S(1)}, bf16[128,2176]{1,0:T(8,128)(2,1)S(1)}, u32[]{:S(2)}, u32[]{:S(2)}) collective-permute-start(bf16[128,2176]{1,0:T(8,128)(2,1)S(1)} %own.7._.refs_10_), channel_id=1, source_target_pairs={{4,5},{12,13},{20,21},{28,29},{6,7},{14,15},{22,23},{30,31}} | collective-permute-start | bytes 1671176 | tf_op jit(solution)/shard_map/ppermute | solution.py:43
  8.5 2.0 %collective-permute-done.2.received_ref = bf16[264,384]{1,0:T(8,128)(2,1)S(1)} collective-permute-done((bf16[264,384]{1,0:T(8,128)(2,1)S(1)}, bf16[264,384]{1,0:T(8,128)(2,1)S(1)}, u32[]{:S(2)}, u32[]{:S(2)}) %collective-permute-start.2) | collective-permute-done | bytes 202784 | tf_op jit(solution)/shard_map/ppermute | solution.py:43
  10.5 1.9 %collective-permute-start.3 = (bf16[128,1920]{1,0:T(8,128)(2,1)S(1)}, bf16[128,1920]{1,0:T(8,128)(2,1)S(1)}, u32[]{:S(2)}, u32[]{:S(2)}) collective-permute-start(bf16[128,1920]{1,0:T(8,128)(2,1)S(1)} %hold.5._.refs_5_), channel_id=1, source_target_pairs={{4,8},{12,16},{20,24},{1,5},{9,13},{17,21},{25,29},{5,9},{13,17},{... | collective-permute-start | bytes 1474568 | tf_op jit(solution)/shard_map/ppermute | solution.py:37
  12.5 3.6 %collective-permute-start.4 = (bf16[128,768]{1,0:T(8,128)(2,1)S(1)}, bf16[128,768]{1,0:T(8,128)(2,1)S(1)}, u32[]{:S(2)}, u32[]{:S(2)}) collective-permute-start(bf16[128,768]{1,0:T(8,128)(2,1)S(1)} %hold.6.product_ref), channel_id=1, source_target_pairs={{0,4},{8,12},{16,20},{24,28},{4,8},{12,16},{20,24},{1,5},{9,13},{1... | collective-permute-start | bytes 589832 | tf_op jit(solution)/shard_map/ppermute | solution.py:37
  16.1 0.0 collective-permute-done.5._.refs_1_
  16.1 0.0 collective-permute-done.1.refs_2_
  16.1 1.3 %collective-permute-start.9 = (bf16[128,1024]{1,0:T(8,128)(2,1)S(1)}, bf16[128,1024]{1,0:T(8,128)(2,1)S(1)}, u32[]{:S(2)}, u32[]{:S(2)}) collective-permute-start(bf16[128,1024]{1,0:T(8,128)(2,1)S(1)} %own.8.refs_6_.refs_11_), channel_id=1, source_target_pairs={{0,1},{8,9},{16,17},{24,25},{2,3},{10,11},{18,19},{26,27}} | collective-permute-start | bytes 786440 | tf_op jit(solution)/shard_map/ppermute | solution.py:43
  17.5 1.3 %collective-permute-start.10 = (bf16[128,768]{1,0:T(8,128)(2,1)S(1)}, bf16[128,768]{1,0:T(8,128)(2,1)S(1)}, u32[]{:S(2)}, u32[]{:S(2)}) collective-permute-start(bf16[128,768]{1,0:T(8,128)(2,1)S(1)} %own.9.refs_6_.refs_12_), channel_id=1, source_target_pairs={{0,1},{8,9},{16,17},{24,25},{2,3},{10,11},{18,19},{26,27}} | collective-permute-start | bytes 589832 | tf_op jit(solution)/shard_map/ppermute | solution.py:43
  18.8 1.9 %collective-permute-done.3.refs_2_.refs_4_ = bf16[128,1920]{1,0:T(8,128)(2,1)S(1)} collective-permute-done((bf16[128,1920]{1,0:T(8,128)(2,1)S(1)}, bf16[128,1920]{1,0:T(8,128)(2,1)S(1)}, u32[]{:S(2)}, u32[]{:S(2)}) %collective-permute-start.3) | collective-permute-done | bytes 491552 | tf_op jit(solution)/shard_map/ppermute | solution.py:37
  20.7 0.0 collective-permute-done.6.refs_7_.refs_2_
  20.7 1.3 %collective-permute-start.8 = (bf16[128,896]{1,0:T(8,128)(2,1)S(1)}, bf16[128,896]{1,0:T(8,128)(2,1)S(1)}, u32[]{:S(2)}, u32[]{:S(2)}) collective-permute-start(bf16[128,896]{1,0:T(8,128)(2,1)S(1)} %own.10.refs_6_.refs_13_), channel_id=1, source_target_pairs={{0,1},{8,9},{16,17},{24,25},{2,3},{10,11},{18,19},{26,27}} | collective-permute-start | bytes 688136 | tf_op jit(solution)/shard_map/ppermute | solution.py:43
  22.0 0.8 %collective-permute-done.4.refs_7_.refs_6_.behind_ref = bf16[128,768]{1,0:T(8,128)(2,1)S(1)} collective-permute-done((bf16[128,768]{1,0:T(8,128)(2,1)S(1)}, bf16[128,768]{1,0:T(8,128)(2,1)S(1)}, u32[]{:S(2)}, u32[]{:S(2)}) %collective-permute-start.4) | collective-permute-done | bytes 196640 | tf_op jit(solution)/shard_map/ppermute | solution.py:37
  22.8 1.3 %collective-permute-start.7 = (bf16[128,1024]{1,0:T(8,128)(2,1)S(1)}, bf16[128,1024]{1,0:T(8,128)(2,1)S(1)}, u32[]{:S(2)}, u32[]{:S(2)}) collective-permute-start(bf16[128,1024]{1,0:T(8,128)(2,1)S(1)} %own.11.refs_14_), channel_id=1, source_target_pairs={{0,1},{8,9},{16,17},{24,25},{2,3},{10,11},{18,19},{26,27}} | collective-permute-start | bytes 786440 | tf_op jit(solution)/shard_map/ppermute | solution.py:43
  24.1 2.7 %later.1 = (bf16[1,128,4096]{2,1,0:T(8,128)(2,1)}, f32[128,4096]{1,0:T(8,128)S(1)}) custom-call(s32[1]{0:T(128)S(6)} %copy.27.refs_0_.start_ref, f32[256,128]{1,0:T(8,128)S(1)} %get-tuple-element.17.refs_1_.refs_6_, bf16[128,1792]{1,0:T(8,128)(2,1)S(1)} %collective-permute-done.1.refs_2_, bf16[128,1792]{1,0:T(8,128)(2,1)S(1)} %hold.4.refs_6_.refs_3_, ...), custom_call_target="tpu_custom_call" | custom-call | flops 20000000000 | bytes 1024 | tf_op jit(solution)/shard_map/later/pallas_call | solution.py:374
  26.8 1.1 %raw.1.refs_3_ = bf16[1,128,4096]{2,1,0:T(8,128)(2,1)} custom-call(s32[1]{0:T(128)S(6)} %copy.27.refs_0_.start_ref, f32[24,128]{1,0:T(8,128)S(1)} %get-tuple-element.25.lines_ref, bf16[128,768]{1,0:T(8,128)(2,1)S(1)} %collective-permute-done.4.refs_7_.refs_6_.behind_ref, bf16[128,768]{1,0:T(8,128)(2,1)S(1)} %hold.6.product_ref, ...), custom_call_target="tpu_custom_call", output_to_operand_aliasing={{}: (7, {})} | custom-call | flops 20000000000 | bytes 1024 | tf_op jit(solution)/shard_map/raw/pallas_call | solution.py:405
  27.9 0.0 collective-permute-done.10.refs_2_
  27.9 0.0 collective-permute-done.9.refs_1_
  27.9 0.8 %finish.5.refs_2_ = bf16[1,128,4096]{2,1,0:T(8,128)(2,1)} custom-call(f32[128,4096]{1,0:T(8,128)S(1)} %get-tuple-element.24.refs_0_.gated_ref, bf16[128,1024]{1,0:T(8,128)(2,1)S(1)} %collective-permute-done.9.refs_1_, bf16[128,768]{1,0:T(8,128)(2,1)S(1)} %collective-permute-done.10.refs_2_, ...), custom_call_target="tpu_custom_call", output_to_operand_aliasing={{}: (3, {})} | custom-call | flops 20000000000 | bytes 1024 | tf_op jit(solution)/shard_map/finish/pallas_call | solution.py:435
  28.8 0.2 collective-permute-done.8.refs_1_
  29.0 0.7 %finish.6.refs_2_ = bf16[1,128,4096]{2,1,0:T(8,128)(2,1)} custom-call(f32[128,4096]{1,0:T(8,128)S(1)} %get-tuple-element.24.refs_0_.gated_ref, bf16[128,896]{1,0:T(8,128)(2,1)S(1)} %collective-permute-done.8.refs_1_, bf16[1,128,4096]{2,1,0:T(8,128)(2,1)} %finish.5.refs_2_), custom_call_target="tpu_custom_call", output_to_operand_aliasing={{}: (2, {})} | custom-call | flops 20000000000 | bytes 1024 | tf_op jit(solution)/shard_map/finish/pallas_call | solution.py:435
  29.7 2.1 %collective-permute-done.7.refs_1_ = bf16[128,1024]{1,0:T(8,128)(2,1)S(1)} collective-permute-done((bf16[128,1024]{1,0:T(8,128)(2,1)S(1)}, bf16[128,1024]{1,0:T(8,128)(2,1)S(1)}, u32[]{:S(2)}, u32[]{:S(2)}) %collective-permute-start.7) | collective-permute-done | bytes 262176 | tf_op jit(solution)/shard_map/ppermute | solution.py:43
  31.8 0.8 %finish.7 = bf16[1,128,4096]{2,1,0:T(8,128)(2,1)} custom-call(f32[128,4096]{1,0:T(8,128)S(1)} %get-tuple-element.24.refs_0_.gated_ref, bf16[128,1024]{1,0:T(8,128)(2,1)S(1)} %collective-permute-done.7.refs_1_, bf16[1,128,4096]{2,1,0:T(8,128)(2,1)} %finish.6.refs_2_), custom_call_target="tpu_custom_call", output_to_operand_aliasing={{}: (2, {})} | custom-call | flops 20000000000 | bytes 1024 | tf_op jit(solution)/shard_map/finish/pallas_call | solution.py:435
  (12 shorter events, 0.2 us)
Async XLA Ops:
  0.0 2.3 %copy-start.2 = (bf16[1,256,128]{2,1,0:T(8,128)(2,1)S(1)}, bf16[1,256,128]{2,1,0:T(8,128)(2,1)}, u32[]{:S(2)}) copy-start(bf16[1,256,128]{2,1,0:T(8,128)(2,1)} %refs_2_.3) | copy-start | bytes 196612
  0.0 2.3 %copy-start.3 = (f32[1,256]{1,0:T(1,128)S(1)}, f32[1,256]{1,0:T(1,128)}, u32[]{:S(2)}) copy-start(f32[1,256]{1,0:T(1,128)} %refs_3_.3) | copy-start | bytes 3076
  0.0 2.3 %copy-start.4 = (s32[1,256]{1,0:T(1,128)S(1)}, s32[1,256]{1,0:T(1,128)}, u32[]{:S(2)}) copy-start(s32[1,256]{1,0:T(1,128)} %refs_4_.9) | copy-start | bytes 3076
  0.1 4.6 %copy-start = (bf16[1,128,4096]{2,1,0:T(8,128)(2,1)S(1)}, bf16[1,128,4096]{2,1,0:T(8,128)(2,1)}, u32[]{:S(2)}) copy-start(bf16[1,128,4096]{2,1,0:T(8,128)(2,1)} %refs_8_.1) | copy-start | bytes 3145732
  0.2 4.6 %copy-start.1 = (bf16[128,4096]{1,0:T(8,128)(2,1)S(1)}, bf16[128,4096]{1,0:T(8,128)(2,1)}, u32[]{:S(2)}) copy-start(bf16[128,4096]{1,0:T(8,128)(2,1)} %residual_ref.1) | copy-start | bytes 3145732
  0.2 4.5 %collective-permute-start = (bf16[128,3712]{1,0:T(8,128)(2,1)S(1)}, bf16[128,3712]{1,0:T(8,128)(2,1)S(1)}, u32[]{:S(2)}, u32[]{:S(2)}) collective-permute-start(bf16[128,3712]{1,0:T(8,128)(2,1)S(1)} %get-tuple-element.16.refs_5_.refs_3_), channel_id=1, source_target_pairs={{0,4},{8,12},{16,20},{24,28},{2,6},{10,14},{18,22},{26,30}} | collective-permute-start | bytes 2850824 | tf_op jit(solution)/shard_map/ppermute | solution.py:37
  1.0 9.5 %collective-permute-start.2 = (bf16[264,384]{1,0:T(8,128)(2,1)S(1)}, bf16[264,384]{1,0:T(8,128)(2,1)S(1)}, u32[]{:S(2)}, u32[]{:S(2)}) collective-permute-start(bf16[264,384]{1,0:T(8,128)(2,1)S(1)} %get-tuple-element.20.raw_ref), channel_id=1, source_target_pairs={{0,1},{4,5},{8,9},{12,13},{16,17},{20,21},{24,25},{28,29},{2,3},{6... | collective-permute-start | bytes 608264 | tf_op jit(solution)/shard_map/ppermute | solution.py:43
  4.8 11.3 %collective-permute-start.5 = (bf16[128,1536]{1,0:T(8,128)(2,1)S(1)}, bf16[128,1536]{1,0:T(8,128)(2,1)S(1)}, u32[]{:S(2)}, u32[]{:S(2)}) collective-permute-start(bf16[128,1536]{1,0:T(8,128)(2,1)S(1)} %own.6._.refs_9_), channel_id=1, source_target_pairs={{4,5},{12,13},{20,21},{28,29},{6,7},{14,15},{22,23},{30,31}} | collective-permute-start | bytes 1179656 | tf_op jit(solution)/shard_map/ppermute | solution.py:43
  5.5 10.7 %collective-permute-start.1 = (bf16[128,1792]{1,0:T(8,128)(2,1)S(1)}, bf16[128,1792]{1,0:T(8,128)(2,1)S(1)}, u32[]{:S(2)}, u32[]{:S(2)}) collective-permute-start(bf16[128,1792]{1,0:T(8,128)(2,1)S(1)} %hold.4.refs_6_.refs_3_), channel_id=1, source_target_pairs={{4,8},{12,16},{20,24},{1,5},{9,13},{17,21},{25,29},{5,9},{13,17},{... | collective-permute-start | bytes 1376264 | tf_op jit(solution)/shard_map/ppermute | solution.py:37
  7.8 12.9 %collective-permute-start.6 = (bf16[128,2176]{1,0:T(8,128)(2,1)S(1)}, bf16[128,2176]{1,0:T(8,128)(2,1)S(1)}, u32[]{:S(2)}, u32[]{:S(2)}) collective-permute-start(bf16[128,2176]{1,0:T(8,128)(2,1)S(1)} %own.7._.refs_10_), channel_id=1, source_target_pairs={{4,5},{12,13},{20,21},{28,29},{6,7},{14,15},{22,23},{30,31}} | collective-permute-start | bytes 1671176 | tf_op jit(solution)/shard_map/ppermute | solution.py:43
  10.5 10.1 %collective-permute-start.3 = (bf16[128,1920]{1,0:T(8,128)(2,1)S(1)}, bf16[128,1920]{1,0:T(8,128)(2,1)S(1)}, u32[]{:S(2)}, u32[]{:S(2)}) collective-permute-start(bf16[128,1920]{1,0:T(8,128)(2,1)S(1)} %hold.5._.refs_5_), channel_id=1, source_target_pairs={{4,8},{12,16},{20,24},{1,5},{9,13},{17,21},{25,29},{5,9},{13,17},{... | collective-permute-start | bytes 1474568 | tf_op jit(solution)/shard_map/ppermute | solution.py:37
  12.5 10.3 %collective-permute-start.4 = (bf16[128,768]{1,0:T(8,128)(2,1)S(1)}, bf16[128,768]{1,0:T(8,128)(2,1)S(1)}, u32[]{:S(2)}, u32[]{:S(2)}) collective-permute-start(bf16[128,768]{1,0:T(8,128)(2,1)S(1)} %hold.6.product_ref), channel_id=1, source_target_pairs={{0,4},{8,12},{16,20},{24,28},{4,8},{12,16},{20,24},{1,5},{9,13},{1... | collective-permute-start | bytes 589832 | tf_op jit(solution)/shard_map/ppermute | solution.py:37
  16.1 11.8 %collective-permute-start.9 = (bf16[128,1024]{1,0:T(8,128)(2,1)S(1)}, bf16[128,1024]{1,0:T(8,128)(2,1)S(1)}, u32[]{:S(2)}, u32[]{:S(2)}) collective-permute-start(bf16[128,1024]{1,0:T(8,128)(2,1)S(1)} %own.8.refs_6_.refs_11_), channel_id=1, source_target_pairs={{0,1},{8,9},{16,17},{24,25},{2,3},{10,11},{18,19},{26,27}} | collective-permute-start | bytes 786440 | tf_op jit(solution)/shard_map/ppermute | solution.py:43
  17.5 10.5 %collective-permute-start.10 = (bf16[128,768]{1,0:T(8,128)(2,1)S(1)}, bf16[128,768]{1,0:T(8,128)(2,1)S(1)}, u32[]{:S(2)}, u32[]{:S(2)}) collective-permute-start(bf16[128,768]{1,0:T(8,128)(2,1)S(1)} %own.9.refs_6_.refs_12_), channel_id=1, source_target_pairs={{0,1},{8,9},{16,17},{24,25},{2,3},{10,11},{18,19},{26,27}} | collective-permute-start | bytes 589832 | tf_op jit(solution)/shard_map/ppermute | solution.py:43
  20.7 8.3 %collective-permute-start.8 = (bf16[128,896]{1,0:T(8,128)(2,1)S(1)}, bf16[128,896]{1,0:T(8,128)(2,1)S(1)}, u32[]{:S(2)}, u32[]{:S(2)}) collective-permute-start(bf16[128,896]{1,0:T(8,128)(2,1)S(1)} %own.10.refs_6_.refs_13_), channel_id=1, source_target_pairs={{0,1},{8,9},{16,17},{24,25},{2,3},{10,11},{18,19},{26,27}} | collective-permute-start | bytes 688136 | tf_op jit(solution)/shard_map/ppermute | solution.py:43
  22.8 9.0 %collective-permute-start.7 = (bf16[128,1024]{1,0:T(8,128)(2,1)S(1)}, bf16[128,1024]{1,0:T(8,128)(2,1)S(1)}, u32[]{:S(2)}, u32[]{:S(2)}) collective-permute-start(bf16[128,1024]{1,0:T(8,128)(2,1)S(1)} %own.11.refs_14_), channel_id=1, source_target_pairs={{0,1},{8,9},{16,17},{24,25},{2,3},{10,11},{18,19},{26,27}} | collective-permute-start | bytes 786440 | tf_op jit(solution)/shard_map/ppermute | solution.py:43

commit v14 on v13

--- a/solution.py
+++ b/solution.py
@@ -14,7 +14,6 @@
 EVEN = (1024, 768, 896, 1024)
 PIECES = 4
 NEAR = 1792
-LINES = 8
 F32 = jnp.float32
 BF16 = jnp.bfloat16
 MIB = 1024 * 1024
@@ -108,60 +107,32 @@
     lines_ref[...] = lax.dot_general(scaled, flip, contract, preferred_element_type=F32)
 
 
-def lead_kernel(*refs):
-    bank_ref, scales_ref, assign_ref, queries_ref, keys_ref, values_ref = refs[:6]
-    raw_ref, rest_ref = refs[6:8]
-    bank_in, scales_in, assign_in, lines_ref, keys_in, values_in, sems, own_sems = refs[8:]
-    count = lines_ref.shape[0]
+def lead_kernel(queries_ref, keys_ref, values_ref, raw_ref, rest_ref, keys_in, values_in, sems, own_sem):
     rows = rest_ref.shape[0]
 
     @pl.when(is_first())
     def _():
-        copies = [
-            pltpu.make_async_copy(bank_ref, bank_in, own_sems.at[0]),
-            pltpu.make_async_copy(scales_ref, scales_in, own_sems.at[1]),
-            pltpu.make_async_copy(assign_ref, assign_in, own_sems.at[2]),
-            pltpu.make_async_copy(queries_ref.at[0, :, pl.ds(0, RAW)], raw_ref.at[pl.ds(0, rows)], own_sems.at[3]),
-        ]
-        for copy in copies:
-            copy.start()
-
-        def taps():
-            for copy in copies[:3]:
-                copy.wait()
-            fill_lines(bank_in[0], scales_in[:, :count], assign_in[:, :count], lines_ref)
-            for part in range(RAW // LANES):
-                taken = lines_ref[part * LINES : (part + 1) * LINES, :].astype(BF16)
-                raw_ref[2 * rows :, part * LANES : (part + 1) * LANES] = taken
-
-        multiply(keys_ref, values_ref, keys_in, values_in, sems, [raw_ref.at[pl.ds(rows, rows)], rest_ref], taps)
-        copies[3].wait()
+        source = queries_ref.at[0, :, pl.ds(0, RAW)]
+        copy = pltpu.make_async_copy(source, raw_ref.at[pl.ds(0, rows)], own_sem)
+        targets = [raw_ref.at[pl.ds(rows, rows)], rest_ref]
+        multiply(keys_ref, values_ref, keys_in, values_in, sems, targets, copy.start)
+        copy.wait()
 
 
 def product_scratch(rows, total):
     return [pltpu.VMEM((rows, total), BF16), pltpu.VMEM((rows, total), BF16), pltpu.SemaphoreType.DMA((2 * PIECES,))]
 
 
-def lead_of(bank, scales, assign, queries, keys, values):
+def lead_of(queries, keys, values):
     rows, total = queries.shape[1:]
     return call(
         lead_kernel,
         "lead",
-        (
-            array(2 * rows + LINES, RAW),
-            array(rows, total - RAW),
-        ),
-        [HBM] * 6,
+        (array(2 * rows, RAW), array(rows, total - RAW)),
+        [HBM] * 3,
         (VMEM,) * 2,
-        [
-            pltpu.VMEM(bank.shape, BF16),
-            pltpu.VMEM(scales.shape, F32),
-            pltpu.VMEM(assign.shape, jnp.int32),
-            pltpu.VMEM((min(LANES, assign.shape[1]), bank.shape[2]), F32),
-        ]
-        + product_scratch(rows, total)
-        + [pltpu.SemaphoreType.DMA((4,))],
-    )(bank, scales, assign, queries, keys, values)
+        product_scratch(rows, total) + [pltpu.SemaphoreType.DMA(())],
+    )(queries, keys, values)
 
 
 def turn_table(lines_ref, row, count, table_ref, at):
@@ -179,7 +150,7 @@
 
 def product_kernel(*refs):
     keys_ref, values_ref, bank_ref, scales_ref, assign_ref, rest_ref = refs[:6]
-    lines_ref, near_ref, far_ref, tail_ref, keys_in, values_in, sems = refs[6:]
+    lines_ref, wire_ref, near_ref, far_ref, tail_ref, keys_in, values_in, sems = refs[6:]
 
     def taps():
         fill_lines(bank_ref[0], scales_ref[...], assign_ref[...], lines_ref)
@@ -187,6 +158,7 @@
     @pl.when(is_first())
     def _():
         taps()
+        wire_ref[...] = lines_ref[: wire_ref.shape[0], :].astype(BF16)
 
     @pl.when(jnp.logical_and(is_first(), is_slab(1)))
     def _():
@@ -196,6 +168,10 @@
     @pl.when(jnp.logical_not(is_first()))
     def _():
         multiply(keys_ref, values_ref, keys_in, values_in, sems, [near_ref, far_ref, tail_ref], taps)
+
+
+def wire_rows(groups, total):
+    return -(-RAW * groups // (total * 16)) * 16
 
 
 def product_of(keys, values, bank, scales, assign, rest):
@@ -204,9 +180,15 @@
     return call(
         product_kernel,
         "product",
-        (array(groups, taps, F32), array(rows, NEAR), array(rows, total - RAW - NEAR), array(rows, RAW)),
+        (
+            array(groups, taps, F32),
+            array(wire_rows(groups, total), taps),
+            array(rows, NEAR),
+            array(rows, total - RAW - NEAR),
+            array(rows, RAW),
+        ),
         [HBM, HBM] + [VMEM] * 4,
-        (VMEM,) * 4,
+        (VMEM,) * 5,
         product_scratch(rows, total),
     )(keys, values, bank, scales, assign, rest)
 
@@ -282,15 +264,12 @@
     )(start, lines, behind, product, queries, residual, *after)
 
 
-def pick_kernel(raw_ref, received_ref, tail_ref, _, queries_ref, product_ref, lines_ref):
+def pick_kernel(raw_ref, received_ref, tail_ref, _, queries_ref, product_ref):
     rows = queries_ref.shape[0]
 
     def take(source):
         queries_ref[...] = source[:rows, :]
-        product_ref[:, :RAW] = source[rows : 2 * rows, :]
-        for part in range(RAW // LANES):
-            taken = source[2 * rows :, part * LANES : (part + 1) * LANES]
-            lines_ref[part * LINES : (part + 1) * LINES, :] = taken.astype(F32)
+        product_ref[:, :RAW] = source[rows:, :]
 
     pl.when(is_first())(lambda: take(raw_ref))
 
@@ -300,14 +279,14 @@
         product_ref[:, RAW:] = tail_ref[...]
 
 
-def pick_of(raw, received, tail, taps, after):
-    rows, width = (raw.shape[0] - LINES) // 2, raw.shape[1]
+def pick_of(raw, received, tail, after):
+    rows, width = raw.shape[0] // 2, raw.shape[1]
     return call(
         pick_kernel,
         "pick",
-        (array(rows, width), array(rows, 2 * width), array(RAW // LANES * LINES, taps, F32)),
+        (array(rows, width), array(rows, 2 * width)),
         [VMEM, VMEM, VMEM, ANY],
-        (VMEM,) * 3,
+        (VMEM,) * 2,
         weight=SLOW,
     )(raw, received, tail, after)
 
@@ -382,16 +361,25 @@
     )(start, lines, near_behind, near, far_behind, far, raw_behind, tail, queries, *own)
 
 
-def raw_kernel(start_ref, lines_ref, behind_ref, product_ref, queries_ref, gated_ref, residual_ref, _, *refs):
-    out_ref, table_ref, buffer, sems = refs
+def raw_kernel(*refs):
+    start_ref, lines_ref, wire_ref, behind_ref, product_ref, queries_ref, gated_ref, residual_ref = refs[:8]
+    out_ref, chosen_ref, table_ref, buffer, sems = refs[9:]
     width = buffer.shape[1]
-    share = share_of(lines_ref, width)
+    share = share_of(lines_ref, residual_ref.shape[1])
+
+    @pl.when(is_first())
+    def _():
+        chosen_ref[...] = lines_ref[: chosen_ref.shape[0], :]
+
+    @pl.when(jnp.logical_not(is_first()))
+    def _():
+        chosen_ref[...] = wire_ref[...].astype(F32)
 
     def store(at, span, mixed):
         gated = queries_ref[span, at].astype(F32) * mixed
         buffer[span, at] = (residual_ref[span, at].astype(F32) + gated).astype(BF16)
 
-    mix_all(width, share, lines_ref, 0, table_ref, start_ref, behind_ref, product_ref, (0, 0), store)
+    mix_all(width, share, chosen_ref, 0, table_ref, start_ref, behind_ref, product_ref, (0, 0), store)
 
     @pl.when(jnp.logical_not(is_first()))
     def _():
@@ -400,18 +388,24 @@
     wait_all(send_out([(buffer, 0)], out_ref, sems))
 
 
-def raw_finish(held, start, lines, behind, product, queries, gated, residual):
+def raw_finish(held, start, lines, wire, behind, product, queries, gated, residual):
     rows, width = queries.shape
+    total = residual.shape[1]
     return call(
         raw_kernel,
         "raw",
         jax.ShapeDtypeStruct(held.shape, BF16),
-        [SMEM] + [VMEM] * 6 + [ANY],
+        [SMEM] + [VMEM] * 7 + [ANY],
         ANY,
-        [table_scratch(lines, width, width), pltpu.VMEM((rows, width), BF16), pltpu.SemaphoreType.DMA((1,))],
+        [
+            pltpu.VMEM(wire.shape, F32),
+            table_scratch(lines, width, total),
+            pltpu.VMEM((rows, width), BF16),
+            pltpu.SemaphoreType.DMA((1,)),
+        ],
         weight=SLOW,
-        aliases={7: 0},
-    )(start, lines, behind, product, queries, gated, residual, held)
+        aliases={8: 0},
+    )(start, lines, wire, behind, product, queries, gated, residual, held)
 
 
 def finish_kernel(odd, places, *refs):
@@ -447,14 +441,13 @@
 def body(queries, keys, values, residual, filter_bank, filter_scales, group_filter, context_start):
     total = queries.shape[2]
     small = (filter_bank, filter_scales, group_filter)
-    far_small = [pltpu.with_memory_space_constraint(value, pltpu.HBM) for value in small]
     far_queries, keys, values = (
         pltpu.with_memory_space_constraint(value, pltpu.HBM) for value in (queries, keys, values)
     )
-    raw, rest = lead_of(*far_small, far_queries, keys, values)
+    raw, rest = lead_of(far_queries, keys, values)
     raw_received = to_next_section(raw)
     chip_behind = to_next_slab(rest, (0, 0))
-    lines, near, far, tail = product_of(keys, values, *small, rest)
+    lines, wire, near, far, tail = product_of(keys, values, *small, rest)
     own, received, places = [], [], []
 
     def send(odd, behind, origin, first, width, *after):
@@ -471,7 +464,7 @@
     near = held_back(near, after)
     near_behind = to_next_slab(near, *links)
     first, after = send(1, chip_behind, RAW, first, ODD[1], near)
-    raw_queries, raw_product, raw_lines = pick_of(raw, raw_received, tail, lines.shape[1], after)
+    raw_queries, raw_product = pick_of(raw, raw_received, tail, after)
     far = held_back(far, raw_queries)
     far_behind = to_next_slab(far, *links)
     raw_product = held_back(raw_product, far)
@@ -482,6 +475,7 @@
     origin = first
     first, after = send(0, far_behind, origin, first, EVEN[2], after, received[1])
     first, after = send(0, far_behind, origin, first, EVEN[3], after, raw_behind)
+    wire_received = to_next_section(held_back(wire, after))
     held, gated = later_of(
         context_start,
         lines,
@@ -497,10 +491,12 @@
     )
     odd = len(ODD)
     held = finish(held, gated, received[:odd], places[:odd])
-    held = raw_finish(held, context_start, raw_lines, raw_behind, raw_product, raw_queries, gated, residual)
-    for last in (odd + 2, odd + 3, odd + 4):
-        begin = odd if last == odd + 2 else last - 1
-        held = finish(held, gated, received[begin:last], places[begin:last])
+    held = finish(held, gated, received[odd : odd + 2], places[odd : odd + 2])
+    held = raw_finish(
+        held, context_start, lines, wire_received, raw_behind, raw_product, raw_queries, gated, residual
+    )
+    for last in (odd + 2, odd + 3):
+        held = finish(held, gated, received[last : last + 1], places[last : last + 1])
     return held
 
 

time: 32.9 us -> 34.6 us (1.052)
  starting transfers between devices: 16.5 us -> 17.8 us
    ppermute x7 -> x8, starting transfers between devices: 7.82 us -> 9.11 us  [to_next_section(): return lax.ppermute(value, ('ctx', 'pipe'), pairs)]
    ppermute x4, waiting for transfers between devices: 2.74 us -> 3.19 us  [to_next_slab(): return lax.ppermute(value, ('ctx', 'pipe'), pairs)]
    ppermute x7 -> x8, waiting for transfers between devices: 4.21 us -> 4.02 us  [to_next_section(): return lax.ppermute(value, ('ctx', 'pipe'), pairs)]
  transfers between devices with their start and end apart: 11 -> 12, of which waited for: 5 -> 4; matrix products, arithmetic and copies ran while one was open for 0% -> 0% of each run, Pallas kernels for 22% -> 21%
where the time goes in v14:
time: 34.6 us; the launch traced here: 34.2 us
  starting transfers between devices  17.8 us (51%)
  Pallas kernels  8.17 us (24%)
  waiting for transfers between devices  7.21 us (21%)
  between operations  0.99 us (3%)
    ppermute x8, starting transfers between devices, to_next_section(): return lax.ppermute(value, ('ctx', 'pipe'), pairs)  9.11 us
    ppermute x4, starting transfers between devices, to_next_slab(): return lax.ppermute(value, ('ctx', 'pipe'), pairs)  8.71 us
    ppermute x8, waiting for transfers between devices, to_next_section(): return lax.ppermute(value, ('ctx', 'pipe'), pairs)  4.02 us
    ppermute x4, waiting for transfers between devices, to_next_slab(): return lax.ppermute(value, ('ctx', 'pipe'), pairs)  3.19 us
    pallas_call x1, Pallas kernels, later_of(): call(functools.partial(later_kernel, places), 'later', (jax.ShapeDtypeStr...  2.67 us
    pallas_call x4, Pallas kernels, finish(): call(functools.partial(finish_kernel, places[0][0], places), 'finish', ja...  2.48 us
    pallas_call x1, Pallas kernels, product_of(): call(product_kernel, 'product', (array(groups, taps, F32), array(wire_row...  1.68 us
    pallas_call x1, Pallas kernels, raw_finish(): call(raw_kernel, 'raw', jax.ShapeDtypeStruct(held.shape, BF16), [SMEM] +...  1.12 us
  transfers between devices with their start and end apart: 12, of which 4 were waited for; matrix products, arithmetic and copies ran while one was open for 0% of the time, Pallas kernels for 21%

profile of v14, /device:TPU:12, one launch (start us, length us, event | category | flops | bytes accessed | tf_op | source)
XLA Modules:
  0.0 34.2 jit_solution(13025365844856329508)
XLA Ops:
  0.0 0.0 copy-start.2
  0.0 0.0 copy-start.3
  0.0 0.0 copy-start.4
  0.0 0.1 lead.1
  0.1 0.0 copy-start
  0.1 0.0 copy-start.1
  0.1 0.9 %collective-permute-start = (bf16[128,3712]{1,0:T(8,128)(2,1)S(1)}, bf16[128,3712]{1,0:T(8,128)(2,1)S(1)}, u32[]{:S(2)}, u32[]{:S(2)}) collective-permute-start(bf16[128,3712]{1,0:T(8,128)(2,1)S(1)} %get-tuple-element.16.refs_5_.refs_3_), channel_id=1, source_target_pairs={{0,4},{8,12},{16,20},{24,28},{2,6},{10,14},{18,22},{26,30}} | collective-permute-start | bytes 2850824 | tf_op jit(solution)/shard_map/ppermute | solution.py:36
  1.0 1.3 %collective-permute-start.2 = (bf16[256,384]{1,0:T(8,128)(2,1)S(1)}, bf16[256,384]{1,0:T(8,128)(2,1)S(1)}, u32[]{:S(2)}, u32[]{:S(2)}) collective-permute-start(bf16[256,384]{1,0:T(8,128)(2,1)S(1)} %get-tuple-element.20.raw_ref), channel_id=1, source_target_pairs={{0,1},{4,5},{8,9},{12,13},{16,17},{20,21},{24,25},{28,29},{2,3},{6... | collective-permute-start | bytes 589832 | tf_op jit(solution)/shard_map/ppermute | solution.py:42
  2.3 0.0 copy-done.2
  2.3 0.0 copy-done.3
  2.3 0.0 copy-done.4
  2.3 1.7 %product.1 = (f32[256,128]{1,0:T(8,128)S(1)}, bf16[32,128]{1,0:T(8,128)(2,1)S(1)}, bf16[128,1792]{1,0:T(8,128)(2,1)S(1)}, bf16[128,1920]{1,0:T(8,128)(2,1)S(1)}, bf16[128,384]{1,0:T(8,128)(2,1)S(1)}) custom-call(bf16[1,128,4096]{2,1,0:T(8,128)(2,1)} %refs_0_.9, bf16[1,128,4096]{2,1,0:T(8,128)(2,1)} %refs_1_.1, bf16[1,256,128]{2,1,0:T(8,128)(2,1)S(1)} %copy-done.2, ...), custom_call_target="tpu_custom_call" | custom-call | flops 1024 | bytes 1024 | tf_op jit(solution)/shard_map/product/pallas_call | solution.py:180
  4.7 0.0 collective-permute-done.refs_2_
  4.7 0.0 copy-done
  4.7 0.0 copy-done.1
  4.7 0.7 %collective-permute-start.5 = (bf16[128,1536]{1,0:T(8,128)(2,1)S(1)}, bf16[128,1536]{1,0:T(8,128)(2,1)S(1)}, u32[]{:S(2)}, u32[]{:S(2)}) collective-permute-start(bf16[128,1536]{1,0:T(8,128)(2,1)S(1)} %own.6._.refs_9_), channel_id=1, source_target_pairs={{4,5},{12,13},{20,21},{28,29},{6,7},{14,15},{22,23},{30,31}} | collective-permute-start | bytes 1179656 | tf_op jit(solution)/shard_map/ppermute | solution.py:42
  5.4 2.3 %collective-permute-start.1 = (bf16[128,1792]{1,0:T(8,128)(2,1)S(1)}, bf16[128,1792]{1,0:T(8,128)(2,1)S(1)}, u32[]{:S(2)}, u32[]{:S(2)}) collective-permute-start(bf16[128,1792]{1,0:T(8,128)(2,1)S(1)} %hold.5.refs_6_.refs_3_), channel_id=1, source_target_pairs={{4,8},{12,16},{20,24},{1,5},{9,13},{17,21},{25,29},{5,9},{13,17},{... | collective-permute-start | bytes 1376264 | tf_op jit(solution)/shard_map/ppermute | solution.py:36
  7.8 0.7 %collective-permute-start.6 = (bf16[128,2176]{1,0:T(8,128)(2,1)S(1)}, bf16[128,2176]{1,0:T(8,128)(2,1)S(1)}, u32[]{:S(2)}, u32[]{:S(2)}) collective-permute-start(bf16[128,2176]{1,0:T(8,128)(2,1)S(1)} %own.7._.refs_10_), channel_id=1, source_target_pairs={{4,5},{12,13},{20,21},{28,29},{6,7},{14,15},{22,23},{30,31}} | collective-permute-start | bytes 1671176 | tf_op jit(solution)/shard_map/ppermute | solution.py:42
  8.5 1.3 %collective-permute-done.2.received_ref = bf16[256,384]{1,0:T(8,128)(2,1)S(1)} collective-permute-done((bf16[256,384]{1,0:T(8,128)(2,1)S(1)}, bf16[256,384]{1,0:T(8,128)(2,1)S(1)}, u32[]{:S(2)}, u32[]{:S(2)}) %collective-permute-start.2) | collective-permute-done | bytes 196640 | tf_op jit(solution)/shard_map/ppermute | solution.py:42
  9.9 2.4 %collective-permute-start.3 = (bf16[128,1920]{1,0:T(8,128)(2,1)S(1)}, bf16[128,1920]{1,0:T(8,128)(2,1)S(1)}, u32[]{:S(2)}, u32[]{:S(2)}) collective-permute-start(bf16[128,1920]{1,0:T(8,128)(2,1)S(1)} %hold.6._.refs_5_), channel_id=1, source_target_pairs={{4,8},{12,16},{20,24},{1,5},{9,13},{17,21},{25,29},{5,9},{13,17},{... | collective-permute-start | bytes 1474568 | tf_op jit(solution)/shard_map/ppermute | solution.py:36
  12.4 3.1 %collective-permute-start.4 = (bf16[128,768]{1,0:T(8,128)(2,1)S(1)}, bf16[128,768]{1,0:T(8,128)(2,1)S(1)}, u32[]{:S(2)}, u32[]{:S(2)}) collective-permute-start(bf16[128,768]{1,0:T(8,128)(2,1)S(1)} %hold.7.refs_4_), channel_id=1, source_target_pairs={{0,4},{8,12},{16,20},{24,28},{4,8},{12,16},{20,24},{1,5},{9,13},{1... | collective-permute-start | bytes 589832 | tf_op jit(solution)/shard_map/ppermute | solution.py:36
  15.4 0.0 collective-permute-done.5._.refs_1_
  15.5 0.0 collective-permute-done.1.refs_2_
  15.5 1.3 %collective-permute-start.10 = (bf16[128,1024]{1,0:T(8,128)(2,1)S(1)}, bf16[128,1024]{1,0:T(8,128)(2,1)S(1)}, u32[]{:S(2)}, u32[]{:S(2)}) collective-permute-start(bf16[128,1024]{1,0:T(8,128)(2,1)S(1)} %own.8.refs_6_.refs_11_), channel_id=1, source_target_pairs={{0,1},{8,9},{16,17},{24,25},{2,3},{10,11},{18,19},{26,27}} | collective-permute-start | bytes 786440 | tf_op jit(solution)/shard_map/ppermute | solution.py:42
  16.8 1.3 %collective-permute-start.11 = (bf16[128,768]{1,0:T(8,128)(2,1)S(1)}, bf16[128,768]{1,0:T(8,128)(2,1)S(1)}, u32[]{:S(2)}, u32[]{:S(2)}) collective-permute-start(bf16[128,768]{1,0:T(8,128)(2,1)S(1)} %own.9.refs_6_.refs_12_), channel_id=1, source_target_pairs={{0,1},{8,9},{16,17},{24,25},{2,3},{10,11},{18,19},{26,27}} | collective-permute-start | bytes 589832 | tf_op jit(solution)/shard_map/ppermute | solution.py:42
  18.1 2.4 %collective-permute-done.3.refs_2_.refs_4_ = bf16[128,1920]{1,0:T(8,128)(2,1)S(1)} collective-permute-done((bf16[128,1920]{1,0:T(8,128)(2,1)S(1)}, bf16[128,1920]{1,0:T(8,128)(2,1)S(1)}, u32[]{:S(2)}, u32[]{:S(2)}) %collective-permute-start.3) | collective-permute-done | bytes 491552 | tf_op jit(solution)/shard_map/ppermute | solution.py:36
  20.5 0.0 collective-permute-done.6.refs_7_.refs_2_
  20.5 1.3 %collective-permute-start.8 = (bf16[128,896]{1,0:T(8,128)(2,1)S(1)}, bf16[128,896]{1,0:T(8,128)(2,1)S(1)}, u32[]{:S(2)}, u32[]{:S(2)}) collective-permute-start(bf16[128,896]{1,0:T(8,128)(2,1)S(1)} %own.10.refs_6_.refs_13_), channel_id=1, source_target_pairs={{0,1},{8,9},{16,17},{24,25},{2,3},{10,11},{18,19},{26,27}} | collective-permute-start | bytes 688136 | tf_op jit(solution)/shard_map/ppermute | solution.py:42
  21.8 0.8 %collective-permute-done.4.refs_7_.refs_6_.refs_3_ = bf16[128,768]{1,0:T(8,128)(2,1)S(1)} collective-permute-done((bf16[128,768]{1,0:T(8,128)(2,1)S(1)}, bf16[128,768]{1,0:T(8,128)(2,1)S(1)}, u32[]{:S(2)}, u32[]{:S(2)}) %collective-permute-start.4) | collective-permute-done | bytes 196640 | tf_op jit(solution)/shard_map/ppermute | solution.py:36
  22.6 1.3 %collective-permute-start.7 = (bf16[128,1024]{1,0:T(8,128)(2,1)S(1)}, bf16[128,1024]{1,0:T(8,128)(2,1)S(1)}, u32[]{:S(2)}, u32[]{:S(2)}) collective-permute-start(bf16[128,1024]{1,0:T(8,128)(2,1)S(1)} %own.11.refs_14_._), channel_id=1, source_target_pairs={{0,1},{8,9},{16,17},{24,25},{2,3},{10,11},{18,19},{26,27}} | collective-permute-start | bytes 786440 | tf_op jit(solution)/shard_map/ppermute | solution.py:42
  23.9 1.3 %collective-permute-start.9 = (bf16[32,128]{1,0:T(8,128)(2,1)S(1)}, bf16[32,128]{1,0:T(8,128)(2,1)S(1)}, u32[]{:S(2)}, u32[]{:S(2)}) collective-permute-start(bf16[32,128]{1,0:T(8,128)(2,1)S(1)} %hold.9), channel_id=1, source_target_pairs={{0,1},{4,5},{8,9},{12,13},{16,17},{20,21},{24,25},{28,29},{2,3},{6... | collective-permute-start | bytes 24584 | tf_op jit(solution)/shard_map/ppermute | solution.py:42
  25.2 2.7 %later.1 = (bf16[1,128,4096]{2,1,0:T(8,128)(2,1)}, f32[128,4096]{1,0:T(8,128)S(1)}) custom-call(s32[1]{0:T(128)S(6)} %copy.29.refs_0_, f32[256,128]{1,0:T(8,128)S(1)} %get-tuple-element.17.refs_1_.refs_6_, bf16[128,1792]{1,0:T(8,128)(2,1)S(1)} %collective-permute-done.1.refs_2_, bf16[128,1792]{1,0:T(8,128)(2,1)S(1)} %hold.5.refs_6_.refs_3_, ...), custom_call_target="tpu_custom_call" | custom-call | flops 20000000000 | bytes 1024 | tf_op jit(solution)/shard_map/later/pallas_call | solution.py:353
  27.9 0.0 collective-permute-done.11.refs_2_
  27.9 0.0 collective-permute-done.10.refs_1_
  27.9 0.9 %finish.5.refs_8_ = bf16[1,128,4096]{2,1,0:T(8,128)(2,1)} custom-call(f32[128,4096]{1,0:T(8,128)S(1)} %get-tuple-element.24.refs_0_.refs_6_, bf16[128,1024]{1,0:T(8,128)(2,1)S(1)} %collective-permute-done.10.refs_1_, bf16[128,768]{1,0:T(8,128)(2,1)S(1)} %collective-permute-done.11.refs_2_, ...), custom_call_target="tpu_custom_call", output_to_operand_aliasing={{}: (3, {})} | custom-call | flops 20000000000 | bytes 1024 | tf_op jit(solution)/shard_map/finish/pallas_call | solution.py:429
  28.8 2.7 %collective-permute-done.9.refs_2_ = bf16[32,128]{1,0:T(8,128)(2,1)S(1)} collective-permute-done((bf16[32,128]{1,0:T(8,128)(2,1)S(1)}, bf16[32,128]{1,0:T(8,128)(2,1)S(1)}, u32[]{:S(2)}, u32[]{:S(2)}) %collective-permute-start.9) | collective-permute-done | bytes 8224 | tf_op jit(solution)/shard_map/ppermute | solution.py:42
  31.5 1.1 %raw.1.refs_2_ = bf16[1,128,4096]{2,1,0:T(8,128)(2,1)} custom-call(s32[1]{0:T(128)S(6)} %copy.29.refs_0_, f32[256,128]{1,0:T(8,128)S(1)} %get-tuple-element.17.refs_1_.refs_6_, bf16[32,128]{1,0:T(8,128)(2,1)S(1)} %collective-permute-done.9.refs_2_, ...), custom_call_target="tpu_custom_call", output_to_operand_aliasing={{}: (8, {})} | custom-call | flops 20000000000 | bytes 1024 | tf_op jit(solution)/shard_map/raw/pallas_call | solution.py:394
  32.6 0.0 collective-permute-done.8.refs_1_
  32.6 0.8 %finish.6.refs_2_ = bf16[1,128,4096]{2,1,0:T(8,128)(2,1)} custom-call(f32[128,4096]{1,0:T(8,128)S(1)} %get-tuple-element.24.refs_0_.refs_6_, bf16[128,896]{1,0:T(8,128)(2,1)S(1)} %collective-permute-done.8.refs_1_, bf16[1,128,4096]{2,1,0:T(8,128)(2,1)} %raw.1.refs_2_), custom_call_target="tpu_custom_call", output_to_operand_aliasing={{}: (2, {})} | custom-call | flops 20000000000 | bytes 1024 | tf_op jit(solution)/shard_map/finish/pallas_call | solution.py:429
  33.4 0.0 collective-permute-done.7.refs_1_
  33.4 0.8 %finish.7 = bf16[1,128,4096]{2,1,0:T(8,128)(2,1)} custom-call(f32[128,4096]{1,0:T(8,128)S(1)} %get-tuple-element.24.refs_0_.refs_6_, bf16[128,1024]{1,0:T(8,128)(2,1)S(1)} %collective-permute-done.7.refs_1_, bf16[1,128,4096]{2,1,0:T(8,128)(2,1)} %finish.6.refs_2_), custom_call_target="tpu_custom_call", output_to_operand_aliasing={{}: (2, {})} | custom-call | flops 20000000000 | bytes 1024 | tf_op jit(solution)/shard_map/finish/pallas_call | solution.py:429
  (13 shorter events, 0.2 us)
Async XLA Ops:
  0.0 2.3 %copy-start.2 = (bf16[1,256,128]{2,1,0:T(8,128)(2,1)S(1)}, bf16[1,256,128]{2,1,0:T(8,128)(2,1)}, u32[]{:S(2)}) copy-start(bf16[1,256,128]{2,1,0:T(8,128)(2,1)} %refs_2_.1) | copy-start | bytes 196612
  0.0 2.3 %copy-start.3 = (f32[1,256]{1,0:T(1,128)S(1)}, f32[1,256]{1,0:T(1,128)}, u32[]{:S(2)}) copy-start(f32[1,256]{1,0:T(1,128)} %refs_3_.1) | copy-start | bytes 3076
  0.0 2.3 %copy-start.4 = (s32[1,256]{1,0:T(1,128)S(1)}, s32[1,256]{1,0:T(1,128)}, u32[]{:S(2)}) copy-start(s32[1,256]{1,0:T(1,128)} %refs_4_.7) | copy-start | bytes 3076
  0.1 4.6 %copy-start = (bf16[1,128,4096]{2,1,0:T(8,128)(2,1)S(1)}, bf16[1,128,4096]{2,1,0:T(8,128)(2,1)}, u32[]{:S(2)}) copy-start(bf16[1,128,4096]{2,1,0:T(8,128)(2,1)} %refs_8_.1) | copy-start | bytes 3145732
  0.1 4.6 %copy-start.1 = (bf16[128,4096]{1,0:T(8,128)(2,1)S(1)}, bf16[128,4096]{1,0:T(8,128)(2,1)}, u32[]{:S(2)}) copy-start(bf16[128,4096]{1,0:T(8,128)(2,1)} %refs_7_.1) | copy-start | bytes 3145732
  0.1 4.5 %collective-permute-start = (bf16[128,3712]{1,0:T(8,128)(2,1)S(1)}, bf16[128,3712]{1,0:T(8,128)(2,1)S(1)}, u32[]{:S(2)}, u32[]{:S(2)}) collective-permute-start(bf16[128,3712]{1,0:T(8,128)(2,1)S(1)} %get-tuple-element.16.refs_5_.refs_3_), channel_id=1, source_target_pairs={{0,4},{8,12},{16,20},{24,28},{2,6},{10,14},{18,22},{26,30}} | collective-permute-start | bytes 2850824 | tf_op jit(solution)/shard_map/ppermute | solution.py:36
  1.0 8.9 %collective-permute-start.2 = (bf16[256,384]{1,0:T(8,128)(2,1)S(1)}, bf16[256,384]{1,0:T(8,128)(2,1)S(1)}, u32[]{:S(2)}, u32[]{:S(2)}) collective-permute-start(bf16[256,384]{1,0:T(8,128)(2,1)S(1)} %get-tuple-element.20.raw_ref), channel_id=1, source_target_pairs={{0,1},{4,5},{8,9},{12,13},{16,17},{20,21},{24,25},{28,29},{2,3},{6... | collective-permute-start | bytes 589832 | tf_op jit(solution)/shard_map/ppermute | solution.py:42
  4.7 10.7 %collective-permute-start.5 = (bf16[128,1536]{1,0:T(8,128)(2,1)S(1)}, bf16[128,1536]{1,0:T(8,128)(2,1)S(1)}, u32[]{:S(2)}, u32[]{:S(2)}) collective-permute-start(bf16[128,1536]{1,0:T(8,128)(2,1)S(1)} %own.6._.refs_9_), channel_id=1, source_target_pairs={{4,5},{12,13},{20,21},{28,29},{6,7},{14,15},{22,23},{30,31}} | collective-permute-start | bytes 1179656 | tf_op jit(solution)/shard_map/ppermute | solution.py:42
  5.4 10.0 %collective-permute-start.1 = (bf16[128,1792]{1,0:T(8,128)(2,1)S(1)}, bf16[128,1792]{1,0:T(8,128)(2,1)S(1)}, u32[]{:S(2)}, u32[]{:S(2)}) collective-permute-start(bf16[128,1792]{1,0:T(8,128)(2,1)S(1)} %hold.5.refs_6_.refs_3_), channel_id=1, source_target_pairs={{4,8},{12,16},{20,24},{1,5},{9,13},{17,21},{25,29},{5,9},{13,17},{... | collective-permute-start | bytes 1376264 | tf_op jit(solution)/shard_map/ppermute | solution.py:36
  7.8 12.7 %collective-permute-start.6 = (bf16[128,2176]{1,0:T(8,128)(2,1)S(1)}, bf16[128,2176]{1,0:T(8,128)(2,1)S(1)}, u32[]{:S(2)}, u32[]{:S(2)}) collective-permute-start(bf16[128,2176]{1,0:T(8,128)(2,1)S(1)} %own.7._.refs_10_), channel_id=1, source_target_pairs={{4,5},{12,13},{20,21},{28,29},{6,7},{14,15},{22,23},{30,31}} | collective-permute-start | bytes 1671176 | tf_op jit(solution)/shard_map/ppermute | solution.py:42
  9.9 10.6 %collective-permute-start.3 = (bf16[128,1920]{1,0:T(8,128)(2,1)S(1)}, bf16[128,1920]{1,0:T(8,128)(2,1)S(1)}, u32[]{:S(2)}, u32[]{:S(2)}) collective-permute-start(bf16[128,1920]{1,0:T(8,128)(2,1)S(1)} %hold.6._.refs_5_), channel_id=1, source_target_pairs={{4,8},{12,16},{20,24},{1,5},{9,13},{17,21},{25,29},{5,9},{13,17},{... | collective-permute-start | bytes 1474568 | tf_op jit(solution)/shard_map/ppermute | solution.py:36
  12.4 10.2 %collective-permute-start.4 = (bf16[128,768]{1,0:T(8,128)(2,1)S(1)}, bf16[128,768]{1,0:T(8,128)(2,1)S(1)}, u32[]{:S(2)}, u32[]{:S(2)}) collective-permute-start(bf16[128,768]{1,0:T(8,128)(2,1)S(1)} %hold.7.refs_4_), channel_id=1, source_target_pairs={{0,4},{8,12},{16,20},{24,28},{4,8},{12,16},{20,24},{1,5},{9,13},{1... | collective-permute-start | bytes 589832 | tf_op jit(solution)/shard_map/ppermute | solution.py:36
  15.5 12.4 %collective-permute-start.10 = (bf16[128,1024]{1,0:T(8,128)(2,1)S(1)}, bf16[128,1024]{1,0:T(8,128)(2,1)S(1)}, u32[]{:S(2)}, u32[]{:S(2)}) collective-permute-start(bf16[128,1024]{1,0:T(8,128)(2,1)S(1)} %own.8.refs_6_.refs_11_), channel_id=1, source_target_pairs={{0,1},{8,9},{16,17},{24,25},{2,3},{10,11},{18,19},{26,27}} | collective-permute-start | bytes 786440 | tf_op jit(solution)/shard_map/ppermute | solution.py:42
  16.8 11.1 %collective-permute-start.11 = (bf16[128,768]{1,0:T(8,128)(2,1)S(1)}, bf16[128,768]{1,0:T(8,128)(2,1)S(1)}, u32[]{:S(2)}, u32[]{:S(2)}) collective-permute-start(bf16[128,768]{1,0:T(8,128)(2,1)S(1)} %own.9.refs_6_.refs_12_), channel_id=1, source_target_pairs={{0,1},{8,9},{16,17},{24,25},{2,3},{10,11},{18,19},{26,27}} | collective-permute-start | bytes 589832 | tf_op jit(solution)/shard_map/ppermute | solution.py:42
  20.5 12.1 %collective-permute-start.8 = (bf16[128,896]{1,0:T(8,128)(2,1)S(1)}, bf16[128,896]{1,0:T(8,128)(2,1)S(1)}, u32[]{:S(2)}, u32[]{:S(2)}) collective-permute-start(bf16[128,896]{1,0:T(8,128)(2,1)S(1)} %own.10.refs_6_.refs_13_), channel_id=1, source_target_pairs={{0,1},{8,9},{16,17},{24,25},{2,3},{10,11},{18,19},{26,27}} | collective-permute-start | bytes 688136 | tf_op jit(solution)/shard_map/ppermute | solution.py:42
  22.6 10.8 %collective-permute-start.7 = (bf16[128,1024]{1,0:T(8,128)(2,1)S(1)}, bf16[128,1024]{1,0:T(8,128)(2,1)S(1)}, u32[]{:S(2)}, u32[]{:S(2)}) collective-permute-start(bf16[128,1024]{1,0:T(8,128)(2,1)S(1)} %own.11.refs_14_._), channel_id=1, source_target_pairs={{0,1},{8,9},{16,17},{24,25},{2,3},{10,11},{18,19},{26,27}} | collective-permute-start | bytes 786440 | tf_op jit(solution)/shard_map/ppermute | solution.py:42
  23.9 7.6 %collective-permute-start.9 = (bf16[32,128]{1,0:T(8,128)(2,1)S(1)}, bf16[32,128]{1,0:T(8,128)(2,1)S(1)}, u32[]{:S(2)}, u32[]{:S(2)}) collective-permute-start(bf16[32,128]{1,0:T(8,128)(2,1)S(1)} %hold.9), channel_id=1, source_target_pairs={{0,1},{4,5},{8,9},{12,13},{16,17},{20,21},{24,25},{28,29},{2,3},{6... | collective-permute-start | bytes 24584 | tf_op jit(solution)/shard_map/ppermute | solution.py:42

commit v15 on v14

--- a/solution.py
+++ b/solution.py
@@ -13,6 +13,7 @@
 ODD = (1536, 2176)
 EVEN = (1024, 768, 896, 1024)
 PIECES = 4
+LINES = 8
 NEAR = 1792
 F32 = jnp.float32
 BF16 = jnp.bfloat16
@@ -228,7 +229,7 @@
     return LANES * lines_ref.shape[0] // total
 
 
-def own_kernel(odd, first, shift, local, *refs):
+def own_kernel(odd, first, shift, local, extra, *refs):
     start_ref, lines_ref, behind_ref, product_ref, queries_ref, residual_ref = refs[:6]
     out_ref, table_ref = refs[-2:]
     width = out_ref.shape[1]
@@ -244,6 +245,11 @@
         line = first // LANES * share
         at = (shift, local)
         mix_all(width, share, lines_ref, line, table_ref, start_ref, behind_ref, product_ref, at, store)
+        if extra:
+            rows = out_ref.shape[0] - extra
+            for part in range(RAW // LANES):
+                taken = lines_ref[part * extra : (part + 1) * extra, :].astype(BF16)
+                out_ref[rows:, part * LANES : (part + 1) * LANES] = taken
 
 
 def table_scratch(lines, width, total):
@@ -251,16 +257,15 @@
     return pltpu.VMEM((width * groups // total * ROW_BLOCK, taps + ROW_BLOCK), BF16)
 
 
-def own_of(odd, origin, start, lines, behind, product, queries, residual, first, width, weight, *after):
+def own_of(odd, origin, extra, start, lines, behind, product, queries, residual, first, width, *after):
     rows, total = residual.shape
     return call(
-        functools.partial(own_kernel, odd, first, first - origin, first - RAW),
+        functools.partial(own_kernel, odd, first, first - origin, first - RAW, extra),
         "own",
-        array(rows, width),
+        array(rows + extra, width),
         [SMEM] + [VMEM] * 5 + [ANY] * len(after),
         VMEM,
         [table_scratch(lines, width, total)],
-        weight=weight,
     )(start, lines, behind, product, queries, residual, *after)
 
 
@@ -327,7 +332,11 @@
 
         @pl.when(jnp.logical_and(is_first(), is_slab(odd)))
         def _():
-            pieces = [(own_ref, first) for own_ref, (side, first, _) in zip(own_refs, places) if side == odd]
+            pieces = [
+                (own_ref.at[pl.ds(0, out_ref.shape[1])], first)
+                for own_ref, (side, first, _) in zip(own_refs, places)
+                if side == odd
+            ]
             wait_all(send_out(pieces, out_ref, sems))
 
     @pl.when(jnp.logical_not(is_first()))
@@ -362,18 +371,25 @@
 
 
 def raw_kernel(*refs):
-    start_ref, lines_ref, wire_ref, behind_ref, product_ref, queries_ref, gated_ref, residual_ref = refs[:8]
-    out_ref, chosen_ref, table_ref, buffer, sems = refs[9:]
-    width = buffer.shape[1]
+    start_ref, lines_ref, wire_ref, received_ref = refs[:4]
+    behind_ref, product_ref, queries_ref, gated_ref, residual_ref = refs[4:9]
+    out_ref, chosen_ref, table_ref, buffer, sems = refs[10:]
+    rows, width = buffer.shape
     share = share_of(lines_ref, residual_ref.shape[1])
 
     @pl.when(is_first())
     def _():
         chosen_ref[...] = lines_ref[: chosen_ref.shape[0], :]
 
-    @pl.when(jnp.logical_not(is_first()))
+    @pl.when(jnp.logical_and(jnp.logical_not(is_first()), is_slab(1)))
     def _():
         chosen_ref[...] = wire_ref[...].astype(F32)
+
+    @pl.when(jnp.logical_and(jnp.logical_not(is_first()), is_slab(0)))
+    def _():
+        for part in range(RAW // LANES):
+            taken = received_ref[rows:, part * LANES : (part + 1) * LANES]
+            chosen_ref[part * LINES : (part + 1) * LINES, :] = taken.astype(F32)
 
     def store(at, span, mixed):
         gated = queries_ref[span, at].astype(F32) * mixed
@@ -388,14 +404,14 @@
     wait_all(send_out([(buffer, 0)], out_ref, sems))
 
 
-def raw_finish(held, start, lines, wire, behind, product, queries, gated, residual):
+def raw_finish(held, start, lines, wire, received, behind, product, queries, gated, residual):
     rows, width = queries.shape
     total = residual.shape[1]
     return call(
         raw_kernel,
         "raw",
         jax.ShapeDtypeStruct(held.shape, BF16),
-        [SMEM] + [VMEM] * 7 + [ANY],
+        [SMEM] + [VMEM] * 8 + [ANY],
         ANY,
         [
             pltpu.VMEM(wire.shape, F32),
@@ -404,8 +420,8 @@
             pltpu.SemaphoreType.DMA((1,)),
         ],
         weight=SLOW,
-        aliases={8: 0},
-    )(start, lines, wire, behind, product, queries, gated, residual, held)
+        aliases={9: 0},
+    )(start, lines, wire, received, behind, product, queries, gated, residual, held)
 
 
 def finish_kernel(odd, places, *refs):
@@ -417,7 +433,7 @@
         copies = []
         for place, (_, first, width) in enumerate(places):
             buffer = buffers[place]
-            total = received_refs[place][...].astype(F32) + gated_ref[:, first : first + width]
+            total = received_refs[place][: buffer.shape[0], :].astype(F32) + gated_ref[:, first : first + width]
             buffer[...] = total.astype(BF16)
             copies += send_out([(buffer, first)], out_ref, sems.at[pl.ds(place, 1)])
         wait_all(copies)
@@ -450,9 +466,9 @@
     lines, wire, near, far, tail = product_of(keys, values, *small, rest)
     own, received, places = [], [], []
 
-    def send(odd, behind, origin, first, width, *after):
+    def send(odd, behind, origin, first, width, *after, extra=0):
         piece = own_of(
-            odd, origin, context_start, lines, behind, rest, queries, residual, first, width, QUICK, *after
+            odd, origin, extra, context_start, lines, behind, rest, queries, residual, first, width, *after
         )
         own.append(piece)
         received.append(to_next_section(piece, (odd,)))
@@ -471,11 +487,11 @@
     raw_behind = to_next_slab(raw_product, (0, 0), *links)
     raw_queries = held_back(raw_queries, received[0], SLOW)
     first, after = send(0, near_behind, RAW, RAW, EVEN[0], raw_queries)
-    first, after = send(0, near_behind, RAW, first, EVEN[1], after)
+    first, after = send(0, near_behind, RAW, first, EVEN[1], after, extra=LINES)
     origin = first
     first, after = send(0, far_behind, origin, first, EVEN[2], after, received[1])
     first, after = send(0, far_behind, origin, first, EVEN[3], after, raw_behind)
-    wire_received = to_next_section(held_back(wire, after))
+    wire_received = to_next_section(held_back(wire, after), (1,))
     held, gated = later_of(
         context_start,
         lines,
@@ -493,7 +509,16 @@
     held = finish(held, gated, received[:odd], places[:odd])
     held = finish(held, gated, received[odd : odd + 2], places[odd : odd + 2])
     held = raw_finish(
-        held, context_start, lines, wire_received, raw_behind, raw_product, raw_queries, gated, residual
+        held,
+        context_start,
+        lines,
+        wire_received,
+        received[odd + 1],
+        raw_behind,
+        raw_product,
+        raw_queries,
+        gated,
+        residual,
     )
     for last in (odd + 2, odd + 3):
         held = finish(held, gated, received[last : last + 1], places[last : last + 1])

time: 34.6 us -> 32.5 us (0.939)
  waiting for transfers between devices: 7.21 us -> 5.8 us
  starting transfers between devices: 17.8 us -> 17.2 us
    ppermute x8, waiting for transfers between devices: 4.02 us -> 2.61 us  [to_next_section(): return lax.ppermute(value, ('ctx', 'pipe'), pairs)]
    ppermute x8, starting transfers between devices: 9.11 us -> 8.48 us  [to_next_section(): return lax.ppermute(value, ('ctx', 'pipe'), pairs)]
  transfers between devices with their start and end apart: 12 -> 12, of which waited for: 4 -> 4; matrix products, arithmetic and copies ran while one was open for 0% -> 0% of each run, Pallas kernels for 21% -> 23%
where the time goes in v15:
time: 32.5 us; the launch traced here: 32.2 us
  starting transfers between devices  17.2 us (53%)
  Pallas kernels  8.18 us (25%)
  waiting for transfers between devices  5.8 us (18%)
  between operations  0.99 us (3%)
    ppermute x4, starting transfers between devices, to_next_slab(): return lax.ppermute(value, ('ctx', 'pipe'), pairs)  8.71 us
    ppermute x8, starting transfers between devices, to_next_section(): return lax.ppermute(value, ('ctx', 'pipe'), pairs)  8.48 us
    ppermute x4, waiting for transfers between devices, to_next_slab(): return lax.ppermute(value, ('ctx', 'pipe'), pairs)  3.19 us
    pallas_call x1, Pallas kernels, later_of(): call(functools.partial(later_kernel, places), 'later', (jax.ShapeDtypeStr...  2.67 us
    ppermute x8, waiting for transfers between devices, to_next_section(): return lax.ppermute(value, ('ctx', 'pipe'), pairs)  2.61 us
    pallas_call x4, Pallas kernels, finish(): call(functools.partial(finish_kernel, places[0][0], places), 'finish', ja...  2.45 us
    pallas_call x1, Pallas kernels, product_of(): call(product_kernel, 'product', (array(groups, taps, F32), array(wire_row...  1.68 us
    pallas_call x1, Pallas kernels, raw_finish(): call(raw_kernel, 'raw', jax.ShapeDtypeStruct(held.shape, BF16), [SMEM] +...  1.16 us
  transfers between devices with their start and end apart: 12, of which 4 were waited for; matrix products, arithmetic and copies ran while one was open for 0% of the time, Pallas kernels for 23%

profile of v15, /device:TPU:12, one launch (start us, length us, event | category | flops | bytes accessed | tf_op | source)
XLA Modules:
  0.0 32.2 jit_solution(12325903086428175646)
XLA Ops:
  0.0 0.0 copy-start.2
  0.0 0.0 copy-start.3
  0.0 0.0 copy-start.4
  0.0 0.1 lead.1
  0.1 0.0 copy-start
  0.1 0.0 copy-start.1
  0.1 0.9 %collective-permute-start = (bf16[128,3712]{1,0:T(8,128)(2,1)S(1)}, bf16[128,3712]{1,0:T(8,128)(2,1)S(1)}, u32[]{:S(2)}, u32[]{:S(2)}) collective-permute-start(bf16[128,3712]{1,0:T(8,128)(2,1)S(1)} %get-tuple-element.16.refs_5_.refs_3_), channel_id=1, source_target_pairs={{0,4},{8,12},{16,20},{24,28},{2,6},{10,14},{18,22},{26,30}} | collective-permute-start | bytes 2850824 | tf_op jit(solution)/shard_map/ppermute | solution.py:37
  1.0 1.3 %collective-permute-start.2 = (bf16[256,384]{1,0:T(8,128)(2,1)S(1)}, bf16[256,384]{1,0:T(8,128)(2,1)S(1)}, u32[]{:S(2)}, u32[]{:S(2)}) collective-permute-start(bf16[256,384]{1,0:T(8,128)(2,1)S(1)} %get-tuple-element.20.raw_ref), channel_id=1, source_target_pairs={{0,1},{4,5},{8,9},{12,13},{16,17},{20,21},{24,25},{28,29},{2,3},{6... | collective-permute-start | bytes 589832 | tf_op jit(solution)/shard_map/ppermute | solution.py:43
  2.3 0.0 copy-done.2
  2.3 0.0 copy-done.3
  2.3 0.0 copy-done.4
  2.3 1.7 %product.1 = (f32[256,128]{1,0:T(8,128)S(1)}, bf16[32,128]{1,0:T(8,128)(2,1)S(1)}, bf16[128,1792]{1,0:T(8,128)(2,1)S(1)}, bf16[128,1920]{1,0:T(8,128)(2,1)S(1)}, bf16[128,384]{1,0:T(8,128)(2,1)S(1)}) custom-call(bf16[1,128,4096]{2,1,0:T(8,128)(2,1)} %refs_0_.9, bf16[1,128,4096]{2,1,0:T(8,128)(2,1)} %refs_1_.1, bf16[1,256,128]{2,1,0:T(8,128)(2,1)S(1)} %copy-done.2, ...), custom_call_target="tpu_custom_call" | custom-call | flops 1024 | bytes 1024 | tf_op jit(solution)/shard_map/product/pallas_call | solution.py:181
  4.7 0.0 collective-permute-done.refs_2_
  4.7 0.0 copy-done
  4.7 0.0 copy-done.1
  4.7 0.7 %collective-permute-start.5 = (bf16[128,1536]{1,0:T(8,128)(2,1)S(1)}, bf16[128,1536]{1,0:T(8,128)(2,1)S(1)}, u32[]{:S(2)}, u32[]{:S(2)}) collective-permute-start(bf16[128,1536]{1,0:T(8,128)(2,1)S(1)} %own.6._.refs_9_), channel_id=1, source_target_pairs={{4,5},{12,13},{20,21},{28,29},{6,7},{14,15},{22,23},{30,31}} | collective-permute-start | bytes 1179656 | tf_op jit(solution)/shard_map/ppermute | solution.py:43
  5.4 2.3 %collective-permute-start.1 = (bf16[128,1792]{1,0:T(8,128)(2,1)S(1)}, bf16[128,1792]{1,0:T(8,128)(2,1)S(1)}, u32[]{:S(2)}, u32[]{:S(2)}) collective-permute-start(bf16[128,1792]{1,0:T(8,128)(2,1)S(1)} %hold.5.refs_6_.refs_3_), channel_id=1, source_target_pairs={{4,8},{12,16},{20,24},{1,5},{9,13},{17,21},{25,29},{5,9},{13,17},{... | collective-permute-start | bytes 1376264 | tf_op jit(solution)/shard_map/ppermute | solution.py:37
  7.8 0.7 %collective-permute-start.6 = (bf16[128,2176]{1,0:T(8,128)(2,1)S(1)}, bf16[128,2176]{1,0:T(8,128)(2,1)S(1)}, u32[]{:S(2)}, u32[]{:S(2)}) collective-permute-start(bf16[128,2176]{1,0:T(8,128)(2,1)S(1)} %own.7._.refs_10_), channel_id=1, source_target_pairs={{4,5},{12,13},{20,21},{28,29},{6,7},{14,15},{22,23},{30,31}} | collective-permute-start | bytes 1671176 | tf_op jit(solution)/shard_map/ppermute | solution.py:43
  8.5 1.3 %collective-permute-done.2.received_ref = bf16[256,384]{1,0:T(8,128)(2,1)S(1)} collective-permute-done((bf16[256,384]{1,0:T(8,128)(2,1)S(1)}, bf16[256,384]{1,0:T(8,128)(2,1)S(1)}, u32[]{:S(2)}, u32[]{:S(2)}) %collective-permute-start.2) | collective-permute-done | bytes 196640 | tf_op jit(solution)/shard_map/ppermute | solution.py:43
  9.9 2.4 %collective-permute-start.3 = (bf16[128,1920]{1,0:T(8,128)(2,1)S(1)}, bf16[128,1920]{1,0:T(8,128)(2,1)S(1)}, u32[]{:S(2)}, u32[]{:S(2)}) collective-permute-start(bf16[128,1920]{1,0:T(8,128)(2,1)S(1)} %hold.6._.refs_5_), channel_id=1, source_target_pairs={{4,8},{12,16},{20,24},{1,5},{9,13},{17,21},{25,29},{5,9},{13,17},{... | collective-permute-start | bytes 1474568 | tf_op jit(solution)/shard_map/ppermute | solution.py:37
  12.4 3.1 %collective-permute-start.4 = (bf16[128,768]{1,0:T(8,128)(2,1)S(1)}, bf16[128,768]{1,0:T(8,128)(2,1)S(1)}, u32[]{:S(2)}, u32[]{:S(2)}) collective-permute-start(bf16[128,768]{1,0:T(8,128)(2,1)S(1)} %hold.7.refs_5_), channel_id=1, source_target_pairs={{0,4},{8,12},{16,20},{24,28},{4,8},{12,16},{20,24},{1,5},{9,13},{1... | collective-permute-start | bytes 589832 | tf_op jit(solution)/shard_map/ppermute | solution.py:37
  15.4 0.0 collective-permute-done.5._.refs_1_
  15.5 0.0 collective-permute-done.1.refs_2_
  15.5 1.3 %collective-permute-start.11 = (bf16[128,1024]{1,0:T(8,128)(2,1)S(1)}, bf16[128,1024]{1,0:T(8,128)(2,1)S(1)}, u32[]{:S(2)}, u32[]{:S(2)}) collective-permute-start(bf16[128,1024]{1,0:T(8,128)(2,1)S(1)} %own.8.refs_6_.refs_11_), channel_id=1, source_target_pairs={{0,1},{8,9},{16,17},{24,25},{2,3},{10,11},{18,19},{26,27}} | collective-permute-start | bytes 786440 | tf_op jit(solution)/shard_map/ppermute | solution.py:43
  16.8 1.3 %collective-permute-start.10 = (bf16[136,768]{1,0:T(8,128)(2,1)S(1)}, bf16[136,768]{1,0:T(8,128)(2,1)S(1)}, u32[]{:S(2)}, u32[]{:S(2)}) collective-permute-start(bf16[136,768]{1,0:T(8,128)(2,1)S(1)} %own.9.refs_6_.refs_12_), channel_id=1, source_target_pairs={{0,1},{8,9},{16,17},{24,25},{2,3},{10,11},{18,19},{26,27}} | collective-permute-start | bytes 626696 | tf_op jit(solution)/shard_map/ppermute | solution.py:43
  18.1 2.4 %collective-permute-done.3.refs_2_.refs_4_ = bf16[128,1920]{1,0:T(8,128)(2,1)S(1)} collective-permute-done((bf16[128,1920]{1,0:T(8,128)(2,1)S(1)}, bf16[128,1920]{1,0:T(8,128)(2,1)S(1)}, u32[]{:S(2)}, u32[]{:S(2)}) %collective-permute-start.3) | collective-permute-done | bytes 491552 | tf_op jit(solution)/shard_map/ppermute | solution.py:37
  20.5 0.0 collective-permute-done.6.refs_7_.refs_2_
  20.5 1.3 %collective-permute-start.8 = (bf16[128,896]{1,0:T(8,128)(2,1)S(1)}, bf16[128,896]{1,0:T(8,128)(2,1)S(1)}, u32[]{:S(2)}, u32[]{:S(2)}) collective-permute-start(bf16[128,896]{1,0:T(8,128)(2,1)S(1)} %own.10.refs_6_.refs_13_), channel_id=1, source_target_pairs={{0,1},{8,9},{16,17},{24,25},{2,3},{10,11},{18,19},{26,27}} | collective-permute-start | bytes 688136 | tf_op jit(solution)/shard_map/ppermute | solution.py:43
  21.8 0.8 %collective-permute-done.4.refs_7_.refs_6_.refs_4_ = bf16[128,768]{1,0:T(8,128)(2,1)S(1)} collective-permute-done((bf16[128,768]{1,0:T(8,128)(2,1)S(1)}, bf16[128,768]{1,0:T(8,128)(2,1)S(1)}, u32[]{:S(2)}, u32[]{:S(2)}) %collective-permute-start.4) | collective-permute-done | bytes 196640 | tf_op jit(solution)/shard_map/ppermute | solution.py:37
  22.6 1.3 %collective-permute-start.7 = (bf16[128,1024]{1,0:T(8,128)(2,1)S(1)}, bf16[128,1024]{1,0:T(8,128)(2,1)S(1)}, u32[]{:S(2)}, u32[]{:S(2)}) collective-permute-start(bf16[128,1024]{1,0:T(8,128)(2,1)S(1)} %own.11.refs_14_._), channel_id=1, source_target_pairs={{0,1},{8,9},{16,17},{24,25},{2,3},{10,11},{18,19},{26,27}} | collective-permute-start | bytes 786440 | tf_op jit(solution)/shard_map/ppermute | solution.py:43
  23.9 0.7 %collective-permute-start.9 = (bf16[32,128]{1,0:T(8,128)(2,1)S(1)}, bf16[32,128]{1,0:T(8,128)(2,1)S(1)}, u32[]{:S(2)}, u32[]{:S(2)}) collective-permute-start(bf16[32,128]{1,0:T(8,128)(2,1)S(1)} %hold.9), channel_id=1, source_target_pairs={{4,5},{12,13},{20,21},{28,29},{6,7},{14,15},{22,23},{30,31}} | collective-permute-start | bytes 24584 | tf_op jit(solution)/shard_map/ppermute | solution.py:43
  24.6 2.7 %later.1 = (bf16[1,128,4096]{2,1,0:T(8,128)(2,1)}, f32[128,4096]{1,0:T(8,128)S(1)}) custom-call(s32[1]{0:T(128)S(6)} %copy.29.refs_0_, f32[256,128]{1,0:T(8,128)S(1)} %get-tuple-element.17.refs_1_.refs_6_, bf16[128,1792]{1,0:T(8,128)(2,1)S(1)} %collective-permute-done.1.refs_2_, bf16[128,1792]{1,0:T(8,128)(2,1)S(1)} %hold.5.refs_6_.refs_3_, ...), custom_call_target="tpu_custom_call" | custom-call | flops 20000000000 | bytes 1024 | tf_op jit(solution)/shard_map/later/pallas_call | solution.py:362
  27.3 0.0 collective-permute-done.10.refs_2_.refs_3_
  27.3 0.0 collective-permute-done.11.refs_1_
  27.3 0.9 %finish.5.refs_9_ = bf16[1,128,4096]{2,1,0:T(8,128)(2,1)} custom-call(f32[128,4096]{1,0:T(8,128)S(1)} %get-tuple-element.24.refs_0_.refs_7_, bf16[128,1024]{1,0:T(8,128)(2,1)S(1)} %collective-permute-done.11.refs_1_, bf16[136,768]{1,0:T(8,128)(2,1)S(1)} %collective-permute-done.10.refs_2_.refs_3_, ...), custom_call_target="tpu_custom_call", output_to_operand_aliasing={{}: (3, {})} | custom-call | flops 20000000000 | bytes 1024 | tf_op jit(solution)/shard_map/finish/pallas_call | solution.py:445
  28.2 0.0 collective-permute-done.9.refs_2_
  28.2 1.2 %raw.1.refs_2_ = bf16[1,128,4096]{2,1,0:T(8,128)(2,1)} custom-call(s32[1]{0:T(128)S(6)} %copy.29.refs_0_, f32[256,128]{1,0:T(8,128)S(1)} %get-tuple-element.17.refs_1_.refs_6_, bf16[32,128]{1,0:T(8,128)(2,1)S(1)} %collective-permute-done.9.refs_2_, bf16[136,768]{1,0:T(8,128)(2,1)S(1)} %collective-permute-done.10.refs_2_.refs_3_, ...), custom_call_target="tpu_custom_call", output_to_operand_aliasing={{}: (9, {})} | custom-call | flops 20000000000 | bytes 1024 | tf_op jit(solution)/shard_map/raw/pallas_call | solution.py:410
  29.4 0.0 collective-permute-done.8.refs_1_
  29.4 0.8 %finish.6.refs_2_ = bf16[1,128,4096]{2,1,0:T(8,128)(2,1)} custom-call(f32[128,4096]{1,0:T(8,128)S(1)} %get-tuple-element.24.refs_0_.refs_7_, bf16[128,896]{1,0:T(8,128)(2,1)S(1)} %collective-permute-done.8.refs_1_, bf16[1,128,4096]{2,1,0:T(8,128)(2,1)} %raw.1.refs_2_), custom_call_target="tpu_custom_call", output_to_operand_aliasing={{}: (2, {})} | custom-call | flops 20000000000 | bytes 1024 | tf_op jit(solution)/shard_map/finish/pallas_call | solution.py:445
  30.2 1.3 %collective-permute-done.7.refs_1_ = bf16[128,1024]{1,0:T(8,128)(2,1)S(1)} collective-permute-done((bf16[128,1024]{1,0:T(8,128)(2,1)S(1)}, bf16[128,1024]{1,0:T(8,128)(2,1)S(1)}, u32[]{:S(2)}, u32[]{:S(2)}) %collective-permute-start.7) | collective-permute-done | bytes 262176 | tf_op jit(solution)/shard_map/ppermute | solution.py:43
  31.4 0.8 %finish.7 = bf16[1,128,4096]{2,1,0:T(8,128)(2,1)} custom-call(f32[128,4096]{1,0:T(8,128)S(1)} %get-tuple-element.24.refs_0_.refs_7_, bf16[128,1024]{1,0:T(8,128)(2,1)S(1)} %collective-permute-done.7.refs_1_, bf16[1,128,4096]{2,1,0:T(8,128)(2,1)} %finish.6.refs_2_), custom_call_target="tpu_custom_call", output_to_operand_aliasing={{}: (2, {})} | custom-call | flops 20000000000 | bytes 1024 | tf_op jit(solution)/shard_map/finish/pallas_call | solution.py:445
  (13 shorter events, 0.2 us)
Async XLA Ops:
  0.0 2.3 %copy-start.2 = (bf16[1,256,128]{2,1,0:T(8,128)(2,1)S(1)}, bf16[1,256,128]{2,1,0:T(8,128)(2,1)}, u32[]{:S(2)}) copy-start(bf16[1,256,128]{2,1,0:T(8,128)(2,1)} %refs_2_.1) | copy-start | bytes 196612
  0.0 2.3 %copy-start.3 = (f32[1,256]{1,0:T(1,128)S(1)}, f32[1,256]{1,0:T(1,128)}, u32[]{:S(2)}) copy-start(f32[1,256]{1,0:T(1,128)} %refs_3_.1) | copy-start | bytes 3076
  0.0 2.3 %copy-start.4 = (s32[1,256]{1,0:T(1,128)S(1)}, s32[1,256]{1,0:T(1,128)}, u32[]{:S(2)}) copy-start(s32[1,256]{1,0:T(1,128)} %refs_4_.7) | copy-start | bytes 3076
  0.1 4.6 %copy-start = (bf16[1,128,4096]{2,1,0:T(8,128)(2,1)S(1)}, bf16[1,128,4096]{2,1,0:T(8,128)(2,1)}, u32[]{:S(2)}) copy-start(bf16[1,128,4096]{2,1,0:T(8,128)(2,1)} %refs_8_.2) | copy-start | bytes 3145732
  0.1 4.6 %copy-start.1 = (bf16[128,4096]{1,0:T(8,128)(2,1)S(1)}, bf16[128,4096]{1,0:T(8,128)(2,1)}, u32[]{:S(2)}) copy-start(bf16[128,4096]{1,0:T(8,128)(2,1)} %refs_8_.3) | copy-start | bytes 3145732
  0.1 4.5 %collective-permute-start = (bf16[128,3712]{1,0:T(8,128)(2,1)S(1)}, bf16[128,3712]{1,0:T(8,128)(2,1)S(1)}, u32[]{:S(2)}, u32[]{:S(2)}) collective-permute-start(bf16[128,3712]{1,0:T(8,128)(2,1)S(1)} %get-tuple-element.16.refs_5_.refs_3_), channel_id=1, source_target_pairs={{0,4},{8,12},{16,20},{24,28},{2,6},{10,14},{18,22},{26,30}} | collective-permute-start | bytes 2850824 | tf_op jit(solution)/shard_map/ppermute | solution.py:37
  1.0 8.9 %collective-permute-start.2 = (bf16[256,384]{1,0:T(8,128)(2,1)S(1)}, bf16[256,384]{1,0:T(8,128)(2,1)S(1)}, u32[]{:S(2)}, u32[]{:S(2)}) collective-permute-start(bf16[256,384]{1,0:T(8,128)(2,1)S(1)} %get-tuple-element.20.raw_ref), channel_id=1, source_target_pairs={{0,1},{4,5},{8,9},{12,13},{16,17},{20,21},{24,25},{28,29},{2,3},{6... | collective-permute-start | bytes 589832 | tf_op jit(solution)/shard_map/ppermute | solution.py:43
  4.7 10.7 %collective-permute-start.5 = (bf16[128,1536]{1,0:T(8,128)(2,1)S(1)}, bf16[128,1536]{1,0:T(8,128)(2,1)S(1)}, u32[]{:S(2)}, u32[]{:S(2)}) collective-permute-start(bf16[128,1536]{1,0:T(8,128)(2,1)S(1)} %own.6._.refs_9_), channel_id=1, source_target_pairs={{4,5},{12,13},{20,21},{28,29},{6,7},{14,15},{22,23},{30,31}} | collective-permute-start | bytes 1179656 | tf_op jit(solution)/shard_map/ppermute | solution.py:43
  5.4 10.0 %collective-permute-start.1 = (bf16[128,1792]{1,0:T(8,128)(2,1)S(1)}, bf16[128,1792]{1,0:T(8,128)(2,1)S(1)}, u32[]{:S(2)}, u32[]{:S(2)}) collective-permute-start(bf16[128,1792]{1,0:T(8,128)(2,1)S(1)} %hold.5.refs_6_.refs_3_), channel_id=1, source_target_pairs={{4,8},{12,16},{20,24},{1,5},{9,13},{17,21},{25,29},{5,9},{13,17},{... | collective-permute-start | bytes 1376264 | tf_op jit(solution)/shard_map/ppermute | solution.py:37
  7.8 12.7 %collective-permute-start.6 = (bf16[128,2176]{1,0:T(8,128)(2,1)S(1)}, bf16[128,2176]{1,0:T(8,128)(2,1)S(1)}, u32[]{:S(2)}, u32[]{:S(2)}) collective-permute-start(bf16[128,2176]{1,0:T(8,128)(2,1)S(1)} %own.7._.refs_10_), channel_id=1, source_target_pairs={{4,5},{12,13},{20,21},{28,29},{6,7},{14,15},{22,23},{30,31}} | collective-permute-start | bytes 1671176 | tf_op jit(solution)/shard_map/ppermute | solution.py:43
  9.9 10.6 %collective-permute-start.3 = (bf16[128,1920]{1,0:T(8,128)(2,1)S(1)}, bf16[128,1920]{1,0:T(8,128)(2,1)S(1)}, u32[]{:S(2)}, u32[]{:S(2)}) collective-permute-start(bf16[128,1920]{1,0:T(8,128)(2,1)S(1)} %hold.6._.refs_5_), channel_id=1, source_target_pairs={{4,8},{12,16},{20,24},{1,5},{9,13},{17,21},{25,29},{5,9},{13,17},{... | collective-permute-start | bytes 1474568 | tf_op jit(solution)/shard_map/ppermute | solution.py:37
  12.4 10.2 %collective-permute-start.4 = (bf16[128,768]{1,0:T(8,128)(2,1)S(1)}, bf16[128,768]{1,0:T(8,128)(2,1)S(1)}, u32[]{:S(2)}, u32[]{:S(2)}) collective-permute-start(bf16[128,768]{1,0:T(8,128)(2,1)S(1)} %hold.7.refs_5_), channel_id=1, source_target_pairs={{0,4},{8,12},{16,20},{24,28},{4,8},{12,16},{20,24},{1,5},{9,13},{1... | collective-permute-start | bytes 589832 | tf_op jit(solution)/shard_map/ppermute | solution.py:37
  15.5 11.8 %collective-permute-start.11 = (bf16[128,1024]{1,0:T(8,128)(2,1)S(1)}, bf16[128,1024]{1,0:T(8,128)(2,1)S(1)}, u32[]{:S(2)}, u32[]{:S(2)}) collective-permute-start(bf16[128,1024]{1,0:T(8,128)(2,1)S(1)} %own.8.refs_6_.refs_11_), channel_id=1, source_target_pairs={{0,1},{8,9},{16,17},{24,25},{2,3},{10,11},{18,19},{26,27}} | collective-permute-start | bytes 786440 | tf_op jit(solution)/shard_map/ppermute | solution.py:43
  16.8 10.5 %collective-permute-start.10 = (bf16[136,768]{1,0:T(8,128)(2,1)S(1)}, bf16[136,768]{1,0:T(8,128)(2,1)S(1)}, u32[]{:S(2)}, u32[]{:S(2)}) collective-permute-start(bf16[136,768]{1,0:T(8,128)(2,1)S(1)} %own.9.refs_6_.refs_12_), channel_id=1, source_target_pairs={{0,1},{8,9},{16,17},{24,25},{2,3},{10,11},{18,19},{26,27}} | collective-permute-start | bytes 626696 | tf_op jit(solution)/shard_map/ppermute | solution.py:43
  20.5 8.9 %collective-permute-start.8 = (bf16[128,896]{1,0:T(8,128)(2,1)S(1)}, bf16[128,896]{1,0:T(8,128)(2,1)S(1)}, u32[]{:S(2)}, u32[]{:S(2)}) collective-permute-start(bf16[128,896]{1,0:T(8,128)(2,1)S(1)} %own.10.refs_6_.refs_13_), channel_id=1, source_target_pairs={{0,1},{8,9},{16,17},{24,25},{2,3},{10,11},{18,19},{26,27}} | collective-permute-start | bytes 688136 | tf_op jit(solution)/shard_map/ppermute | solution.py:43
  22.6 8.8 %collective-permute-start.7 = (bf16[128,1024]{1,0:T(8,128)(2,1)S(1)}, bf16[128,1024]{1,0:T(8,128)(2,1)S(1)}, u32[]{:S(2)}, u32[]{:S(2)}) collective-permute-start(bf16[128,1024]{1,0:T(8,128)(2,1)S(1)} %own.11.refs_14_._), channel_id=1, source_target_pairs={{0,1},{8,9},{16,17},{24,25},{2,3},{10,11},{18,19},{26,27}} | collective-permute-start | bytes 786440 | tf_op jit(solution)/shard_map/ppermute | solution.py:43
  23.9 4.3 %collective-permute-start.9 = (bf16[32,128]{1,0:T(8,128)(2,1)S(1)}, bf16[32,128]{1,0:T(8,128)(2,1)S(1)}, u32[]{:S(2)}, u32[]{:S(2)}) collective-permute-start(bf16[32,128]{1,0:T(8,128)(2,1)S(1)} %hold.9), channel_id=1, source_target_pairs={{4,5},{12,13},{20,21},{28,29},{6,7},{14,15},{22,23},{30,31}} | collective-permute-start | bytes 24584 | tf_op jit(solution)/shard_map/ppermute | solution.py:43

commit v16 on v15

--- a/solution.py
+++ b/solution.py
@@ -11,10 +11,10 @@
 ROW_BLOCK = 32
 RAW = 384
 ODD = (1536, 2176)
-EVEN = (1024, 768, 896, 1024)
+EVEN = (1024, 896, 1280, 512)
 PIECES = 4
 LINES = 8
-NEAR = 1792
+NEAR = 1920
 F32 = jnp.float32
 BF16 = jnp.bfloat16
 MIB = 1024 * 1024
@@ -156,13 +156,10 @@
     def taps():
         fill_lines(bank_ref[0], scales_ref[...], assign_ref[...], lines_ref)
 
-    @pl.when(is_first())
+    @pl.when(jnp.logical_and(is_first(), is_slab(1)))
     def _():
         taps()
         wire_ref[...] = lines_ref[: wire_ref.shape[0], :].astype(BF16)
-
-    @pl.when(jnp.logical_and(is_first(), is_slab(1)))
-    def _():
         near_ref[...] = rest_ref[:, :NEAR]
         far_ref[...] = rest_ref[:, NEAR:]
 
@@ -269,8 +266,14 @@
     )(start, lines, behind, product, queries, residual, *after)
 
 
-def pick_kernel(raw_ref, received_ref, tail_ref, _, queries_ref, product_ref):
+def pick_kernel(*refs):
+    raw_ref, received_ref, tail_ref, bank_ref, scales_ref, assign_ref = refs[:6]
+    queries_ref, product_ref, lines_ref = refs[8:]
     rows = queries_ref.shape[0]
+
+    @pl.when(jnp.logical_and(is_first(), is_slab(0)))
+    def _():
+        fill_lines(bank_ref[0], scales_ref[...], assign_ref[...], lines_ref)
 
     def take(source):
         queries_ref[...] = source[:rows, :]
@@ -284,16 +287,17 @@
         product_ref[:, RAW:] = tail_ref[...]
 
 
-def pick_of(raw, received, tail, after):
+def pick_of(raw, received, tail, bank, scales, assign, lines, after):
     rows, width = raw.shape[0] // 2, raw.shape[1]
     return call(
         pick_kernel,
         "pick",
-        (array(rows, width), array(rows, 2 * width)),
-        [VMEM, VMEM, VMEM, ANY],
-        (VMEM,) * 2,
+        (array(rows, width), array(rows, 2 * width), array(*lines.shape, F32)),
+        [VMEM] * 7 + [ANY],
+        (VMEM,) * 3,
         weight=SLOW,
-    )(raw, received, tail, after)
+        aliases={6: 2},
+    )(raw, received, tail, bank, scales, assign, lines, after)
 
 
 def hold_kernel(value_ref, _, out_ref):
@@ -365,7 +369,7 @@
         (jax.ShapeDtypeStruct((1, rows, total), BF16), array(rows, total, F32)),
         [SMEM] + [VMEM] * (8 + len(own)),
         (ANY, VMEM),
-        [table_scratch(lines, total - RAW - NEAR, total), pltpu.SemaphoreType.DMA((len(own),))],
+        [table_scratch(lines, max(NEAR, total - RAW - NEAR), total), pltpu.SemaphoreType.DMA((len(own),))],
         weight=SLOW,
     )(start, lines, near_behind, near, far_behind, far, raw_behind, tail, queries, *own)
 
@@ -480,7 +484,7 @@
     near = held_back(near, after)
     near_behind = to_next_slab(near, *links)
     first, after = send(1, chip_behind, RAW, first, ODD[1], near)
-    raw_queries, raw_product = pick_of(raw, raw_received, tail, after)
+    raw_queries, raw_product, lines = pick_of(raw, raw_received, tail, *small, lines, after)
     far = held_back(far, raw_queries)
     far_behind = to_next_slab(far, *links)
     raw_product = held_back(raw_product, far)

time: 32.5 us -> 32.5 us (level)
  transfers between devices with their start and end apart: 12 -> 12, of which waited for: 4 -> 6; matrix products, arithmetic and copies ran while one was open for 0% -> 0% of each run, Pallas kernels for 23% -> 23%
where the time goes in v16:
time: 32.5 us; the launch traced here: 32.1 us
  starting transfers between devices  17.2 us (53%)
  Pallas kernels  8.11 us (25%)
  waiting for transfers between devices  5.85 us (18%)
  between operations  0.97 us (3%)
    ppermute x4, starting transfers between devices, to_next_slab(): return lax.ppermute(value, ('ctx', 'pipe'), pairs)  8.71 us
    ppermute x8, starting transfers between devices, to_next_section(): return lax.ppermute(value, ('ctx', 'pipe'), pairs)  8.47 us
    ppermute x4, waiting for transfers between devices, to_next_slab(): return lax.ppermute(value, ('ctx', 'pipe'), pairs)  3.23 us
    pallas_call x1, Pallas kernels, later_of(): call(functools.partial(later_kernel, places), 'later', (jax.ShapeDtypeStr...  2.71 us
    ppermute x8, waiting for transfers between devices, to_next_section(): return lax.ppermute(value, ('ctx', 'pipe'), pairs)  2.63 us
    pallas_call x4, Pallas kernels, finish(): call(functools.partial(finish_kernel, places[0][0], places), 'finish', ja...  2.38 us
    pallas_call x1, Pallas kernels, product_of(): call(product_kernel, 'product', (array(groups, taps, F32), array(wire_row...  1.67 us
    pallas_call x1, Pallas kernels, raw_finish(): call(raw_kernel, 'raw', jax.ShapeDtypeStruct(held.shape, BF16), [SMEM] +...  1.15 us
  transfers between devices with their start and end apart: 12, of which 6 were waited for; matrix products, arithmetic and copies ran while one was open for 0% of the time, Pallas kernels for 23%

profile of v16, /device:TPU:12, one launch (start us, length us, event | category | flops | bytes accessed | tf_op | source)
XLA Modules:
  0.0 32.1 jit_solution(11468590341796040551)
XLA Ops:
  0.0 0.0 copy-start.2
  0.0 0.0 copy-start.3
  0.0 0.0 copy-start.4
  0.0 0.1 lead.1
  0.1 0.0 copy-start
  0.1 0.0 copy-start.1
  0.1 0.9 %collective-permute-start.1 = (bf16[128,3712]{1,0:T(8,128)(2,1)S(1)}, bf16[128,3712]{1,0:T(8,128)(2,1)S(1)}, u32[]{:S(2)}, u32[]{:S(2)}) collective-permute-start(bf16[128,3712]{1,0:T(8,128)(2,1)S(1)} %get-tuple-element.18.refs_5_.refs_3_), channel_id=1, source_target_pairs={{0,4},{8,12},{16,20},{24,28},{2,6},{10,14},{18,22},{26,30}} | collective-permute-start | bytes 2850824 | tf_op jit(solution)/shard_map/ppermute | solution.py:37
  1.0 1.3 %collective-permute-start = (bf16[256,384]{1,0:T(8,128)(2,1)S(1)}, bf16[256,384]{1,0:T(8,128)(2,1)S(1)}, u32[]{:S(2)}, u32[]{:S(2)}) collective-permute-start(bf16[256,384]{1,0:T(8,128)(2,1)S(1)} %get-tuple-element.17.refs_0_), channel_id=1, source_target_pairs={{0,1},{4,5},{8,9},{12,13},{16,17},{20,21},{24,25},{28,29},{2,3},{6... | collective-permute-start | bytes 589832 | tf_op jit(solution)/shard_map/ppermute | solution.py:43
  2.3 0.0 copy-done.2
  2.3 0.0 copy-done.3
  2.3 0.0 copy-done.4
  2.3 1.7 %product.1 = (f32[256,128]{1,0:T(8,128)S(1)}, bf16[32,128]{1,0:T(8,128)(2,1)S(1)}, bf16[128,1920]{1,0:T(8,128)(2,1)S(1)}, bf16[128,1792]{1,0:T(8,128)(2,1)S(1)}, bf16[128,384]{1,0:T(8,128)(2,1)S(1)}) custom-call(bf16[1,128,4096]{2,1,0:T(8,128)(2,1)} %refs_0_.9, bf16[1,128,4096]{2,1,0:T(8,128)(2,1)} %refs_1_.1, bf16[1,256,128]{2,1,0:T(8,128)(2,1)S(1)} %copy-done.2, ...), custom_call_target="tpu_custom_call" | custom-call | flops 1024 | bytes 1024 | tf_op jit(solution)/shard_map/product/pallas_call | solution.py:178
  4.7 0.0 collective-permute-done.1.refs_2_
  4.7 0.0 copy-done
  4.7 0.0 copy-done.1
  4.7 0.7 %collective-permute-start.5 = (bf16[128,1536]{1,0:T(8,128)(2,1)S(1)}, bf16[128,1536]{1,0:T(8,128)(2,1)S(1)}, u32[]{:S(2)}, u32[]{:S(2)}) collective-permute-start(bf16[128,1536]{1,0:T(8,128)(2,1)S(1)} %own.6._.refs_9_), channel_id=1, source_target_pairs={{4,5},{12,13},{20,21},{28,29},{6,7},{14,15},{22,23},{30,31}} | collective-permute-start | bytes 1179656 | tf_op jit(solution)/shard_map/ppermute | solution.py:43
  5.4 2.3 %collective-permute-start.2 = (bf16[128,1920]{1,0:T(8,128)(2,1)S(1)}, bf16[128,1920]{1,0:T(8,128)(2,1)S(1)}, u32[]{:S(2)}, u32[]{:S(2)}) collective-permute-start(bf16[128,1920]{1,0:T(8,128)(2,1)S(1)} %hold.5.refs_6_.refs_3_), channel_id=1, source_target_pairs={{4,8},{12,16},{20,24},{1,5},{9,13},{17,21},{25,29},{5,9},{13,17},{... | collective-permute-start | bytes 1474568 | tf_op jit(solution)/shard_map/ppermute | solution.py:37
  7.8 0.7 %collective-permute-start.6 = (bf16[128,2176]{1,0:T(8,128)(2,1)S(1)}, bf16[128,2176]{1,0:T(8,128)(2,1)S(1)}, u32[]{:S(2)}, u32[]{:S(2)}) collective-permute-start(bf16[128,2176]{1,0:T(8,128)(2,1)S(1)} %own.7.refs_7_.refs_10_), channel_id=1, source_target_pairs={{4,5},{12,13},{20,21},{28,29},{6,7},{14,15},{22,23},{30,31}} | collective-permute-start | bytes 1671176 | tf_op jit(solution)/shard_map/ppermute | solution.py:43
  8.5 1.3 %collective-permute-done.refs_1_ = bf16[256,384]{1,0:T(8,128)(2,1)S(1)} collective-permute-done((bf16[256,384]{1,0:T(8,128)(2,1)S(1)}, bf16[256,384]{1,0:T(8,128)(2,1)S(1)}, u32[]{:S(2)}, u32[]{:S(2)}) %collective-permute-start) | collective-permute-done | bytes 196640 | tf_op jit(solution)/shard_map/ppermute | solution.py:43
  9.9 2.5 %collective-permute-start.3 = (bf16[128,1792]{1,0:T(8,128)(2,1)S(1)}, bf16[128,1792]{1,0:T(8,128)(2,1)S(1)}, u32[]{:S(2)}, u32[]{:S(2)}) collective-permute-start(bf16[128,1792]{1,0:T(8,128)(2,1)S(1)} %hold.6._.refs_5_), channel_id=1, source_target_pairs={{4,8},{12,16},{20,24},{1,5},{9,13},{17,21},{25,29},{5,9},{13,17},{... | collective-permute-start | bytes 1376264 | tf_op jit(solution)/shard_map/ppermute | solution.py:37
  12.4 3.1 %collective-permute-start.4 = (bf16[128,768]{1,0:T(8,128)(2,1)S(1)}, bf16[128,768]{1,0:T(8,128)(2,1)S(1)}, u32[]{:S(2)}, u32[]{:S(2)}) collective-permute-start(bf16[128,768]{1,0:T(8,128)(2,1)S(1)} %hold.7.refs_5_), channel_id=1, source_target_pairs={{0,4},{8,12},{16,20},{24,28},{4,8},{12,16},{20,24},{1,5},{9,13},{1... | collective-permute-start | bytes 589832 | tf_op jit(solution)/shard_map/ppermute | solution.py:37
  15.4 0.0 collective-permute-done.5._.refs_1_
  15.5 0.1 collective-permute-done.2.refs_2_
  15.6 1.3 %collective-permute-start.11 = (bf16[128,1024]{1,0:T(8,128)(2,1)S(1)}, bf16[128,1024]{1,0:T(8,128)(2,1)S(1)}, u32[]{:S(2)}, u32[]{:S(2)}) collective-permute-start(bf16[128,1024]{1,0:T(8,128)(2,1)S(1)} %own.8.refs_6_.refs_11_), channel_id=1, source_target_pairs={{0,1},{8,9},{16,17},{24,25},{2,3},{10,11},{18,19},{26,27}} | collective-permute-start | bytes 786440 | tf_op jit(solution)/shard_map/ppermute | solution.py:43
  16.9 1.3 %collective-permute-start.10 = (bf16[136,896]{1,0:T(8,128)(2,1)S(1)}, bf16[136,896]{1,0:T(8,128)(2,1)S(1)}, u32[]{:S(2)}, u32[]{:S(2)}) collective-permute-start(bf16[136,896]{1,0:T(8,128)(2,1)S(1)} %own.9.refs_6_.refs_12_), channel_id=1, source_target_pairs={{0,1},{8,9},{16,17},{24,25},{2,3},{10,11},{18,19},{26,27}} | collective-permute-start | bytes 731144 | tf_op jit(solution)/shard_map/ppermute | solution.py:43
  18.2 2.3 %collective-permute-done.3.refs_2_.refs_4_ = bf16[128,1792]{1,0:T(8,128)(2,1)S(1)} collective-permute-done((bf16[128,1792]{1,0:T(8,128)(2,1)S(1)}, bf16[128,1792]{1,0:T(8,128)(2,1)S(1)}, u32[]{:S(2)}, u32[]{:S(2)}) %collective-permute-start.3) | collective-permute-done | bytes 458784 | tf_op jit(solution)/shard_map/ppermute | solution.py:37
  20.5 0.0 collective-permute-done.6.refs_7_.refs_2_
  20.5 1.3 %collective-permute-start.8 = (bf16[128,1280]{1,0:T(8,128)(2,1)S(1)}, bf16[128,1280]{1,0:T(8,128)(2,1)S(1)}, u32[]{:S(2)}, u32[]{:S(2)}) collective-permute-start(bf16[128,1280]{1,0:T(8,128)(2,1)S(1)} %own.10.refs_6_.refs_13_), channel_id=1, source_target_pairs={{0,1},{8,9},{16,17},{24,25},{2,3},{10,11},{18,19},{26,27}} | collective-permute-start | bytes 983048 | tf_op jit(solution)/shard_map/ppermute | solution.py:43
  21.8 0.8 %collective-permute-done.4.refs_7_.refs_6_.refs_4_ = bf16[128,768]{1,0:T(8,128)(2,1)S(1)} collective-permute-done((bf16[128,768]{1,0:T(8,128)(2,1)S(1)}, bf16[128,768]{1,0:T(8,128)(2,1)S(1)}, u32[]{:S(2)}, u32[]{:S(2)}) %collective-permute-start.4) | collective-permute-done | bytes 196640 | tf_op jit(solution)/shard_map/ppermute | solution.py:37
  22.6 1.3 %collective-permute-start.7 = (bf16[128,512]{1,0:T(8,128)(2,1)S(1)}, bf16[128,512]{1,0:T(8,128)(2,1)S(1)}, u32[]{:S(2)}, u32[]{:S(2)}) collective-permute-start(bf16[128,512]{1,0:T(8,128)(2,1)S(1)} %own.11.refs_14_._), channel_id=1, source_target_pairs={{0,1},{8,9},{16,17},{24,25},{2,3},{10,11},{18,19},{26,27}} | collective-permute-start | bytes 393224 | tf_op jit(solution)/shard_map/ppermute | solution.py:43
  23.9 0.7 %collective-permute-start.9 = (bf16[32,128]{1,0:T(8,128)(2,1)S(1)}, bf16[32,128]{1,0:T(8,128)(2,1)S(1)}, u32[]{:S(2)}, u32[]{:S(2)}) collective-permute-start(bf16[32,128]{1,0:T(8,128)(2,1)S(1)} %hold.9), channel_id=1, source_target_pairs={{4,5},{12,13},{20,21},{28,29},{6,7},{14,15},{22,23},{30,31}} | collective-permute-start | bytes 24584 | tf_op jit(solution)/shard_map/ppermute | solution.py:43
  24.6 2.7 %later.1 = (bf16[1,128,4096]{2,1,0:T(8,128)(2,1)}, f32[128,4096]{1,0:T(8,128)S(1)}) custom-call(s32[1]{0:T(128)S(6)} %copy.31.refs_0_, f32[256,128]{1,0:T(8,128)S(1)} %get-tuple-element.22.refs_1_, bf16[128,1920]{1,0:T(8,128)(2,1)S(1)} %collective-permute-done.2.refs_2_, bf16[128,1920]{1,0:T(8,128)(2,1)S(1)} %hold.5.refs_6_.refs_3_, ...), custom_call_target="tpu_custom_call" | custom-call | flops 20000000000 | bytes 1024 | tf_op jit(solution)/shard_map/later/pallas_call | solution.py:366
  27.3 0.0 collective-permute-done.10.refs_2_.refs_3_
  27.3 0.0 collective-permute-done.11.refs_1_
  27.3 0.9 %finish.5.refs_9_ = bf16[1,128,4096]{2,1,0:T(8,128)(2,1)} custom-call(f32[128,4096]{1,0:T(8,128)S(1)} %get-tuple-element.26.refs_0_.refs_7_, bf16[128,1024]{1,0:T(8,128)(2,1)S(1)} %collective-permute-done.11.refs_1_, bf16[136,896]{1,0:T(8,128)(2,1)S(1)} %collective-permute-done.10.refs_2_.refs_3_, ...), custom_call_target="tpu_custom_call", output_to_operand_aliasing={{}: (3, {})} | custom-call | flops 20000000000 | bytes 1024 | tf_op jit(solution)/shard_map/finish/pallas_call | solution.py:449
  28.2 0.0 collective-permute-done.9.refs_2_
  28.2 1.1 %raw.1.refs_2_ = bf16[1,128,4096]{2,1,0:T(8,128)(2,1)} custom-call(s32[1]{0:T(128)S(6)} %copy.31.refs_0_, f32[256,128]{1,0:T(8,128)S(1)} %get-tuple-element.22.refs_1_, bf16[32,128]{1,0:T(8,128)(2,1)S(1)} %collective-permute-done.9.refs_2_, bf16[136,896]{1,0:T(8,128)(2,1)S(1)} %collective-permute-done.10.refs_2_.refs_3_, ...), custom_call_target="tpu_custom_call", output_to_operand_aliasing={{}: (9, {})} | custom-call | flops 20000000000 | bytes 1024 | tf_op jit(solution)/shard_map/raw/pallas_call | solution.py:414
  29.4 0.7 %collective-permute-done.8.refs_1_ = bf16[128,1280]{1,0:T(8,128)(2,1)S(1)} collective-permute-done((bf16[128,1280]{1,0:T(8,128)(2,1)S(1)}, bf16[128,1280]{1,0:T(8,128)(2,1)S(1)}, u32[]{:S(2)}, u32[]{:S(2)}) %collective-permute-start.8) | collective-permute-done | bytes 327712 | tf_op jit(solution)/shard_map/ppermute | solution.py:43
  30.0 0.8 %finish.6.refs_2_ = bf16[1,128,4096]{2,1,0:T(8,128)(2,1)} custom-call(f32[128,4096]{1,0:T(8,128)S(1)} %get-tuple-element.26.refs_0_.refs_7_, bf16[128,1280]{1,0:T(8,128)(2,1)S(1)} %collective-permute-done.8.refs_1_, bf16[1,128,4096]{2,1,0:T(8,128)(2,1)} %raw.1.refs_2_), custom_call_target="tpu_custom_call", output_to_operand_aliasing={{}: (2, {})} | custom-call | flops 20000000000 | bytes 1024 | tf_op jit(solution)/shard_map/finish/pallas_call | solution.py:449
  30.8 0.6 %collective-permute-done.7.refs_1_ = bf16[128,512]{1,0:T(8,128)(2,1)S(1)} collective-permute-done((bf16[128,512]{1,0:T(8,128)(2,1)S(1)}, bf16[128,512]{1,0:T(8,128)(2,1)S(1)}, u32[]{:S(2)}, u32[]{:S(2)}) %collective-permute-start.7) | collective-permute-done | bytes 131104 | tf_op jit(solution)/shard_map/ppermute | solution.py:43
  31.4 0.7 %finish.7 = bf16[1,128,4096]{2,1,0:T(8,128)(2,1)} custom-call(f32[128,4096]{1,0:T(8,128)S(1)} %get-tuple-element.26.refs_0_.refs_7_, bf16[128,512]{1,0:T(8,128)(2,1)S(1)} %collective-permute-done.7.refs_1_, bf16[1,128,4096]{2,1,0:T(8,128)(2,1)} %finish.6.refs_2_), custom_call_target="tpu_custom_call", output_to_operand_aliasing={{}: (2, {})} | custom-call | flops 20000000000 | bytes 1024 | tf_op jit(solution)/shard_map/finish/pallas_call | solution.py:449
  (13 shorter events, 0.1 us)
Async XLA Ops:
  0.0 2.3 %copy-start.2 = (bf16[1,256,128]{2,1,0:T(8,128)(2,1)S(1)}, bf16[1,256,128]{2,1,0:T(8,128)(2,1)}, u32[]{:S(2)}) copy-start(bf16[1,256,128]{2,1,0:T(8,128)(2,1)} %refs_3_.3) | copy-start | bytes 196612
  0.0 2.3 %copy-start.3 = (f32[1,256]{1,0:T(1,128)S(1)}, f32[1,256]{1,0:T(1,128)}, u32[]{:S(2)}) copy-start(f32[1,256]{1,0:T(1,128)} %refs_4_.11) | copy-start | bytes 3076
  0.0 2.3 %copy-start.4 = (s32[1,256]{1,0:T(1,128)S(1)}, s32[1,256]{1,0:T(1,128)}, u32[]{:S(2)}) copy-start(s32[1,256]{1,0:T(1,128)} %refs_5_.9) | copy-start | bytes 3076
  0.1 4.6 %copy-start = (bf16[1,128,4096]{2,1,0:T(8,128)(2,1)S(1)}, bf16[1,128,4096]{2,1,0:T(8,128)(2,1)}, u32[]{:S(2)}) copy-start(bf16[1,128,4096]{2,1,0:T(8,128)(2,1)} %refs_8_.2) | copy-start | bytes 3145732
  0.1 4.6 %copy-start.1 = (bf16[128,4096]{1,0:T(8,128)(2,1)S(1)}, bf16[128,4096]{1,0:T(8,128)(2,1)}, u32[]{:S(2)}) copy-start(bf16[128,4096]{1,0:T(8,128)(2,1)} %refs_8_.3) | copy-start | bytes 3145732
  0.1 4.5 %collective-permute-start.1 = (bf16[128,3712]{1,0:T(8,128)(2,1)S(1)}, bf16[128,3712]{1,0:T(8,128)(2,1)S(1)}, u32[]{:S(2)}, u32[]{:S(2)}) collective-permute-start(bf16[128,3712]{1,0:T(8,128)(2,1)S(1)} %get-tuple-element.18.refs_5_.refs_3_), channel_id=1, source_target_pairs={{0,4},{8,12},{16,20},{24,28},{2,6},{10,14},{18,22},{26,30}} | collective-permute-start | bytes 2850824 | tf_op jit(solution)/shard_map/ppermute | solution.py:37
  1.0 8.9 %collective-permute-start = (bf16[256,384]{1,0:T(8,128)(2,1)S(1)}, bf16[256,384]{1,0:T(8,128)(2,1)S(1)}, u32[]{:S(2)}, u32[]{:S(2)}) collective-permute-start(bf16[256,384]{1,0:T(8,128)(2,1)S(1)} %get-tuple-element.17.refs_0_), channel_id=1, source_target_pairs={{0,1},{4,5},{8,9},{12,13},{16,17},{20,21},{24,25},{28,29},{2,3},{6... | collective-permute-start | bytes 589832 | tf_op jit(solution)/shard_map/ppermute | solution.py:43
  4.7 10.7 %collective-permute-start.5 = (bf16[128,1536]{1,0:T(8,128)(2,1)S(1)}, bf16[128,1536]{1,0:T(8,128)(2,1)S(1)}, u32[]{:S(2)}, u32[]{:S(2)}) collective-permute-start(bf16[128,1536]{1,0:T(8,128)(2,1)S(1)} %own.6._.refs_9_), channel_id=1, source_target_pairs={{4,5},{12,13},{20,21},{28,29},{6,7},{14,15},{22,23},{30,31}} | collective-permute-start | bytes 1179656 | tf_op jit(solution)/shard_map/ppermute | solution.py:43
  5.4 10.1 %collective-permute-start.2 = (bf16[128,1920]{1,0:T(8,128)(2,1)S(1)}, bf16[128,1920]{1,0:T(8,128)(2,1)S(1)}, u32[]{:S(2)}, u32[]{:S(2)}) collective-permute-start(bf16[128,1920]{1,0:T(8,128)(2,1)S(1)} %hold.5.refs_6_.refs_3_), channel_id=1, source_target_pairs={{4,8},{12,16},{20,24},{1,5},{9,13},{17,21},{25,29},{5,9},{13,17},{... | collective-permute-start | bytes 1474568 | tf_op jit(solution)/shard_map/ppermute | solution.py:37
  7.8 12.7 %collective-permute-start.6 = (bf16[128,2176]{1,0:T(8,128)(2,1)S(1)}, bf16[128,2176]{1,0:T(8,128)(2,1)S(1)}, u32[]{:S(2)}, u32[]{:S(2)}) collective-permute-start(bf16[128,2176]{1,0:T(8,128)(2,1)S(1)} %own.7.refs_7_.refs_10_), channel_id=1, source_target_pairs={{4,5},{12,13},{20,21},{28,29},{6,7},{14,15},{22,23},{30,31}} | collective-permute-start | bytes 1671176 | tf_op jit(solution)/shard_map/ppermute | solution.py:43
  9.9 10.6 %collective-permute-start.3 = (bf16[128,1792]{1,0:T(8,128)(2,1)S(1)}, bf16[128,1792]{1,0:T(8,128)(2,1)S(1)}, u32[]{:S(2)}, u32[]{:S(2)}) collective-permute-start(bf16[128,1792]{1,0:T(8,128)(2,1)S(1)} %hold.6._.refs_5_), channel_id=1, source_target_pairs={{4,8},{12,16},{20,24},{1,5},{9,13},{17,21},{25,29},{5,9},{13,17},{... | collective-permute-start | bytes 1376264 | tf_op jit(solution)/shard_map/ppermute | solution.py:37
  12.4 10.2 %collective-permute-start.4 = (bf16[128,768]{1,0:T(8,128)(2,1)S(1)}, bf16[128,768]{1,0:T(8,128)(2,1)S(1)}, u32[]{:S(2)}, u32[]{:S(2)}) collective-permute-start(bf16[128,768]{1,0:T(8,128)(2,1)S(1)} %hold.7.refs_5_), channel_id=1, source_target_pairs={{0,4},{8,12},{16,20},{24,28},{4,8},{12,16},{20,24},{1,5},{9,13},{1... | collective-permute-start | bytes 589832 | tf_op jit(solution)/shard_map/ppermute | solution.py:37
  15.6 11.8 %collective-permute-start.11 = (bf16[128,1024]{1,0:T(8,128)(2,1)S(1)}, bf16[128,1024]{1,0:T(8,128)(2,1)S(1)}, u32[]{:S(2)}, u32[]{:S(2)}) collective-permute-start(bf16[128,1024]{1,0:T(8,128)(2,1)S(1)} %own.8.refs_6_.refs_11_), channel_id=1, source_target_pairs={{0,1},{8,9},{16,17},{24,25},{2,3},{10,11},{18,19},{26,27}} | collective-permute-start | bytes 786440 | tf_op jit(solution)/shard_map/ppermute | solution.py:43
  16.9 10.4 %collective-permute-start.10 = (bf16[136,896]{1,0:T(8,128)(2,1)S(1)}, bf16[136,896]{1,0:T(8,128)(2,1)S(1)}, u32[]{:S(2)}, u32[]{:S(2)}) collective-permute-start(bf16[136,896]{1,0:T(8,128)(2,1)S(1)} %own.9.refs_6_.refs_12_), channel_id=1, source_target_pairs={{0,1},{8,9},{16,17},{24,25},{2,3},{10,11},{18,19},{26,27}} | collective-permute-start | bytes 731144 | tf_op jit(solution)/shard_map/ppermute | solution.py:43
  20.5 9.5 %collective-permute-start.8 = (bf16[128,1280]{1,0:T(8,128)(2,1)S(1)}, bf16[128,1280]{1,0:T(8,128)(2,1)S(1)}, u32[]{:S(2)}, u32[]{:S(2)}) collective-permute-start(bf16[128,1280]{1,0:T(8,128)(2,1)S(1)} %own.10.refs_6_.refs_13_), channel_id=1, source_target_pairs={{0,1},{8,9},{16,17},{24,25},{2,3},{10,11},{18,19},{26,27}} | collective-permute-start | bytes 983048 | tf_op jit(solution)/shard_map/ppermute | solution.py:43
  22.6 8.8 %collective-permute-start.7 = (bf16[128,512]{1,0:T(8,128)(2,1)S(1)}, bf16[128,512]{1,0:T(8,128)(2,1)S(1)}, u32[]{:S(2)}, u32[]{:S(2)}) collective-permute-start(bf16[128,512]{1,0:T(8,128)(2,1)S(1)} %own.11.refs_14_._), channel_id=1, source_target_pairs={{0,1},{8,9},{16,17},{24,25},{2,3},{10,11},{18,19},{26,27}} | collective-permute-start | bytes 393224 | tf_op jit(solution)/shard_map/ppermute | solution.py:43
  23.9 4.3 %collective-permute-start.9 = (bf16[32,128]{1,0:T(8,128)(2,1)S(1)}, bf16[32,128]{1,0:T(8,128)(2,1)S(1)}, u32[]{:S(2)}, u32[]{:S(2)}) collective-permute-start(bf16[32,128]{1,0:T(8,128)(2,1)S(1)} %hold.9), channel_id=1, source_target_pairs={{4,5},{12,13},{20,21},{28,29},{6,7},{14,15},{22,23},{30,31}} | collective-permute-start | bytes 24584 | tf_op jit(solution)/shard_map/ppermute | solution.py:43

commit v17 on v16

--- a/solution.py
+++ b/solution.py
@@ -11,10 +11,10 @@
 ROW_BLOCK = 32
 RAW = 384
 ODD = (1536, 2176)
-EVEN = (1024, 896, 1280, 512)
+EVEN = (1024, 768, 1280, 640)
 PIECES = 4
 LINES = 8
-NEAR = 1920
+NEAR = 1792
 F32 = jnp.float32
 BF16 = jnp.bfloat16
 MIB = 1024 * 1024

time: 32.5 us -> 32.4 us (level)
  transfers between devices with their start and end apart: 12 -> 12, of which waited for: 6 -> 5; matrix products, arithmetic and copies ran while one was open for 0% -> 0% of each run, Pallas kernels for 23% -> 23%
where the time goes in v17:
time: 32.4 us; the launch traced here: 32.1 us
  starting transfers between devices  17.2 us (53%)
  Pallas kernels  8.1 us (25%)
  waiting for transfers between devices  5.76 us (18%)
  between operations  0.98 us (3%)
    ppermute x4, starting transfers between devices, to_next_slab(): return lax.ppermute(value, ('ctx', 'pipe'), pairs)  8.71 us
    ppermute x8, starting transfers between devices, to_next_section(): return lax.ppermute(value, ('ctx', 'pipe'), pairs)  8.48 us
    ppermute x4, waiting for transfers between devices, to_next_slab(): return lax.ppermute(value, ('ctx', 'pipe'), pairs)  3.18 us
    pallas_call x1, Pallas kernels, later_of(): call(functools.partial(later_kernel, places), 'later', (jax.ShapeDtypeStr...  2.67 us
    ppermute x8, waiting for transfers between devices, to_next_section(): return lax.ppermute(value, ('ctx', 'pipe'), pairs)  2.58 us
    pallas_call x4, Pallas kernels, finish(): call(functools.partial(finish_kernel, places[0][0], places), 'finish', ja...  2.39 us
    pallas_call x1, Pallas kernels, product_of(): call(product_kernel, 'product', (array(groups, taps, F32), array(wire_row...  1.67 us
    pallas_call x1, Pallas kernels, raw_finish(): call(raw_kernel, 'raw', jax.ShapeDtypeStruct(held.shape, BF16), [SMEM] +...  1.15 us
  transfers between devices with their start and end apart: 12, of which 5 were waited for; matrix products, arithmetic and copies ran while one was open for 0% of the time, Pallas kernels for 23%

profile of v17, /device:TPU:12, one launch (start us, length us, event | category | flops | bytes accessed | tf_op | source)
XLA Modules:
  0.0 32.1 jit_solution(16563993453250904226)
XLA Ops:
  0.0 0.0 copy-start.2
  0.0 0.0 copy-start.3
  0.0 0.0 copy-start.4
  0.0 0.1 lead.1
  0.1 0.0 copy-start
  0.1 0.0 copy-start.1
  0.1 0.9 %collective-permute-start.1 = (bf16[128,3712]{1,0:T(8,128)(2,1)S(1)}, bf16[128,3712]{1,0:T(8,128)(2,1)S(1)}, u32[]{:S(2)}, u32[]{:S(2)}) collective-permute-start(bf16[128,3712]{1,0:T(8,128)(2,1)S(1)} %get-tuple-element.18.refs_5_.refs_3_), channel_id=1, source_target_pairs={{0,4},{8,12},{16,20},{24,28},{2,6},{10,14},{18,22},{26,30}} | collective-permute-start | bytes 2850824 | tf_op jit(solution)/shard_map/ppermute | solution.py:37
  1.0 1.3 %collective-permute-start = (bf16[256,384]{1,0:T(8,128)(2,1)S(1)}, bf16[256,384]{1,0:T(8,128)(2,1)S(1)}, u32[]{:S(2)}, u32[]{:S(2)}) collective-permute-start(bf16[256,384]{1,0:T(8,128)(2,1)S(1)} %get-tuple-element.17.refs_0_), channel_id=1, source_target_pairs={{0,1},{4,5},{8,9},{12,13},{16,17},{20,21},{24,25},{28,29},{2,3},{6... | collective-permute-start | bytes 589832 | tf_op jit(solution)/shard_map/ppermute | solution.py:43
  2.3 0.0 copy-done.2
  2.3 0.0 copy-done.3
  2.3 0.0 copy-done.4
  2.3 1.7 %product.1 = (f32[256,128]{1,0:T(8,128)S(1)}, bf16[32,128]{1,0:T(8,128)(2,1)S(1)}, bf16[128,1792]{1,0:T(8,128)(2,1)S(1)}, bf16[128,1920]{1,0:T(8,128)(2,1)S(1)}, bf16[128,384]{1,0:T(8,128)(2,1)S(1)}) custom-call(bf16[1,128,4096]{2,1,0:T(8,128)(2,1)} %refs_0_.9, bf16[1,128,4096]{2,1,0:T(8,128)(2,1)} %refs_1_.1, bf16[1,256,128]{2,1,0:T(8,128)(2,1)S(1)} %copy-done.2, ...), custom_call_target="tpu_custom_call" | custom-call | flops 1024 | bytes 1024 | tf_op jit(solution)/shard_map/product/pallas_call | solution.py:178
  4.7 0.0 collective-permute-done.1.refs_2_
  4.7 0.0 copy-done
  4.7 0.0 copy-done.1
  4.7 0.7 %collective-permute-start.5 = (bf16[128,1536]{1,0:T(8,128)(2,1)S(1)}, bf16[128,1536]{1,0:T(8,128)(2,1)S(1)}, u32[]{:S(2)}, u32[]{:S(2)}) collective-permute-start(bf16[128,1536]{1,0:T(8,128)(2,1)S(1)} %own.6._.refs_9_), channel_id=1, source_target_pairs={{4,5},{12,13},{20,21},{28,29},{6,7},{14,15},{22,23},{30,31}} | collective-permute-start | bytes 1179656 | tf_op jit(solution)/shard_map/ppermute | solution.py:43
  5.4 2.3 %collective-permute-start.2 = (bf16[128,1792]{1,0:T(8,128)(2,1)S(1)}, bf16[128,1792]{1,0:T(8,128)(2,1)S(1)}, u32[]{:S(2)}, u32[]{:S(2)}) collective-permute-start(bf16[128,1792]{1,0:T(8,128)(2,1)S(1)} %hold.5.refs_6_.refs_3_), channel_id=1, source_target_pairs={{4,8},{12,16},{20,24},{1,5},{9,13},{17,21},{25,29},{5,9},{13,17},{... | collective-permute-start | bytes 1376264 | tf_op jit(solution)/shard_map/ppermute | solution.py:37
  7.8 0.7 %collective-permute-start.6 = (bf16[128,2176]{1,0:T(8,128)(2,1)S(1)}, bf16[128,2176]{1,0:T(8,128)(2,1)S(1)}, u32[]{:S(2)}, u32[]{:S(2)}) collective-permute-start(bf16[128,2176]{1,0:T(8,128)(2,1)S(1)} %own.7.refs_7_.refs_10_), channel_id=1, source_target_pairs={{4,5},{12,13},{20,21},{28,29},{6,7},{14,15},{22,23},{30,31}} | collective-permute-start | bytes 1671176 | tf_op jit(solution)/shard_map/ppermute | solution.py:43
  8.5 1.3 %collective-permute-done.refs_1_ = bf16[256,384]{1,0:T(8,128)(2,1)S(1)} collective-permute-done((bf16[256,384]{1,0:T(8,128)(2,1)S(1)}, bf16[256,384]{1,0:T(8,128)(2,1)S(1)}, u32[]{:S(2)}, u32[]{:S(2)}) %collective-permute-start) | collective-permute-done | bytes 196640 | tf_op jit(solution)/shard_map/ppermute | solution.py:43
  9.9 2.5 %collective-permute-start.3 = (bf16[128,1920]{1,0:T(8,128)(2,1)S(1)}, bf16[128,1920]{1,0:T(8,128)(2,1)S(1)}, u32[]{:S(2)}, u32[]{:S(2)}) collective-permute-start(bf16[128,1920]{1,0:T(8,128)(2,1)S(1)} %hold.6._.refs_5_), channel_id=1, source_target_pairs={{4,8},{12,16},{20,24},{1,5},{9,13},{17,21},{25,29},{5,9},{13,17},{... | collective-permute-start | bytes 1474568 | tf_op jit(solution)/shard_map/ppermute | solution.py:37
  12.4 3.1 %collective-permute-start.4 = (bf16[128,768]{1,0:T(8,128)(2,1)S(1)}, bf16[128,768]{1,0:T(8,128)(2,1)S(1)}, u32[]{:S(2)}, u32[]{:S(2)}) collective-permute-start(bf16[128,768]{1,0:T(8,128)(2,1)S(1)} %hold.7.refs_5_), channel_id=1, source_target_pairs={{0,4},{8,12},{16,20},{24,28},{4,8},{12,16},{20,24},{1,5},{9,13},{1... | collective-permute-start | bytes 589832 | tf_op jit(solution)/shard_map/ppermute | solution.py:37
  15.4 0.0 collective-permute-done.5._.refs_1_
  15.5 0.0 collective-permute-done.2.refs_2_
  15.5 1.3 %collective-permute-start.11 = (bf16[128,1024]{1,0:T(8,128)(2,1)S(1)}, bf16[128,1024]{1,0:T(8,128)(2,1)S(1)}, u32[]{:S(2)}, u32[]{:S(2)}) collective-permute-start(bf16[128,1024]{1,0:T(8,128)(2,1)S(1)} %own.8.refs_6_.refs_11_), channel_id=1, source_target_pairs={{0,1},{8,9},{16,17},{24,25},{2,3},{10,11},{18,19},{26,27}} | collective-permute-start | bytes 786440 | tf_op jit(solution)/shard_map/ppermute | solution.py:43
  16.8 1.3 %collective-permute-start.10 = (bf16[136,768]{1,0:T(8,128)(2,1)S(1)}, bf16[136,768]{1,0:T(8,128)(2,1)S(1)}, u32[]{:S(2)}, u32[]{:S(2)}) collective-permute-start(bf16[136,768]{1,0:T(8,128)(2,1)S(1)} %own.9.refs_6_.refs_12_), channel_id=1, source_target_pairs={{0,1},{8,9},{16,17},{24,25},{2,3},{10,11},{18,19},{26,27}} | collective-permute-start | bytes 626696 | tf_op jit(solution)/shard_map/ppermute | solution.py:43
  18.1 2.4 %collective-permute-done.3.refs_2_.refs_4_ = bf16[128,1920]{1,0:T(8,128)(2,1)S(1)} collective-permute-done((bf16[128,1920]{1,0:T(8,128)(2,1)S(1)}, bf16[128,1920]{1,0:T(8,128)(2,1)S(1)}, u32[]{:S(2)}, u32[]{:S(2)}) %collective-permute-start.3) | collective-permute-done | bytes 491552 | tf_op jit(solution)/shard_map/ppermute | solution.py:37
  20.5 0.0 collective-permute-done.6.refs_7_.refs_2_
  20.5 1.3 %collective-permute-start.8 = (bf16[128,1280]{1,0:T(8,128)(2,1)S(1)}, bf16[128,1280]{1,0:T(8,128)(2,1)S(1)}, u32[]{:S(2)}, u32[]{:S(2)}) collective-permute-start(bf16[128,1280]{1,0:T(8,128)(2,1)S(1)} %own.10.refs_6_.refs_13_), channel_id=1, source_target_pairs={{0,1},{8,9},{16,17},{24,25},{2,3},{10,11},{18,19},{26,27}} | collective-permute-start | bytes 983048 | tf_op jit(solution)/shard_map/ppermute | solution.py:43
  21.8 0.8 %collective-permute-done.4.refs_7_.refs_6_.refs_4_ = bf16[128,768]{1,0:T(8,128)(2,1)S(1)} collective-permute-done((bf16[128,768]{1,0:T(8,128)(2,1)S(1)}, bf16[128,768]{1,0:T(8,128)(2,1)S(1)}, u32[]{:S(2)}, u32[]{:S(2)}) %collective-permute-start.4) | collective-permute-done | bytes 196640 | tf_op jit(solution)/shard_map/ppermute | solution.py:37
  22.6 1.3 %collective-permute-start.7 = (bf16[128,640]{1,0:T(8,128)(2,1)S(1)}, bf16[128,640]{1,0:T(8,128)(2,1)S(1)}, u32[]{:S(2)}, u32[]{:S(2)}) collective-permute-start(bf16[128,640]{1,0:T(8,128)(2,1)S(1)} %own.11.refs_14_._), channel_id=1, source_target_pairs={{0,1},{8,9},{16,17},{24,25},{2,3},{10,11},{18,19},{26,27}} | collective-permute-start | bytes 491528 | tf_op jit(solution)/shard_map/ppermute | solution.py:43
  23.9 0.7 %collective-permute-start.9 = (bf16[32,128]{1,0:T(8,128)(2,1)S(1)}, bf16[32,128]{1,0:T(8,128)(2,1)S(1)}, u32[]{:S(2)}, u32[]{:S(2)}) collective-permute-start(bf16[32,128]{1,0:T(8,128)(2,1)S(1)} %hold.9), channel_id=1, source_target_pairs={{4,5},{12,13},{20,21},{28,29},{6,7},{14,15},{22,23},{30,31}} | collective-permute-start | bytes 24584 | tf_op jit(solution)/shard_map/ppermute | solution.py:43
  24.6 2.7 %later.1 = (bf16[1,128,4096]{2,1,0:T(8,128)(2,1)}, f32[128,4096]{1,0:T(8,128)S(1)}) custom-call(s32[1]{0:T(128)S(6)} %copy.31.refs_0_, f32[256,128]{1,0:T(8,128)S(1)} %get-tuple-element.22.refs_1_, bf16[128,1792]{1,0:T(8,128)(2,1)S(1)} %collective-permute-done.2.refs_2_, bf16[128,1792]{1,0:T(8,128)(2,1)S(1)} %hold.5.refs_6_.refs_3_, ...), custom_call_target="tpu_custom_call" | custom-call | flops 20000000000 | bytes 1024 | tf_op jit(solution)/shard_map/later/pallas_call | solution.py:366
  27.3 0.0 collective-permute-done.10.refs_2_.refs_3_
  27.3 0.0 collective-permute-done.11.refs_1_
  27.3 0.8 %finish.5.refs_9_ = bf16[1,128,4096]{2,1,0:T(8,128)(2,1)} custom-call(f32[128,4096]{1,0:T(8,128)S(1)} %get-tuple-element.26.refs_0_.refs_7_, bf16[128,1024]{1,0:T(8,128)(2,1)S(1)} %collective-permute-done.11.refs_1_, bf16[136,768]{1,0:T(8,128)(2,1)S(1)} %collective-permute-done.10.refs_2_.refs_3_, ...), custom_call_target="tpu_custom_call", output_to_operand_aliasing={{}: (3, {})} | custom-call | flops 20000000000 | bytes 1024 | tf_op jit(solution)/shard_map/finish/pallas_call | solution.py:449
  28.2 0.0 collective-permute-done.9.refs_2_
  28.2 1.1 %raw.1.refs_2_ = bf16[1,128,4096]{2,1,0:T(8,128)(2,1)} custom-call(s32[1]{0:T(128)S(6)} %copy.31.refs_0_, f32[256,128]{1,0:T(8,128)S(1)} %get-tuple-element.22.refs_1_, bf16[32,128]{1,0:T(8,128)(2,1)S(1)} %collective-permute-done.9.refs_2_, bf16[136,768]{1,0:T(8,128)(2,1)S(1)} %collective-permute-done.10.refs_2_.refs_3_, ...), custom_call_target="tpu_custom_call", output_to_operand_aliasing={{}: (9, {})} | custom-call | flops 20000000000 | bytes 1024 | tf_op jit(solution)/shard_map/raw/pallas_call | solution.py:414
  29.3 0.3 collective-permute-done.8.refs_1_
  29.6 0.8 %finish.6.refs_2_ = bf16[1,128,4096]{2,1,0:T(8,128)(2,1)} custom-call(f32[128,4096]{1,0:T(8,128)S(1)} %get-tuple-element.26.refs_0_.refs_7_, bf16[128,1280]{1,0:T(8,128)(2,1)S(1)} %collective-permute-done.8.refs_1_, bf16[1,128,4096]{2,1,0:T(8,128)(2,1)} %raw.1.refs_2_), custom_call_target="tpu_custom_call", output_to_operand_aliasing={{}: (2, {})} | custom-call | flops 20000000000 | bytes 1024 | tf_op jit(solution)/shard_map/finish/pallas_call | solution.py:449
  30.4 1.0 %collective-permute-done.7.refs_1_ = bf16[128,640]{1,0:T(8,128)(2,1)S(1)} collective-permute-done((bf16[128,640]{1,0:T(8,128)(2,1)S(1)}, bf16[128,640]{1,0:T(8,128)(2,1)S(1)}, u32[]{:S(2)}, u32[]{:S(2)}) %collective-permute-start.7) | collective-permute-done | bytes 163872 | tf_op jit(solution)/shard_map/ppermute | solution.py:43
  31.4 0.7 %finish.7 = bf16[1,128,4096]{2,1,0:T(8,128)(2,1)} custom-call(f32[128,4096]{1,0:T(8,128)S(1)} %get-tuple-element.26.refs_0_.refs_7_, bf16[128,640]{1,0:T(8,128)(2,1)S(1)} %collective-permute-done.7.refs_1_, bf16[1,128,4096]{2,1,0:T(8,128)(2,1)} %finish.6.refs_2_), custom_call_target="tpu_custom_call", output_to_operand_aliasing={{}: (2, {})} | custom-call | flops 20000000000 | bytes 1024 | tf_op jit(solution)/shard_map/finish/pallas_call | solution.py:449
  (13 shorter events, 0.2 us)
Async XLA Ops:
  0.0 2.3 %copy-start.2 = (bf16[1,256,128]{2,1,0:T(8,128)(2,1)S(1)}, bf16[1,256,128]{2,1,0:T(8,128)(2,1)}, u32[]{:S(2)}) copy-start(bf16[1,256,128]{2,1,0:T(8,128)(2,1)} %refs_3_.3) | copy-start | bytes 196612
  0.0 2.3 %copy-start.3 = (f32[1,256]{1,0:T(1,128)S(1)}, f32[1,256]{1,0:T(1,128)}, u32[]{:S(2)}) copy-start(f32[1,256]{1,0:T(1,128)} %refs_4_.11) | copy-start | bytes 3076
  0.0 2.3 %copy-start.4 = (s32[1,256]{1,0:T(1,128)S(1)}, s32[1,256]{1,0:T(1,128)}, u32[]{:S(2)}) copy-start(s32[1,256]{1,0:T(1,128)} %refs_5_.9) | copy-start | bytes 3076
  0.1 4.6 %copy-start = (bf16[1,128,4096]{2,1,0:T(8,128)(2,1)S(1)}, bf16[1,128,4096]{2,1,0:T(8,128)(2,1)}, u32[]{:S(2)}) copy-start(bf16[1,128,4096]{2,1,0:T(8,128)(2,1)} %refs_8_.2) | copy-start | bytes 3145732
  0.1 4.6 %copy-start.1 = (bf16[128,4096]{1,0:T(8,128)(2,1)S(1)}, bf16[128,4096]{1,0:T(8,128)(2,1)}, u32[]{:S(2)}) copy-start(bf16[128,4096]{1,0:T(8,128)(2,1)} %refs_8_.3) | copy-start | bytes 3145732
  0.1 4.5 %collective-permute-start.1 = (bf16[128,3712]{1,0:T(8,128)(2,1)S(1)}, bf16[128,3712]{1,0:T(8,128)(2,1)S(1)}, u32[]{:S(2)}, u32[]{:S(2)}) collective-permute-start(bf16[128,3712]{1,0:T(8,128)(2,1)S(1)} %get-tuple-element.18.refs_5_.refs_3_), channel_id=1, source_target_pairs={{0,4},{8,12},{16,20},{24,28},{2,6},{10,14},{18,22},{26,30}} | collective-permute-start | bytes 2850824 | tf_op jit(solution)/shard_map/ppermute | solution.py:37
  1.0 8.9 %collective-permute-start = (bf16[256,384]{1,0:T(8,128)(2,1)S(1)}, bf16[256,384]{1,0:T(8,128)(2,1)S(1)}, u32[]{:S(2)}, u32[]{:S(2)}) collective-permute-start(bf16[256,384]{1,0:T(8,128)(2,1)S(1)} %get-tuple-element.17.refs_0_), channel_id=1, source_target_pairs={{0,1},{4,5},{8,9},{12,13},{16,17},{20,21},{24,25},{28,29},{2,3},{6... | collective-permute-start | bytes 589832 | tf_op jit(solution)/shard_map/ppermute | solution.py:43
  4.7 10.7 %collective-permute-start.5 = (bf16[128,1536]{1,0:T(8,128)(2,1)S(1)}, bf16[128,1536]{1,0:T(8,128)(2,1)S(1)}, u32[]{:S(2)}, u32[]{:S(2)}) collective-permute-start(bf16[128,1536]{1,0:T(8,128)(2,1)S(1)} %own.6._.refs_9_), channel_id=1, source_target_pairs={{4,5},{12,13},{20,21},{28,29},{6,7},{14,15},{22,23},{30,31}} | collective-permute-start | bytes 1179656 | tf_op jit(solution)/shard_map/ppermute | solution.py:43
  5.4 10.0 %collective-permute-start.2 = (bf16[128,1792]{1,0:T(8,128)(2,1)S(1)}, bf16[128,1792]{1,0:T(8,128)(2,1)S(1)}, u32[]{:S(2)}, u32[]{:S(2)}) collective-permute-start(bf16[128,1792]{1,0:T(8,128)(2,1)S(1)} %hold.5.refs_6_.refs_3_), channel_id=1, source_target_pairs={{4,8},{12,16},{20,24},{1,5},{9,13},{17,21},{25,29},{5,9},{13,17},{... | collective-permute-start | bytes 1376264 | tf_op jit(solution)/shard_map/ppermute | solution.py:37
  7.8 12.7 %collective-permute-start.6 = (bf16[128,2176]{1,0:T(8,128)(2,1)S(1)}, bf16[128,2176]{1,0:T(8,128)(2,1)S(1)}, u32[]{:S(2)}, u32[]{:S(2)}) collective-permute-start(bf16[128,2176]{1,0:T(8,128)(2,1)S(1)} %own.7.refs_7_.refs_10_), channel_id=1, source_target_pairs={{4,5},{12,13},{20,21},{28,29},{6,7},{14,15},{22,23},{30,31}} | collective-permute-start | bytes 1671176 | tf_op jit(solution)/shard_map/ppermute | solution.py:43
  9.9 10.6 %collective-permute-start.3 = (bf16[128,1920]{1,0:T(8,128)(2,1)S(1)}, bf16[128,1920]{1,0:T(8,128)(2,1)S(1)}, u32[]{:S(2)}, u32[]{:S(2)}) collective-permute-start(bf16[128,1920]{1,0:T(8,128)(2,1)S(1)} %hold.6._.refs_5_), channel_id=1, source_target_pairs={{4,8},{12,16},{20,24},{1,5},{9,13},{17,21},{25,29},{5,9},{13,17},{... | collective-permute-start | bytes 1474568 | tf_op jit(solution)/shard_map/ppermute | solution.py:37
  12.4 10.2 %collective-permute-start.4 = (bf16[128,768]{1,0:T(8,128)(2,1)S(1)}, bf16[128,768]{1,0:T(8,128)(2,1)S(1)}, u32[]{:S(2)}, u32[]{:S(2)}) collective-permute-start(bf16[128,768]{1,0:T(8,128)(2,1)S(1)} %hold.7.refs_5_), channel_id=1, source_target_pairs={{0,4},{8,12},{16,20},{24,28},{4,8},{12,16},{20,24},{1,5},{9,13},{1... | collective-permute-start | bytes 589832 | tf_op jit(solution)/shard_map/ppermute | solution.py:37
  15.5 11.8 %collective-permute-start.11 = (bf16[128,1024]{1,0:T(8,128)(2,1)S(1)}, bf16[128,1024]{1,0:T(8,128)(2,1)S(1)}, u32[]{:S(2)}, u32[]{:S(2)}) collective-permute-start(bf16[128,1024]{1,0:T(8,128)(2,1)S(1)} %own.8.refs_6_.refs_11_), channel_id=1, source_target_pairs={{0,1},{8,9},{16,17},{24,25},{2,3},{10,11},{18,19},{26,27}} | collective-permute-start | bytes 786440 | tf_op jit(solution)/shard_map/ppermute | solution.py:43
  16.8 10.5 %collective-permute-start.10 = (bf16[136,768]{1,0:T(8,128)(2,1)S(1)}, bf16[136,768]{1,0:T(8,128)(2,1)S(1)}, u32[]{:S(2)}, u32[]{:S(2)}) collective-permute-start(bf16[136,768]{1,0:T(8,128)(2,1)S(1)} %own.9.refs_6_.refs_12_), channel_id=1, source_target_pairs={{0,1},{8,9},{16,17},{24,25},{2,3},{10,11},{18,19},{26,27}} | collective-permute-start | bytes 626696 | tf_op jit(solution)/shard_map/ppermute | solution.py:43
  20.5 9.1 %collective-permute-start.8 = (bf16[128,1280]{1,0:T(8,128)(2,1)S(1)}, bf16[128,1280]{1,0:T(8,128)(2,1)S(1)}, u32[]{:S(2)}, u32[]{:S(2)}) collective-permute-start(bf16[128,1280]{1,0:T(8,128)(2,1)S(1)} %own.10.refs_6_.refs_13_), channel_id=1, source_target_pairs={{0,1},{8,9},{16,17},{24,25},{2,3},{10,11},{18,19},{26,27}} | collective-permute-start | bytes 983048 | tf_op jit(solution)/shard_map/ppermute | solution.py:43
  22.6 8.8 %collective-permute-start.7 = (bf16[128,640]{1,0:T(8,128)(2,1)S(1)}, bf16[128,640]{1,0:T(8,128)(2,1)S(1)}, u32[]{:S(2)}, u32[]{:S(2)}) collective-permute-start(bf16[128,640]{1,0:T(8,128)(2,1)S(1)} %own.11.refs_14_._), channel_id=1, source_target_pairs={{0,1},{8,9},{16,17},{24,25},{2,3},{10,11},{18,19},{26,27}} | collective-permute-start | bytes 491528 | tf_op jit(solution)/shard_map/ppermute | solution.py:43
  23.9 4.3 %collective-permute-start.9 = (bf16[32,128]{1,0:T(8,128)(2,1)S(1)}, bf16[32,128]{1,0:T(8,128)(2,1)S(1)}, u32[]{:S(2)}, u32[]{:S(2)}) collective-permute-start(bf16[32,128]{1,0:T(8,128)(2,1)S(1)} %hold.9), channel_id=1, source_target_pairs={{4,5},{12,13},{20,21},{28,29},{6,7},{14,15},{22,23},{30,31}} | collective-permute-start | bytes 24584 | tf_op jit(solution)/shard_map/ppermute | solution.py:43

commit v18 on v16

--- a/solution.py
+++ b/solution.py
@@ -12,8 +12,7 @@
 RAW = 384
 ODD = (1536, 2176)
 EVEN = (1024, 896, 1280, 512)
-PIECES = 4
-LINES = 8
+PIECES = 8
 NEAR = 1920
 F32 = jnp.float32
 BF16 = jnp.bfloat16
@@ -151,7 +150,7 @@
 
 def product_kernel(*refs):
     keys_ref, values_ref, bank_ref, scales_ref, assign_ref, rest_ref = refs[:6]
-    lines_ref, wire_ref, near_ref, far_ref, tail_ref, keys_in, values_in, sems = refs[6:]
+    lines_ref, near_ref, far_ref, tail_ref, keys_in, values_in, sems = refs[6:]
 
     def taps():
         fill_lines(bank_ref[0], scales_ref[...], assign_ref[...], lines_ref)
@@ -159,7 +158,6 @@
     @pl.when(jnp.logical_and(is_first(), is_slab(1)))
     def _():
         taps()
-        wire_ref[...] = lines_ref[: wire_ref.shape[0], :].astype(BF16)
         near_ref[...] = rest_ref[:, :NEAR]
         far_ref[...] = rest_ref[:, NEAR:]
 
@@ -180,13 +178,12 @@
         "product",
         (
             array(groups, taps, F32),
-            array(wire_rows(groups, total), taps),
             array(rows, NEAR),
             array(rows, total - RAW - NEAR),
             array(rows, RAW),
         ),
         [HBM, HBM] + [VMEM] * 4,
-        (VMEM,) * 5,
+        (VMEM,) * 4,
         product_scratch(rows, total),
     )(keys, values, bank, scales, assign, rest)
 
@@ -226,7 +223,7 @@
     return LANES * lines_ref.shape[0] // total
 
 
-def own_kernel(odd, first, shift, local, extra, *refs):
+def own_kernel(odd, first, shift, local, *refs):
     start_ref, lines_ref, behind_ref, product_ref, queries_ref, residual_ref = refs[:6]
     out_ref, table_ref = refs[-2:]
     width = out_ref.shape[1]
@@ -242,11 +239,6 @@
         line = first // LANES * share
         at = (shift, local)
         mix_all(width, share, lines_ref, line, table_ref, start_ref, behind_ref, product_ref, at, store)
-        if extra:
-            rows = out_ref.shape[0] - extra
-            for part in range(RAW // LANES):
-                taken = lines_ref[part * extra : (part + 1) * extra, :].astype(BF16)
-                out_ref[rows:, part * LANES : (part + 1) * LANES] = taken
 
 
 def table_scratch(lines, width, total):
@@ -254,12 +246,12 @@
     return pltpu.VMEM((width * groups // total * ROW_BLOCK, taps + ROW_BLOCK), BF16)
 
 
-def own_of(odd, origin, extra, start, lines, behind, product, queries, residual, first, width, *after):
+def own_of(odd, origin, start, lines, behind, product, queries, residual, first, width, *after):
     rows, total = residual.shape
     return call(
-        functools.partial(own_kernel, odd, first, first - origin, first - RAW, extra),
+        functools.partial(own_kernel, odd, first, first - origin, first - RAW),
         "own",
-        array(rows + extra, width),
+        array(rows, width),
         [SMEM] + [VMEM] * 5 + [ANY] * len(after),
         VMEM,
         [table_scratch(lines, width, total)],
@@ -268,12 +260,16 @@
 
 def pick_kernel(*refs):
     raw_ref, received_ref, tail_ref, bank_ref, scales_ref, assign_ref = refs[:6]
-    queries_ref, product_ref, lines_ref = refs[8:]
+    queries_ref, product_ref, lines_ref, wire_ref = refs[8:]
     rows = queries_ref.shape[0]
 
     @pl.when(jnp.logical_and(is_first(), is_slab(0)))
     def _():
         fill_lines(bank_ref[0], scales_ref[...], assign_ref[...], lines_ref)
+
+    @pl.when(is_first())
+    def _():
+        wire_ref[...] = lines_ref[: wire_ref.shape[0], :].astype(BF16)
 
     def take(source):
         queries_ref[...] = source[:rows, :]
@@ -287,14 +283,20 @@
         product_ref[:, RAW:] = tail_ref[...]
 
 
-def pick_of(raw, received, tail, bank, scales, assign, lines, after):
+def pick_of(raw, received, tail, bank, scales, assign, lines, total, after):
     rows, width = raw.shape[0] // 2, raw.shape[1]
+    groups, taps = lines.shape
     return call(
         pick_kernel,
         "pick",
-        (array(rows, width), array(rows, 2 * width), array(*lines.shape, F32)),
+        (
+            array(rows, width),
+            array(rows, 2 * width),
+            array(groups, taps, F32),
+            array(wire_rows(groups, total), taps),
+        ),
         [VMEM] * 7 + [ANY],
-        (VMEM,) * 3,
+        (VMEM,) * 4,
         weight=SLOW,
         aliases={6: 2},
     )(raw, received, tail, bank, scales, assign, lines, after)
@@ -375,25 +377,19 @@
 
 
 def raw_kernel(*refs):
-    start_ref, lines_ref, wire_ref, received_ref = refs[:4]
-    behind_ref, product_ref, queries_ref, gated_ref, residual_ref = refs[4:9]
-    out_ref, chosen_ref, table_ref, buffer, sems = refs[10:]
-    rows, width = buffer.shape
+    start_ref, lines_ref, wire_ref = refs[:3]
+    behind_ref, product_ref, queries_ref, gated_ref, residual_ref = refs[3:8]
+    out_ref, chosen_ref, table_ref, buffer, sems = refs[9:]
+    width = buffer.shape[1]
     share = share_of(lines_ref, residual_ref.shape[1])
 
     @pl.when(is_first())
     def _():
         chosen_ref[...] = lines_ref[: chosen_ref.shape[0], :]
 
-    @pl.when(jnp.logical_and(jnp.logical_not(is_first()), is_slab(1)))
+    @pl.when(jnp.logical_not(is_first()))
     def _():
         chosen_ref[...] = wire_ref[...].astype(F32)
-
-    @pl.when(jnp.logical_and(jnp.logical_not(is_first()), is_slab(0)))
-    def _():
-        for part in range(RAW // LANES):
-            taken = received_ref[rows:, part * LANES : (part + 1) * LANES]
-            chosen_ref[part * LINES : (part + 1) * LINES, :] = taken.astype(F32)
 
     def store(at, span, mixed):
         gated = queries_ref[span, at].astype(F32) * mixed
@@ -408,14 +404,14 @@
     wait_all(send_out([(buffer, 0)], out_ref, sems))
 
 
-def raw_finish(held, start, lines, wire, received, behind, product, queries, gated, residual):
+def raw_finish(held, start, lines, wire, behind, product, queries, gated, residual):
     rows, width = queries.shape
     total = residual.shape[1]
     return call(
         raw_kernel,
         "raw",
         jax.ShapeDtypeStruct(held.shape, BF16),
-        [SMEM] + [VMEM] * 8 + [ANY],
+        [SMEM] + [VMEM] * 7 + [ANY],
         ANY,
         [
             pltpu.VMEM(wire.shape, F32),
@@ -424,8 +420,8 @@
             pltpu.SemaphoreType.DMA((1,)),
         ],
         weight=SLOW,
-        aliases={9: 0},
-    )(start, lines, wire, received, behind, product, queries, gated, residual, held)
+        aliases={8: 0},
+    )(start, lines, wire, behind, product, queries, gated, residual, held)
 
 
 def finish_kernel(odd, places, *refs):
@@ -467,12 +463,12 @@
     raw, rest = lead_of(far_queries, keys, values)
     raw_received = to_next_section(raw)
     chip_behind = to_next_slab(rest, (0, 0))
-    lines, wire, near, far, tail = product_of(keys, values, *small, rest)
+    lines, near, far, tail = product_of(keys, values, *small, rest)
     own, received, places = [], [], []
 
-    def send(odd, behind, origin, first, width, *after, extra=0):
+    def send(odd, behind, origin, first, width, *after):
         piece = own_of(
-            odd, origin, extra, context_start, lines, behind, rest, queries, residual, first, width, *after
+            odd, origin, context_start, lines, behind, rest, queries, residual, first, width, *after
         )
         own.append(piece)
         received.append(to_next_section(piece, (odd,)))
@@ -484,18 +480,19 @@
     near = held_back(near, after)
     near_behind = to_next_slab(near, *links)
     first, after = send(1, chip_behind, RAW, first, ODD[1], near)
-    raw_queries, raw_product, lines = pick_of(raw, raw_received, tail, *small, lines, after)
+    raw_queries, raw_product, lines, wire = pick_of(raw, raw_received, tail, *small, lines, total, after)
     far = held_back(far, raw_queries)
     far_behind = to_next_slab(far, *links)
     raw_product = held_back(raw_product, far)
     raw_behind = to_next_slab(raw_product, (0, 0), *links)
     raw_queries = held_back(raw_queries, received[0], SLOW)
     first, after = send(0, near_behind, RAW, RAW, EVEN[0], raw_queries)
-    first, after = send(0, near_behind, RAW, first, EVEN[1], after, extra=LINES)
+    first, after = send(0, near_behind, RAW, first, EVEN[1], after)
     origin = first
     first, after = send(0, far_behind, origin, first, EVEN[2], after, received[1])
-    first, after = send(0, far_behind, origin, first, EVEN[3], after, raw_behind)
-    wire_received = to_next_section(held_back(wire, after), (1,))
+    wire = held_back(wire, after)
+    wire_received = to_next_section(wire)
+    first, after = send(0, far_behind, origin, first, EVEN[3], wire, raw_behind)
     held, gated = later_of(
         context_start,
         lines,
@@ -517,7 +514,6 @@
         context_start,
         lines,
         wire_received,
-        received[odd + 1],
         raw_behind,
         raw_product,
         raw_queries,

time: 32.5 us -> 33.2 us (1.022)
  starting transfers between devices: 17.2 us -> 17.8 us
    ppermute x4, waiting for transfers between devices: 3.23 us -> 2.5 us  [to_next_slab(): return lax.ppermute(value, ('ctx', 'pipe'), pairs)]
    ppermute x8, starting transfers between devices: 8.47 us -> 9.11 us  [to_next_section(): return lax.ppermute(value, ('ctx', 'pipe'), pairs)]
    ppermute x8, waiting for transfers between devices: 2.63 us -> 3.18 us  [to_next_section(): return lax.ppermute(value, ('ctx', 'pipe'), pairs)]
  transfers between devices with their start and end apart: 12 -> 12, of which waited for: 6 -> 4; matrix products, arithmetic and copies ran while one was open for 0% -> 0% of each run, Pallas kernels for 23% -> 23%
where the time goes in v18:
time: 33.2 us; the launch traced here: 32.8 us
  starting transfers between devices  17.8 us (54%)
  Pallas kernels  8.33 us (25%)
  waiting for transfers between devices  5.67 us (17%)
  between operations  0.99 us (3%)
    ppermute x8, starting transfers between devices, to_next_section(): return lax.ppermute(value, ('ctx', 'pipe'), pairs)  9.11 us
    ppermute x4, starting transfers between devices, to_next_slab(): return lax.ppermute(value, ('ctx', 'pipe'), pairs)  8.71 us
    ppermute x8, waiting for transfers between devices, to_next_section(): return lax.ppermute(value, ('ctx', 'pipe'), pairs)  3.18 us
    pallas_call x1, Pallas kernels, later_of(): call(functools.partial(later_kernel, places), 'later', (jax.ShapeDtypeStr...  2.7 us
    ppermute x4, waiting for transfers between devices, to_next_slab(): return lax.ppermute(value, ('ctx', 'pipe'), pairs)  2.5 us
    pallas_call x4, Pallas kernels, finish(): call(functools.partial(finish_kernel, places[0][0], places), 'finish', ja...  2.41 us
    pallas_call x1, Pallas kernels, product_of(): call(product_kernel, 'product', (array(groups, taps, F32), array(rows, NE...  1.8 us
    pallas_call x1, Pallas kernels, raw_finish(): call(raw_kernel, 'raw', jax.ShapeDtypeStruct(held.shape, BF16), [SMEM] +...  1.12 us
  transfers between devices with their start and end apart: 12, of which 4 were waited for; matrix products, arithmetic and copies ran while one was open for 0% of the time, Pallas kernels for 23%

profile of v18, /device:TPU:12, one launch (start us, length us, event | category | flops | bytes accessed | tf_op | source)
XLA Modules:
  0.0 32.8 jit_solution(6733416979272676992)
XLA Ops:
  0.0 0.0 copy-start.2
  0.0 0.0 copy-start.3
  0.0 0.0 copy-start.4
  0.0 0.2 lead.1
  0.2 0.0 copy-start
  0.2 0.0 copy-start.1
  0.2 0.9 %collective-permute-start.1 = (bf16[128,3712]{1,0:T(8,128)(2,1)S(1)}, bf16[128,3712]{1,0:T(8,128)(2,1)S(1)}, u32[]{:S(2)}, u32[]{:S(2)}) collective-permute-start(bf16[128,3712]{1,0:T(8,128)(2,1)S(1)} %get-tuple-element.18.refs_5_.refs_3_), channel_id=1, source_target_pairs={{0,4},{8,12},{16,20},{24,28},{2,6},{10,14},{18,22},{26,30}} | collective-permute-start | bytes 2850824 | tf_op jit(solution)/shard_map/ppermute | solution.py:36
  1.1 1.3 %collective-permute-start = (bf16[256,384]{1,0:T(8,128)(2,1)S(1)}, bf16[256,384]{1,0:T(8,128)(2,1)S(1)}, u32[]{:S(2)}, u32[]{:S(2)}) collective-permute-start(bf16[256,384]{1,0:T(8,128)(2,1)S(1)} %get-tuple-element.17.refs_0_), channel_id=1, source_target_pairs={{0,1},{4,5},{8,9},{12,13},{16,17},{20,21},{24,25},{28,29},{2,3},{6... | collective-permute-start | bytes 589832 | tf_op jit(solution)/shard_map/ppermute | solution.py:42
  2.4 0.0 copy-done.2
  2.4 0.0 copy-done.3
  2.4 0.0 copy-done.4
  2.4 1.8 %product.1 = (f32[256,128]{1,0:T(8,128)S(1)}, bf16[128,1920]{1,0:T(8,128)(2,1)S(1)}, bf16[128,1792]{1,0:T(8,128)(2,1)S(1)}, bf16[128,384]{1,0:T(8,128)(2,1)S(1)}) custom-call(bf16[1,128,4096]{2,1,0:T(8,128)(2,1)} %refs_0_.9, bf16[1,128,4096]{2,1,0:T(8,128)(2,1)} %refs_1_.1, bf16[1,256,128]{2,1,0:T(8,128)(2,1)S(1)} %copy-done.2, f32[1,256]{1,0:T(1,128)S(1)} %copy-done.3, ...), custom_call_target="tpu_custom_call" | custom-call | flops 1024 | bytes 1024 | tf_op jit(solution)/shard_map/product/pallas_call | solution.py:176
  4.9 0.0 collective-permute-done.1.refs_2_
  4.9 0.0 copy-done
  4.9 0.0 copy-done.1
  4.9 0.7 %collective-permute-start.5 = (bf16[128,1536]{1,0:T(8,128)(2,1)S(1)}, bf16[128,1536]{1,0:T(8,128)(2,1)S(1)}, u32[]{:S(2)}, u32[]{:S(2)}) collective-permute-start(bf16[128,1536]{1,0:T(8,128)(2,1)S(1)} %own.6._.refs_9_), channel_id=1, source_target_pairs={{4,5},{12,13},{20,21},{28,29},{6,7},{14,15},{22,23},{30,31}} | collective-permute-start | bytes 1179656 | tf_op jit(solution)/shard_map/ppermute | solution.py:42
  5.6 2.3 %collective-permute-start.2 = (bf16[128,1920]{1,0:T(8,128)(2,1)S(1)}, bf16[128,1920]{1,0:T(8,128)(2,1)S(1)}, u32[]{:S(2)}, u32[]{:S(2)}) collective-permute-start(bf16[128,1920]{1,0:T(8,128)(2,1)S(1)} %hold.5.refs_6_.refs_3_), channel_id=1, source_target_pairs={{4,8},{12,16},{20,24},{1,5},{9,13},{17,21},{25,29},{5,9},{13,17},{... | collective-permute-start | bytes 1474568 | tf_op jit(solution)/shard_map/ppermute | solution.py:36
  8.0 0.7 %collective-permute-start.6 = (bf16[128,2176]{1,0:T(8,128)(2,1)S(1)}, bf16[128,2176]{1,0:T(8,128)(2,1)S(1)}, u32[]{:S(2)}, u32[]{:S(2)}) collective-permute-start(bf16[128,2176]{1,0:T(8,128)(2,1)S(1)} %own.7.refs_7_.refs_10_), channel_id=1, source_target_pairs={{4,5},{12,13},{20,21},{28,29},{6,7},{14,15},{22,23},{30,31}} | collective-permute-start | bytes 1671176 | tf_op jit(solution)/shard_map/ppermute | solution.py:42
  8.7 1.3 %collective-permute-done.refs_1_ = bf16[256,384]{1,0:T(8,128)(2,1)S(1)} collective-permute-done((bf16[256,384]{1,0:T(8,128)(2,1)S(1)}, bf16[256,384]{1,0:T(8,128)(2,1)S(1)}, u32[]{:S(2)}, u32[]{:S(2)}) %collective-permute-start) | collective-permute-done | bytes 196640 | tf_op jit(solution)/shard_map/ppermute | solution.py:42
  10.0 2.5 %collective-permute-start.3 = (bf16[128,1792]{1,0:T(8,128)(2,1)S(1)}, bf16[128,1792]{1,0:T(8,128)(2,1)S(1)}, u32[]{:S(2)}, u32[]{:S(2)}) collective-permute-start(bf16[128,1792]{1,0:T(8,128)(2,1)S(1)} %hold.6._.refs_5_), channel_id=1, source_target_pairs={{4,8},{12,16},{20,24},{1,5},{9,13},{17,21},{25,29},{5,9},{13,17},{... | collective-permute-start | bytes 1376264 | tf_op jit(solution)/shard_map/ppermute | solution.py:36
  12.6 3.0 %collective-permute-start.4 = (bf16[128,768]{1,0:T(8,128)(2,1)S(1)}, bf16[128,768]{1,0:T(8,128)(2,1)S(1)}, u32[]{:S(2)}, u32[]{:S(2)}) collective-permute-start(bf16[128,768]{1,0:T(8,128)(2,1)S(1)} %hold.7.refs_4_), channel_id=1, source_target_pairs={{0,4},{8,12},{16,20},{24,28},{4,8},{12,16},{20,24},{1,5},{9,13},{1... | collective-permute-start | bytes 589832 | tf_op jit(solution)/shard_map/ppermute | solution.py:36
  15.6 0.0 collective-permute-done.5._.refs_1_
  15.6 0.2 collective-permute-done.2.refs_2_
  15.8 1.3 %collective-permute-start.10 = (bf16[128,1024]{1,0:T(8,128)(2,1)S(1)}, bf16[128,1024]{1,0:T(8,128)(2,1)S(1)}, u32[]{:S(2)}, u32[]{:S(2)}) collective-permute-start(bf16[128,1024]{1,0:T(8,128)(2,1)S(1)} %own.8.refs_6_.refs_11_), channel_id=1, source_target_pairs={{0,1},{8,9},{16,17},{24,25},{2,3},{10,11},{18,19},{26,27}} | collective-permute-start | bytes 786440 | tf_op jit(solution)/shard_map/ppermute | solution.py:42
  17.1 1.3 %collective-permute-start.11 = (bf16[128,896]{1,0:T(8,128)(2,1)S(1)}, bf16[128,896]{1,0:T(8,128)(2,1)S(1)}, u32[]{:S(2)}, u32[]{:S(2)}) collective-permute-start(bf16[128,896]{1,0:T(8,128)(2,1)S(1)} %own.9.refs_6_.refs_12_), channel_id=1, source_target_pairs={{0,1},{8,9},{16,17},{24,25},{2,3},{10,11},{18,19},{26,27}} | collective-permute-start | bytes 688136 | tf_op jit(solution)/shard_map/ppermute | solution.py:42
  18.4 2.3 %collective-permute-done.3.refs_2_.refs_4_ = bf16[128,1792]{1,0:T(8,128)(2,1)S(1)} collective-permute-done((bf16[128,1792]{1,0:T(8,128)(2,1)S(1)}, bf16[128,1792]{1,0:T(8,128)(2,1)S(1)}, u32[]{:S(2)}, u32[]{:S(2)}) %collective-permute-start.3) | collective-permute-done | bytes 458784 | tf_op jit(solution)/shard_map/ppermute | solution.py:36
  20.7 0.0 collective-permute-done.6.refs_7_.refs_2_
  20.7 1.3 %collective-permute-start.8 = (bf16[128,1280]{1,0:T(8,128)(2,1)S(1)}, bf16[128,1280]{1,0:T(8,128)(2,1)S(1)}, u32[]{:S(2)}, u32[]{:S(2)}) collective-permute-start(bf16[128,1280]{1,0:T(8,128)(2,1)S(1)} %own.10._.refs_13_), channel_id=1, source_target_pairs={{0,1},{8,9},{16,17},{24,25},{2,3},{10,11},{18,19},{26,27}} | collective-permute-start | bytes 983048 | tf_op jit(solution)/shard_map/ppermute | solution.py:42
  22.0 1.3 %collective-permute-start.9 = (bf16[32,128]{1,0:T(8,128)(2,1)S(1)}, bf16[32,128]{1,0:T(8,128)(2,1)S(1)}, u32[]{:S(2)}, u32[]{:S(2)}) collective-permute-start(bf16[32,128]{1,0:T(8,128)(2,1)S(1)} %hold.9.refs_6_), channel_id=1, source_target_pairs={{0,1},{4,5},{8,9},{12,13},{16,17},{20,21},{24,25},{28,29},{2,3},{6... | collective-permute-start | bytes 24584 | tf_op jit(solution)/shard_map/ppermute | solution.py:42
  23.3 0.0 collective-permute-done.4.refs_7_.refs_6_.refs_3_
  23.3 1.3 %collective-permute-start.7 = (bf16[128,512]{1,0:T(8,128)(2,1)S(1)}, bf16[128,512]{1,0:T(8,128)(2,1)S(1)}, u32[]{:S(2)}, u32[]{:S(2)}) collective-permute-start(bf16[128,512]{1,0:T(8,128)(2,1)S(1)} %own.11.refs_14_), channel_id=1, source_target_pairs={{0,1},{8,9},{16,17},{24,25},{2,3},{10,11},{18,19},{26,27}} | collective-permute-start | bytes 393224 | tf_op jit(solution)/shard_map/ppermute | solution.py:42
  24.6 2.7 %later.1 = (bf16[1,128,4096]{2,1,0:T(8,128)(2,1)}, f32[128,4096]{1,0:T(8,128)S(1)}) custom-call(s32[1]{0:T(128)S(6)} %copy.31.refs_0_, f32[256,128]{1,0:T(8,128)S(1)} %get-tuple-element.22.refs_1_, bf16[128,1920]{1,0:T(8,128)(2,1)S(1)} %collective-permute-done.2.refs_2_, bf16[128,1920]{1,0:T(8,128)(2,1)S(1)} %hold.5.refs_6_.refs_3_, ...), custom_call_target="tpu_custom_call" | custom-call | flops 20000000000 | bytes 1024 | tf_op jit(solution)/shard_map/later/pallas_call | solution.py:368
  27.4 0.0 collective-permute-done.11.refs_2_
  27.4 0.0 collective-permute-done.10.refs_1_
  27.4 0.9 %finish.5.refs_8_ = bf16[1,128,4096]{2,1,0:T(8,128)(2,1)} custom-call(f32[128,4096]{1,0:T(8,128)S(1)} %get-tuple-element.27.refs_0_.refs_6_, bf16[128,1024]{1,0:T(8,128)(2,1)S(1)} %collective-permute-done.10.refs_1_, bf16[128,896]{1,0:T(8,128)(2,1)S(1)} %collective-permute-done.11.refs_2_, ...), custom_call_target="tpu_custom_call", output_to_operand_aliasing={{}: (3, {})} | custom-call | flops 20000000000 | bytes 1024 | tf_op jit(solution)/shard_map/finish/pallas_call | solution.py:445
  28.3 1.9 %collective-permute-done.9.refs_2_ = bf16[32,128]{1,0:T(8,128)(2,1)S(1)} collective-permute-done((bf16[32,128]{1,0:T(8,128)(2,1)S(1)}, bf16[32,128]{1,0:T(8,128)(2,1)S(1)}, u32[]{:S(2)}, u32[]{:S(2)}) %collective-permute-start.9) | collective-permute-done | bytes 8224 | tf_op jit(solution)/shard_map/ppermute | solution.py:42
  30.2 1.1 %raw.1.refs_2_ = bf16[1,128,4096]{2,1,0:T(8,128)(2,1)} custom-call(s32[1]{0:T(128)S(6)} %copy.31.refs_0_, f32[256,128]{1,0:T(8,128)S(1)} %get-tuple-element.22.refs_1_, bf16[32,128]{1,0:T(8,128)(2,1)S(1)} %collective-permute-done.9.refs_2_, bf16[128,768]{1,0:T(8,128)(2,1)S(1)} %collective-permute-done.4.refs_7_.refs_6_.refs_3_, ...), custom_call_target="tpu_custom_call", output_to_operand_aliasing={{}: (8, {})} | custom-call | flops 20000000000 | bytes 1024 | tf_op jit(solution)/shard_map/raw/pallas_call | solution.py:410
  31.3 0.0 collective-permute-done.8.refs_1_
  31.3 0.8 %finish.6.refs_2_ = bf16[1,128,4096]{2,1,0:T(8,128)(2,1)} custom-call(f32[128,4096]{1,0:T(8,128)S(1)} %get-tuple-element.27.refs_0_.refs_6_, bf16[128,1280]{1,0:T(8,128)(2,1)S(1)} %collective-permute-done.8.refs_1_, bf16[1,128,4096]{2,1,0:T(8,128)(2,1)} %raw.1.refs_2_), custom_call_target="tpu_custom_call", output_to_operand_aliasing={{}: (2, {})} | custom-call | flops 20000000000 | bytes 1024 | tf_op jit(solution)/shard_map/finish/pallas_call | solution.py:445
  32.1 0.0 collective-permute-done.7.refs_1_
  32.1 0.7 %finish.7 = bf16[1,128,4096]{2,1,0:T(8,128)(2,1)} custom-call(f32[128,4096]{1,0:T(8,128)S(1)} %get-tuple-element.27.refs_0_.refs_6_, bf16[128,512]{1,0:T(8,128)(2,1)S(1)} %collective-permute-done.7.refs_1_, bf16[1,128,4096]{2,1,0:T(8,128)(2,1)} %finish.6.refs_2_), custom_call_target="tpu_custom_call", output_to_operand_aliasing={{}: (2, {})} | custom-call | flops 20000000000 | bytes 1024 | tf_op jit(solution)/shard_map/finish/pallas_call | solution.py:445
  (13 shorter events, 0.2 us)
Async XLA Ops:
  0.0 2.4 %copy-start.2 = (bf16[1,256,128]{2,1,0:T(8,128)(2,1)S(1)}, bf16[1,256,128]{2,1,0:T(8,128)(2,1)}, u32[]{:S(2)}) copy-start(bf16[1,256,128]{2,1,0:T(8,128)(2,1)} %refs_3_.3) | copy-start | bytes 196612
  0.0 2.4 %copy-start.3 = (f32[1,256]{1,0:T(1,128)S(1)}, f32[1,256]{1,0:T(1,128)}, u32[]{:S(2)}) copy-start(f32[1,256]{1,0:T(1,128)} %refs_4_.11) | copy-start | bytes 3076
  0.0 2.4 %copy-start.4 = (s32[1,256]{1,0:T(1,128)S(1)}, s32[1,256]{1,0:T(1,128)}, u32[]{:S(2)}) copy-start(s32[1,256]{1,0:T(1,128)} %refs_5_.9) | copy-start | bytes 3076
  0.2 4.7 %copy-start = (bf16[1,128,4096]{2,1,0:T(8,128)(2,1)S(1)}, bf16[1,128,4096]{2,1,0:T(8,128)(2,1)}, u32[]{:S(2)}) copy-start(bf16[1,128,4096]{2,1,0:T(8,128)(2,1)} %refs_8_.1) | copy-start | bytes 3145732
  0.2 4.7 %copy-start.1 = (bf16[128,4096]{1,0:T(8,128)(2,1)S(1)}, bf16[128,4096]{1,0:T(8,128)(2,1)}, u32[]{:S(2)}) copy-start(bf16[128,4096]{1,0:T(8,128)(2,1)} %refs_7_.1) | copy-start | bytes 3145732
  0.2 4.7 %collective-permute-start.1 = (bf16[128,3712]{1,0:T(8,128)(2,1)S(1)}, bf16[128,3712]{1,0:T(8,128)(2,1)S(1)}, u32[]{:S(2)}, u32[]{:S(2)}) collective-permute-start(bf16[128,3712]{1,0:T(8,128)(2,1)S(1)} %get-tuple-element.18.refs_5_.refs_3_), channel_id=1, source_target_pairs={{0,4},{8,12},{16,20},{24,28},{2,6},{10,14},{18,22},{26,30}} | collective-permute-start | bytes 2850824 | tf_op jit(solution)/shard_map/ppermute | solution.py:36
  1.1 8.9 %collective-permute-start = (bf16[256,384]{1,0:T(8,128)(2,1)S(1)}, bf16[256,384]{1,0:T(8,128)(2,1)S(1)}, u32[]{:S(2)}, u32[]{:S(2)}) collective-permute-start(bf16[256,384]{1,0:T(8,128)(2,1)S(1)} %get-tuple-element.17.refs_0_), channel_id=1, source_target_pairs={{0,1},{4,5},{8,9},{12,13},{16,17},{20,21},{24,25},{28,29},{2,3},{6... | collective-permute-start | bytes 589832 | tf_op jit(solution)/shard_map/ppermute | solution.py:42
  4.9 10.6 %collective-permute-start.5 = (bf16[128,1536]{1,0:T(8,128)(2,1)S(1)}, bf16[128,1536]{1,0:T(8,128)(2,1)S(1)}, u32[]{:S(2)}, u32[]{:S(2)}) collective-permute-start(bf16[128,1536]{1,0:T(8,128)(2,1)S(1)} %own.6._.refs_9_), channel_id=1, source_target_pairs={{4,5},{12,13},{20,21},{28,29},{6,7},{14,15},{22,23},{30,31}} | collective-permute-start | bytes 1179656 | tf_op jit(solution)/shard_map/ppermute | solution.py:42
  5.6 10.1 %collective-permute-start.2 = (bf16[128,1920]{1,0:T(8,128)(2,1)S(1)}, bf16[128,1920]{1,0:T(8,128)(2,1)S(1)}, u32[]{:S(2)}, u32[]{:S(2)}) collective-permute-start(bf16[128,1920]{1,0:T(8,128)(2,1)S(1)} %hold.5.refs_6_.refs_3_), channel_id=1, source_target_pairs={{4,8},{12,16},{20,24},{1,5},{9,13},{17,21},{25,29},{5,9},{13,17},{... | collective-permute-start | bytes 1474568 | tf_op jit(solution)/shard_map/ppermute | solution.py:36
  8.0 12.7 %collective-permute-start.6 = (bf16[128,2176]{1,0:T(8,128)(2,1)S(1)}, bf16[128,2176]{1,0:T(8,128)(2,1)S(1)}, u32[]{:S(2)}, u32[]{:S(2)}) collective-permute-start(bf16[128,2176]{1,0:T(8,128)(2,1)S(1)} %own.7.refs_7_.refs_10_), channel_id=1, source_target_pairs={{4,5},{12,13},{20,21},{28,29},{6,7},{14,15},{22,23},{30,31}} | collective-permute-start | bytes 1671176 | tf_op jit(solution)/shard_map/ppermute | solution.py:42
  10.0 10.7 %collective-permute-start.3 = (bf16[128,1792]{1,0:T(8,128)(2,1)S(1)}, bf16[128,1792]{1,0:T(8,128)(2,1)S(1)}, u32[]{:S(2)}, u32[]{:S(2)}) collective-permute-start(bf16[128,1792]{1,0:T(8,128)(2,1)S(1)} %hold.6._.refs_5_), channel_id=1, source_target_pairs={{4,8},{12,16},{20,24},{1,5},{9,13},{17,21},{25,29},{5,9},{13,17},{... | collective-permute-start | bytes 1376264 | tf_op jit(solution)/shard_map/ppermute | solution.py:36
  12.6 10.7 %collective-permute-start.4 = (bf16[128,768]{1,0:T(8,128)(2,1)S(1)}, bf16[128,768]{1,0:T(8,128)(2,1)S(1)}, u32[]{:S(2)}, u32[]{:S(2)}) collective-permute-start(bf16[128,768]{1,0:T(8,128)(2,1)S(1)} %hold.7.refs_4_), channel_id=1, source_target_pairs={{0,4},{8,12},{16,20},{24,28},{4,8},{12,16},{20,24},{1,5},{9,13},{1... | collective-permute-start | bytes 589832 | tf_op jit(solution)/shard_map/ppermute | solution.py:36
  15.8 11.6 %collective-permute-start.10 = (bf16[128,1024]{1,0:T(8,128)(2,1)S(1)}, bf16[128,1024]{1,0:T(8,128)(2,1)S(1)}, u32[]{:S(2)}, u32[]{:S(2)}) collective-permute-start(bf16[128,1024]{1,0:T(8,128)(2,1)S(1)} %own.8.refs_6_.refs_11_), channel_id=1, source_target_pairs={{0,1},{8,9},{16,17},{24,25},{2,3},{10,11},{18,19},{26,27}} | collective-permute-start | bytes 786440 | tf_op jit(solution)/shard_map/ppermute | solution.py:42
  17.1 10.3 %collective-permute-start.11 = (bf16[128,896]{1,0:T(8,128)(2,1)S(1)}, bf16[128,896]{1,0:T(8,128)(2,1)S(1)}, u32[]{:S(2)}, u32[]{:S(2)}) collective-permute-start(bf16[128,896]{1,0:T(8,128)(2,1)S(1)} %own.9.refs_6_.refs_12_), channel_id=1, source_target_pairs={{0,1},{8,9},{16,17},{24,25},{2,3},{10,11},{18,19},{26,27}} | collective-permute-start | bytes 688136 | tf_op jit(solution)/shard_map/ppermute | solution.py:42
  20.7 10.6 %collective-permute-start.8 = (bf16[128,1280]{1,0:T(8,128)(2,1)S(1)}, bf16[128,1280]{1,0:T(8,128)(2,1)S(1)}, u32[]{:S(2)}, u32[]{:S(2)}) collective-permute-start(bf16[128,1280]{1,0:T(8,128)(2,1)S(1)} %own.10._.refs_13_), channel_id=1, source_target_pairs={{0,1},{8,9},{16,17},{24,25},{2,3},{10,11},{18,19},{26,27}} | collective-permute-start | bytes 983048 | tf_op jit(solution)/shard_map/ppermute | solution.py:42
  22.0 8.2 %collective-permute-start.9 = (bf16[32,128]{1,0:T(8,128)(2,1)S(1)}, bf16[32,128]{1,0:T(8,128)(2,1)S(1)}, u32[]{:S(2)}, u32[]{:S(2)}) collective-permute-start(bf16[32,128]{1,0:T(8,128)(2,1)S(1)} %hold.9.refs_6_), channel_id=1, source_target_pairs={{0,1},{4,5},{8,9},{12,13},{16,17},{20,21},{24,25},{28,29},{2,3},{6... | collective-permute-start | bytes 24584 | tf_op jit(solution)/shard_map/ppermute | solution.py:42
  23.3 8.8 %collective-permute-start.7 = (bf16[128,512]{1,0:T(8,128)(2,1)S(1)}, bf16[128,512]{1,0:T(8,128)(2,1)S(1)}, u32[]{:S(2)}, u32[]{:S(2)}) collective-permute-start(bf16[128,512]{1,0:T(8,128)(2,1)S(1)} %own.11.refs_14_), channel_id=1, source_target_pairs={{0,1},{8,9},{16,17},{24,25},{2,3},{10,11},{18,19},{26,27}} | collective-permute-start | bytes 393224 | tf_op jit(solution)/shard_map/ppermute | solution.py:42

commit v19 on v16

--- a/solution.py
+++ b/solution.py
@@ -12,7 +12,7 @@
 RAW = 384
 ODD = (1536, 2176)
 EVEN = (1024, 896, 1280, 512)
-PIECES = 4
+PIECES = 2
 LINES = 8
 NEAR = 1920
 F32 = jnp.float32

time: 32.5 us -> 32.5 us (level)
  no operation moved by 1% of the time
where the time goes in v19:
time: 32.5 us; the launch traced here: 32.1 us
  starting transfers between devices  17.2 us (53%)
  Pallas kernels  8.12 us (25%)
  waiting for transfers between devices  5.86 us (18%)
  between operations  0.97 us (3%)
    ppermute x4, starting transfers between devices, to_next_slab(): return lax.ppermute(value, ('ctx', 'pipe'), pairs)  8.71 us
    ppermute x8, starting transfers between devices, to_next_section(): return lax.ppermute(value, ('ctx', 'pipe'), pairs)  8.47 us
    ppermute x4, waiting for transfers between devices, to_next_slab(): return lax.ppermute(value, ('ctx', 'pipe'), pairs)  3.19 us
    pallas_call x1, Pallas kernels, later_of(): call(functools.partial(later_kernel, places), 'later', (jax.ShapeDtypeStr...  2.7 us
    ppermute x8, waiting for transfers between devices, to_next_section(): return lax.ppermute(value, ('ctx', 'pipe'), pairs)  2.67 us
    pallas_call x4, Pallas kernels, finish(): call(functools.partial(finish_kernel, places[0][0], places), 'finish', ja...  2.38 us
    pallas_call x1, Pallas kernels, product_of(): call(product_kernel, 'product', (array(groups, taps, F32), array(wire_row...  1.72 us
    pallas_call x1, Pallas kernels, raw_finish(): call(raw_kernel, 'raw', jax.ShapeDtypeStruct(held.shape, BF16), [SMEM] +...  1.15 us
  transfers between devices with their start and end apart: 12, of which 6 were waited for; matrix products, arithmetic and copies ran while one was open for 0% of the time, Pallas kernels for 23%

profile of v19, /device:TPU:12, one launch (start us, length us, event | category | flops | bytes accessed | tf_op | source)
XLA Modules:
  0.0 32.1 jit_solution(7352971852869677306)
XLA Ops:
  0.0 0.0 copy-start.2
  0.0 0.0 copy-start.3
  0.0 0.0 copy-start.4
  0.0 0.1 lead.1
  0.1 0.0 copy-start
  0.1 0.0 copy-start.1
  0.1 0.9 %collective-permute-start.1 = (bf16[128,3712]{1,0:T(8,128)(2,1)S(1)}, bf16[128,3712]{1,0:T(8,128)(2,1)S(1)}, u32[]{:S(2)}, u32[]{:S(2)}) collective-permute-start(bf16[128,3712]{1,0:T(8,128)(2,1)S(1)} %get-tuple-element.18.refs_5_.refs_3_), channel_id=1, source_target_pairs={{0,4},{8,12},{16,20},{24,28},{2,6},{10,14},{18,22},{26,30}} | collective-permute-start | bytes 2850824 | tf_op jit(solution)/shard_map/ppermute | solution.py:37
  1.0 1.3 %collective-permute-start = (bf16[256,384]{1,0:T(8,128)(2,1)S(1)}, bf16[256,384]{1,0:T(8,128)(2,1)S(1)}, u32[]{:S(2)}, u32[]{:S(2)}) collective-permute-start(bf16[256,384]{1,0:T(8,128)(2,1)S(1)} %get-tuple-element.17.refs_0_), channel_id=1, source_target_pairs={{0,1},{4,5},{8,9},{12,13},{16,17},{20,21},{24,25},{28,29},{2,3},{6... | collective-permute-start | bytes 589832 | tf_op jit(solution)/shard_map/ppermute | solution.py:43
  2.3 0.0 copy-done.2
  2.3 0.0 copy-done.3
  2.3 0.0 copy-done.4
  2.3 1.7 %product.1 = (f32[256,128]{1,0:T(8,128)S(1)}, bf16[32,128]{1,0:T(8,128)(2,1)S(1)}, bf16[128,1920]{1,0:T(8,128)(2,1)S(1)}, bf16[128,1792]{1,0:T(8,128)(2,1)S(1)}, bf16[128,384]{1,0:T(8,128)(2,1)S(1)}) custom-call(bf16[1,128,4096]{2,1,0:T(8,128)(2,1)} %refs_0_.9, bf16[1,128,4096]{2,1,0:T(8,128)(2,1)} %refs_1_.1, bf16[1,256,128]{2,1,0:T(8,128)(2,1)S(1)} %copy-done.2, ...), custom_call_target="tpu_custom_call" | custom-call | flops 1024 | bytes 1024 | tf_op jit(solution)/shard_map/product/pallas_call | solution.py:178
  4.7 0.0 collective-permute-done.1.refs_2_
  4.7 0.0 copy-done
  4.7 0.0 copy-done.1
  4.7 0.7 %collective-permute-start.5 = (bf16[128,1536]{1,0:T(8,128)(2,1)S(1)}, bf16[128,1536]{1,0:T(8,128)(2,1)S(1)}, u32[]{:S(2)}, u32[]{:S(2)}) collective-permute-start(bf16[128,1536]{1,0:T(8,128)(2,1)S(1)} %own.6._.refs_9_), channel_id=1, source_target_pairs={{4,5},{12,13},{20,21},{28,29},{6,7},{14,15},{22,23},{30,31}} | collective-permute-start | bytes 1179656 | tf_op jit(solution)/shard_map/ppermute | solution.py:43
  5.4 2.3 %collective-permute-start.2 = (bf16[128,1920]{1,0:T(8,128)(2,1)S(1)}, bf16[128,1920]{1,0:T(8,128)(2,1)S(1)}, u32[]{:S(2)}, u32[]{:S(2)}) collective-permute-start(bf16[128,1920]{1,0:T(8,128)(2,1)S(1)} %hold.5.refs_6_.refs_3_), channel_id=1, source_target_pairs={{4,8},{12,16},{20,24},{1,5},{9,13},{17,21},{25,29},{5,9},{13,17},{... | collective-permute-start | bytes 1474568 | tf_op jit(solution)/shard_map/ppermute | solution.py:37
  7.8 0.7 %collective-permute-start.6 = (bf16[128,2176]{1,0:T(8,128)(2,1)S(1)}, bf16[128,2176]{1,0:T(8,128)(2,1)S(1)}, u32[]{:S(2)}, u32[]{:S(2)}) collective-permute-start(bf16[128,2176]{1,0:T(8,128)(2,1)S(1)} %own.7.refs_7_.refs_10_), channel_id=1, source_target_pairs={{4,5},{12,13},{20,21},{28,29},{6,7},{14,15},{22,23},{30,31}} | collective-permute-start | bytes 1671176 | tf_op jit(solution)/shard_map/ppermute | solution.py:43
  8.5 1.4 %collective-permute-done.refs_1_ = bf16[256,384]{1,0:T(8,128)(2,1)S(1)} collective-permute-done((bf16[256,384]{1,0:T(8,128)(2,1)S(1)}, bf16[256,384]{1,0:T(8,128)(2,1)S(1)}, u32[]{:S(2)}, u32[]{:S(2)}) %collective-permute-start) | collective-permute-done | bytes 196640 | tf_op jit(solution)/shard_map/ppermute | solution.py:43
  9.9 2.4 %collective-permute-start.3 = (bf16[128,1792]{1,0:T(8,128)(2,1)S(1)}, bf16[128,1792]{1,0:T(8,128)(2,1)S(1)}, u32[]{:S(2)}, u32[]{:S(2)}) collective-permute-start(bf16[128,1792]{1,0:T(8,128)(2,1)S(1)} %hold.6._.refs_5_), channel_id=1, source_target_pairs={{4,8},{12,16},{20,24},{1,5},{9,13},{17,21},{25,29},{5,9},{13,17},{... | collective-permute-start | bytes 1376264 | tf_op jit(solution)/shard_map/ppermute | solution.py:37
  12.4 3.1 %collective-permute-start.4 = (bf16[128,768]{1,0:T(8,128)(2,1)S(1)}, bf16[128,768]{1,0:T(8,128)(2,1)S(1)}, u32[]{:S(2)}, u32[]{:S(2)}) collective-permute-start(bf16[128,768]{1,0:T(8,128)(2,1)S(1)} %hold.7.refs_5_), channel_id=1, source_target_pairs={{0,4},{8,12},{16,20},{24,28},{4,8},{12,16},{20,24},{1,5},{9,13},{1... | collective-permute-start | bytes 589832 | tf_op jit(solution)/shard_map/ppermute | solution.py:37
  15.5 0.0 collective-permute-done.5._.refs_1_
  15.5 0.1 collective-permute-done.2.refs_2_
  15.6 1.3 %collective-permute-start.11 = (bf16[128,1024]{1,0:T(8,128)(2,1)S(1)}, bf16[128,1024]{1,0:T(8,128)(2,1)S(1)}, u32[]{:S(2)}, u32[]{:S(2)}) collective-permute-start(bf16[128,1024]{1,0:T(8,128)(2,1)S(1)} %own.8.refs_6_.refs_11_), channel_id=1, source_target_pairs={{0,1},{8,9},{16,17},{24,25},{2,3},{10,11},{18,19},{26,27}} | collective-permute-start | bytes 786440 | tf_op jit(solution)/shard_map/ppermute | solution.py:43
  16.9 1.3 %collective-permute-start.10 = (bf16[136,896]{1,0:T(8,128)(2,1)S(1)}, bf16[136,896]{1,0:T(8,128)(2,1)S(1)}, u32[]{:S(2)}, u32[]{:S(2)}) collective-permute-start(bf16[136,896]{1,0:T(8,128)(2,1)S(1)} %own.9.refs_6_.refs_12_), channel_id=1, source_target_pairs={{0,1},{8,9},{16,17},{24,25},{2,3},{10,11},{18,19},{26,27}} | collective-permute-start | bytes 731144 | tf_op jit(solution)/shard_map/ppermute | solution.py:43
  18.2 2.3 %collective-permute-done.3.refs_2_.refs_4_ = bf16[128,1792]{1,0:T(8,128)(2,1)S(1)} collective-permute-done((bf16[128,1792]{1,0:T(8,128)(2,1)S(1)}, bf16[128,1792]{1,0:T(8,128)(2,1)S(1)}, u32[]{:S(2)}, u32[]{:S(2)}) %collective-permute-start.3) | collective-permute-done | bytes 458784 | tf_op jit(solution)/shard_map/ppermute | solution.py:37
  20.5 0.0 collective-permute-done.6.refs_7_.refs_2_
  20.5 1.3 %collective-permute-start.8 = (bf16[128,1280]{1,0:T(8,128)(2,1)S(1)}, bf16[128,1280]{1,0:T(8,128)(2,1)S(1)}, u32[]{:S(2)}, u32[]{:S(2)}) collective-permute-start(bf16[128,1280]{1,0:T(8,128)(2,1)S(1)} %own.10.refs_6_.refs_13_), channel_id=1, source_target_pairs={{0,1},{8,9},{16,17},{24,25},{2,3},{10,11},{18,19},{26,27}} | collective-permute-start | bytes 983048 | tf_op jit(solution)/shard_map/ppermute | solution.py:43
  21.8 0.8 %collective-permute-done.4.refs_7_.refs_6_.refs_4_ = bf16[128,768]{1,0:T(8,128)(2,1)S(1)} collective-permute-done((bf16[128,768]{1,0:T(8,128)(2,1)S(1)}, bf16[128,768]{1,0:T(8,128)(2,1)S(1)}, u32[]{:S(2)}, u32[]{:S(2)}) %collective-permute-start.4) | collective-permute-done | bytes 196640 | tf_op jit(solution)/shard_map/ppermute | solution.py:37
  22.6 1.3 %collective-permute-start.7 = (bf16[128,512]{1,0:T(8,128)(2,1)S(1)}, bf16[128,512]{1,0:T(8,128)(2,1)S(1)}, u32[]{:S(2)}, u32[]{:S(2)}) collective-permute-start(bf16[128,512]{1,0:T(8,128)(2,1)S(1)} %own.11.refs_14_._), channel_id=1, source_target_pairs={{0,1},{8,9},{16,17},{24,25},{2,3},{10,11},{18,19},{26,27}} | collective-permute-start | bytes 393224 | tf_op jit(solution)/shard_map/ppermute | solution.py:43
  23.9 0.7 %collective-permute-start.9 = (bf16[32,128]{1,0:T(8,128)(2,1)S(1)}, bf16[32,128]{1,0:T(8,128)(2,1)S(1)}, u32[]{:S(2)}, u32[]{:S(2)}) collective-permute-start(bf16[32,128]{1,0:T(8,128)(2,1)S(1)} %hold.9), channel_id=1, source_target_pairs={{4,5},{12,13},{20,21},{28,29},{6,7},{14,15},{22,23},{30,31}} | collective-permute-start | bytes 24584 | tf_op jit(solution)/shard_map/ppermute | solution.py:43
  24.6 2.7 %later.1 = (bf16[1,128,4096]{2,1,0:T(8,128)(2,1)}, f32[128,4096]{1,0:T(8,128)S(1)}) custom-call(s32[1]{0:T(128)S(6)} %copy.31.refs_0_, f32[256,128]{1,0:T(8,128)S(1)} %get-tuple-element.22.refs_1_, bf16[128,1920]{1,0:T(8,128)(2,1)S(1)} %collective-permute-done.2.refs_2_, bf16[128,1920]{1,0:T(8,128)(2,1)S(1)} %hold.5.refs_6_.refs_3_, ...), custom_call_target="tpu_custom_call" | custom-call | flops 20000000000 | bytes 1024 | tf_op jit(solution)/shard_map/later/pallas_call | solution.py:366
  27.3 0.0 collective-permute-done.10.refs_2_.refs_3_
  27.3 0.0 collective-permute-done.11.refs_1_
  27.4 0.9 %finish.5.refs_9_ = bf16[1,128,4096]{2,1,0:T(8,128)(2,1)} custom-call(f32[128,4096]{1,0:T(8,128)S(1)} %get-tuple-element.26.refs_0_.refs_7_, bf16[128,1024]{1,0:T(8,128)(2,1)S(1)} %collective-permute-done.11.refs_1_, bf16[136,896]{1,0:T(8,128)(2,1)S(1)} %collective-permute-done.10.refs_2_.refs_3_, ...), custom_call_target="tpu_custom_call", output_to_operand_aliasing={{}: (3, {})} | custom-call | flops 20000000000 | bytes 1024 | tf_op jit(solution)/shard_map/finish/pallas_call | solution.py:449
  28.2 0.0 collective-permute-done.9.refs_2_
  28.2 1.1 %raw.1.refs_2_ = bf16[1,128,4096]{2,1,0:T(8,128)(2,1)} custom-call(s32[1]{0:T(128)S(6)} %copy.31.refs_0_, f32[256,128]{1,0:T(8,128)S(1)} %get-tuple-element.22.refs_1_, bf16[32,128]{1,0:T(8,128)(2,1)S(1)} %collective-permute-done.9.refs_2_, bf16[136,896]{1,0:T(8,128)(2,1)S(1)} %collective-permute-done.10.refs_2_.refs_3_, ...), custom_call_target="tpu_custom_call", output_to_operand_aliasing={{}: (9, {})} | custom-call | flops 20000000000 | bytes 1024 | tf_op jit(solution)/shard_map/raw/pallas_call | solution.py:414
  29.4 0.7 %collective-permute-done.8.refs_1_ = bf16[128,1280]{1,0:T(8,128)(2,1)S(1)} collective-permute-done((bf16[128,1280]{1,0:T(8,128)(2,1)S(1)}, bf16[128,1280]{1,0:T(8,128)(2,1)S(1)}, u32[]{:S(2)}, u32[]{:S(2)}) %collective-permute-start.8) | collective-permute-done | bytes 327712 | tf_op jit(solution)/shard_map/ppermute | solution.py:43
  30.0 0.8 %finish.6.refs_2_ = bf16[1,128,4096]{2,1,0:T(8,128)(2,1)} custom-call(f32[128,4096]{1,0:T(8,128)S(1)} %get-tuple-element.26.refs_0_.refs_7_, bf16[128,1280]{1,0:T(8,128)(2,1)S(1)} %collective-permute-done.8.refs_1_, bf16[1,128,4096]{2,1,0:T(8,128)(2,1)} %raw.1.refs_2_), custom_call_target="tpu_custom_call", output_to_operand_aliasing={{}: (2, {})} | custom-call | flops 20000000000 | bytes 1024 | tf_op jit(solution)/shard_map/finish/pallas_call | solution.py:449
  30.8 0.6 %collective-permute-done.7.refs_1_ = bf16[128,512]{1,0:T(8,128)(2,1)S(1)} collective-permute-done((bf16[128,512]{1,0:T(8,128)(2,1)S(1)}, bf16[128,512]{1,0:T(8,128)(2,1)S(1)}, u32[]{:S(2)}, u32[]{:S(2)}) %collective-permute-start.7) | collective-permute-done | bytes 131104 | tf_op jit(solution)/shard_map/ppermute | solution.py:43
  31.5 0.7 %finish.7 = bf16[1,128,4096]{2,1,0:T(8,128)(2,1)} custom-call(f32[128,4096]{1,0:T(8,128)S(1)} %get-tuple-element.26.refs_0_.refs_7_, bf16[128,512]{1,0:T(8,128)(2,1)S(1)} %collective-permute-done.7.refs_1_, bf16[1,128,4096]{2,1,0:T(8,128)(2,1)} %finish.6.refs_2_), custom_call_target="tpu_custom_call", output_to_operand_aliasing={{}: (2, {})} | custom-call | flops 20000000000 | bytes 1024 | tf_op jit(solution)/shard_map/finish/pallas_call | solution.py:449
  (13 shorter events, 0.1 us)
Async XLA Ops:
  0.0 2.3 %copy-start.2 = (bf16[1,256,128]{2,1,0:T(8,128)(2,1)S(1)}, bf16[1,256,128]{2,1,0:T(8,128)(2,1)}, u32[]{:S(2)}) copy-start(bf16[1,256,128]{2,1,0:T(8,128)(2,1)} %refs_3_.3) | copy-start | bytes 196612
  0.0 2.3 %copy-start.3 = (f32[1,256]{1,0:T(1,128)S(1)}, f32[1,256]{1,0:T(1,128)}, u32[]{:S(2)}) copy-start(f32[1,256]{1,0:T(1,128)} %refs_4_.11) | copy-start | bytes 3076
  0.0 2.3 %copy-start.4 = (s32[1,256]{1,0:T(1,128)S(1)}, s32[1,256]{1,0:T(1,128)}, u32[]{:S(2)}) copy-start(s32[1,256]{1,0:T(1,128)} %refs_5_.9) | copy-start | bytes 3076
  0.1 4.6 %copy-start = (bf16[1,128,4096]{2,1,0:T(8,128)(2,1)S(1)}, bf16[1,128,4096]{2,1,0:T(8,128)(2,1)}, u32[]{:S(2)}) copy-start(bf16[1,128,4096]{2,1,0:T(8,128)(2,1)} %refs_8_.2) | copy-start | bytes 3145732
  0.1 4.6 %copy-start.1 = (bf16[128,4096]{1,0:T(8,128)(2,1)S(1)}, bf16[128,4096]{1,0:T(8,128)(2,1)}, u32[]{:S(2)}) copy-start(bf16[128,4096]{1,0:T(8,128)(2,1)} %refs_8_.3) | copy-start | bytes 3145732
  0.1 4.6 %collective-permute-start.1 = (bf16[128,3712]{1,0:T(8,128)(2,1)S(1)}, bf16[128,3712]{1,0:T(8,128)(2,1)S(1)}, u32[]{:S(2)}, u32[]{:S(2)}) collective-permute-start(bf16[128,3712]{1,0:T(8,128)(2,1)S(1)} %get-tuple-element.18.refs_5_.refs_3_), channel_id=1, source_target_pairs={{0,4},{8,12},{16,20},{24,28},{2,6},{10,14},{18,22},{26,30}} | collective-permute-start | bytes 2850824 | tf_op jit(solution)/shard_map/ppermute | solution.py:37
  1.0 8.9 %collective-permute-start = (bf16[256,384]{1,0:T(8,128)(2,1)S(1)}, bf16[256,384]{1,0:T(8,128)(2,1)S(1)}, u32[]{:S(2)}, u32[]{:S(2)}) collective-permute-start(bf16[256,384]{1,0:T(8,128)(2,1)S(1)} %get-tuple-element.17.refs_0_), channel_id=1, source_target_pairs={{0,1},{4,5},{8,9},{12,13},{16,17},{20,21},{24,25},{28,29},{2,3},{6... | collective-permute-start | bytes 589832 | tf_op jit(solution)/shard_map/ppermute | solution.py:43
  4.7 10.8 %collective-permute-start.5 = (bf16[128,1536]{1,0:T(8,128)(2,1)S(1)}, bf16[128,1536]{1,0:T(8,128)(2,1)S(1)}, u32[]{:S(2)}, u32[]{:S(2)}) collective-permute-start(bf16[128,1536]{1,0:T(8,128)(2,1)S(1)} %own.6._.refs_9_), channel_id=1, source_target_pairs={{4,5},{12,13},{20,21},{28,29},{6,7},{14,15},{22,23},{30,31}} | collective-permute-start | bytes 1179656 | tf_op jit(solution)/shard_map/ppermute | solution.py:43
  5.4 10.1 %collective-permute-start.2 = (bf16[128,1920]{1,0:T(8,128)(2,1)S(1)}, bf16[128,1920]{1,0:T(8,128)(2,1)S(1)}, u32[]{:S(2)}, u32[]{:S(2)}) collective-permute-start(bf16[128,1920]{1,0:T(8,128)(2,1)S(1)} %hold.5.refs_6_.refs_3_), channel_id=1, source_target_pairs={{4,8},{12,16},{20,24},{1,5},{9,13},{17,21},{25,29},{5,9},{13,17},{... | collective-permute-start | bytes 1474568 | tf_op jit(solution)/shard_map/ppermute | solution.py:37
  7.8 12.7 %collective-permute-start.6 = (bf16[128,2176]{1,0:T(8,128)(2,1)S(1)}, bf16[128,2176]{1,0:T(8,128)(2,1)S(1)}, u32[]{:S(2)}, u32[]{:S(2)}) collective-permute-start(bf16[128,2176]{1,0:T(8,128)(2,1)S(1)} %own.7.refs_7_.refs_10_), channel_id=1, source_target_pairs={{4,5},{12,13},{20,21},{28,29},{6,7},{14,15},{22,23},{30,31}} | collective-permute-start | bytes 1671176 | tf_op jit(solution)/shard_map/ppermute | solution.py:43
  9.9 10.6 %collective-permute-start.3 = (bf16[128,1792]{1,0:T(8,128)(2,1)S(1)}, bf16[128,1792]{1,0:T(8,128)(2,1)S(1)}, u32[]{:S(2)}, u32[]{:S(2)}) collective-permute-start(bf16[128,1792]{1,0:T(8,128)(2,1)S(1)} %hold.6._.refs_5_), channel_id=1, source_target_pairs={{4,8},{12,16},{20,24},{1,5},{9,13},{17,21},{25,29},{5,9},{13,17},{... | collective-permute-start | bytes 1376264 | tf_op jit(solution)/shard_map/ppermute | solution.py:37
  12.4 10.2 %collective-permute-start.4 = (bf16[128,768]{1,0:T(8,128)(2,1)S(1)}, bf16[128,768]{1,0:T(8,128)(2,1)S(1)}, u32[]{:S(2)}, u32[]{:S(2)}) collective-permute-start(bf16[128,768]{1,0:T(8,128)(2,1)S(1)} %hold.7.refs_5_), channel_id=1, source_target_pairs={{0,4},{8,12},{16,20},{24,28},{4,8},{12,16},{20,24},{1,5},{9,13},{1... | collective-permute-start | bytes 589832 | tf_op jit(solution)/shard_map/ppermute | solution.py:37
  15.6 11.8 %collective-permute-start.11 = (bf16[128,1024]{1,0:T(8,128)(2,1)S(1)}, bf16[128,1024]{1,0:T(8,128)(2,1)S(1)}, u32[]{:S(2)}, u32[]{:S(2)}) collective-permute-start(bf16[128,1024]{1,0:T(8,128)(2,1)S(1)} %own.8.refs_6_.refs_11_), channel_id=1, source_target_pairs={{0,1},{8,9},{16,17},{24,25},{2,3},{10,11},{18,19},{26,27}} | collective-permute-start | bytes 786440 | tf_op jit(solution)/shard_map/ppermute | solution.py:43
  16.9 10.4 %collective-permute-start.10 = (bf16[136,896]{1,0:T(8,128)(2,1)S(1)}, bf16[136,896]{1,0:T(8,128)(2,1)S(1)}, u32[]{:S(2)}, u32[]{:S(2)}) collective-permute-start(bf16[136,896]{1,0:T(8,128)(2,1)S(1)} %own.9.refs_6_.refs_12_), channel_id=1, source_target_pairs={{0,1},{8,9},{16,17},{24,25},{2,3},{10,11},{18,19},{26,27}} | collective-permute-start | bytes 731144 | tf_op jit(solution)/shard_map/ppermute | solution.py:43
  20.5 9.5 %collective-permute-start.8 = (bf16[128,1280]{1,0:T(8,128)(2,1)S(1)}, bf16[128,1280]{1,0:T(8,128)(2,1)S(1)}, u32[]{:S(2)}, u32[]{:S(2)}) collective-permute-start(bf16[128,1280]{1,0:T(8,128)(2,1)S(1)} %own.10.refs_6_.refs_13_), channel_id=1, source_target_pairs={{0,1},{8,9},{16,17},{24,25},{2,3},{10,11},{18,19},{26,27}} | collective-permute-start | bytes 983048 | tf_op jit(solution)/shard_map/ppermute | solution.py:43
  22.6 8.8 %collective-permute-start.7 = (bf16[128,512]{1,0:T(8,128)(2,1)S(1)}, bf16[128,512]{1,0:T(8,128)(2,1)S(1)}, u32[]{:S(2)}, u32[]{:S(2)}) collective-permute-start(bf16[128,512]{1,0:T(8,128)(2,1)S(1)} %own.11.refs_14_._), channel_id=1, source_target_pairs={{0,1},{8,9},{16,17},{24,25},{2,3},{10,11},{18,19},{26,27}} | collective-permute-start | bytes 393224 | tf_op jit(solution)/shard_map/ppermute | solution.py:43
  23.9 4.3 %collective-permute-start.9 = (bf16[32,128]{1,0:T(8,128)(2,1)S(1)}, bf16[32,128]{1,0:T(8,128)(2,1)S(1)}, u32[]{:S(2)}, u32[]{:S(2)}) collective-permute-start(bf16[32,128]{1,0:T(8,128)(2,1)S(1)} %hold.9), channel_id=1, source_target_pairs={{4,5},{12,13},{20,21},{28,29},{6,7},{14,15},{22,23},{30,31}} | collective-permute-start | bytes 24584 | tf_op jit(solution)/shard_map/ppermute | solution.py:43

commit v20 on v16

--- a/solution.py
+++ b/solution.py
@@ -91,8 +91,7 @@
         for out_ref in out_refs:
             for tile in range(0, out_ref.shape[1], LANES):
                 at = slice(first + tile, first + tile + LANES)
-                product = keys_in[span, at].astype(F32) * values_in[span, at].astype(F32)
-                out_ref[span, tile : tile + LANES] = product.astype(BF16)
+                out_ref[span, tile : tile + LANES] = keys_in[span, at] * values_in[span, at]
             first += out_ref.shape[1]
 
 

time: 32.5 us -> 32.5 us (level)
  no operation moved by 1% of the time
where the time goes in v20:
time: 32.5 us; the launch traced here: 32.1 us
  starting transfers between devices  17.2 us (53%)
  Pallas kernels  8.1 us (25%)
  waiting for transfers between devices  5.86 us (18%)
  between operations  0.97 us (3%)
    ppermute x4, starting transfers between devices, to_next_slab(): return lax.ppermute(value, ('ctx', 'pipe'), pairs)  8.71 us
    ppermute x8, starting transfers between devices, to_next_section(): return lax.ppermute(value, ('ctx', 'pipe'), pairs)  8.47 us
    ppermute x4, waiting for transfers between devices, to_next_slab(): return lax.ppermute(value, ('ctx', 'pipe'), pairs)  3.23 us
    pallas_call x1, Pallas kernels, later_of(): call(functools.partial(later_kernel, places), 'later', (jax.ShapeDtypeStr...  2.7 us
    ppermute x8, waiting for transfers between devices, to_next_section(): return lax.ppermute(value, ('ctx', 'pipe'), pairs)  2.63 us
    pallas_call x4, Pallas kernels, finish(): call(functools.partial(finish_kernel, places[0][0], places), 'finish', ja...  2.38 us
    pallas_call x1, Pallas kernels, product_of(): call(product_kernel, 'product', (array(groups, taps, F32), array(wire_row...  1.67 us
    pallas_call x1, Pallas kernels, raw_finish(): call(raw_kernel, 'raw', jax.ShapeDtypeStruct(held.shape, BF16), [SMEM] +...  1.14 us
  transfers between devices with their start and end apart: 12, of which 6 were waited for; matrix products, arithmetic and copies ran while one was open for 0% of the time, Pallas kernels for 23%

profile of v20, /device:TPU:12, one launch (start us, length us, event | category | flops | bytes accessed | tf_op | source)
XLA Modules:
  0.0 32.1 jit_solution(8928386737019776180)
XLA Ops:
  0.0 0.0 copy-start.2
  0.0 0.0 copy-start.3
  0.0 0.0 copy-start.4
  0.0 0.1 lead.1
  0.1 0.0 copy-start
  0.1 0.0 copy-start.1
  0.1 0.9 %collective-permute-start.1 = (bf16[128,3712]{1,0:T(8,128)(2,1)S(1)}, bf16[128,3712]{1,0:T(8,128)(2,1)S(1)}, u32[]{:S(2)}, u32[]{:S(2)}) collective-permute-start(bf16[128,3712]{1,0:T(8,128)(2,1)S(1)} %get-tuple-element.18.refs_5_.refs_3_), channel_id=1, source_target_pairs={{0,4},{8,12},{16,20},{24,28},{2,6},{10,14},{18,22},{26,30}} | collective-permute-start | bytes 2850824 | tf_op jit(solution)/shard_map/ppermute | solution.py:37
  1.0 1.3 %collective-permute-start = (bf16[256,384]{1,0:T(8,128)(2,1)S(1)}, bf16[256,384]{1,0:T(8,128)(2,1)S(1)}, u32[]{:S(2)}, u32[]{:S(2)}) collective-permute-start(bf16[256,384]{1,0:T(8,128)(2,1)S(1)} %get-tuple-element.17.refs_0_), channel_id=1, source_target_pairs={{0,1},{4,5},{8,9},{12,13},{16,17},{20,21},{24,25},{28,29},{2,3},{6... | collective-permute-start | bytes 589832 | tf_op jit(solution)/shard_map/ppermute | solution.py:43
  2.3 0.0 copy-done.2
  2.3 0.0 copy-done.3
  2.3 0.0 copy-done.4
  2.3 1.7 %product.1 = (f32[256,128]{1,0:T(8,128)S(1)}, bf16[32,128]{1,0:T(8,128)(2,1)S(1)}, bf16[128,1920]{1,0:T(8,128)(2,1)S(1)}, bf16[128,1792]{1,0:T(8,128)(2,1)S(1)}, bf16[128,384]{1,0:T(8,128)(2,1)S(1)}) custom-call(bf16[1,128,4096]{2,1,0:T(8,128)(2,1)} %refs_0_.9, bf16[1,128,4096]{2,1,0:T(8,128)(2,1)} %refs_1_.1, bf16[1,256,128]{2,1,0:T(8,128)(2,1)S(1)} %copy-done.2, ...), custom_call_target="tpu_custom_call" | custom-call | flops 1024 | bytes 1024 | tf_op jit(solution)/shard_map/product/pallas_call | solution.py:177
  4.7 0.0 collective-permute-done.1.refs_2_
  4.7 0.0 copy-done
  4.7 0.0 copy-done.1
  4.7 0.7 %collective-permute-start.5 = (bf16[128,1536]{1,0:T(8,128)(2,1)S(1)}, bf16[128,1536]{1,0:T(8,128)(2,1)S(1)}, u32[]{:S(2)}, u32[]{:S(2)}) collective-permute-start(bf16[128,1536]{1,0:T(8,128)(2,1)S(1)} %own.6._.refs_9_), channel_id=1, source_target_pairs={{4,5},{12,13},{20,21},{28,29},{6,7},{14,15},{22,23},{30,31}} | collective-permute-start | bytes 1179656 | tf_op jit(solution)/shard_map/ppermute | solution.py:43
  5.4 2.3 %collective-permute-start.2 = (bf16[128,1920]{1,0:T(8,128)(2,1)S(1)}, bf16[128,1920]{1,0:T(8,128)(2,1)S(1)}, u32[]{:S(2)}, u32[]{:S(2)}) collective-permute-start(bf16[128,1920]{1,0:T(8,128)(2,1)S(1)} %hold.5.refs_6_.refs_3_), channel_id=1, source_target_pairs={{4,8},{12,16},{20,24},{1,5},{9,13},{17,21},{25,29},{5,9},{13,17},{... | collective-permute-start | bytes 1474568 | tf_op jit(solution)/shard_map/ppermute | solution.py:37
  7.8 0.7 %collective-permute-start.6 = (bf16[128,2176]{1,0:T(8,128)(2,1)S(1)}, bf16[128,2176]{1,0:T(8,128)(2,1)S(1)}, u32[]{:S(2)}, u32[]{:S(2)}) collective-permute-start(bf16[128,2176]{1,0:T(8,128)(2,1)S(1)} %own.7.refs_7_.refs_10_), channel_id=1, source_target_pairs={{4,5},{12,13},{20,21},{28,29},{6,7},{14,15},{22,23},{30,31}} | collective-permute-start | bytes 1671176 | tf_op jit(solution)/shard_map/ppermute | solution.py:43
  8.5 1.3 %collective-permute-done.refs_1_ = bf16[256,384]{1,0:T(8,128)(2,1)S(1)} collective-permute-done((bf16[256,384]{1,0:T(8,128)(2,1)S(1)}, bf16[256,384]{1,0:T(8,128)(2,1)S(1)}, u32[]{:S(2)}, u32[]{:S(2)}) %collective-permute-start) | collective-permute-done | bytes 196640 | tf_op jit(solution)/shard_map/ppermute | solution.py:43
  9.9 2.5 %collective-permute-start.3 = (bf16[128,1792]{1,0:T(8,128)(2,1)S(1)}, bf16[128,1792]{1,0:T(8,128)(2,1)S(1)}, u32[]{:S(2)}, u32[]{:S(2)}) collective-permute-start(bf16[128,1792]{1,0:T(8,128)(2,1)S(1)} %hold.6._.refs_5_), channel_id=1, source_target_pairs={{4,8},{12,16},{20,24},{1,5},{9,13},{17,21},{25,29},{5,9},{13,17},{... | collective-permute-start | bytes 1376264 | tf_op jit(solution)/shard_map/ppermute | solution.py:37
  12.4 3.1 %collective-permute-start.4 = (bf16[128,768]{1,0:T(8,128)(2,1)S(1)}, bf16[128,768]{1,0:T(8,128)(2,1)S(1)}, u32[]{:S(2)}, u32[]{:S(2)}) collective-permute-start(bf16[128,768]{1,0:T(8,128)(2,1)S(1)} %hold.7.refs_5_), channel_id=1, source_target_pairs={{0,4},{8,12},{16,20},{24,28},{4,8},{12,16},{20,24},{1,5},{9,13},{1... | collective-permute-start | bytes 589832 | tf_op jit(solution)/shard_map/ppermute | solution.py:37
  15.4 0.0 collective-permute-done.5._.refs_1_
  15.5 0.1 collective-permute-done.2.refs_2_
  15.6 1.3 %collective-permute-start.11 = (bf16[128,1024]{1,0:T(8,128)(2,1)S(1)}, bf16[128,1024]{1,0:T(8,128)(2,1)S(1)}, u32[]{:S(2)}, u32[]{:S(2)}) collective-permute-start(bf16[128,1024]{1,0:T(8,128)(2,1)S(1)} %own.8.refs_6_.refs_11_), channel_id=1, source_target_pairs={{0,1},{8,9},{16,17},{24,25},{2,3},{10,11},{18,19},{26,27}} | collective-permute-start | bytes 786440 | tf_op jit(solution)/shard_map/ppermute | solution.py:43
  16.9 1.3 %collective-permute-start.10 = (bf16[136,896]{1,0:T(8,128)(2,1)S(1)}, bf16[136,896]{1,0:T(8,128)(2,1)S(1)}, u32[]{:S(2)}, u32[]{:S(2)}) collective-permute-start(bf16[136,896]{1,0:T(8,128)(2,1)S(1)} %own.9.refs_6_.refs_12_), channel_id=1, source_target_pairs={{0,1},{8,9},{16,17},{24,25},{2,3},{10,11},{18,19},{26,27}} | collective-permute-start | bytes 731144 | tf_op jit(solution)/shard_map/ppermute | solution.py:43
  18.2 2.3 %collective-permute-done.3.refs_2_.refs_4_ = bf16[128,1792]{1,0:T(8,128)(2,1)S(1)} collective-permute-done((bf16[128,1792]{1,0:T(8,128)(2,1)S(1)}, bf16[128,1792]{1,0:T(8,128)(2,1)S(1)}, u32[]{:S(2)}, u32[]{:S(2)}) %collective-permute-start.3) | collective-permute-done | bytes 458784 | tf_op jit(solution)/shard_map/ppermute | solution.py:37
  20.5 0.0 collective-permute-done.6.refs_7_.refs_2_
  20.5 1.3 %collective-permute-start.8 = (bf16[128,1280]{1,0:T(8,128)(2,1)S(1)}, bf16[128,1280]{1,0:T(8,128)(2,1)S(1)}, u32[]{:S(2)}, u32[]{:S(2)}) collective-permute-start(bf16[128,1280]{1,0:T(8,128)(2,1)S(1)} %own.10.refs_6_.refs_13_), channel_id=1, source_target_pairs={{0,1},{8,9},{16,17},{24,25},{2,3},{10,11},{18,19},{26,27}} | collective-permute-start | bytes 983048 | tf_op jit(solution)/shard_map/ppermute | solution.py:43
  21.8 0.8 %collective-permute-done.4.refs_7_.refs_6_.refs_4_ = bf16[128,768]{1,0:T(8,128)(2,1)S(1)} collective-permute-done((bf16[128,768]{1,0:T(8,128)(2,1)S(1)}, bf16[128,768]{1,0:T(8,128)(2,1)S(1)}, u32[]{:S(2)}, u32[]{:S(2)}) %collective-permute-start.4) | collective-permute-done | bytes 196640 | tf_op jit(solution)/shard_map/ppermute | solution.py:37
  22.6 1.3 %collective-permute-start.7 = (bf16[128,512]{1,0:T(8,128)(2,1)S(1)}, bf16[128,512]{1,0:T(8,128)(2,1)S(1)}, u32[]{:S(2)}, u32[]{:S(2)}) collective-permute-start(bf16[128,512]{1,0:T(8,128)(2,1)S(1)} %own.11.refs_14_._), channel_id=1, source_target_pairs={{0,1},{8,9},{16,17},{24,25},{2,3},{10,11},{18,19},{26,27}} | collective-permute-start | bytes 393224 | tf_op jit(solution)/shard_map/ppermute | solution.py:43
  23.9 0.7 %collective-permute-start.9 = (bf16[32,128]{1,0:T(8,128)(2,1)S(1)}, bf16[32,128]{1,0:T(8,128)(2,1)S(1)}, u32[]{:S(2)}, u32[]{:S(2)}) collective-permute-start(bf16[32,128]{1,0:T(8,128)(2,1)S(1)} %hold.9), channel_id=1, source_target_pairs={{4,5},{12,13},{20,21},{28,29},{6,7},{14,15},{22,23},{30,31}} | collective-permute-start | bytes 24584 | tf_op jit(solution)/shard_map/ppermute | solution.py:43
  24.6 2.7 %later.1 = (bf16[1,128,4096]{2,1,0:T(8,128)(2,1)}, f32[128,4096]{1,0:T(8,128)S(1)}) custom-call(s32[1]{0:T(128)S(6)} %copy.31.refs_0_, f32[256,128]{1,0:T(8,128)S(1)} %get-tuple-element.22.refs_1_, bf16[128,1920]{1,0:T(8,128)(2,1)S(1)} %collective-permute-done.2.refs_2_, bf16[128,1920]{1,0:T(8,128)(2,1)S(1)} %hold.5.refs_6_.refs_3_, ...), custom_call_target="tpu_custom_call" | custom-call | flops 20000000000 | bytes 1024 | tf_op jit(solution)/shard_map/later/pallas_call | solution.py:365
  27.3 0.0 collective-permute-done.10.refs_2_.refs_3_
  27.3 0.0 collective-permute-done.11.refs_1_
  27.3 0.9 %finish.5.refs_9_ = bf16[1,128,4096]{2,1,0:T(8,128)(2,1)} custom-call(f32[128,4096]{1,0:T(8,128)S(1)} %get-tuple-element.26.refs_0_.refs_7_, bf16[128,1024]{1,0:T(8,128)(2,1)S(1)} %collective-permute-done.11.refs_1_, bf16[136,896]{1,0:T(8,128)(2,1)S(1)} %collective-permute-done.10.refs_2_.refs_3_, ...), custom_call_target="tpu_custom_call", output_to_operand_aliasing={{}: (3, {})} | custom-call | flops 20000000000 | bytes 1024 | tf_op jit(solution)/shard_map/finish/pallas_call | solution.py:448
  28.2 0.0 collective-permute-done.9.refs_2_
  28.2 1.1 %raw.1.refs_2_ = bf16[1,128,4096]{2,1,0:T(8,128)(2,1)} custom-call(s32[1]{0:T(128)S(6)} %copy.31.refs_0_, f32[256,128]{1,0:T(8,128)S(1)} %get-tuple-element.22.refs_1_, bf16[32,128]{1,0:T(8,128)(2,1)S(1)} %collective-permute-done.9.refs_2_, bf16[136,896]{1,0:T(8,128)(2,1)S(1)} %collective-permute-done.10.refs_2_.refs_3_, ...), custom_call_target="tpu_custom_call", output_to_operand_aliasing={{}: (9, {})} | custom-call | flops 20000000000 | bytes 1024 | tf_op jit(solution)/shard_map/raw/pallas_call | solution.py:413
  29.4 0.7 %collective-permute-done.8.refs_1_ = bf16[128,1280]{1,0:T(8,128)(2,1)S(1)} collective-permute-done((bf16[128,1280]{1,0:T(8,128)(2,1)S(1)}, bf16[128,1280]{1,0:T(8,128)(2,1)S(1)}, u32[]{:S(2)}, u32[]{:S(2)}) %collective-permute-start.8) | collective-permute-done | bytes 327712 | tf_op jit(solution)/shard_map/ppermute | solution.py:43
  30.0 0.8 %finish.6.refs_2_ = bf16[1,128,4096]{2,1,0:T(8,128)(2,1)} custom-call(f32[128,4096]{1,0:T(8,128)S(1)} %get-tuple-element.26.refs_0_.refs_7_, bf16[128,1280]{1,0:T(8,128)(2,1)S(1)} %collective-permute-done.8.refs_1_, bf16[1,128,4096]{2,1,0:T(8,128)(2,1)} %raw.1.refs_2_), custom_call_target="tpu_custom_call", output_to_operand_aliasing={{}: (2, {})} | custom-call | flops 20000000000 | bytes 1024 | tf_op jit(solution)/shard_map/finish/pallas_call | solution.py:448
  30.8 0.6 %collective-permute-done.7.refs_1_ = bf16[128,512]{1,0:T(8,128)(2,1)S(1)} collective-permute-done((bf16[128,512]{1,0:T(8,128)(2,1)S(1)}, bf16[128,512]{1,0:T(8,128)(2,1)S(1)}, u32[]{:S(2)}, u32[]{:S(2)}) %collective-permute-start.7) | collective-permute-done | bytes 131104 | tf_op jit(solution)/shard_map/ppermute | solution.py:43
  31.4 0.7 %finish.7 = bf16[1,128,4096]{2,1,0:T(8,128)(2,1)} custom-call(f32[128,4096]{1,0:T(8,128)S(1)} %get-tuple-element.26.refs_0_.refs_7_, bf16[128,512]{1,0:T(8,128)(2,1)S(1)} %collective-permute-done.7.refs_1_, bf16[1,128,4096]{2,1,0:T(8,128)(2,1)} %finish.6.refs_2_), custom_call_target="tpu_custom_call", output_to_operand_aliasing={{}: (2, {})} | custom-call | flops 20000000000 | bytes 1024 | tf_op jit(solution)/shard_map/finish/pallas_call | solution.py:448
  (13 shorter events, 0.1 us)
Async XLA Ops:
  0.0 2.3 %copy-start.2 = (bf16[1,256,128]{2,1,0:T(8,128)(2,1)S(1)}, bf16[1,256,128]{2,1,0:T(8,128)(2,1)}, u32[]{:S(2)}) copy-start(bf16[1,256,128]{2,1,0:T(8,128)(2,1)} %refs_3_.3) | copy-start | bytes 196612
  0.0 2.3 %copy-start.3 = (f32[1,256]{1,0:T(1,128)S(1)}, f32[1,256]{1,0:T(1,128)}, u32[]{:S(2)}) copy-start(f32[1,256]{1,0:T(1,128)} %refs_4_.11) | copy-start | bytes 3076
  0.0 2.3 %copy-start.4 = (s32[1,256]{1,0:T(1,128)S(1)}, s32[1,256]{1,0:T(1,128)}, u32[]{:S(2)}) copy-start(s32[1,256]{1,0:T(1,128)} %refs_5_.9) | copy-start | bytes 3076
  0.1 4.6 %copy-start = (bf16[1,128,4096]{2,1,0:T(8,128)(2,1)S(1)}, bf16[1,128,4096]{2,1,0:T(8,128)(2,1)}, u32[]{:S(2)}) copy-start(bf16[1,128,4096]{2,1,0:T(8,128)(2,1)} %refs_8_.2) | copy-start | bytes 3145732
  0.1 4.6 %copy-start.1 = (bf16[128,4096]{1,0:T(8,128)(2,1)S(1)}, bf16[128,4096]{1,0:T(8,128)(2,1)}, u32[]{:S(2)}) copy-start(bf16[128,4096]{1,0:T(8,128)(2,1)} %refs_8_.3) | copy-start | bytes 3145732
  0.1 4.5 %collective-permute-start.1 = (bf16[128,3712]{1,0:T(8,128)(2,1)S(1)}, bf16[128,3712]{1,0:T(8,128)(2,1)S(1)}, u32[]{:S(2)}, u32[]{:S(2)}) collective-permute-start(bf16[128,3712]{1,0:T(8,128)(2,1)S(1)} %get-tuple-element.18.refs_5_.refs_3_), channel_id=1, source_target_pairs={{0,4},{8,12},{16,20},{24,28},{2,6},{10,14},{18,22},{26,30}} | collective-permute-start | bytes 2850824 | tf_op jit(solution)/shard_map/ppermute | solution.py:37
  1.0 8.9 %collective-permute-start = (bf16[256,384]{1,0:T(8,128)(2,1)S(1)}, bf16[256,384]{1,0:T(8,128)(2,1)S(1)}, u32[]{:S(2)}, u32[]{:S(2)}) collective-permute-start(bf16[256,384]{1,0:T(8,128)(2,1)S(1)} %get-tuple-element.17.refs_0_), channel_id=1, source_target_pairs={{0,1},{4,5},{8,9},{12,13},{16,17},{20,21},{24,25},{28,29},{2,3},{6... | collective-permute-start | bytes 589832 | tf_op jit(solution)/shard_map/ppermute | solution.py:43
  4.7 10.7 %collective-permute-start.5 = (bf16[128,1536]{1,0:T(8,128)(2,1)S(1)}, bf16[128,1536]{1,0:T(8,128)(2,1)S(1)}, u32[]{:S(2)}, u32[]{:S(2)}) collective-permute-start(bf16[128,1536]{1,0:T(8,128)(2,1)S(1)} %own.6._.refs_9_), channel_id=1, source_target_pairs={{4,5},{12,13},{20,21},{28,29},{6,7},{14,15},{22,23},{30,31}} | collective-permute-start | bytes 1179656 | tf_op jit(solution)/shard_map/ppermute | solution.py:43
  5.4 10.1 %collective-permute-start.2 = (bf16[128,1920]{1,0:T(8,128)(2,1)S(1)}, bf16[128,1920]{1,0:T(8,128)(2,1)S(1)}, u32[]{:S(2)}, u32[]{:S(2)}) collective-permute-start(bf16[128,1920]{1,0:T(8,128)(2,1)S(1)} %hold.5.refs_6_.refs_3_), channel_id=1, source_target_pairs={{4,8},{12,16},{20,24},{1,5},{9,13},{17,21},{25,29},{5,9},{13,17},{... | collective-permute-start | bytes 1474568 | tf_op jit(solution)/shard_map/ppermute | solution.py:37
  7.8 12.7 %collective-permute-start.6 = (bf16[128,2176]{1,0:T(8,128)(2,1)S(1)}, bf16[128,2176]{1,0:T(8,128)(2,1)S(1)}, u32[]{:S(2)}, u32[]{:S(2)}) collective-permute-start(bf16[128,2176]{1,0:T(8,128)(2,1)S(1)} %own.7.refs_7_.refs_10_), channel_id=1, source_target_pairs={{4,5},{12,13},{20,21},{28,29},{6,7},{14,15},{22,23},{30,31}} | collective-permute-start | bytes 1671176 | tf_op jit(solution)/shard_map/ppermute | solution.py:43
  9.9 10.6 %collective-permute-start.3 = (bf16[128,1792]{1,0:T(8,128)(2,1)S(1)}, bf16[128,1792]{1,0:T(8,128)(2,1)S(1)}, u32[]{:S(2)}, u32[]{:S(2)}) collective-permute-start(bf16[128,1792]{1,0:T(8,128)(2,1)S(1)} %hold.6._.refs_5_), channel_id=1, source_target_pairs={{4,8},{12,16},{20,24},{1,5},{9,13},{17,21},{25,29},{5,9},{13,17},{... | collective-permute-start | bytes 1376264 | tf_op jit(solution)/shard_map/ppermute | solution.py:37
  12.4 10.2 %collective-permute-start.4 = (bf16[128,768]{1,0:T(8,128)(2,1)S(1)}, bf16[128,768]{1,0:T(8,128)(2,1)S(1)}, u32[]{:S(2)}, u32[]{:S(2)}) collective-permute-start(bf16[128,768]{1,0:T(8,128)(2,1)S(1)} %hold.7.refs_5_), channel_id=1, source_target_pairs={{0,4},{8,12},{16,20},{24,28},{4,8},{12,16},{20,24},{1,5},{9,13},{1... | collective-permute-start | bytes 589832 | tf_op jit(solution)/shard_map/ppermute | solution.py:37
  15.6 11.8 %collective-permute-start.11 = (bf16[128,1024]{1,0:T(8,128)(2,1)S(1)}, bf16[128,1024]{1,0:T(8,128)(2,1)S(1)}, u32[]{:S(2)}, u32[]{:S(2)}) collective-permute-start(bf16[128,1024]{1,0:T(8,128)(2,1)S(1)} %own.8.refs_6_.refs_11_), channel_id=1, source_target_pairs={{0,1},{8,9},{16,17},{24,25},{2,3},{10,11},{18,19},{26,27}} | collective-permute-start | bytes 786440 | tf_op jit(solution)/shard_map/ppermute | solution.py:43
  16.9 10.4 %collective-permute-start.10 = (bf16[136,896]{1,0:T(8,128)(2,1)S(1)}, bf16[136,896]{1,0:T(8,128)(2,1)S(1)}, u32[]{:S(2)}, u32[]{:S(2)}) collective-permute-start(bf16[136,896]{1,0:T(8,128)(2,1)S(1)} %own.9.refs_6_.refs_12_), channel_id=1, source_target_pairs={{0,1},{8,9},{16,17},{24,25},{2,3},{10,11},{18,19},{26,27}} | collective-permute-start | bytes 731144 | tf_op jit(solution)/shard_map/ppermute | solution.py:43
  20.5 9.5 %collective-permute-start.8 = (bf16[128,1280]{1,0:T(8,128)(2,1)S(1)}, bf16[128,1280]{1,0:T(8,128)(2,1)S(1)}, u32[]{:S(2)}, u32[]{:S(2)}) collective-permute-start(bf16[128,1280]{1,0:T(8,128)(2,1)S(1)} %own.10.refs_6_.refs_13_), channel_id=1, source_target_pairs={{0,1},{8,9},{16,17},{24,25},{2,3},{10,11},{18,19},{26,27}} | collective-permute-start | bytes 983048 | tf_op jit(solution)/shard_map/ppermute | solution.py:43
  22.6 8.8 %collective-permute-start.7 = (bf16[128,512]{1,0:T(8,128)(2,1)S(1)}, bf16[128,512]{1,0:T(8,128)(2,1)S(1)}, u32[]{:S(2)}, u32[]{:S(2)}) collective-permute-start(bf16[128,512]{1,0:T(8,128)(2,1)S(1)} %own.11.refs_14_._), channel_id=1, source_target_pairs={{0,1},{8,9},{16,17},{24,25},{2,3},{10,11},{18,19},{26,27}} | collective-permute-start | bytes 393224 | tf_op jit(solution)/shard_map/ppermute | solution.py:43
  23.9 4.3 %collective-permute-start.9 = (bf16[32,128]{1,0:T(8,128)(2,1)S(1)}, bf16[32,128]{1,0:T(8,128)(2,1)S(1)}, u32[]{:S(2)}, u32[]{:S(2)}) collective-permute-start(bf16[32,128]{1,0:T(8,128)(2,1)S(1)} %hold.9), channel_id=1, source_target_pairs={{4,5},{12,13},{20,21},{28,29},{6,7},{14,15},{22,23},{30,31}} | collective-permute-start | bytes 24584 | tf_op jit(solution)/shard_map/ppermute | solution.py:43

commit v21 on v20

--- a/solution.py
+++ b/solution.py
@@ -10,7 +10,7 @@
 LANES = 128
 ROW_BLOCK = 32
 RAW = 384
-ODD = (1536, 2176)
+ODD = (1792, 1920)
 EVEN = (1024, 896, 1280, 512)
 PIECES = 4
 LINES = 8

time: 32.5 us -> 32.5 us (level)
  no operation moved by 1% of the time
where the time goes in v21:
time: 32.5 us; the launch traced here: 32.1 us
  starting transfers between devices  17.2 us (53%)
  Pallas kernels  8.16 us (25%)
  waiting for transfers between devices  5.82 us (18%)
  between operations  0.97 us (3%)
    ppermute x4, starting transfers between devices, to_next_slab(): return lax.ppermute(value, ('ctx', 'pipe'), pairs)  8.71 us
    ppermute x8, starting transfers between devices, to_next_section(): return lax.ppermute(value, ('ctx', 'pipe'), pairs)  8.47 us
    ppermute x4, waiting for transfers between devices, to_next_slab(): return lax.ppermute(value, ('ctx', 'pipe'), pairs)  3.23 us
    pallas_call x1, Pallas kernels, later_of(): call(functools.partial(later_kernel, places), 'later', (jax.ShapeDtypeStr...  2.7 us
    ppermute x8, waiting for transfers between devices, to_next_section(): return lax.ppermute(value, ('ctx', 'pipe'), pairs)  2.58 us
    pallas_call x4, Pallas kernels, finish(): call(functools.partial(finish_kernel, places[0][0], places), 'finish', ja...  2.43 us
    pallas_call x1, Pallas kernels, product_of(): call(product_kernel, 'product', (array(groups, taps, F32), array(wire_row...  1.67 us
    pallas_call x1, Pallas kernels, raw_finish(): call(raw_kernel, 'raw', jax.ShapeDtypeStruct(held.shape, BF16), [SMEM] +...  1.15 us
  transfers between devices with their start and end apart: 12, of which 6 were waited for; matrix products, arithmetic and copies ran while one was open for 0% of the time, Pallas kernels for 23%

profile of v21, /device:TPU:12, one launch (start us, length us, event | category | flops | bytes accessed | tf_op | source)
XLA Modules:
  0.0 32.1 jit_solution(13545971971516305808)
XLA Ops:
  0.0 0.0 copy-start.2
  0.0 0.0 copy-start.3
  0.0 0.0 copy-start.4
  0.0 0.1 lead.1
  0.1 0.0 copy-start
  0.1 0.0 copy-start.1
  0.1 0.9 %collective-permute-start.1 = (bf16[128,3712]{1,0:T(8,128)(2,1)S(1)}, bf16[128,3712]{1,0:T(8,128)(2,1)S(1)}, u32[]{:S(2)}, u32[]{:S(2)}) collective-permute-start(bf16[128,3712]{1,0:T(8,128)(2,1)S(1)} %get-tuple-element.18.refs_5_.refs_3_), channel_id=1, source_target_pairs={{0,4},{8,12},{16,20},{24,28},{2,6},{10,14},{18,22},{26,30}} | collective-permute-start | bytes 2850824 | tf_op jit(solution)/shard_map/ppermute | solution.py:37
  1.0 1.3 %collective-permute-start = (bf16[256,384]{1,0:T(8,128)(2,1)S(1)}, bf16[256,384]{1,0:T(8,128)(2,1)S(1)}, u32[]{:S(2)}, u32[]{:S(2)}) collective-permute-start(bf16[256,384]{1,0:T(8,128)(2,1)S(1)} %get-tuple-element.17.refs_0_), channel_id=1, source_target_pairs={{0,1},{4,5},{8,9},{12,13},{16,17},{20,21},{24,25},{28,29},{2,3},{6... | collective-permute-start | bytes 589832 | tf_op jit(solution)/shard_map/ppermute | solution.py:43
  2.3 0.0 copy-done.2
  2.3 0.0 copy-done.3
  2.3 0.0 copy-done.4
  2.3 1.7 %product.1 = (f32[256,128]{1,0:T(8,128)S(1)}, bf16[32,128]{1,0:T(8,128)(2,1)S(1)}, bf16[128,1920]{1,0:T(8,128)(2,1)S(1)}, bf16[128,1792]{1,0:T(8,128)(2,1)S(1)}, bf16[128,384]{1,0:T(8,128)(2,1)S(1)}) custom-call(bf16[1,128,4096]{2,1,0:T(8,128)(2,1)} %refs_0_.9, bf16[1,128,4096]{2,1,0:T(8,128)(2,1)} %refs_1_.1, bf16[1,256,128]{2,1,0:T(8,128)(2,1)S(1)} %copy-done.2, ...), custom_call_target="tpu_custom_call" | custom-call | flops 1024 | bytes 1024 | tf_op jit(solution)/shard_map/product/pallas_call | solution.py:177
  4.7 0.0 collective-permute-done.1.refs_2_
  4.7 0.0 copy-done
  4.7 0.0 copy-done.1
  4.7 0.7 %collective-permute-start.5 = (bf16[128,1792]{1,0:T(8,128)(2,1)S(1)}, bf16[128,1792]{1,0:T(8,128)(2,1)S(1)}, u32[]{:S(2)}, u32[]{:S(2)}) collective-permute-start(bf16[128,1792]{1,0:T(8,128)(2,1)S(1)} %own.6._.refs_9_), channel_id=1, source_target_pairs={{4,5},{12,13},{20,21},{28,29},{6,7},{14,15},{22,23},{30,31}} | collective-permute-start | bytes 1376264 | tf_op jit(solution)/shard_map/ppermute | solution.py:43
  5.4 2.3 %collective-permute-start.2 = (bf16[128,1920]{1,0:T(8,128)(2,1)S(1)}, bf16[128,1920]{1,0:T(8,128)(2,1)S(1)}, u32[]{:S(2)}, u32[]{:S(2)}) collective-permute-start(bf16[128,1920]{1,0:T(8,128)(2,1)S(1)} %hold.5.refs_6_.refs_3_), channel_id=1, source_target_pairs={{4,8},{12,16},{20,24},{1,5},{9,13},{17,21},{25,29},{5,9},{13,17},{... | collective-permute-start | bytes 1474568 | tf_op jit(solution)/shard_map/ppermute | solution.py:37
  7.8 0.7 %collective-permute-start.6 = (bf16[128,1920]{1,0:T(8,128)(2,1)S(1)}, bf16[128,1920]{1,0:T(8,128)(2,1)S(1)}, u32[]{:S(2)}, u32[]{:S(2)}) collective-permute-start(bf16[128,1920]{1,0:T(8,128)(2,1)S(1)} %own.7.refs_7_.refs_10_), channel_id=1, source_target_pairs={{4,5},{12,13},{20,21},{28,29},{6,7},{14,15},{22,23},{30,31}} | collective-permute-start | bytes 1474568 | tf_op jit(solution)/shard_map/ppermute | solution.py:43
  8.5 1.3 %collective-permute-done.refs_1_ = bf16[256,384]{1,0:T(8,128)(2,1)S(1)} collective-permute-done((bf16[256,384]{1,0:T(8,128)(2,1)S(1)}, bf16[256,384]{1,0:T(8,128)(2,1)S(1)}, u32[]{:S(2)}, u32[]{:S(2)}) %collective-permute-start) | collective-permute-done | bytes 196640 | tf_op jit(solution)/shard_map/ppermute | solution.py:43
  9.9 2.5 %collective-permute-start.3 = (bf16[128,1792]{1,0:T(8,128)(2,1)S(1)}, bf16[128,1792]{1,0:T(8,128)(2,1)S(1)}, u32[]{:S(2)}, u32[]{:S(2)}) collective-permute-start(bf16[128,1792]{1,0:T(8,128)(2,1)S(1)} %hold.6._.refs_5_), channel_id=1, source_target_pairs={{4,8},{12,16},{20,24},{1,5},{9,13},{17,21},{25,29},{5,9},{13,17},{... | collective-permute-start | bytes 1376264 | tf_op jit(solution)/shard_map/ppermute | solution.py:37
  12.4 3.1 %collective-permute-start.4 = (bf16[128,768]{1,0:T(8,128)(2,1)S(1)}, bf16[128,768]{1,0:T(8,128)(2,1)S(1)}, u32[]{:S(2)}, u32[]{:S(2)}) collective-permute-start(bf16[128,768]{1,0:T(8,128)(2,1)S(1)} %hold.7.refs_5_), channel_id=1, source_target_pairs={{0,4},{8,12},{16,20},{24,28},{4,8},{12,16},{20,24},{1,5},{9,13},{1... | collective-permute-start | bytes 589832 | tf_op jit(solution)/shard_map/ppermute | solution.py:37
  15.4 0.0 collective-permute-done.5._.refs_1_
  15.5 0.1 collective-permute-done.2.refs_2_
  15.6 1.3 %collective-permute-start.11 = (bf16[128,1024]{1,0:T(8,128)(2,1)S(1)}, bf16[128,1024]{1,0:T(8,128)(2,1)S(1)}, u32[]{:S(2)}, u32[]{:S(2)}) collective-permute-start(bf16[128,1024]{1,0:T(8,128)(2,1)S(1)} %own.8.refs_6_.refs_11_), channel_id=1, source_target_pairs={{0,1},{8,9},{16,17},{24,25},{2,3},{10,11},{18,19},{26,27}} | collective-permute-start | bytes 786440 | tf_op jit(solution)/shard_map/ppermute | solution.py:43
  16.9 1.3 %collective-permute-start.10 = (bf16[136,896]{1,0:T(8,128)(2,1)S(1)}, bf16[136,896]{1,0:T(8,128)(2,1)S(1)}, u32[]{:S(2)}, u32[]{:S(2)}) collective-permute-start(bf16[136,896]{1,0:T(8,128)(2,1)S(1)} %own.9.refs_6_.refs_12_), channel_id=1, source_target_pairs={{0,1},{8,9},{16,17},{24,25},{2,3},{10,11},{18,19},{26,27}} | collective-permute-start | bytes 731144 | tf_op jit(solution)/shard_map/ppermute | solution.py:43
  18.2 2.3 %collective-permute-done.3.refs_2_.refs_4_ = bf16[128,1792]{1,0:T(8,128)(2,1)S(1)} collective-permute-done((bf16[128,1792]{1,0:T(8,128)(2,1)S(1)}, bf16[128,1792]{1,0:T(8,128)(2,1)S(1)}, u32[]{:S(2)}, u32[]{:S(2)}) %collective-permute-start.3) | collective-permute-done | bytes 458784 | tf_op jit(solution)/shard_map/ppermute | solution.py:37
  20.5 0.0 collective-permute-done.6.refs_7_.refs_2_
  20.5 1.3 %collective-permute-start.8 = (bf16[128,1280]{1,0:T(8,128)(2,1)S(1)}, bf16[128,1280]{1,0:T(8,128)(2,1)S(1)}, u32[]{:S(2)}, u32[]{:S(2)}) collective-permute-start(bf16[128,1280]{1,0:T(8,128)(2,1)S(1)} %own.10.refs_6_.refs_13_), channel_id=1, source_target_pairs={{0,1},{8,9},{16,17},{24,25},{2,3},{10,11},{18,19},{26,27}} | collective-permute-start | bytes 983048 | tf_op jit(solution)/shard_map/ppermute | solution.py:43
  21.8 0.8 %collective-permute-done.4.refs_7_.refs_6_.refs_4_ = bf16[128,768]{1,0:T(8,128)(2,1)S(1)} collective-permute-done((bf16[128,768]{1,0:T(8,128)(2,1)S(1)}, bf16[128,768]{1,0:T(8,128)(2,1)S(1)}, u32[]{:S(2)}, u32[]{:S(2)}) %collective-permute-start.4) | collective-permute-done | bytes 196640 | tf_op jit(solution)/shard_map/ppermute | solution.py:37
  22.6 1.3 %collective-permute-start.7 = (bf16[128,512]{1,0:T(8,128)(2,1)S(1)}, bf16[128,512]{1,0:T(8,128)(2,1)S(1)}, u32[]{:S(2)}, u32[]{:S(2)}) collective-permute-start(bf16[128,512]{1,0:T(8,128)(2,1)S(1)} %own.11.refs_14_._), channel_id=1, source_target_pairs={{0,1},{8,9},{16,17},{24,25},{2,3},{10,11},{18,19},{26,27}} | collective-permute-start | bytes 393224 | tf_op jit(solution)/shard_map/ppermute | solution.py:43
  23.9 0.7 %collective-permute-start.9 = (bf16[32,128]{1,0:T(8,128)(2,1)S(1)}, bf16[32,128]{1,0:T(8,128)(2,1)S(1)}, u32[]{:S(2)}, u32[]{:S(2)}) collective-permute-start(bf16[32,128]{1,0:T(8,128)(2,1)S(1)} %hold.9), channel_id=1, source_target_pairs={{4,5},{12,13},{20,21},{28,29},{6,7},{14,15},{22,23},{30,31}} | collective-permute-start | bytes 24584 | tf_op jit(solution)/shard_map/ppermute | solution.py:43
  24.6 2.7 %later.1 = (bf16[1,128,4096]{2,1,0:T(8,128)(2,1)}, f32[128,4096]{1,0:T(8,128)S(1)}) custom-call(s32[1]{0:T(128)S(6)} %copy.31.refs_0_, f32[256,128]{1,0:T(8,128)S(1)} %get-tuple-element.22.refs_1_, bf16[128,1920]{1,0:T(8,128)(2,1)S(1)} %collective-permute-done.2.refs_2_, bf16[128,1920]{1,0:T(8,128)(2,1)S(1)} %hold.5.refs_6_.refs_3_, ...), custom_call_target="tpu_custom_call" | custom-call | flops 20000000000 | bytes 1024 | tf_op jit(solution)/shard_map/later/pallas_call | solution.py:365
  27.3 0.0 collective-permute-done.10.refs_2_.refs_3_
  27.3 0.0 collective-permute-done.11.refs_1_
  27.3 0.9 %finish.5.refs_9_ = bf16[1,128,4096]{2,1,0:T(8,128)(2,1)} custom-call(f32[128,4096]{1,0:T(8,128)S(1)} %get-tuple-element.26.refs_0_.refs_7_, bf16[128,1024]{1,0:T(8,128)(2,1)S(1)} %collective-permute-done.11.refs_1_, bf16[136,896]{1,0:T(8,128)(2,1)S(1)} %collective-permute-done.10.refs_2_.refs_3_, ...), custom_call_target="tpu_custom_call", output_to_operand_aliasing={{}: (3, {})} | custom-call | flops 20000000000 | bytes 1024 | tf_op jit(solution)/shard_map/finish/pallas_call | solution.py:448
  28.2 0.0 collective-permute-done.9.refs_2_
  28.3 1.1 %raw.1.refs_2_ = bf16[1,128,4096]{2,1,0:T(8,128)(2,1)} custom-call(s32[1]{0:T(128)S(6)} %copy.31.refs_0_, f32[256,128]{1,0:T(8,128)S(1)} %get-tuple-element.22.refs_1_, bf16[32,128]{1,0:T(8,128)(2,1)S(1)} %collective-permute-done.9.refs_2_, bf16[136,896]{1,0:T(8,128)(2,1)S(1)} %collective-permute-done.10.refs_2_.refs_3_, ...), custom_call_target="tpu_custom_call", output_to_operand_aliasing={{}: (9, {})} | custom-call | flops 20000000000 | bytes 1024 | tf_op jit(solution)/shard_map/raw/pallas_call | solution.py:413
  29.4 0.6 %collective-permute-done.8.refs_1_ = bf16[128,1280]{1,0:T(8,128)(2,1)S(1)} collective-permute-done((bf16[128,1280]{1,0:T(8,128)(2,1)S(1)}, bf16[128,1280]{1,0:T(8,128)(2,1)S(1)}, u32[]{:S(2)}, u32[]{:S(2)}) %collective-permute-start.8) | collective-permute-done | bytes 327712 | tf_op jit(solution)/shard_map/ppermute | solution.py:43
  30.0 0.8 %finish.6.refs_2_ = bf16[1,128,4096]{2,1,0:T(8,128)(2,1)} custom-call(f32[128,4096]{1,0:T(8,128)S(1)} %get-tuple-element.26.refs_0_.refs_7_, bf16[128,1280]{1,0:T(8,128)(2,1)S(1)} %collective-permute-done.8.refs_1_, bf16[1,128,4096]{2,1,0:T(8,128)(2,1)} %raw.1.refs_2_), custom_call_target="tpu_custom_call", output_to_operand_aliasing={{}: (2, {})} | custom-call | flops 20000000000 | bytes 1024 | tf_op jit(solution)/shard_map/finish/pallas_call | solution.py:448
  30.9 0.6 %collective-permute-done.7.refs_1_ = bf16[128,512]{1,0:T(8,128)(2,1)S(1)} collective-permute-done((bf16[128,512]{1,0:T(8,128)(2,1)S(1)}, bf16[128,512]{1,0:T(8,128)(2,1)S(1)}, u32[]{:S(2)}, u32[]{:S(2)}) %collective-permute-start.7) | collective-permute-done | bytes 131104 | tf_op jit(solution)/shard_map/ppermute | solution.py:43
  31.4 0.7 %finish.7 = bf16[1,128,4096]{2,1,0:T(8,128)(2,1)} custom-call(f32[128,4096]{1,0:T(8,128)S(1)} %get-tuple-element.26.refs_0_.refs_7_, bf16[128,512]{1,0:T(8,128)(2,1)S(1)} %collective-permute-done.7.refs_1_, bf16[1,128,4096]{2,1,0:T(8,128)(2,1)} %finish.6.refs_2_), custom_call_target="tpu_custom_call", output_to_operand_aliasing={{}: (2, {})} | custom-call | flops 20000000000 | bytes 1024 | tf_op jit(solution)/shard_map/finish/pallas_call | solution.py:448
  (13 shorter events, 0.1 us)
Async XLA Ops:
  0.0 2.3 %copy-start.2 = (bf16[1,256,128]{2,1,0:T(8,128)(2,1)S(1)}, bf16[1,256,128]{2,1,0:T(8,128)(2,1)}, u32[]{:S(2)}) copy-start(bf16[1,256,128]{2,1,0:T(8,128)(2,1)} %refs_3_.3) | copy-start | bytes 196612
  0.0 2.3 %copy-start.3 = (f32[1,256]{1,0:T(1,128)S(1)}, f32[1,256]{1,0:T(1,128)}, u32[]{:S(2)}) copy-start(f32[1,256]{1,0:T(1,128)} %refs_4_.11) | copy-start | bytes 3076
  0.0 2.3 %copy-start.4 = (s32[1,256]{1,0:T(1,128)S(1)}, s32[1,256]{1,0:T(1,128)}, u32[]{:S(2)}) copy-start(s32[1,256]{1,0:T(1,128)} %refs_5_.9) | copy-start | bytes 3076
  0.1 4.6 %copy-start = (bf16[1,128,4096]{2,1,0:T(8,128)(2,1)S(1)}, bf16[1,128,4096]{2,1,0:T(8,128)(2,1)}, u32[]{:S(2)}) copy-start(bf16[1,128,4096]{2,1,0:T(8,128)(2,1)} %refs_8_.2) | copy-start | bytes 3145732
  0.1 4.6 %copy-start.1 = (bf16[128,4096]{1,0:T(8,128)(2,1)S(1)}, bf16[128,4096]{1,0:T(8,128)(2,1)}, u32[]{:S(2)}) copy-start(bf16[128,4096]{1,0:T(8,128)(2,1)} %refs_8_.3) | copy-start | bytes 3145732
  0.1 4.5 %collective-permute-start.1 = (bf16[128,3712]{1,0:T(8,128)(2,1)S(1)}, bf16[128,3712]{1,0:T(8,128)(2,1)S(1)}, u32[]{:S(2)}, u32[]{:S(2)}) collective-permute-start(bf16[128,3712]{1,0:T(8,128)(2,1)S(1)} %get-tuple-element.18.refs_5_.refs_3_), channel_id=1, source_target_pairs={{0,4},{8,12},{16,20},{24,28},{2,6},{10,14},{18,22},{26,30}} | collective-permute-start | bytes 2850824 | tf_op jit(solution)/shard_map/ppermute | solution.py:37
  1.0 8.9 %collective-permute-start = (bf16[256,384]{1,0:T(8,128)(2,1)S(1)}, bf16[256,384]{1,0:T(8,128)(2,1)S(1)}, u32[]{:S(2)}, u32[]{:S(2)}) collective-permute-start(bf16[256,384]{1,0:T(8,128)(2,1)S(1)} %get-tuple-element.17.refs_0_), channel_id=1, source_target_pairs={{0,1},{4,5},{8,9},{12,13},{16,17},{20,21},{24,25},{28,29},{2,3},{6... | collective-permute-start | bytes 589832 | tf_op jit(solution)/shard_map/ppermute | solution.py:43
  4.7 10.7 %collective-permute-start.5 = (bf16[128,1792]{1,0:T(8,128)(2,1)S(1)}, bf16[128,1792]{1,0:T(8,128)(2,1)S(1)}, u32[]{:S(2)}, u32[]{:S(2)}) collective-permute-start(bf16[128,1792]{1,0:T(8,128)(2,1)S(1)} %own.6._.refs_9_), channel_id=1, source_target_pairs={{4,5},{12,13},{20,21},{28,29},{6,7},{14,15},{22,23},{30,31}} | collective-permute-start | bytes 1376264 | tf_op jit(solution)/shard_map/ppermute | solution.py:43
  5.4 10.1 %collective-permute-start.2 = (bf16[128,1920]{1,0:T(8,128)(2,1)S(1)}, bf16[128,1920]{1,0:T(8,128)(2,1)S(1)}, u32[]{:S(2)}, u32[]{:S(2)}) collective-permute-start(bf16[128,1920]{1,0:T(8,128)(2,1)S(1)} %hold.5.refs_6_.refs_3_), channel_id=1, source_target_pairs={{4,8},{12,16},{20,24},{1,5},{9,13},{17,21},{25,29},{5,9},{13,17},{... | collective-permute-start | bytes 1474568 | tf_op jit(solution)/shard_map/ppermute | solution.py:37
  7.8 12.7 %collective-permute-start.6 = (bf16[128,1920]{1,0:T(8,128)(2,1)S(1)}, bf16[128,1920]{1,0:T(8,128)(2,1)S(1)}, u32[]{:S(2)}, u32[]{:S(2)}) collective-permute-start(bf16[128,1920]{1,0:T(8,128)(2,1)S(1)} %own.7.refs_7_.refs_10_), channel_id=1, source_target_pairs={{4,5},{12,13},{20,21},{28,29},{6,7},{14,15},{22,23},{30,31}} | collective-permute-start | bytes 1474568 | tf_op jit(solution)/shard_map/ppermute | solution.py:43
  9.9 10.6 %collective-permute-start.3 = (bf16[128,1792]{1,0:T(8,128)(2,1)S(1)}, bf16[128,1792]{1,0:T(8,128)(2,1)S(1)}, u32[]{:S(2)}, u32[]{:S(2)}) collective-permute-start(bf16[128,1792]{1,0:T(8,128)(2,1)S(1)} %hold.6._.refs_5_), channel_id=1, source_target_pairs={{4,8},{12,16},{20,24},{1,5},{9,13},{17,21},{25,29},{5,9},{13,17},{... | collective-permute-start | bytes 1376264 | tf_op jit(solution)/shard_map/ppermute | solution.py:37
  12.4 10.2 %collective-permute-start.4 = (bf16[128,768]{1,0:T(8,128)(2,1)S(1)}, bf16[128,768]{1,0:T(8,128)(2,1)S(1)}, u32[]{:S(2)}, u32[]{:S(2)}) collective-permute-start(bf16[128,768]{1,0:T(8,128)(2,1)S(1)} %hold.7.refs_5_), channel_id=1, source_target_pairs={{0,4},{8,12},{16,20},{24,28},{4,8},{12,16},{20,24},{1,5},{9,13},{1... | collective-permute-start | bytes 589832 | tf_op jit(solution)/shard_map/ppermute | solution.py:37
  15.6 11.8 %collective-permute-start.11 = (bf16[128,1024]{1,0:T(8,128)(2,1)S(1)}, bf16[128,1024]{1,0:T(8,128)(2,1)S(1)}, u32[]{:S(2)}, u32[]{:S(2)}) collective-permute-start(bf16[128,1024]{1,0:T(8,128)(2,1)S(1)} %own.8.refs_6_.refs_11_), channel_id=1, source_target_pairs={{0,1},{8,9},{16,17},{24,25},{2,3},{10,11},{18,19},{26,27}} | collective-permute-start | bytes 786440 | tf_op jit(solution)/shard_map/ppermute | solution.py:43
  16.9 10.4 %collective-permute-start.10 = (bf16[136,896]{1,0:T(8,128)(2,1)S(1)}, bf16[136,896]{1,0:T(8,128)(2,1)S(1)}, u32[]{:S(2)}, u32[]{:S(2)}) collective-permute-start(bf16[136,896]{1,0:T(8,128)(2,1)S(1)} %own.9.refs_6_.refs_12_), channel_id=1, source_target_pairs={{0,1},{8,9},{16,17},{24,25},{2,3},{10,11},{18,19},{26,27}} | collective-permute-start | bytes 731144 | tf_op jit(solution)/shard_map/ppermute | solution.py:43
  20.5 9.5 %collective-permute-start.8 = (bf16[128,1280]{1,0:T(8,128)(2,1)S(1)}, bf16[128,1280]{1,0:T(8,128)(2,1)S(1)}, u32[]{:S(2)}, u32[]{:S(2)}) collective-permute-start(bf16[128,1280]{1,0:T(8,128)(2,1)S(1)} %own.10.refs_6_.refs_13_), channel_id=1, source_target_pairs={{0,1},{8,9},{16,17},{24,25},{2,3},{10,11},{18,19},{26,27}} | collective-permute-start | bytes 983048 | tf_op jit(solution)/shard_map/ppermute | solution.py:43
  22.6 8.8 %collective-permute-start.7 = (bf16[128,512]{1,0:T(8,128)(2,1)S(1)}, bf16[128,512]{1,0:T(8,128)(2,1)S(1)}, u32[]{:S(2)}, u32[]{:S(2)}) collective-permute-start(bf16[128,512]{1,0:T(8,128)(2,1)S(1)} %own.11.refs_14_._), channel_id=1, source_target_pairs={{0,1},{8,9},{16,17},{24,25},{2,3},{10,11},{18,19},{26,27}} | collective-permute-start | bytes 393224 | tf_op jit(solution)/shard_map/ppermute | solution.py:43
  23.9 4.3 %collective-permute-start.9 = (bf16[32,128]{1,0:T(8,128)(2,1)S(1)}, bf16[32,128]{1,0:T(8,128)(2,1)S(1)}, u32[]{:S(2)}, u32[]{:S(2)}) collective-permute-start(bf16[32,128]{1,0:T(8,128)(2,1)S(1)} %hold.9), channel_id=1, source_target_pairs={{4,5},{12,13},{20,21},{28,29},{6,7},{14,15},{22,23},{30,31}} | collective-permute-start | bytes 24584 | tf_op jit(solution)/shard_map/ppermute | solution.py:43
